TPU v7x, 32 devices: a whole 2x2x4 slice. The times are simulated.
32 devices in a mesh: parts: 2 (over y), blk: 16 (over z, x, core).
Axes of the slice: x: 2, y: 2, z: 4, core: 2. Of those that a mesh axis runs over, the one named last changes fastest.
Arguments:
- embedding: float32 [16384, 768], P(('parts', 'blk')), parts along dimension 0
- row_owner: int32 [16384], P(('parts', 'blk')), parts along dimension 0, may hold values from 0 to 15, as said below
- cluster_id: int32 [16384], P(('parts', 'blk')), parts along dimension 0, may hold values from 0 to 63, as said below
Outputs:
- nearest: float32 [16384], P(('parts', 'blk')), parts along dimension 0
There are 2 independent parts, one for each index of `parts`. A program takes and returns all parts, laid end to end along the dimension named above; each array names one. Nothing has to cross between parts.
Inputs may be any that keep to these rules, and one draw needn't show every extreme that they name: Among the 512 rows of one blk device at most 64 have the same owner, and some owner gets exactly 64; row_owner // 4 equals cluster_id // 16. cluster_id // 16 is the owner group of the cluster.
All inputs are finite; a program needn't handle non-finite values.
Results may differ from a plain program's by a relative error of at most 0.0003.
Values may be sent and summed in bfloat16 or wider, within the bound.
No kernel may reach another device: no remote copies, remote signals or barrier semaphores. Data moves between devices by JAX's collectives and lax.ppermute only.
A program may use at most 64 MiB of HBM per device.

v0:
```python
import jax
import jax.numpy as jnp
from jax import lax
from jax.experimental import pallas as pl
from jax.experimental.pallas import tpu as pltpu
from jax.sharding import PartitionSpec as P

GROUP = 4
UNITS = (4, 4, 4, 2, 2)
NT = (((1,), (1,)), ((), ()))


def iota(shape, axis):
    return lax.broadcasted_iota(jnp.int32, shape, axis)


def spans(widths):
    start, out = 0, []
    for width in widths:
        out.append((start, width))
        start += width
    return out


def label_kernel(groups, cap, pieces, owner_ref, cluster_ref, *refs):
    labels, slot_ref = refs[:-1], refs[-1]
    rows = owner_ref.shape[1]
    earlier = (iota((rows, rows), 0) < iota((rows, rows), 1)).astype(jnp.bfloat16)
    mine = lax.axis_index("blk") // GROUP
    rel = ((owner_ref[...] >> 2) - mine + groups) & (groups - 1)
    place = jnp.where(rel > groups // 2, 2 * (groups - rel), jnp.maximum(2 * rel - 1, 0))
    member = iota((max(groups, 16), rows), 0) == place
    count = jnp.dot(member.astype(jnp.bfloat16), earlier, preferred_element_type=jnp.float32)
    rank = jnp.sum(jnp.where(member, count, 0.0), axis=0, keepdims=True)
    slot = place * cap + rank.astype(jnp.int32)
    slot_ref[...] = slot
    label = ((cluster_ref[...] & 15) + 1).astype(jnp.float32).astype(jnp.bfloat16)
    label = jnp.broadcast_to(label, (16, rows))
    for ref, (start, size) in zip(labels, pieces):
        hot = (iota((size, rows), 0) + start == slot).astype(jnp.bfloat16)
        packed = lax.dot_general(label, hot, NT, preferred_element_type=jnp.float32)
        ref[...] = packed[0:1, :] - 1.0


def place_labels(groups, cap, pieces, owner, cluster):
    (rows,) = owner.shape
    return pl.pallas_call(
        lambda *refs: label_kernel(groups, cap, pieces, *refs),
        out_shape=[jax.ShapeDtypeStruct((1, n), jnp.float32) for _, n in pieces]
        + [jax.ShapeDtypeStruct((1, rows), jnp.int32)],
        name="labels",
    )(owner.reshape(1, rows), cluster.reshape(1, rows))


def pack_kernel(units, emb_ref, slot_ref, *blocks):
    x = emb_ref[...]
    squares = jnp.sum(x * x, axis=1, keepdims=True)
    unit = (x * lax.rsqrt(squares + 1e-06)).astype(jnp.bfloat16)
    slot = slot_ref[...]
    for ref, (start, size) in zip(blocks, units):
        hot = (iota((size, x.shape[0]), 0) + start == slot).astype(jnp.bfloat16)
        ref[...] = jnp.dot(hot, unit, preferred_element_type=jnp.float32).astype(jnp.bfloat16)


def pack(units, embedding, slot):
    width = embedding.shape[1]
    return pl.pallas_call(
        lambda *refs: pack_kernel(units, *refs),
        out_shape=[jax.ShapeDtypeStruct((n, width), jnp.bfloat16) for _, n in units],
        name="pack",
    )(embedding, slot)


def compare_kernel(units, outs, *refs):
    last = len(units) - 1
    labels, refs = refs[:4], refs[4:]
    keys, refs = refs[: 4 * last + 4], refs[4 * last + 4 :]
    if last:
        best_ref, refs = refs[0], refs[1:]
    columns = []
    for low, width in units:
        wide = jnp.concatenate([ref[:, low : low + width] for ref in labels] * 2, axis=0)
        columns.append(wide.T)

    def tile(q, k, peer, best):
        low, width = units[q]
        scores = lax.dot_general(
            keys[4 * k + peer][...], keys[4 * q][...], NT, preferred_element_type=jnp.float32
        )
        allowed = columns[k][:, peer : peer + 1] == labels[0][:, low : low + width]
        if peer == 0 and q == k:
            allowed = allowed & (iota(scores.shape, 0) != iota(scores.shape, 1))
        return jnp.maximum(best, jnp.max(jnp.where(allowed, scores, -1.0), axis=0, keepdims=True))

    bests = []
    for q, (low, width) in enumerate(units):
        best = best_ref[:, low : low + width] if q < last else jnp.full((1, width), -1.0)
        for k in range(last + 1) if q == last else [last]:
            for peer in range(4):
                best = tile(q, k, peer, best)
        bests.append(best)
    for ref, (low, width) in zip(refs, outs):
        for q, (a, n) in enumerate(units):
            x, y = max(low, a), min(low + width, a + n)
            if x < y:
                ref[:, x - low : y - low] = bests[q][:, x - a : y - a]


def compare(units, outs, labels, keys, best):
    start, size = units[-1]
    width = keys[0].shape[1]
    pairs = 4 * size * (start + size) + 4 * start * size
    return pl.pallas_call(
        lambda *refs: compare_kernel(units, outs, *refs),
        out_shape=[jax.ShapeDtypeStruct((1, n), jnp.float32) for _, n in outs],
        cost_estimate=pl.CostEstimate(
            flops=2 * pairs * width,
            bytes_accessed=8 * (start + size) * width,
            transcendentals=0,
        ),
        name=f"compare{len(units)}",
    )(*labels, *keys, *best)


def unpack_kernel(slot_ref, *refs):
    out_ref = refs[-1]
    slot = slot_ref[...]
    rows = slot.shape[1]
    total = jnp.zeros((8, rows), jnp.float32)
    start = 0
    for ref in refs[:-1]:
        size = ref.shape[1]
        column = jnp.broadcast_to(ref[...], (8, size)).T[:, 0:1]
        hit = iota((size, rows), 0) + start == slot
        part = jnp.where(hit, column, 0.0)
        total = total + jnp.sum(part.reshape(size // 8, 8, rows), axis=0)
        start += size
    out_ref[...] = jnp.sum(total, axis=0, keepdims=True)


def unpack(slot, backs):
    return pl.pallas_call(
        unpack_kernel,
        out_shape=jax.ShapeDtypeStruct(slot.shape, jnp.float32),
        name="unpack",
    )(slot, *backs)


def join(parts, axis):
    return parts[0] if len(parts) == 1 else jnp.concatenate(parts, axis=axis)


def on_device(embedding, row_owner, cluster_id):
    rows, _ = embedding.shape
    devices = lax.axis_size("blk")
    groups = devices // GROUP
    cap = GROUP * max(2, 2 * rows // devices)
    slots = groups * cap
    units = spans([n * slots // sum(UNITS) for n in UNITS])
    pieces = spans([max(cap, 128)] * (slots // max(cap, 128)))
    shifts = [0] + [(k + 1) // 2 if k % 2 else groups - k // 2 for k in range(1, groups)]

    def shift(array, distance):
        step = distance * GROUP
        return lax.ppermute(array, "blk", [(i, (i + step) % devices) for i in range(devices)])

    def swap(array, mask):
        return lax.ppermute(array, "blk", [(i, i ^ mask) for i in range(devices)])

    def exchange(array, start, axis, sign):
        size, out = array.shape[axis], []
        for k in range(start // cap, (start + size - 1) // cap + 1):
            a, b = max(k * cap - start, 0), min((k + 1) * cap - start, size)
            part = lax.slice_in_dim(array, a, b, axis=axis)
            out.append(shift(part, sign * shifts[k]) if shifts[k] else part)
        return join(out, axis)

    *label, slot = place_labels(groups, cap, pieces, row_owner, cluster_id)
    blocks = pack(units, embedding, slot)
    own = join([exchange(l, low, 1, 1) for l, (low, _) in zip(label, pieces)], 1)
    across = swap(own, 2)
    labels = [own, swap(own, 1), across, swap(across, 1)]

    queries = []
    for u, (start, _) in enumerate(units):
        block = blocks[u]
        if u == 2:
            block, labels = lax.optimization_barrier((block, labels))
        if u >= 3:
            block, queries[u - 2] = lax.optimization_barrier((block, queries[u - 2]))
        queries.append(exchange(block, start, 0, 1))
    keys, best = [], []
    for u, (start, size) in enumerate(units):
        across = swap(queries[u], 2)
        keys += [queries[u], swap(queries[u], 1), across, swap(across, 1)]
        outs = pieces if u == len(units) - 1 else [(0, start + size)]
        best = compare(units[: u + 1], outs, labels, keys, best)
    backs = [exchange(b, low, 1, -1) for b, (low, _) in zip(best, pieces)]
    return unpack(slot, backs).reshape(rows)


def solution(mesh):
    placed = (P(("parts", "blk"), None), P(("parts", "blk")), P(("parts", "blk")))
    return jax.shard_map(
        on_device, mesh=mesh, in_specs=placed, out_specs=P(("parts", "blk")), check_vma=False
    )
```

profile of v0, /device:TPU:0, one launch (start us, length us, event | category | flops | bytes accessed | tf_op | source)
XLA Modules:
  0.0 92.3 jit_solution(11665279894653932678)
XLA Ops:
  0.0 1.9 %labels.1 = (f32[1,256]{1,0:T(1,128)}, f32[1,256]{1,0:T(1,128)}, f32[1,256]{1,0:T(1,128)}, f32[1,256]{1,0:T(1,128)}, s32[1,512]{1,0:T(1,128)}) custom-call(s32[1,512]{1,0:T(1,128)} %bitcast.3, s32[1,512]{1,0:T(1,128)} %bitcast.4), custom_call_target="tpu_custom_call" | custom-call | tf_op jit(solution)/shard_map/labels/pallas_call | solution.py:47
  1.9 3.0 %collective-permute-start = (f32[1,256]{1,0:T(1,128)}, f32[1,256]{1,0:T(1,128)S(1)}, u32[]{:S(2)}, u32[]{:S(2)}) collective-permute-start(f32[1,256]{1,0:T(1,128)} %get-tuple-element.31), channel_id=1, source_target_pairs={{0,4},{1,5},{2,6},{3,7},{4,8},{5,9},{6,10},{7,11},{8,12},{9,13},{1... | collective-permute-start | bytes 3080 | tf_op jit(solution)/shard_map/ppermute | solution.py:165
  4.9 2.1 %collective-permute-start.1 = (f32[1,256]{1,0:T(1,128)}, f32[1,256]{1,0:T(1,128)S(1)}, u32[]{:S(2)}, u32[]{:S(2)}) collective-permute-start(f32[1,256]{1,0:T(1,128)} %get-tuple-element.32), channel_id=1, source_target_pairs={{0,12},{1,13},{2,14},{3,15},{4,0},{5,1},{6,2},{7,3},{8,4},{9,5},{1... | collective-permute-start | bytes 3080 | tf_op jit(solution)/shard_map/ppermute | solution.py:165
  7.0 1.0 %collective-permute-start.2 = (f32[1,256]{1,0:T(1,128)}, f32[1,256]{1,0:T(1,128)S(1)}, u32[]{:S(2)}, u32[]{:S(2)}) collective-permute-start(f32[1,256]{1,0:T(1,128)} %get-tuple-element.33), channel_id=1, source_target_pairs={{0,8},{1,9},{2,10},{3,11},{4,12},{5,13},{6,14},{7,15},{8,0},{9,1},... | collective-permute-start | bytes 3080 | tf_op jit(solution)/shard_map/ppermute | solution.py:165
  8.0 3.3 %pack.1 = (bf16[256,768]{1,0:T(8,128)(2,1)}, bf16[256,768]{1,0:T(8,128)(2,1)}, bf16[256,768]{1,0:T(8,128)(2,1)}, bf16[128,768]{1,0:T(8,128)(2,1)}, bf16[128,768]{1,0:T(8,128)(2,1)}) custom-call(f32[512,768]{1,0:T(8,128)} %refs_0_.1, s32[1,512]{1,0:T(1,128)} %get-tuple-element.28.refs_1_.slot_ref), custom_call_target="tpu_custom_call" | custom-call | tf_op jit(solution)/shard_map/pack/pallas_call | solution.py:67
  11.2 1.6 %collective-permute-start.9 = (bf16[256,768]{1,0:T(8,128)(2,1)}, bf16[256,768]{1,0:T(8,128)(2,1)S(1)}, u32[]{:S(2)}, u32[]{:S(2)}) collective-permute-start(bf16[256,768]{1,0:T(8,128)(2,1)} %get-tuple-element.40), channel_id=1, source_target_pairs={{0,4},{1,5},{2,6},{3,7},{4,8},{5,9},{6,10},{7,11},{8,12},{9,13},{1... | collective-permute-start | bytes 1179656 | tf_op jit(solution)/shard_map/ppermute | solution.py:165
  12.8 0.0 collective-permute-done.1
  12.9 1.6 %collective-permute-start.4 = (f32[1,1024]{1,0:T(1,128)S(1)}, f32[1,1024]{1,0:T(1,128)S(1)}, u32[]{:S(2)}, u32[]{:S(2)}) collective-permute-start(f32[1,1024]{1,0:T(1,128)S(1)} %constant_dynamic-update-slice_fusion.refs_0_), channel_id=1, source_target_pairs={{0,2},{1,3},{2,0},{3,1},{4,6},{5,7},{6,4},{7,5},{8,10},{9,11},{10,... | collective-permute-start | bytes 12296 | tf_op jit(solution)/shard_map/ppermute | solution.py:168
  14.4 0.0 collective-permute-start.3
  14.4 2.1 %collective-permute-done.4.refs_2_ = f32[1,1024]{1,0:T(1,128)S(1)} collective-permute-done((f32[1,1024]{1,0:T(1,128)S(1)}, f32[1,1024]{1,0:T(1,128)S(1)}, u32[]{:S(2)}, u32[]{:S(2)}) %collective-permute-start.4) | collective-permute-done | bytes 4128 | tf_op jit(solution)/shard_map/ppermute | solution.py:168
  16.6 0.0 collective-permute-start.5
  16.6 0.0 collective-permute-done.3.refs_1_
  16.6 1.1 %collective-permute-done.5.refs_3_ = f32[1,1024]{1,0:T(1,128)S(1)} collective-permute-done((f32[1,1024]{1,0:T(1,128)S(1)}, f32[1,1024]{1,0:T(1,128)S(1)}, u32[]{:S(2)}, u32[]{:S(2)}) %collective-permute-start.5) | collective-permute-done | bytes 4128 | tf_op jit(solution)/shard_map/ppermute | solution.py:168
  17.7 2.2 %collective-permute-start.13 = (bf16[256,768]{1,0:T(8,128)(2,1)}, bf16[256,768]{1,0:T(8,128)(2,1)S(1)}, u32[]{:S(2)}, u32[]{:S(2)}) collective-permute-start(bf16[256,768]{1,0:T(8,128)(2,1)} %get-tuple-element.43), channel_id=1, source_target_pairs={{0,12},{1,13},{2,14},{3,15},{4,0},{5,1},{6,2},{7,3},{8,4},{9,5},{1... | collective-permute-start | bytes 1179656 | tf_op jit(solution)/shard_map/ppermute | solution.py:165
  20.0 1.5 %collective-permute-start.7 = (bf16[256,768]{1,0:T(8,128)(2,1)}, bf16[256,768]{1,0:T(8,128)(2,1)S(1)}, u32[]{:S(2)}, u32[]{:S(2)}) collective-permute-start(bf16[256,768]{1,0:T(8,128)(2,1)} %get-tuple-element.38.refs_4_), channel_id=1, source_target_pairs={{0,2},{1,3},{2,0},{3,1},{4,6},{5,7},{6,4},{7,5},{8,10},{9,11},{10,... | collective-permute-start | bytes 1179656 | tf_op jit(solution)/shard_map/ppermute | solution.py:168
  21.5 3.8 %collective-permute-done.9.refs_8_ = bf16[256,768]{1,0:T(8,128)(2,1)S(1)} collective-permute-done((bf16[256,768]{1,0:T(8,128)(2,1)}, bf16[256,768]{1,0:T(8,128)(2,1)S(1)}, u32[]{:S(2)}, u32[]{:S(2)}) %collective-permute-start.9) | collective-permute-done | bytes 393248 | tf_op jit(solution)/shard_map/ppermute | solution.py:165
  25.3 1.5 %collective-permute-start.11 = (bf16[256,768]{1,0:T(8,128)(2,1)S(1)}, bf16[256,768]{1,0:T(8,128)(2,1)S(1)}, u32[]{:S(2)}, u32[]{:S(2)}) collective-permute-start(bf16[256,768]{1,0:T(8,128)(2,1)S(1)} %collective-permute-done.9.refs_8_), channel_id=1, source_target_pairs={{0,2},{1,3},{2,0},{3,1},{4,6},{5,7},{6,4},{7,5},{8,10},{9,11},{10,... | collective-permute-start | bytes 1179656 | tf_op jit(solution)/shard_map/ppermute | solution.py:168
  26.8 0.0 collective-permute-start.17
  26.8 4.9 %collective-permute-done.13.refs_12_ = bf16[256,768]{1,0:T(8,128)(2,1)S(1)} collective-permute-done((bf16[256,768]{1,0:T(8,128)(2,1)}, bf16[256,768]{1,0:T(8,128)(2,1)S(1)}, u32[]{:S(2)}, u32[]{:S(2)}) %collective-permute-start.13) | collective-permute-done | bytes 393248 | tf_op jit(solution)/shard_map/ppermute | solution.py:165
  31.7 1.5 %collective-permute-start.15 = (bf16[256,768]{1,0:T(8,128)(2,1)S(1)}, bf16[256,768]{1,0:T(8,128)(2,1)S(1)}, u32[]{:S(2)}, u32[]{:S(2)}) collective-permute-start(bf16[256,768]{1,0:T(8,128)(2,1)S(1)} %collective-permute-done.13.refs_12_), channel_id=1, source_target_pairs={{0,2},{1,3},{2,0},{3,1},{4,6},{5,7},{6,4},{7,5},{8,10},{9,11},{10,... | collective-permute-start | bytes 1179656 | tf_op jit(solution)/shard_map/ppermute | solution.py:168
  33.2 0.0 collective-permute-done.7.refs_6_
  33.2 2.6 %collective-permute-start.21 = (bf16[128,768]{1,0:T(8,128)(2,1)}, bf16[128,768]{1,0:T(8,128)(2,1)}, u32[]{:S(2)}, u32[]{:S(2)}) collective-permute-start(bf16[128,768]{1,0:T(8,128)(2,1)} %get-tuple-element.46), channel_id=1, source_target_pairs={{0,8},{1,9},{2,10},{3,11},{4,12},{5,13},{6,14},{7,15},{8,0},{9,1},... | collective-permute-start | bytes 589832 | tf_op jit(solution)/shard_map/ppermute | solution.py:165
  35.8 6.8 %collective-permute-done.17.refs_16_ = bf16[128,768]{1,0:T(8,128)(2,1)S(1)} collective-permute-done((bf16[128,768]{1,0:T(8,128)(2,1)}, bf16[128,768]{1,0:T(8,128)(2,1)S(1)}, u32[]{:S(2)}, u32[]{:S(2)}) %collective-permute-start.17) | collective-permute-done | bytes 196640 | tf_op jit(solution)/shard_map/ppermute | solution.py:165
  42.5 3.7 %collective-permute-start.19 = (bf16[128,768]{1,0:T(8,128)(2,1)S(1)}, bf16[128,768]{1,0:T(8,128)(2,1)S(1)}, u32[]{:S(2)}, u32[]{:S(2)}) collective-permute-start(bf16[128,768]{1,0:T(8,128)(2,1)S(1)} %collective-permute-done.17.refs_16_), channel_id=1, source_target_pairs={{0,2},{1,3},{2,0},{3,1},{4,6},{5,7},{6,4},{7,5},{8,10},{9,11},{10,... | collective-permute-start | bytes 589832 | tf_op jit(solution)/shard_map/ppermute | solution.py:168
  46.2 2.4 %collective-permute-done.21.refs_20_ = bf16[128,768]{1,0:T(8,128)(2,1)} collective-permute-done((bf16[128,768]{1,0:T(8,128)(2,1)}, bf16[128,768]{1,0:T(8,128)(2,1)}, u32[]{:S(2)}, u32[]{:S(2)}) %collective-permute-start.21) | collective-permute-done | bytes 196640 | tf_op jit(solution)/shard_map/ppermute | solution.py:165
  48.6 0.0 collective-permute-start.10
  48.6 0.0 collective-permute-done.11.refs_10_
  48.6 0.5 collective-permute-start.12
  49.2 3.0 %collective-permute-done.19.refs_18_ = bf16[128,768]{1,0:T(8,128)(2,1)S(1)} collective-permute-done((bf16[128,768]{1,0:T(8,128)(2,1)S(1)}, bf16[128,768]{1,0:T(8,128)(2,1)S(1)}, u32[]{:S(2)}, u32[]{:S(2)}) %collective-permute-start.19) | collective-permute-done | bytes 196640 | tf_op jit(solution)/shard_map/ppermute | solution.py:168
  52.2 0.0 collective-permute-start.14
  52.2 0.0 collective-permute-done.15.refs_14_
  52.2 0.5 collective-permute-start.16
  52.7 0.0 collective-permute-done.8.refs_7_
  52.7 0.2 copy-done.10
  52.8 1.5 %collective-permute-start.23 = (bf16[128,768]{1,0:T(8,128)(2,1)}, bf16[128,768]{1,0:T(8,128)(2,1)}, u32[]{:S(2)}, u32[]{:S(2)}) collective-permute-start(bf16[128,768]{1,0:T(8,128)(2,1)} %collective-permute-done.21.refs_20_), channel_id=1, source_target_pairs={{0,2},{1,3},{2,0},{3,1},{4,6},{5,7},{6,4},{7,5},{8,10},{9,11},{10,... | collective-permute-start | bytes 589832 | tf_op jit(solution)/shard_map/ppermute | solution.py:168
  54.4 2.6 %compare1.1.refs_12_ = f32[1,256]{1,0:T(1,128)} custom-call(f32[1,1024]{1,0:T(1,128)} %copy-done.15, f32[1,1024]{1,0:T(1,128)} %copy-done.17, f32[1,1024]{1,0:T(1,128)} %copy-done.16, f32[1,1024]{1,0:T(1,128)} %copy-done.18, bf16[256,768]{1,0:T(8,128)(2,1)} %get-tuple-element.38.refs_4_, bf16[256,768]{1,0:T(8,128)(2,1)} %copy-done.1, ...), custom_call_target="tpu_custom_call" | custom-call | flops 402653184 | bytes 1572864 | tf_op jit(solution)/shard_map/compare1/pallas_call | solution.py:113
  57.0 0.1 collective-permute-start.18
  57.0 0.0 collective-permute-done.12.refs_11_
  57.0 0.5 collective-permute-start.20
  57.5 0.2 copy-done.7
  57.7 0.1 copy-done.8
  57.8 3.9 %compare2.1.refs_16_ = f32[1,512]{1,0:T(1,128)} custom-call(f32[1,1024]{1,0:T(1,128)} %copy-done.15, f32[1,1024]{1,0:T(1,128)} %copy-done.17, f32[1,1024]{1,0:T(1,128)} %copy-done.16, f32[1,1024]{1,0:T(1,128)} %copy-done.18, bf16[256,768]{1,0:T(8,128)(2,1)} %get-tuple-element.38.refs_4_, bf16[256,768]{1,0:T(8,128)(2,1)} %copy-done.1, ...), custom_call_target="tpu_custom_call" | custom-call | flops 1207959552 | bytes 3145728 | tf_op jit(solution)/shard_map/compare2/pallas_call | solution.py:113
  61.7 0.0 collective-permute-done.23.refs_22_
  61.7 0.4 collective-permute-start.22
  62.2 0.0 collective-permute-done.14.refs_13_
  62.2 0.1 collective-permute-start.24
  62.2 0.0 collective-permute-done.16.refs_15_
  62.2 5.2 %compare3.1.refs_20_ = f32[1,768]{1,0:T(1,128)} custom-call(f32[1,1024]{1,0:T(1,128)} %copy-done.15, f32[1,1024]{1,0:T(1,128)} %copy-done.17, f32[1,1024]{1,0:T(1,128)} %copy-done.16, f32[1,1024]{1,0:T(1,128)} %copy-done.18, bf16[256,768]{1,0:T(8,128)(2,1)} %get-tuple-element.38.refs_4_, bf16[256,768]{1,0:T(8,128)(2,1)} %copy-done.1, ...), custom_call_target="tpu_custom_call" | custom-call | flops 2013265920 | bytes 4718592 | tf_op jit(solution)/shard_map/compare3/pallas_call | solution.py:113
  67.5 0.0 collective-permute-done.18.refs_17_
  67.5 0.7 copy-done.11
  68.2 0.7 copy-done.12
  68.8 6.3 %compare4.1.refs_24_ = f32[1,896]{1,0:T(1,128)} custom-call(f32[1,1024]{1,0:T(1,128)} %copy-done.15, f32[1,1024]{1,0:T(1,128)} %copy-done.17, f32[1,1024]{1,0:T(1,128)} %copy-done.16, f32[1,1024]{1,0:T(1,128)} %copy-done.18, bf16[256,768]{1,0:T(8,128)(2,1)} %get-tuple-element.38.refs_4_, bf16[256,768]{1,0:T(8,128)(2,1)} %copy-done.1, ...), custom_call_target="tpu_custom_call" | custom-call | flops 1308622848 | bytes 5505024 | tf_op jit(solution)/shard_map/compare4/pallas_call | solution.py:113
  75.2 0.7 copy-done.13
  75.8 0.7 copy-done.14
  76.5 6.9 %compare5.1 = (f32[1,256]{1,0:T(1,128)}, f32[1,256]{1,0:T(1,128)}, f32[1,256]{1,0:T(1,128)}, f32[1,256]{1,0:T(1,128)}) custom-call(f32[1,1024]{1,0:T(1,128)} %copy-done.15, f32[1,1024]{1,0:T(1,128)} %copy-done.17, f32[1,1024]{1,0:T(1,128)} %copy-done.16, f32[1,1024]{1,0:T(1,128)} %copy-done.18, bf16[256,768]{1,0:T(8,128)(2,1)} %get-tuple-element.38.refs_4_, ...), custom_call_target="tpu_custom_call" | custom-call | flops 1509949440 | bytes 6291456 | tf_op jit(solution)/shard_map/compare5/pallas_call | solution.py:113
  83.4 0.6 collective-permute-start.25
  84.0 1.4 %collective-permute-start.26 = (f32[1,256]{1,0:T(1,128)}, f32[1,256]{1,0:T(1,128)S(1)}, u32[]{:S(2)}, u32[]{:S(2)}) collective-permute-start(f32[1,256]{1,0:T(1,128)} %get-tuple-element.49), channel_id=1, source_target_pairs={{0,4},{1,5},{2,6},{3,7},{4,8},{5,9},{6,10},{7,11},{8,12},{9,13},{1... | collective-permute-start | bytes 3080 | tf_op jit(solution)/shard_map/ppermute | solution.py:165
  85.5 0.3 collective-permute-start.27
  85.8 1.4 %collective-permute-done.25.refs_1_ = f32[1,256]{1,0:T(1,128)S(1)} collective-permute-done((f32[1,256]{1,0:T(1,128)}, f32[1,256]{1,0:T(1,128)S(1)}, u32[]{:S(2)}, u32[]{:S(2)}) %collective-permute-start.25) | collective-permute-done | bytes 1056 | tf_op jit(solution)/shard_map/ppermute | solution.py:165
  87.2 2.4 %collective-permute-done.26.refs_2_ = f32[1,256]{1,0:T(1,128)S(1)} collective-permute-done((f32[1,256]{1,0:T(1,128)}, f32[1,256]{1,0:T(1,128)S(1)}, u32[]{:S(2)}, u32[]{:S(2)}) %collective-permute-start.26) | collective-permute-done | bytes 1056 | tf_op jit(solution)/shard_map/ppermute | solution.py:165
  89.6 0.4 collective-permute-done.27.refs_3_
  90.0 0.2 copy-done.21
  90.2 0.4 copy-done.22
  90.5 1.8 %unpack.1 = f32[1,512]{1,0:T(1,128)} custom-call(s32[1,512]{1,0:T(1,128)} %get-tuple-element.28.refs_1_.slot_ref, f32[1,256]{1,0:T(1,128)} %get-tuple-element.47.refs_0_, f32[1,256]{1,0:T(1,128)} %copy-done.20, f32[1,256]{1,0:T(1,128)} %copy-done.21, f32[1,256]{1,0:T(1,128)} %copy-done.22), custom_call_target="tpu_custom_call" | custom-call | tf_op jit(solution)/shard_map/unpack/pallas_call | solution.py:142
  (50 shorter events, 0.1 us)
Async XLA Ops:
  1.9 10.9 %copy-start.19 = (f32[1,256]{1,0:T(1,128)S(1)}, f32[1,256]{1,0:T(1,128)}, u32[]{:S(2)}) copy-start(f32[1,256]{1,0:T(1,128)} %get-tuple-element.30) | copy-start | bytes 3076
  1.9 10.9 %collective-permute-start = (f32[1,256]{1,0:T(1,128)}, f32[1,256]{1,0:T(1,128)S(1)}, u32[]{:S(2)}, u32[]{:S(2)}) collective-permute-start(f32[1,256]{1,0:T(1,128)} %get-tuple-element.31), channel_id=1, source_target_pairs={{0,4},{1,5},{2,6},{3,7},{4,8},{5,9},{6,10},{7,11},{8,12},{9,13},{1... | collective-permute-start | bytes 3080 | tf_op jit(solution)/shard_map/ppermute | solution.py:165
  4.9 7.9 %collective-permute-start.1 = (f32[1,256]{1,0:T(1,128)}, f32[1,256]{1,0:T(1,128)S(1)}, u32[]{:S(2)}, u32[]{:S(2)}) collective-permute-start(f32[1,256]{1,0:T(1,128)} %get-tuple-element.32), channel_id=1, source_target_pairs={{0,12},{1,13},{2,14},{3,15},{4,0},{5,1},{6,2},{7,3},{8,4},{9,5},{1... | collective-permute-start | bytes 3080 | tf_op jit(solution)/shard_map/ppermute | solution.py:165
  7.0 5.9 %collective-permute-start.2 = (f32[1,256]{1,0:T(1,128)}, f32[1,256]{1,0:T(1,128)S(1)}, u32[]{:S(2)}, u32[]{:S(2)}) collective-permute-start(f32[1,256]{1,0:T(1,128)} %get-tuple-element.33), channel_id=1, source_target_pairs={{0,8},{1,9},{2,10},{3,11},{4,12},{5,13},{6,14},{7,15},{8,0},{9,1},... | collective-permute-start | bytes 3080 | tf_op jit(solution)/shard_map/ppermute | solution.py:165
  11.2 14.1 %collective-permute-start.9 = (bf16[256,768]{1,0:T(8,128)(2,1)}, bf16[256,768]{1,0:T(8,128)(2,1)S(1)}, u32[]{:S(2)}, u32[]{:S(2)}) collective-permute-start(bf16[256,768]{1,0:T(8,128)(2,1)} %get-tuple-element.40), channel_id=1, source_target_pairs={{0,4},{1,5},{2,6},{3,7},{4,8},{5,9},{6,10},{7,11},{8,12},{9,13},{1... | collective-permute-start | bytes 1179656 | tf_op jit(solution)/shard_map/ppermute | solution.py:165
  12.9 41.5 %copy-start.15 = (f32[1,1024]{1,0:T(1,128)}, f32[1,1024]{1,0:T(1,128)S(1)}, u32[]{:S(2)}) copy-start(f32[1,1024]{1,0:T(1,128)S(1)} %constant_dynamic-update-slice_fusion.refs_0_) | copy-start | bytes 12292
  12.9 3.7 %collective-permute-start.4 = (f32[1,1024]{1,0:T(1,128)S(1)}, f32[1,1024]{1,0:T(1,128)S(1)}, u32[]{:S(2)}, u32[]{:S(2)}) collective-permute-start(f32[1,1024]{1,0:T(1,128)S(1)} %constant_dynamic-update-slice_fusion.refs_0_), channel_id=1, source_target_pairs={{0,2},{1,3},{2,0},{3,1},{4,6},{5,7},{6,4},{7,5},{8,10},{9,11},{10,... | collective-permute-start | bytes 12296 | tf_op jit(solution)/shard_map/ppermute | solution.py:168
  14.4 2.1 %collective-permute-start.3 = (f32[1,1024]{1,0:T(1,128)S(1)}, f32[1,1024]{1,0:T(1,128)S(1)}, u32[]{:S(2)}, u32[]{:S(2)}) collective-permute-start(f32[1,1024]{1,0:T(1,128)S(1)} %constant_dynamic-update-slice_fusion.refs_0_), channel_id=1, source_target_pairs={{0,1},{1,0},{2,3},{3,2},{4,5},{5,4},{6,7},{7,6},{8,9},{9,8},{10,11... | collective-permute-start | bytes 12296 | tf_op jit(solution)/shard_map/ppermute | solution.py:168
  16.6 37.8 %copy-start.16 = (f32[1,1024]{1,0:T(1,128)}, f32[1,1024]{1,0:T(1,128)S(1)}, u32[]{:S(2)}) copy-start(f32[1,1024]{1,0:T(1,128)S(1)} %collective-permute-done.4.refs_2_) | copy-start | bytes 12292
  16.6 1.2 %collective-permute-start.5 = (f32[1,1024]{1,0:T(1,128)S(1)}, f32[1,1024]{1,0:T(1,128)S(1)}, u32[]{:S(2)}, u32[]{:S(2)}) collective-permute-start(f32[1,1024]{1,0:T(1,128)S(1)} %collective-permute-done.4.refs_2_), channel_id=1, source_target_pairs={{0,1},{1,0},{2,3},{3,2},{4,5},{5,4},{6,7},{7,6},{8,9},{9,8},{10,11... | collective-permute-start | bytes 12296 | tf_op jit(solution)/shard_map/ppermute | solution.py:168
  16.6 37.8 %copy-start.17 = (f32[1,1024]{1,0:T(1,128)}, f32[1,1024]{1,0:T(1,128)S(1)}, u32[]{:S(2)}) copy-start(f32[1,1024]{1,0:T(1,128)S(1)} %collective-permute-done.3.refs_1_) | copy-start | bytes 12292
  17.7 36.6 %copy-start.18 = (f32[1,1024]{1,0:T(1,128)}, f32[1,1024]{1,0:T(1,128)S(1)}, u32[]{:S(2)}) copy-start(f32[1,1024]{1,0:T(1,128)S(1)} %collective-permute-done.5.refs_3_) | copy-start | bytes 12292
  17.7 14.0 %collective-permute-start.13 = (bf16[256,768]{1,0:T(8,128)(2,1)}, bf16[256,768]{1,0:T(8,128)(2,1)S(1)}, u32[]{:S(2)}, u32[]{:S(2)}) collective-permute-start(bf16[256,768]{1,0:T(8,128)(2,1)} %get-tuple-element.43), channel_id=1, source_target_pairs={{0,12},{1,13},{2,14},{3,15},{4,0},{5,1},{6,2},{7,3},{8,4},{9,5},{1... | collective-permute-start | bytes 1179656 | tf_op jit(solution)/shard_map/ppermute | solution.py:165
  20.0 13.2 %collective-permute-start.7 = (bf16[256,768]{1,0:T(8,128)(2,1)}, bf16[256,768]{1,0:T(8,128)(2,1)S(1)}, u32[]{:S(2)}, u32[]{:S(2)}) collective-permute-start(bf16[256,768]{1,0:T(8,128)(2,1)} %get-tuple-element.38.refs_4_), channel_id=1, source_target_pairs={{0,2},{1,3},{2,0},{3,1},{4,6},{5,7},{6,4},{7,5},{8,10},{9,11},{10,... | collective-permute-start | bytes 1179656 | tf_op jit(solution)/shard_map/ppermute | solution.py:168
  21.5 14.3 %collective-permute-start.6 = (bf16[256,768]{1,0:T(8,128)(2,1)}, bf16[256,768]{1,0:T(8,128)(2,1)S(1)}, u32[]{:S(2)}, u32[]{:S(2)}) collective-permute-start(bf16[256,768]{1,0:T(8,128)(2,1)} %get-tuple-element.38.refs_4_), channel_id=1, source_target_pairs={{0,1},{1,0},{2,3},{3,2},{4,5},{5,4},{6,7},{7,6},{8,9},{9,8},{10,11... | collective-permute-start | bytes 1179656 | tf_op jit(solution)/shard_map/ppermute | solution.py:168
  25.3 32.2 %copy-start.3 = (bf16[256,768]{1,0:T(8,128)(2,1)}, bf16[256,768]{1,0:T(8,128)(2,1)S(1)}, u32[]{:S(2)}) copy-start(bf16[256,768]{1,0:T(8,128)(2,1)S(1)} %collective-permute-done.9.refs_8_) | copy-start | bytes 1179652
  25.3 23.3 %collective-permute-start.11 = (bf16[256,768]{1,0:T(8,128)(2,1)S(1)}, bf16[256,768]{1,0:T(8,128)(2,1)S(1)}, u32[]{:S(2)}, u32[]{:S(2)}) collective-permute-start(bf16[256,768]{1,0:T(8,128)(2,1)S(1)} %collective-permute-done.9.refs_8_), channel_id=1, source_target_pairs={{0,2},{1,3},{2,0},{3,1},{4,6},{5,7},{6,4},{7,5},{8,10},{9,11},{10,... | collective-permute-start | bytes 1179656 | tf_op jit(solution)/shard_map/ppermute | solution.py:168
  26.8 15.8 %collective-permute-start.17 = (bf16[128,768]{1,0:T(8,128)(2,1)}, bf16[128,768]{1,0:T(8,128)(2,1)S(1)}, u32[]{:S(2)}, u32[]{:S(2)}) collective-permute-start(bf16[128,768]{1,0:T(8,128)(2,1)} %get-tuple-element.45), channel_id=1, source_target_pairs={{0,8},{1,9},{2,10},{3,11},{4,12},{5,13},{6,14},{7,15},{8,0},{9,1},... | collective-permute-start | bytes 589832 | tf_op jit(solution)/shard_map/ppermute | solution.py:165
  31.7 30.6 %copy-start.4 = (bf16[256,768]{1,0:T(8,128)(2,1)}, bf16[256,768]{1,0:T(8,128)(2,1)S(1)}, u32[]{:S(2)}) copy-start(bf16[256,768]{1,0:T(8,128)(2,1)S(1)} %collective-permute-done.13.refs_12_) | copy-start | bytes 1179652
  31.7 20.5 %collective-permute-start.15 = (bf16[256,768]{1,0:T(8,128)(2,1)S(1)}, bf16[256,768]{1,0:T(8,128)(2,1)S(1)}, u32[]{:S(2)}, u32[]{:S(2)}) collective-permute-start(bf16[256,768]{1,0:T(8,128)(2,1)S(1)} %collective-permute-done.13.refs_12_), channel_id=1, source_target_pairs={{0,2},{1,3},{2,0},{3,1},{4,6},{5,7},{6,4},{7,5},{8,10},{9,11},{10,... | collective-permute-start | bytes 1179656 | tf_op jit(solution)/shard_map/ppermute | solution.py:168
  33.2 21.2 %copy-start = (bf16[256,768]{1,0:T(8,128)(2,1)}, bf16[256,768]{1,0:T(8,128)(2,1)S(1)}, u32[]{:S(2)}) copy-start(bf16[256,768]{1,0:T(8,128)(2,1)S(1)} %collective-permute-done.7.refs_6_) | copy-start | bytes 1179652
  33.2 15.5 %collective-permute-start.21 = (bf16[128,768]{1,0:T(8,128)(2,1)}, bf16[128,768]{1,0:T(8,128)(2,1)}, u32[]{:S(2)}, u32[]{:S(2)}) collective-permute-start(bf16[128,768]{1,0:T(8,128)(2,1)} %get-tuple-element.46), channel_id=1, source_target_pairs={{0,8},{1,9},{2,10},{3,11},{4,12},{5,13},{6,14},{7,15},{8,0},{9,1},... | collective-permute-start | bytes 589832 | tf_op jit(solution)/shard_map/ppermute | solution.py:165
  35.8 18.6 %copy-start.1 = (bf16[256,768]{1,0:T(8,128)(2,1)}, bf16[256,768]{1,0:T(8,128)(2,1)S(1)}, u32[]{:S(2)}) copy-start(bf16[256,768]{1,0:T(8,128)(2,1)S(1)} %collective-permute-done.6.refs_5_) | copy-start | bytes 1179652
  35.8 16.9 %collective-permute-start.8 = (bf16[256,768]{1,0:T(8,128)(2,1)S(1)}, bf16[256,768]{1,0:T(8,128)(2,1)S(1)}, u32[]{:S(2)}, u32[]{:S(2)}) collective-permute-start(bf16[256,768]{1,0:T(8,128)(2,1)S(1)} %collective-permute-done.7.refs_6_), channel_id=1, source_target_pairs={{0,1},{1,0},{2,3},{3,2},{4,5},{5,4},{6,7},{7,6},{8,9},{9,8},{10,11... | collective-permute-start | bytes 1179656 | tf_op jit(solution)/shard_map/ppermute | solution.py:168
  42.5 10.1 %copy-start.9 = (bf16[128,768]{1,0:T(8,128)(2,1)}, bf16[128,768]{1,0:T(8,128)(2,1)S(1)}, u32[]{:S(2)}) copy-start(bf16[128,768]{1,0:T(8,128)(2,1)S(1)} %collective-permute-done.17.refs_16_) | copy-start | bytes 589828
  42.5 9.6 %collective-permute-start.19 = (bf16[128,768]{1,0:T(8,128)(2,1)S(1)}, bf16[128,768]{1,0:T(8,128)(2,1)S(1)}, u32[]{:S(2)}, u32[]{:S(2)}) collective-permute-start(bf16[128,768]{1,0:T(8,128)(2,1)S(1)} %collective-permute-done.17.refs_16_), channel_id=1, source_target_pairs={{0,2},{1,3},{2,0},{3,1},{4,6},{5,7},{6,4},{7,5},{8,10},{9,11},{10,... | collective-permute-start | bytes 589832 | tf_op jit(solution)/shard_map/ppermute | solution.py:168
  48.6 8.3 %collective-permute-start.10 = (bf16[256,768]{1,0:T(8,128)(2,1)S(1)}, bf16[256,768]{1,0:T(8,128)(2,1)S(1)}, u32[]{:S(2)}, u32[]{:S(2)}) collective-permute-start(bf16[256,768]{1,0:T(8,128)(2,1)S(1)} %collective-permute-done.9.refs_8_), channel_id=1, source_target_pairs={{0,1},{1,0},{2,3},{3,2},{4,5},{5,4},{6,7},{7,6},{8,9},{9,8},{10,11... | collective-permute-start | bytes 1179656 | tf_op jit(solution)/shard_map/ppermute | solution.py:168
  48.6 8.9 %copy-start.5 = (bf16[256,768]{1,0:T(8,128)(2,1)}, bf16[256,768]{1,0:T(8,128)(2,1)S(1)}, u32[]{:S(2)}) copy-start(bf16[256,768]{1,0:T(8,128)(2,1)S(1)} %collective-permute-done.11.refs_10_) | copy-start | bytes 1179652
  48.6 8.4 %collective-permute-start.12 = (bf16[256,768]{1,0:T(8,128)(2,1)S(1)}, bf16[256,768]{1,0:T(8,128)(2,1)S(1)}, u32[]{:S(2)}, u32[]{:S(2)}) collective-permute-start(bf16[256,768]{1,0:T(8,128)(2,1)S(1)} %collective-permute-done.11.refs_10_), channel_id=1, source_target_pairs={{0,1},{1,0},{2,3},{3,2},{4,5},{5,4},{6,7},{7,6},{8,9},{9,8},{10,11... | collective-permute-start | bytes 1179656 | tf_op jit(solution)/shard_map/ppermute | solution.py:168
  52.2 0.7 copy-start.10
  52.2 10.0 %collective-permute-start.14 = (bf16[256,768]{1,0:T(8,128)(2,1)S(1)}, bf16[256,768]{1,0:T(8,128)(2,1)}, u32[]{:S(2)}, u32[]{:S(2)}) collective-permute-start(bf16[256,768]{1,0:T(8,128)(2,1)S(1)} %collective-permute-done.13.refs_12_), channel_id=1, source_target_pairs={{0,1},{1,0},{2,3},{3,2},{4,5},{5,4},{6,7},{7,6},{8,9},{9,8},{10,11... | collective-permute-start | bytes 1179656 | tf_op jit(solution)/shard_map/ppermute | solution.py:168
  52.2 10.1 %copy-start.6 = (bf16[256,768]{1,0:T(8,128)(2,1)}, bf16[256,768]{1,0:T(8,128)(2,1)S(1)}, u32[]{:S(2)}) copy-start(bf16[256,768]{1,0:T(8,128)(2,1)S(1)} %collective-permute-done.15.refs_14_) | copy-start | bytes 1179652
  52.2 10.1 %collective-permute-start.16 = (bf16[256,768]{1,0:T(8,128)(2,1)S(1)}, bf16[256,768]{1,0:T(8,128)(2,1)}, u32[]{:S(2)}, u32[]{:S(2)}) collective-permute-start(bf16[256,768]{1,0:T(8,128)(2,1)S(1)} %collective-permute-done.15.refs_14_), channel_id=1, source_target_pairs={{0,1},{1,0},{2,3},{3,2},{4,5},{5,4},{6,7},{7,6},{8,9},{9,8},{10,11... | collective-permute-start | bytes 1179656 | tf_op jit(solution)/shard_map/ppermute | solution.py:168
  52.8 1.5 %copy-start.2 = (bf16[256,768]{1,0:T(8,128)(2,1)}, bf16[256,768]{1,0:T(8,128)(2,1)S(1)}, u32[]{:S(2)}) copy-start(bf16[256,768]{1,0:T(8,128)(2,1)S(1)} %collective-permute-done.8.refs_7_) | copy-start | bytes 1179652
  52.8 8.9 %collective-permute-start.23 = (bf16[128,768]{1,0:T(8,128)(2,1)}, bf16[128,768]{1,0:T(8,128)(2,1)}, u32[]{:S(2)}, u32[]{:S(2)}) collective-permute-start(bf16[128,768]{1,0:T(8,128)(2,1)} %collective-permute-done.21.refs_20_), channel_id=1, source_target_pairs={{0,2},{1,3},{2,0},{3,1},{4,6},{5,7},{6,4},{7,5},{8,10},{9,11},{10,... | collective-permute-start | bytes 589832 | tf_op jit(solution)/shard_map/ppermute | solution.py:168
  56.9 0.8 copy-start.7
  57.0 10.5 %collective-permute-start.18 = (bf16[128,768]{1,0:T(8,128)(2,1)}, bf16[128,768]{1,0:T(8,128)(2,1)S(1)}, u32[]{:S(2)}, u32[]{:S(2)}) collective-permute-start(bf16[128,768]{1,0:T(8,128)(2,1)} %copy-done.9), channel_id=1, source_target_pairs={{0,1},{1,0},{2,3},{3,2},{4,5},{5,4},{6,7},{7,6},{8,9},{9,8},{10,11... | collective-permute-start | bytes 589832 | tf_op jit(solution)/shard_map/ppermute | solution.py:168
  57.0 0.8 copy-start.8
  57.0 10.4 %collective-permute-start.20 = (bf16[128,768]{1,0:T(8,128)(2,1)}, bf16[128,768]{1,0:T(8,128)(2,1)S(1)}, u32[]{:S(2)}, u32[]{:S(2)}) collective-permute-start(bf16[128,768]{1,0:T(8,128)(2,1)} %copy-done.10), channel_id=1, source_target_pairs={{0,1},{1,0},{2,3},{3,2},{4,5},{5,4},{6,7},{7,6},{8,9},{9,8},{10,11... | collective-permute-start | bytes 589832 | tf_op jit(solution)/shard_map/ppermute | solution.py:168
  61.7 13.4 %collective-permute-start.22 = (bf16[128,768]{1,0:T(8,128)(2,1)}, bf16[128,768]{1,0:T(8,128)(2,1)S(1)}, u32[]{:S(2)}, u32[]{:S(2)}) collective-permute-start(bf16[128,768]{1,0:T(8,128)(2,1)} %collective-permute-done.21.refs_20_), channel_id=1, source_target_pairs={{0,1},{1,0},{2,3},{3,2},{4,5},{5,4},{6,7},{7,6},{8,9},{9,8},{10,11... | collective-permute-start | bytes 589832 | tf_op jit(solution)/shard_map/ppermute | solution.py:168
  62.2 13.0 %collective-permute-start.24 = (bf16[128,768]{1,0:T(8,128)(2,1)}, bf16[128,768]{1,0:T(8,128)(2,1)S(1)}, u32[]{:S(2)}, u32[]{:S(2)}) collective-permute-start(bf16[128,768]{1,0:T(8,128)(2,1)} %collective-permute-done.23.refs_22_), channel_id=1, source_target_pairs={{0,1},{1,0},{2,3},{3,2},{4,5},{5,4},{6,7},{7,6},{8,9},{9,8},{10,11... | collective-permute-start | bytes 589832 | tf_op jit(solution)/shard_map/ppermute | solution.py:168
  67.5 0.7 copy-start.11
  68.2 0.7 copy-start.12
  75.1 0.7 copy-start.13
  75.8 0.7 copy-start.14
  83.4 3.8 %collective-permute-start.25 = (f32[1,256]{1,0:T(1,128)}, f32[1,256]{1,0:T(1,128)S(1)}, u32[]{:S(2)}, u32[]{:S(2)}) collective-permute-start(f32[1,256]{1,0:T(1,128)} %get-tuple-element.48), channel_id=1, source_target_pairs={{0,12},{1,13},{2,14},{3,15},{4,0},{5,1},{6,2},{7,3},{8,4},{9,5},{1... | collective-permute-start | bytes 3080 | tf_op jit(solution)/shard_map/ppermute | solution.py:165
  84.0 5.6 %collective-permute-start.26 = (f32[1,256]{1,0:T(1,128)}, f32[1,256]{1,0:T(1,128)S(1)}, u32[]{:S(2)}, u32[]{:S(2)}) collective-permute-start(f32[1,256]{1,0:T(1,128)} %get-tuple-element.49), channel_id=1, source_target_pairs={{0,4},{1,5},{2,6},{3,7},{4,8},{5,9},{6,10},{7,11},{8,12},{9,13},{1... | collective-permute-start | bytes 3080 | tf_op jit(solution)/shard_map/ppermute | solution.py:165
  85.5 4.5 %collective-permute-start.27 = (f32[1,256]{1,0:T(1,128)}, f32[1,256]{1,0:T(1,128)S(1)}, u32[]{:S(2)}, u32[]{:S(2)}) collective-permute-start(f32[1,256]{1,0:T(1,128)} %get-tuple-element.50), channel_id=1, source_target_pairs={{0,8},{1,9},{2,10},{3,11},{4,12},{5,13},{6,14},{7,15},{8,0},{9,1},... | collective-permute-start | bytes 3080 | tf_op jit(solution)/shard_map/ppermute | solution.py:165
  87.2 2.8 %copy-start.20 = (f32[1,256]{1,0:T(1,128)}, f32[1,256]{1,0:T(1,128)S(1)}, u32[]{:S(2)}) copy-start(f32[1,256]{1,0:T(1,128)S(1)} %collective-permute-done.25.refs_1_) | copy-start | bytes 3076
  89.6 0.6 copy-start.21
  90.0 0.5 copy-start.22
where the time goes:
time: 92.6 us; the launch traced here: 92.3 us
  Pallas kernels  31.8 us (34%)
  waiting for transfers between devices  28.4 us (31%)
  starting transfers between devices  28.2 us (30%)
  local copies, waits for them, and re-layouts  3.76 us (4%)
    pallas_call x5, Pallas kernels, compare(): pl.pallas_call(lambda *refs: compare_kernel(units, outs, *refs), out_shap...  24.9 us
    ppermute x10, waiting for transfers between devices, shift(): lax.ppermute(array, 'blk', [(i, (i + step) % devices) for i in range(devi...  22.1 us
    ppermute x10, starting transfers between devices, shift(): lax.ppermute(array, 'blk', [(i, (i + step) % devices) for i in range(devi...  14.9 us
    ppermute x18, starting transfers between devices, swap(): return lax.ppermute(array, 'blk', [(i, i ^ mask) for i in range(devices)])  13.3 us
    ppermute x18, waiting for transfers between devices, swap(): return lax.ppermute(array, 'blk', [(i, i ^ mask) for i in range(devices)])  6.3 us
    unnamed x49, local copies, waits for them, and re-layouts  3.76 us
    pallas_call x1, Pallas kernels, pack(): pl.pallas_call(lambda *refs: pack_kernel(units, *refs), out_shape=[jax.Sh...  3.27 us
    pallas_call x1, Pallas kernels, place_labels(): pl.pallas_call(lambda *refs: label_kernel(groups, cap, pieces, *refs), ou...  1.89 us
  transfers between devices with their start and end apart: 28, of which 10 were waited for; matrix products, arithmetic and copies ran while one was open for 0% of the time, Pallas kernels for 23%

commit v1 on v0

v1 whole, which is shorter than its diff:
```python
import jax
import jax.numpy as jnp
from jax import lax
from jax.experimental import pallas as pl
from jax.experimental.pallas import tpu as pltpu
from jax.sharding import PartitionSpec as P

GROUP = 4
UNITS = (4, 4, 4, 2, 2)
GRANT = 16 << 20
NT = (((1,), (1,)), ((), ()))


def iota(shape, axis):
    return lax.broadcasted_iota(jnp.int32, shape, axis)


def spans(widths):
    start, out = 0, []
    for width in widths:
        out.append((start, width))
        start += width
    return out


def pack_kernel(groups, cap, units, pieces, emb_hbm, owner_hbm, cluster_hbm, *refs):
    blocks, refs = refs[: len(units)], refs[len(units) :]
    labels, refs = refs[: len(pieces)], refs[len(pieces) :]
    slot_ref, emb_ref, unit_ref, owner_ref, cluster_ref, sems = refs
    rows = emb_ref.shape[0]
    part = rows // 4
    copies = [
        pltpu.make_async_copy(owner_hbm, owner_ref, sems.at[0]),
        pltpu.make_async_copy(cluster_hbm, cluster_ref, sems.at[1]),
    ]
    for i in range(4):
        span = pl.ds(i * part, part)
        copies.append(pltpu.make_async_copy(emb_hbm.at[span], emb_ref.at[span], sems.at[2 + i]))
    for copy in copies:
        copy.start()
    earlier = (iota((rows, rows), 0) < iota((rows, rows), 1)).astype(jnp.bfloat16)
    mine = lax.axis_index("blk") // GROUP
    copies[0].wait()
    rel = ((owner_ref[...] >> 2) - mine + groups) & (groups - 1)
    place = jnp.where(rel > groups // 2, 2 * (groups - rel), jnp.maximum(2 * rel - 1, 0))
    member = iota((max(groups, 16), rows), 0) == place
    count = jnp.dot(member.astype(jnp.bfloat16), earlier, preferred_element_type=jnp.float32)
    rank = jnp.sum(jnp.where(member, count, 0.0), axis=0, keepdims=True)
    slot = place * cap + rank.astype(jnp.int32)
    slot_ref[...] = slot
    copies[1].wait()
    label = ((cluster_ref[...] & 15) + 1).astype(jnp.float32).astype(jnp.bfloat16)
    label = jnp.broadcast_to(label, (16, rows))
    for i in range(4):
        copies[2 + i].wait()
        x = emb_ref[i * part : (i + 1) * part, :]
        squares = jnp.sum(x * x, axis=1, keepdims=True)
        unit_ref[i * part : (i + 1) * part, :] = (x * lax.rsqrt(squares + 1e-06)).astype(
            jnp.bfloat16
        )
    unit = unit_ref[...]
    for u, (start, size) in enumerate(units):
        hot = (iota((size, rows), 0) + start == slot).astype(jnp.bfloat16)
        blocks[u][...] = jnp.dot(hot, unit, preferred_element_type=jnp.float32).astype(jnp.bfloat16)
        packed = lax.dot_general(label, hot, NT, preferred_element_type=jnp.float32)
        packed = packed[0:1, :] - 1.0
        for i, (low, width) in enumerate(pieces):
            a, b = max(low, start), min(low + width, start + size)
            if a < b:
                labels[i][:, a - low : b - low] = packed[:, a - start : b - start]


def pack(groups, cap, units, pieces, embedding, owner, cluster):
    rows, width = embedding.shape
    return pl.pallas_call(
        lambda *refs: pack_kernel(groups, cap, units, pieces, *refs),
        in_specs=[pl.BlockSpec(memory_space=pltpu.HBM)] * 3,
        out_shape=[jax.ShapeDtypeStruct((n, width), jnp.bfloat16) for _, n in units]
        + [jax.ShapeDtypeStruct((1, n), jnp.float32) for _, n in pieces]
        + [jax.ShapeDtypeStruct((1, rows), jnp.int32)],
        scratch_shapes=[
            pltpu.VMEM((rows, width), jnp.float32),
            pltpu.VMEM((rows, width), jnp.bfloat16),
            pltpu.VMEM((1, rows), jnp.int32),
            pltpu.VMEM((1, rows), jnp.int32),
            pltpu.SemaphoreType.DMA((6,)),
        ],
        compiler_params=pltpu.CompilerParams(vmem_limit_bytes=GRANT),
        name="pack",
    )(embedding, owner.reshape(1, rows), cluster.reshape(1, rows))


def compare_kernel(units, outs, *refs):
    last = len(units) - 1
    near, far, refs = refs[0], refs[1], refs[2:]
    keys, refs = refs[: 4 * last + 4], refs[4 * last + 4 :]
    if last:
        best_ref, refs = refs[0], refs[1:]
    outputs, query_ref = refs[:-1], refs[-1]
    for q, (low, width) in enumerate(units):
        query_ref[low : low + width, :] = keys[4 * q][...]
    columns = []
    for low, width in units:
        span = slice(low, low + width)
        wide = jnp.concatenate([near[:, span], far[:, span]] * 2, axis=0)
        columns.append(wide.T)

    def block(k, peer, low, width, same):
        scores = lax.dot_general(
            keys[4 * k + peer][...],
            query_ref[low : low + width, :],
            NT,
            preferred_element_type=jnp.float32,
        )
        allowed = columns[k][:, peer : peer + 1] == near[0:1, low : low + width]
        if same is not None:
            allowed = allowed & (iota(scores.shape, 0) + same != iota(scores.shape, 1))
        return jnp.max(jnp.where(allowed, scores, -1.0), axis=0, keepdims=True)

    start, size = units[last]
    total = start + size
    step = 256
    for low in range(0, total, step):
        width = min(step, total - low)
        best = jnp.full((1, width), -1.0)
        for peer in range(4):
            inside = peer == 0 and low <= start < low + width
            best = jnp.maximum(best, block(last, peer, low, width, start - low if inside else None))
        head = min(max(start - low, 0), width)
        if head:
            old = jnp.maximum(best[:, :head], best_ref[:, low : low + head])
            spread(outputs, outs, low, old)
        if head < width:
            new = best[:, head:]
            for k in range(last):
                for peer in range(4):
                    new = jnp.maximum(new, block(k, peer, start, size, None))
            spread(outputs, outs, start, new)


def spread(refs, outs, start, row):
    for ref, (low, width) in zip(refs, outs):
        a, b = max(low, start), min(low + width, start + row.shape[1])
        if a < b:
            ref[:, a - low : b - low] = row[:, a - start : b - start]


def compare(units, outs, labels, keys, best):
    start, size = units[-1]
    width = keys[0].shape[1]
    pairs = 4 * size * (start + size) + 4 * start * size
    return pl.pallas_call(
        lambda *refs: compare_kernel(units, outs, *refs),
        out_shape=[jax.ShapeDtypeStruct((1, n), jnp.float32) for _, n in outs],
        scratch_shapes=[pltpu.VMEM((start + size, width), jnp.bfloat16)],
        compiler_params=pltpu.CompilerParams(vmem_limit_bytes=GRANT),
        cost_estimate=pl.CostEstimate(
            flops=2 * pairs * width,
            bytes_accessed=8 * (start + size) * width,
            transcendentals=0,
        ),
        name=f"compare{len(units)}",
    )(*labels, *keys, *best)


def unpack_kernel(slot_ref, *refs):
    out_ref = refs[-1]
    slot = slot_ref[...]
    rows = slot.shape[1]
    total = jnp.zeros((8, rows), jnp.float32)
    start = 0
    for ref in refs[:-1]:
        size = ref.shape[1]
        column = jnp.broadcast_to(ref[...], (8, size)).T[:, 0:1]
        hit = iota((size, rows), 0) + start == slot
        part = jnp.where(hit, column, 0.0)
        total = total + jnp.sum(part.reshape(size // 8, 8, rows), axis=0)
        start += size
    out_ref[...] = jnp.sum(total, axis=0, keepdims=True)


def unpack(slot, backs):
    return pl.pallas_call(
        unpack_kernel,
        out_shape=jax.ShapeDtypeStruct(slot.shape, jnp.float32),
        compiler_params=pltpu.CompilerParams(vmem_limit_bytes=GRANT),
        name="unpack",
    )(slot, *backs)


def join(parts, axis):
    return parts[0] if len(parts) == 1 else jnp.concatenate(parts, axis=axis)


def on_device(embedding, row_owner, cluster_id):
    rows, _ = embedding.shape
    devices = lax.axis_size("blk")
    groups = devices // GROUP
    cap = GROUP * max(2, 2 * rows // devices)
    slots = groups * cap
    units = spans([n * slots // sum(UNITS) for n in UNITS])
    pieces = spans([max(cap, 128)] * (slots // max(cap, 128)))
    shifts = [0] + [(k + 1) // 2 if k % 2 else groups - k // 2 for k in range(1, groups)]

    def shift(array, distance):
        step = distance * GROUP
        return lax.ppermute(array, "blk", [(i, (i + step) % devices) for i in range(devices)])

    def swap(array, mask):
        return lax.ppermute(array, "blk", [(i, i ^ mask) for i in range(devices)])

    def exchange(array, start, axis, sign):
        size, out = array.shape[axis], []
        for k in range(start // cap, (start + size - 1) // cap + 1):
            a, b = max(k * cap - start, 0), min((k + 1) * cap - start, size)
            part = lax.slice_in_dim(array, a, b, axis=axis)
            out.append(shift(part, sign * shifts[k]) if shifts[k] else part)
        return join(out, axis)

    sent = pack(groups, cap, units, pieces, embedding, row_owner, cluster_id)
    blocks, label, slot = list(sent[: len(units)]), sent[len(units) : -1], sent[-1]

    def tie(*arrays):
        return lax.optimization_barrier(arrays)

    def send(u):
        return exchange(blocks[u], units[u][0], 0, 1)

    def cross(array):
        return swap(array, 2)

    def core(array):
        return swap(array, 1)

    last = len(units) - 1
    own = join([exchange(l, low, 1, 1) for l, (low, _) in zip(label, pieces)], 1)
    label_x = cross(own)
    near = jnp.concatenate([own, label_x], axis=0)
    labels = [near, core(near)]
    queries = []
    for u in range(last + 1):
        block = blocks[u]
        if u == 2:
            block, labels[1] = tie(block, labels[1])
        if u >= 3:
            block, queries[u - 2] = tie(block, queries[u - 2])
        queries.append(exchange(block, units[u][0], 0, 1))
    keys, best = [], []
    for u, (start, size) in enumerate(units):
        across = cross(queries[u])
        keys += [queries[u], across, core(queries[u]), core(across)]
        outs = pieces if u == last else [(0, start + size)]
        best = list(compare(units[: u + 1], outs, labels, keys, best))
    backs = [exchange(b, low, 1, -1) for b, (low, _) in zip(best, pieces)]
    return unpack(slot, backs).reshape(rows)


def solution(mesh):
    placed = (P(("parts", "blk"), None), P(("parts", "blk")), P(("parts", "blk")))
    return jax.shard_map(
        on_device, mesh=mesh, in_specs=placed, out_specs=P(("parts", "blk")), check_vma=False
    )
```

time: 92.6 us -> 80.5 us (0.87)
  Pallas kernels: 31.8 us -> 15.1 us
  waiting for transfers between devices: 28.4 us -> 42.2 us
  starting transfers between devices: 28.2 us -> 20.1 us
  local copies, waits for them, and re-layouts: 3.76 us -> 2.79 us
    pallas_call x5, Pallas kernels: 24.9 us -> 11.4 us  [compare(): pl.pallas_call(lambda *refs: compare_kernel(units, outs, *refs), out_shap...]
    ppermute x10, waiting for transfers between devices: 22.1 us -> 33.3 us  [shift(): lax.ppermute(array, 'blk', [(i, (i + step) % devices) for i in range(devi...]
    ppermute x18 -> x17, starting transfers between devices: 13.3 us -> 7.31 us  [swap(): return lax.ppermute(array, 'blk', [(i, i ^ mask) for i in range(devices)])]
    ppermute x18 -> x17, waiting for transfers between devices: 6.3 us -> 8.89 us  [swap(): return lax.ppermute(array, 'blk', [(i, i ^ mask) for i in range(devices)])]
    pallas_call x2 -> x1, Pallas kernels: 5.16 us -> 2.63 us  [pack(): pl.pallas_call(lambda *refs: pack_kernel(groups, cap, units, pieces, *ref...]
    ppermute x10, starting transfers between devices: 14.9 us -> 12.8 us  [shift(): lax.ppermute(array, 'blk', [(i, (i + step) % devices) for i in range(devi...]
    unnamed x49 -> x9, local copies, waits for them, and re-layouts: 3.76 us -> 2.79 us
  transfers between devices with their start and end apart: 28 -> 27, of which waited for: 10 -> 13; matrix products, arithmetic and copies ran while one was open for 0% -> 0% of each run, Pallas kernels for 23% -> 10%
where the time goes in v1:
time: 80.5 us; the launch traced here: 80.3 us
  waiting for transfers between devices  42.2 us (52%)
  starting transfers between devices  20.1 us (25%)
  Pallas kernels  15.1 us (19%)
  local copies, waits for them, and re-layouts  2.79 us (3%)
    ppermute x10, waiting for transfers between devices, shift(): lax.ppermute(array, 'blk', [(i, (i + step) % devices) for i in range(devi...  33.3 us
    ppermute x10, starting transfers between devices, shift(): lax.ppermute(array, 'blk', [(i, (i + step) % devices) for i in range(devi...  12.8 us
    pallas_call x5, Pallas kernels, compare(): pl.pallas_call(lambda *refs: compare_kernel(units, outs, *refs), out_shap...  11.4 us
    ppermute x17, waiting for transfers between devices, swap(): return lax.ppermute(array, 'blk', [(i, i ^ mask) for i in range(devices)])  8.89 us
    ppermute x17, starting transfers between devices, swap(): return lax.ppermute(array, 'blk', [(i, i ^ mask) for i in range(devices)])  7.31 us
    unnamed x9, local copies, waits for them, and re-layouts  2.79 us
    pallas_call x1, Pallas kernels, pack(): pl.pallas_call(lambda *refs: pack_kernel(groups, cap, units, pieces, *ref...  2.63 us
  transfers between devices with their start and end apart: 27, of which 13 were waited for; matrix products, arithmetic and copies ran while one was open for 0% of the time, Pallas kernels for 10%

profile of v1, /device:TPU:0, one launch (start us, length us, event | category | flops | bytes accessed | tf_op | source)
XLA Modules:
  0.0 80.3 jit_solution(177862896682753818)
XLA Ops:
  0.0 1.4 %copy-done = f32[512,768]{1,0:T(8,128)S(1)} copy-done((f32[512,768]{1,0:T(8,128)S(1)}, f32[512,768]{1,0:T(8,128)}, u32[]{:S(2)}) %copy-start) | copy-done | bytes 1572888
  1.4 0.7 copy-done.1
  2.1 0.7 copy-done.2
  2.8 2.6 %pack.1 = (bf16[256,768]{1,0:T(8,128)(2,1)S(1)}, bf16[256,768]{1,0:T(8,128)(2,1)S(1)}, bf16[256,768]{1,0:T(8,128)(2,1)S(1)}, bf16[128,768]{1,0:T(8,128)(2,1)S(1)...) custom-call(f32[512,768]{1,0:T(8,128)S(1)} %copy-done, ...), custom_call_target="tpu_custom_call" | custom-call | tf_op jit(solution)/shard_map/pack/pallas_call | solution.py:75
  5.4 3.1 %collective-permute-start = (f32[1,256]{1,0:T(1,128)S(1)}, f32[1,256]{1,0:T(1,128)S(1)}, u32[]{:S(2)}, u32[]{:S(2)}) collective-permute-start(f32[1,256]{1,0:T(1,128)S(1)} %get-tuple-element.27), channel_id=1, source_target_pairs={{0,4},{1,5},{2,6},{3,7},{4,8},{5,9},{6,10},{7,11},{8,12},{9,13},{1... | collective-permute-start | bytes 3080 | tf_op jit(solution)/shard_map/ppermute | solution.py:207
  8.5 2.1 %collective-permute-start.1 = (f32[1,256]{1,0:T(1,128)S(1)}, f32[1,256]{1,0:T(1,128)S(1)}, u32[]{:S(2)}, u32[]{:S(2)}) collective-permute-start(f32[1,256]{1,0:T(1,128)S(1)} %get-tuple-element.28), channel_id=1, source_target_pairs={{0,12},{1,13},{2,14},{3,15},{4,0},{5,1},{6,2},{7,3},{8,4},{9,5},{1... | collective-permute-start | bytes 3080 | tf_op jit(solution)/shard_map/ppermute | solution.py:207
  10.6 0.9 %collective-permute-start.2 = (f32[1,256]{1,0:T(1,128)S(1)}, f32[1,256]{1,0:T(1,128)S(1)}, u32[]{:S(2)}, u32[]{:S(2)}) collective-permute-start(f32[1,256]{1,0:T(1,128)S(1)} %get-tuple-element.29), channel_id=1, source_target_pairs={{0,8},{1,9},{2,10},{3,11},{4,12},{5,13},{6,14},{7,15},{8,0},{9,1},... | collective-permute-start | bytes 3080 | tf_op jit(solution)/shard_map/ppermute | solution.py:207
  11.5 0.5 collective-permute-done
  12.1 0.0 collective-permute-done.1
  12.1 3.0 %collective-permute-done.2 = f32[1,256]{1,0:T(1,128)S(1)} collective-permute-done((f32[1,256]{1,0:T(1,128)S(1)}, f32[1,256]{1,0:T(1,128)S(1)}, u32[]{:S(2)}, u32[]{:S(2)}) %collective-permute-start.2) | collective-permute-done | bytes 1056 | tf_op jit(solution)/shard_map/ppermute | solution.py:207
  15.1 1.6 %collective-permute-start.3 = (f32[1,1024]{1,0:T(1,128)S(1)}, f32[1,1024]{1,0:T(1,128)S(1)}, u32[]{:S(2)}, u32[]{:S(2)}) collective-permute-start(f32[1,1024]{1,0:T(1,128)S(1)} %constant_dynamic-update-slice_fusion), channel_id=1, source_target_pairs={{0,2},{1,3},{2,0},{3,1},{4,6},{5,7},{6,4},{7,5},{8,10},{9,11},{10,... | collective-permute-start | bytes 12296 | tf_op jit(solution)/shard_map/ppermute | solution.py:210
  16.7 0.0 collective-permute-start.8
  16.7 2.0 %collective-permute-done.3 = f32[1,1024]{1,0:T(1,128)S(1)} collective-permute-done((f32[1,1024]{1,0:T(1,128)S(1)}, f32[1,1024]{1,0:T(1,128)S(1)}, u32[]{:S(2)}, u32[]{:S(2)}) %collective-permute-start.3) | collective-permute-done | bytes 4128 | tf_op jit(solution)/shard_map/ppermute | solution.py:210
  18.7 0.1 collective-permute-start.4
  18.8 1.2 %collective-permute-done.4.refs_1_ = f32[2,1024]{1,0:T(2,128)S(1)} collective-permute-done((f32[2,1024]{1,0:T(2,128)S(1)}, f32[2,1024]{1,0:T(2,128)S(1)}, u32[]{:S(2)}, u32[]{:S(2)}) %collective-permute-start.4) | collective-permute-done | bytes 8224 | tf_op jit(solution)/shard_map/ppermute | solution.py:210
  19.9 2.0 %collective-permute-start.12 = (bf16[256,768]{1,0:T(8,128)(2,1)S(1)}, bf16[256,768]{1,0:T(8,128)(2,1)S(1)}, u32[]{:S(2)}, u32[]{:S(2)}) collective-permute-start(bf16[256,768]{1,0:T(8,128)(2,1)S(1)} %get-tuple-element.37), channel_id=1, source_target_pairs={{0,12},{1,13},{2,14},{3,15},{4,0},{5,1},{6,2},{7,3},{8,4},{9,5},{1... | collective-permute-start | bytes 1179656 | tf_op jit(solution)/shard_map/ppermute | solution.py:207
  21.9 0.0 collective-permute-start.6
  21.9 1.5 %collective-permute-start.5 = (bf16[256,768]{1,0:T(8,128)(2,1)S(1)}, bf16[256,768]{1,0:T(8,128)(2,1)S(1)}, u32[]{:S(2)}, u32[]{:S(2)}) collective-permute-start(bf16[256,768]{1,0:T(8,128)(2,1)S(1)} %get-tuple-element.32.refs_2_), channel_id=1, source_target_pairs={{0,2},{1,3},{2,0},{3,1},{4,6},{5,7},{6,4},{7,5},{8,10},{9,11},{10,... | collective-permute-start | bytes 1179656 | tf_op jit(solution)/shard_map/ppermute | solution.py:210
  23.4 7.2 %collective-permute-done.8.refs_6_ = bf16[256,768]{1,0:T(8,128)(2,1)S(1)} collective-permute-done((bf16[256,768]{1,0:T(8,128)(2,1)S(1)}, bf16[256,768]{1,0:T(8,128)(2,1)S(1)}, u32[]{:S(2)}, u32[]{:S(2)}) %collective-permute-start.8) | collective-permute-done | bytes 393248 | tf_op jit(solution)/shard_map/ppermute | solution.py:207
  30.6 0.3 collective-permute-start.9
  30.9 0.0 collective-permute-start.16
  30.9 5.0 %collective-permute-done.12.refs_10_ = bf16[256,768]{1,0:T(8,128)(2,1)S(1)} collective-permute-done((bf16[256,768]{1,0:T(8,128)(2,1)S(1)}, bf16[256,768]{1,0:T(8,128)(2,1)S(1)}, u32[]{:S(2)}, u32[]{:S(2)}) %collective-permute-start.12) | collective-permute-done | bytes 393248 | tf_op jit(solution)/shard_map/ppermute | solution.py:207
  36.0 0.6 collective-permute-start.13
  36.5 0.0 collective-permute-done.6.refs_4_
  36.5 2.6 %collective-permute-start.20 = (bf16[128,768]{1,0:T(8,128)(2,1)S(1)}, bf16[128,768]{1,0:T(8,128)(2,1)S(1)}, u32[]{:S(2)}, u32[]{:S(2)}) collective-permute-start(bf16[128,768]{1,0:T(8,128)(2,1)S(1)} %get-tuple-element.40), channel_id=1, source_target_pairs={{0,8},{1,9},{2,10},{3,11},{4,12},{5,13},{6,14},{7,15},{8,0},{9,1},... | collective-permute-start | bytes 589832 | tf_op jit(solution)/shard_map/ppermute | solution.py:207
  39.1 0.0 collective-permute-done.5.refs_3_
  39.1 0.0 collective-permute-start.7
  39.1 9.5 %collective-permute-done.16.refs_14_ = bf16[128,768]{1,0:T(8,128)(2,1)S(1)} collective-permute-done((bf16[128,768]{1,0:T(8,128)(2,1)S(1)}, bf16[128,768]{1,0:T(8,128)(2,1)S(1)}, u32[]{:S(2)}, u32[]{:S(2)}) %collective-permute-start.16) | collective-permute-done | bytes 196640 | tf_op jit(solution)/shard_map/ppermute | solution.py:207
  48.6 0.5 collective-permute-start.17
  49.2 3.6 %collective-permute-done.20.refs_18_ = bf16[128,768]{1,0:T(8,128)(2,1)S(1)} collective-permute-done((bf16[128,768]{1,0:T(8,128)(2,1)S(1)}, bf16[128,768]{1,0:T(8,128)(2,1)S(1)}, u32[]{:S(2)}, u32[]{:S(2)}) %collective-permute-start.20) | collective-permute-done | bytes 196640 | tf_op jit(solution)/shard_map/ppermute | solution.py:207
  52.8 0.0 collective-permute-start.10
  52.8 0.0 collective-permute-done.9.refs_7_
  52.8 0.5 collective-permute-start.11
  53.3 2.1 %collective-permute-done.17.refs_15_ = bf16[128,768]{1,0:T(8,128)(2,1)S(1)} collective-permute-done((bf16[128,768]{1,0:T(8,128)(2,1)S(1)}, bf16[128,768]{1,0:T(8,128)(2,1)S(1)}, u32[]{:S(2)}, u32[]{:S(2)}) %collective-permute-start.17) | collective-permute-done | bytes 196640 | tf_op jit(solution)/shard_map/ppermute | solution.py:210
  55.4 0.0 collective-permute-start.14
  55.4 0.0 collective-permute-done.13.refs_11_
  55.4 0.5 collective-permute-start.15
  55.9 0.0 collective-permute-done.7.refs_5_
  55.9 0.6 collective-permute-start.21
  56.5 0.6 compare1.1.refs_10_
  57.1 0.0 collective-permute-done.10.refs_8_
  57.1 0.1 collective-permute-start.18
  57.2 0.0 collective-permute-done.11.refs_9_
  57.2 0.5 collective-permute-start.19
  57.7 1.5 %compare2.1.refs_14_ = f32[1,512]{1,0:T(1,128)S(1)} custom-call(f32[2,1024]{1,0:T(2,128)S(1)} %pad_maximum_fusion.refs_0_, f32[2,1024]{1,0:T(2,128)S(1)} %collective-permute-done.4.refs_1_, bf16[256,768]{1,0:T(8,128)(2,1)S(1)} %get-tuple-element.32.refs_2_, bf16[256,768]{1,0:T(8,128)(2,1)S(1)} %collective-permute-done.5.refs_3_, ...), custom_call_target="tpu_custom_call" | custom-call | flops 1207959552 | bytes 3145728 | tf_op jit(solution)/shard_map/compare2/pallas_call | solution.py:152
  59.2 3.6 %collective-permute-done.21.refs_19_ = bf16[128,768]{1,0:T(8,128)(2,1)S(1)} collective-permute-done((bf16[128,768]{1,0:T(8,128)(2,1)S(1)}, bf16[128,768]{1,0:T(8,128)(2,1)S(1)}, u32[]{:S(2)}, u32[]{:S(2)}) %collective-permute-start.21) | collective-permute-done | bytes 196640 | tf_op jit(solution)/shard_map/ppermute | solution.py:210
  62.8 0.0 collective-permute-start.22
  62.8 0.0 collective-permute-done.14.refs_12_
  62.8 0.5 collective-permute-start.23
  63.3 0.0 collective-permute-done.15.refs_13_
  63.3 2.3 %compare3.1.refs_18_ = f32[1,768]{1,0:T(1,128)S(1)} custom-call(f32[2,1024]{1,0:T(2,128)S(1)} %pad_maximum_fusion.refs_0_, f32[2,1024]{1,0:T(2,128)S(1)} %collective-permute-done.4.refs_1_, bf16[256,768]{1,0:T(8,128)(2,1)S(1)} %get-tuple-element.32.refs_2_, bf16[256,768]{1,0:T(8,128)(2,1)S(1)} %collective-permute-done.5.refs_3_, ...), custom_call_target="tpu_custom_call" | custom-call | flops 2013265920 | bytes 4718592 | tf_op jit(solution)/shard_map/compare3/pallas_call | solution.py:152
  65.7 0.0 collective-permute-done.18.refs_16_
  65.7 0.0 collective-permute-done.19.refs_17_
  65.7 3.2 %compare4.1.refs_22_ = f32[1,896]{1,0:T(1,128)S(1)} custom-call(f32[2,1024]{1,0:T(2,128)S(1)} %pad_maximum_fusion.refs_0_, f32[2,1024]{1,0:T(2,128)S(1)} %collective-permute-done.4.refs_1_, bf16[256,768]{1,0:T(8,128)(2,1)S(1)} %get-tuple-element.32.refs_2_, bf16[256,768]{1,0:T(8,128)(2,1)S(1)} %collective-permute-done.5.refs_3_, ...), custom_call_target="tpu_custom_call" | custom-call | flops 1308622848 | bytes 5505024 | tf_op jit(solution)/shard_map/compare4/pallas_call | solution.py:152
  68.9 0.0 collective-permute-done.22.refs_20_
  68.9 0.0 collective-permute-done.23.refs_21_
  68.9 3.7 %compare5.1 = (f32[1,256]{1,0:T(1,128)S(1)}, f32[1,256]{1,0:T(1,128)S(1)}, f32[1,256]{1,0:T(1,128)S(1)}, f32[1,256]{1,0:T(1,128)S(1)}) custom-call(f32[2,1024]{1,0:T(2,128)S(1)} %pad_maximum_fusion.refs_0_, f32[2,1024]{1,0:T(2,128)S(1)} %collective-permute-done.4.refs_1_, bf16[256,768]{1,0:T(8,128)(2,1)S(1)} %get-tuple-element.32.refs_2_, ...), custom_call_target="tpu_custom_call" | custom-call | flops 1509949440 | bytes 6291456 | tf_op jit(solution)/shard_map/compare5/pallas_call | solution.py:152
  72.6 0.1 collective-permute-start.24
  72.7 2.0 %collective-permute-start.25 = (f32[1,256]{1,0:T(1,128)S(1)}, f32[1,256]{1,0:T(1,128)S(1)}, u32[]{:S(2)}, u32[]{:S(2)}) collective-permute-start(f32[1,256]{1,0:T(1,128)S(1)} %get-tuple-element.43), channel_id=1, source_target_pairs={{0,4},{1,5},{2,6},{3,7},{4,8},{5,9},{6,10},{7,11},{8,12},{9,13},{1... | collective-permute-start | bytes 3080 | tf_op jit(solution)/shard_map/ppermute | solution.py:207
  74.7 0.0 collective-permute-start.26
  74.7 1.5 %collective-permute-done.24.refs_1_ = f32[1,256]{1,0:T(1,128)S(1)} collective-permute-done((f32[1,256]{1,0:T(1,128)S(1)}, f32[1,256]{1,0:T(1,128)S(1)}, u32[]{:S(2)}, u32[]{:S(2)}) %collective-permute-start.24) | collective-permute-done | bytes 1056 | tf_op jit(solution)/shard_map/ppermute | solution.py:207
  76.3 1.9 %collective-permute-done.25.refs_2_ = f32[1,256]{1,0:T(1,128)S(1)} collective-permute-done((f32[1,256]{1,0:T(1,128)S(1)}, f32[1,256]{1,0:T(1,128)S(1)}, u32[]{:S(2)}, u32[]{:S(2)}) %collective-permute-start.25) | collective-permute-done | bytes 1056 | tf_op jit(solution)/shard_map/ppermute | solution.py:207
  78.1 1.1 %collective-permute-done.26.refs_3_ = f32[1,256]{1,0:T(1,128)S(1)} collective-permute-done((f32[1,256]{1,0:T(1,128)S(1)}, f32[1,256]{1,0:T(1,128)S(1)}, u32[]{:S(2)}, u32[]{:S(2)}) %collective-permute-start.26) | collective-permute-done | bytes 1056 | tf_op jit(solution)/shard_map/ppermute | solution.py:207
  79.2 1.1 %unpack.1 = f32[1,512]{1,0:T(1,128)} custom-call(s32[1,512]{1,0:T(1,128)S(1)} %get-tuple-element.25.slot_ref, f32[1,256]{1,0:T(1,128)S(1)} %get-tuple-element.41.refs_0_, f32[1,256]{1,0:T(1,128)S(1)} %collective-permute-done.24.refs_1_, f32[1,256]{1,0:T(1,128)S(1)} %collective-permute-done.25.refs_2_, f32[1,256]{1,0:T(1,128)S(1)} %collective-permute-done.26.refs_3_), custom_call_target="tpu_custom_call" | custom-call | tf_op jit(solution)/shard_map/unpack/pallas_call | solution.py:183
  (8 shorter events, 0.0 us)
Async XLA Ops:
  0.0 1.4 %copy-start = (f32[512,768]{1,0:T(8,128)S(1)}, f32[512,768]{1,0:T(8,128)}, u32[]{:S(2)}) copy-start(f32[512,768]{1,0:T(8,128)} %refs_0_.1) | copy-start | bytes 4718596
  1.4 0.7 copy-start.1
  2.1 0.7 copy-start.2
  5.4 6.7 %collective-permute-start = (f32[1,256]{1,0:T(1,128)S(1)}, f32[1,256]{1,0:T(1,128)S(1)}, u32[]{:S(2)}, u32[]{:S(2)}) collective-permute-start(f32[1,256]{1,0:T(1,128)S(1)} %get-tuple-element.27), channel_id=1, source_target_pairs={{0,4},{1,5},{2,6},{3,7},{4,8},{5,9},{6,10},{7,11},{8,12},{9,13},{1... | collective-permute-start | bytes 3080 | tf_op jit(solution)/shard_map/ppermute | solution.py:207
  8.5 3.6 %collective-permute-start.1 = (f32[1,256]{1,0:T(1,128)S(1)}, f32[1,256]{1,0:T(1,128)S(1)}, u32[]{:S(2)}, u32[]{:S(2)}) collective-permute-start(f32[1,256]{1,0:T(1,128)S(1)} %get-tuple-element.28), channel_id=1, source_target_pairs={{0,12},{1,13},{2,14},{3,15},{4,0},{5,1},{6,2},{7,3},{8,4},{9,5},{1... | collective-permute-start | bytes 3080 | tf_op jit(solution)/shard_map/ppermute | solution.py:207
  10.6 4.5 %collective-permute-start.2 = (f32[1,256]{1,0:T(1,128)S(1)}, f32[1,256]{1,0:T(1,128)S(1)}, u32[]{:S(2)}, u32[]{:S(2)}) collective-permute-start(f32[1,256]{1,0:T(1,128)S(1)} %get-tuple-element.29), channel_id=1, source_target_pairs={{0,8},{1,9},{2,10},{3,11},{4,12},{5,13},{6,14},{7,15},{8,0},{9,1},... | collective-permute-start | bytes 3080 | tf_op jit(solution)/shard_map/ppermute | solution.py:207
  15.1 3.6 %collective-permute-start.3 = (f32[1,1024]{1,0:T(1,128)S(1)}, f32[1,1024]{1,0:T(1,128)S(1)}, u32[]{:S(2)}, u32[]{:S(2)}) collective-permute-start(f32[1,1024]{1,0:T(1,128)S(1)} %constant_dynamic-update-slice_fusion), channel_id=1, source_target_pairs={{0,2},{1,3},{2,0},{3,1},{4,6},{5,7},{6,4},{7,5},{8,10},{9,11},{10,... | collective-permute-start | bytes 12296 | tf_op jit(solution)/shard_map/ppermute | solution.py:210
  16.7 13.9 %collective-permute-start.8 = (bf16[256,768]{1,0:T(8,128)(2,1)S(1)}, bf16[256,768]{1,0:T(8,128)(2,1)S(1)}, u32[]{:S(2)}, u32[]{:S(2)}) collective-permute-start(bf16[256,768]{1,0:T(8,128)(2,1)S(1)} %get-tuple-element.34), channel_id=1, source_target_pairs={{0,4},{1,5},{2,6},{3,7},{4,8},{5,9},{6,10},{7,11},{8,12},{9,13},{1... | collective-permute-start | bytes 1179656 | tf_op jit(solution)/shard_map/ppermute | solution.py:207
  18.7 1.2 %collective-permute-start.4 = (f32[2,1024]{1,0:T(2,128)S(1)}, f32[2,1024]{1,0:T(2,128)S(1)}, u32[]{:S(2)}, u32[]{:S(2)}) collective-permute-start(f32[2,1024]{1,0:T(2,128)S(1)} %pad_maximum_fusion.refs_0_), channel_id=1, source_target_pairs={{0,1},{1,0},{2,3},{3,2},{4,5},{5,4},{6,7},{7,6},{8,9},{9,8},{10,11... | collective-permute-start | bytes 24584 | tf_op jit(solution)/shard_map/ppermute | solution.py:210
  19.9 16.1 %collective-permute-start.12 = (bf16[256,768]{1,0:T(8,128)(2,1)S(1)}, bf16[256,768]{1,0:T(8,128)(2,1)S(1)}, u32[]{:S(2)}, u32[]{:S(2)}) collective-permute-start(bf16[256,768]{1,0:T(8,128)(2,1)S(1)} %get-tuple-element.37), channel_id=1, source_target_pairs={{0,12},{1,13},{2,14},{3,15},{4,0},{5,1},{6,2},{7,3},{8,4},{9,5},{1... | collective-permute-start | bytes 1179656 | tf_op jit(solution)/shard_map/ppermute | solution.py:207
  21.9 14.7 %collective-permute-start.6 = (bf16[256,768]{1,0:T(8,128)(2,1)S(1)}, bf16[256,768]{1,0:T(8,128)(2,1)S(1)}, u32[]{:S(2)}, u32[]{:S(2)}) collective-permute-start(bf16[256,768]{1,0:T(8,128)(2,1)S(1)} %get-tuple-element.32.refs_2_), channel_id=1, source_target_pairs={{0,1},{1,0},{2,3},{3,2},{4,5},{5,4},{6,7},{7,6},{8,9},{9,8},{10,11... | collective-permute-start | bytes 1179656 | tf_op jit(solution)/shard_map/ppermute | solution.py:210
  21.9 17.3 %collective-permute-start.5 = (bf16[256,768]{1,0:T(8,128)(2,1)S(1)}, bf16[256,768]{1,0:T(8,128)(2,1)S(1)}, u32[]{:S(2)}, u32[]{:S(2)}) collective-permute-start(bf16[256,768]{1,0:T(8,128)(2,1)S(1)} %get-tuple-element.32.refs_2_), channel_id=1, source_target_pairs={{0,2},{1,3},{2,0},{3,1},{4,6},{5,7},{6,4},{7,5},{8,10},{9,11},{10,... | collective-permute-start | bytes 1179656 | tf_op jit(solution)/shard_map/ppermute | solution.py:210
  30.6 22.2 %collective-permute-start.9 = (bf16[256,768]{1,0:T(8,128)(2,1)S(1)}, bf16[256,768]{1,0:T(8,128)(2,1)S(1)}, u32[]{:S(2)}, u32[]{:S(2)}) collective-permute-start(bf16[256,768]{1,0:T(8,128)(2,1)S(1)} %collective-permute-done.8.refs_6_), channel_id=1, source_target_pairs={{0,2},{1,3},{2,0},{3,1},{4,6},{5,7},{6,4},{7,5},{8,10},{9,11},{10,... | collective-permute-start | bytes 1179656 | tf_op jit(solution)/shard_map/ppermute | solution.py:210
  30.9 17.7 %collective-permute-start.16 = (bf16[128,768]{1,0:T(8,128)(2,1)S(1)}, bf16[128,768]{1,0:T(8,128)(2,1)S(1)}, u32[]{:S(2)}, u32[]{:S(2)}) collective-permute-start(bf16[128,768]{1,0:T(8,128)(2,1)S(1)} %get-tuple-element.39), channel_id=1, source_target_pairs={{0,8},{1,9},{2,10},{3,11},{4,12},{5,13},{6,14},{7,15},{8,0},{9,1},... | collective-permute-start | bytes 589832 | tf_op jit(solution)/shard_map/ppermute | solution.py:207
  36.0 19.4 %collective-permute-start.13 = (bf16[256,768]{1,0:T(8,128)(2,1)S(1)}, bf16[256,768]{1,0:T(8,128)(2,1)S(1)}, u32[]{:S(2)}, u32[]{:S(2)}) collective-permute-start(bf16[256,768]{1,0:T(8,128)(2,1)S(1)} %collective-permute-done.12.refs_10_), channel_id=1, source_target_pairs={{0,2},{1,3},{2,0},{3,1},{4,6},{5,7},{6,4},{7,5},{8,10},{9,11},{10,... | collective-permute-start | bytes 1179656 | tf_op jit(solution)/shard_map/ppermute | solution.py:210
  36.5 16.2 %collective-permute-start.20 = (bf16[128,768]{1,0:T(8,128)(2,1)S(1)}, bf16[128,768]{1,0:T(8,128)(2,1)S(1)}, u32[]{:S(2)}, u32[]{:S(2)}) collective-permute-start(bf16[128,768]{1,0:T(8,128)(2,1)S(1)} %get-tuple-element.40), channel_id=1, source_target_pairs={{0,8},{1,9},{2,10},{3,11},{4,12},{5,13},{6,14},{7,15},{8,0},{9,1},... | collective-permute-start | bytes 589832 | tf_op jit(solution)/shard_map/ppermute | solution.py:207
  39.1 16.8 %collective-permute-start.7 = (bf16[256,768]{1,0:T(8,128)(2,1)S(1)}, bf16[256,768]{1,0:T(8,128)(2,1)S(1)}, u32[]{:S(2)}, u32[]{:S(2)}) collective-permute-start(bf16[256,768]{1,0:T(8,128)(2,1)S(1)} %collective-permute-done.5.refs_3_), channel_id=1, source_target_pairs={{0,1},{1,0},{2,3},{3,2},{4,5},{5,4},{6,7},{7,6},{8,9},{9,8},{10,11... | collective-permute-start | bytes 1179656 | tf_op jit(solution)/shard_map/ppermute | solution.py:210
  48.6 6.8 %collective-permute-start.17 = (bf16[128,768]{1,0:T(8,128)(2,1)S(1)}, bf16[128,768]{1,0:T(8,128)(2,1)S(1)}, u32[]{:S(2)}, u32[]{:S(2)}) collective-permute-start(bf16[128,768]{1,0:T(8,128)(2,1)S(1)} %collective-permute-done.16.refs_14_), channel_id=1, source_target_pairs={{0,2},{1,3},{2,0},{3,1},{4,6},{5,7},{6,4},{7,5},{8,10},{9,11},{10,... | collective-permute-start | bytes 589832 | tf_op jit(solution)/shard_map/ppermute | solution.py:210
  52.8 4.4 %collective-permute-start.10 = (bf16[256,768]{1,0:T(8,128)(2,1)S(1)}, bf16[256,768]{1,0:T(8,128)(2,1)S(1)}, u32[]{:S(2)}, u32[]{:S(2)}) collective-permute-start(bf16[256,768]{1,0:T(8,128)(2,1)S(1)} %collective-permute-done.8.refs_6_), channel_id=1, source_target_pairs={{0,1},{1,0},{2,3},{3,2},{4,5},{5,4},{6,7},{7,6},{8,9},{9,8},{10,11... | collective-permute-start | bytes 1179656 | tf_op jit(solution)/shard_map/ppermute | solution.py:210
  52.8 4.4 %collective-permute-start.11 = (bf16[256,768]{1,0:T(8,128)(2,1)S(1)}, bf16[256,768]{1,0:T(8,128)(2,1)S(1)}, u32[]{:S(2)}, u32[]{:S(2)}) collective-permute-start(bf16[256,768]{1,0:T(8,128)(2,1)S(1)} %collective-permute-done.9.refs_7_), channel_id=1, source_target_pairs={{0,1},{1,0},{2,3},{3,2},{4,5},{5,4},{6,7},{7,6},{8,9},{9,8},{10,11... | collective-permute-start | bytes 1179656 | tf_op jit(solution)/shard_map/ppermute | solution.py:210
  55.4 7.4 %collective-permute-start.14 = (bf16[256,768]{1,0:T(8,128)(2,1)S(1)}, bf16[256,768]{1,0:T(8,128)(2,1)S(1)}, u32[]{:S(2)}, u32[]{:S(2)}) collective-permute-start(bf16[256,768]{1,0:T(8,128)(2,1)S(1)} %collective-permute-done.12.refs_10_), channel_id=1, source_target_pairs={{0,1},{1,0},{2,3},{3,2},{4,5},{5,4},{6,7},{7,6},{8,9},{9,8},{10,11... | collective-permute-start | bytes 1179656 | tf_op jit(solution)/shard_map/ppermute | solution.py:210
  55.4 7.9 %collective-permute-start.15 = (bf16[256,768]{1,0:T(8,128)(2,1)S(1)}, bf16[256,768]{1,0:T(8,128)(2,1)S(1)}, u32[]{:S(2)}, u32[]{:S(2)}) collective-permute-start(bf16[256,768]{1,0:T(8,128)(2,1)S(1)} %collective-permute-done.13.refs_11_), channel_id=1, source_target_pairs={{0,1},{1,0},{2,3},{3,2},{4,5},{5,4},{6,7},{7,6},{8,9},{9,8},{10,11... | collective-permute-start | bytes 1179656 | tf_op jit(solution)/shard_map/ppermute | solution.py:210
  55.9 6.9 %collective-permute-start.21 = (bf16[128,768]{1,0:T(8,128)(2,1)S(1)}, bf16[128,768]{1,0:T(8,128)(2,1)S(1)}, u32[]{:S(2)}, u32[]{:S(2)}) collective-permute-start(bf16[128,768]{1,0:T(8,128)(2,1)S(1)} %collective-permute-done.20.refs_18_), channel_id=1, source_target_pairs={{0,2},{1,3},{2,0},{3,1},{4,6},{5,7},{6,4},{7,5},{8,10},{9,11},{10,... | collective-permute-start | bytes 589832 | tf_op jit(solution)/shard_map/ppermute | solution.py:210
  57.1 8.5 %collective-permute-start.18 = (bf16[128,768]{1,0:T(8,128)(2,1)S(1)}, bf16[128,768]{1,0:T(8,128)(2,1)S(1)}, u32[]{:S(2)}, u32[]{:S(2)}) collective-permute-start(bf16[128,768]{1,0:T(8,128)(2,1)S(1)} %collective-permute-done.16.refs_14_), channel_id=1, source_target_pairs={{0,1},{1,0},{2,3},{3,2},{4,5},{5,4},{6,7},{7,6},{8,9},{9,8},{10,11... | collective-permute-start | bytes 589832 | tf_op jit(solution)/shard_map/ppermute | solution.py:210
  57.2 8.5 %collective-permute-start.19 = (bf16[128,768]{1,0:T(8,128)(2,1)S(1)}, bf16[128,768]{1,0:T(8,128)(2,1)S(1)}, u32[]{:S(2)}, u32[]{:S(2)}) collective-permute-start(bf16[128,768]{1,0:T(8,128)(2,1)S(1)} %collective-permute-done.17.refs_15_), channel_id=1, source_target_pairs={{0,1},{1,0},{2,3},{3,2},{4,5},{5,4},{6,7},{7,6},{8,9},{9,8},{10,11... | collective-permute-start | bytes 589832 | tf_op jit(solution)/shard_map/ppermute | solution.py:210
  62.8 6.1 %collective-permute-start.22 = (bf16[128,768]{1,0:T(8,128)(2,1)S(1)}, bf16[128,768]{1,0:T(8,128)(2,1)S(1)}, u32[]{:S(2)}, u32[]{:S(2)}) collective-permute-start(bf16[128,768]{1,0:T(8,128)(2,1)S(1)} %collective-permute-done.20.refs_18_), channel_id=1, source_target_pairs={{0,1},{1,0},{2,3},{3,2},{4,5},{5,4},{6,7},{7,6},{8,9},{9,8},{10,11... | collective-permute-start | bytes 589832 | tf_op jit(solution)/shard_map/ppermute | solution.py:210
  62.8 6.1 %collective-permute-start.23 = (bf16[128,768]{1,0:T(8,128)(2,1)S(1)}, bf16[128,768]{1,0:T(8,128)(2,1)S(1)}, u32[]{:S(2)}, u32[]{:S(2)}) collective-permute-start(bf16[128,768]{1,0:T(8,128)(2,1)S(1)} %collective-permute-done.21.refs_19_), channel_id=1, source_target_pairs={{0,1},{1,0},{2,3},{3,2},{4,5},{5,4},{6,7},{7,6},{8,9},{9,8},{10,11... | collective-permute-start | bytes 589832 | tf_op jit(solution)/shard_map/ppermute | solution.py:210
  72.6 3.6 %collective-permute-start.24 = (f32[1,256]{1,0:T(1,128)S(1)}, f32[1,256]{1,0:T(1,128)S(1)}, u32[]{:S(2)}, u32[]{:S(2)}) collective-permute-start(f32[1,256]{1,0:T(1,128)S(1)} %get-tuple-element.42), channel_id=1, source_target_pairs={{0,12},{1,13},{2,14},{3,15},{4,0},{5,1},{6,2},{7,3},{8,4},{9,5},{1... | collective-permute-start | bytes 3080 | tf_op jit(solution)/shard_map/ppermute | solution.py:207
  72.7 5.4 %collective-permute-start.25 = (f32[1,256]{1,0:T(1,128)S(1)}, f32[1,256]{1,0:T(1,128)S(1)}, u32[]{:S(2)}, u32[]{:S(2)}) collective-permute-start(f32[1,256]{1,0:T(1,128)S(1)} %get-tuple-element.43), channel_id=1, source_target_pairs={{0,4},{1,5},{2,6},{3,7},{4,8},{5,9},{6,10},{7,11},{8,12},{9,13},{1... | collective-permute-start | bytes 3080 | tf_op jit(solution)/shard_map/ppermute | solution.py:207
  74.7 4.5 %collective-permute-start.26 = (f32[1,256]{1,0:T(1,128)S(1)}, f32[1,256]{1,0:T(1,128)S(1)}, u32[]{:S(2)}, u32[]{:S(2)}) collective-permute-start(f32[1,256]{1,0:T(1,128)S(1)} %get-tuple-element.44), channel_id=1, source_target_pairs={{0,8},{1,9},{2,10},{3,11},{4,12},{5,13},{6,14},{7,15},{8,0},{9,1},... | collective-permute-start | bytes 3080 | tf_op jit(solution)/shard_map/ppermute | solution.py:207

commit v2 on v1

--- a/solution.py
+++ b/solution.py
@@ -6,7 +6,9 @@
 from jax.sharding import PartitionSpec as P
 
 GROUP = 4
-UNITS = (4, 4, 4, 2, 2)
+UNITS = (4, 4, 4, 4)
+BLOCKS = 4
+STEP = 512
 GRANT = 16 << 20
 NT = (((1,), (1,)), ((), ()))
 
@@ -85,57 +87,64 @@
             pltpu.VMEM((1, rows), jnp.int32),
             pltpu.SemaphoreType.DMA((6,)),
         ],
-        compiler_params=pltpu.CompilerParams(vmem_limit_bytes=GRANT),
         name="pack",
     )(embedding, owner.reshape(1, rows), cluster.reshape(1, rows))
 
 
-def compare_kernel(units, outs, *refs):
-    last = len(units) - 1
-    near, far, refs = refs[0], refs[1], refs[2:]
-    keys, refs = refs[: 4 * last + 4], refs[4 * last + 4 :]
-    if last:
-        best_ref, refs = refs[0], refs[1:]
-    outputs, query_ref = refs[:-1], refs[-1]
-    for q, (low, width) in enumerate(units):
-        query_ref[low : low + width, :] = keys[4 * q][...]
-    columns = []
-    for low, width in units:
-        span = slice(low, low + width)
-        wide = jnp.concatenate([near[:, span], far[:, span]] * 2, axis=0)
-        columns.append(wide.T)
-
-    def block(k, peer, low, width, same):
-        scores = lax.dot_general(
-            keys[4 * k + peer][...],
-            query_ref[low : low + width, :],
-            NT,
-            preferred_element_type=jnp.float32,
-        )
-        allowed = columns[k][:, peer : peer + 1] == near[0:1, low : low + width]
-        if same is not None:
-            allowed = allowed & (iota(scores.shape, 0) + same != iota(scores.shape, 1))
-        return jnp.max(jnp.where(allowed, scores, -1.0), axis=0, keepdims=True)
-
-    start, size = units[last]
-    total = start + size
-    step = 256
-    for low in range(0, total, step):
-        width = min(step, total - low)
-        best = jnp.full((1, width), -1.0)
-        for peer in range(4):
-            inside = peer == 0 and low <= start < low + width
-            best = jnp.maximum(best, block(last, peer, low, width, start - low if inside else None))
-        head = min(max(start - low, 0), width)
-        if head:
-            old = jnp.maximum(best[:, :head], best_ref[:, low : low + head])
-            spread(outputs, outs, low, old)
-        if head < width:
-            new = best[:, head:]
-            for k in range(last):
-                for peer in range(4):
-                    new = jnp.maximum(new, block(k, peer, start, size, None))
-            spread(outputs, outs, start, new)
+def compare_kernel(size, outs, jobs, shape, *refs):
+    near, far, best_ref, refs = refs[0], refs[1], refs[2], refs[3:]
+    count = sum(shape.values())
+    pieces, refs = refs[:count], refs[count:]
+    outputs, scratch = refs[: len(outs)], refs[len(outs) :]
+    place = {}
+    for index, key in enumerate(shape):
+        start = sum(list(shape.values())[:index])
+        low = 0
+        for ref in pieces[start : start + shape[key]]:
+            place.setdefault(key, []).append((low, ref))
+            low += ref.shape[0]
+    query_ref, extra = scratch[0], list(scratch[1:])
+    own = [k for p, k in shape if p == 0]
+    for k in own:
+        for low, ref in place[0, k]:
+            query_ref[k * size + low : k * size + low + ref.shape[0], :] = ref[...]
+    keys = {}
+    for key, parts in place.items():
+        if key[0] == 0:
+            keys[key] = query_ref.at[key[1] * size : (key[1] + 1) * size]
+        elif len(parts) == 1:
+            keys[key] = parts[0][1]
+        else:
+            keys[key] = extra.pop()
+            for low, ref in parts:
+                keys[key][low : low + ref.shape[0], :] = ref[...]
+    table = jnp.concatenate([near[...], far[...]] * 2, axis=0)
+    columns = {k: table[:, k * size : (k + 1) * size].T for k in sorted({k for _, k in shape})}
+    bests = [best_ref[:, k * size : (k + 1) * size] for k in range(BLOCKS)]
+    for low, high, k, peers in jobs:
+        for left in range(low, high, STEP // size):
+            right = min(left + STEP // size, high)
+            span = slice(left * size, right * size)
+            row = near[0:1, span]
+            best = None
+            for peer in peers:
+                scores = lax.dot_general(
+                    keys[peer, k][...],
+                    query_ref[span, :],
+                    NT,
+                    preferred_element_type=jnp.float32,
+                )
+                allowed = columns[k][:, peer : peer + 1] == row
+                if peer == 0 and left <= k < right:
+                    shift = (k - left) * size
+                    allowed = allowed & (iota(scores.shape, 0) + shift != iota(scores.shape, 1))
+                top = jnp.max(jnp.where(allowed, scores, -1.0), axis=0, keepdims=True)
+                best = top if best is None else jnp.maximum(best, top)
+            for q in range(left, right):
+                part = best[:, (q - left) * size : (q - left + 1) * size]
+                bests[q] = jnp.maximum(bests[q], part)
+    for q in range(BLOCKS):
+        spread(outputs, outs, q * size, bests[q])
 
 
 def spread(refs, outs, start, row):
@@ -145,22 +154,24 @@
             ref[:, a - low : b - low] = row[:, a - start : b - start]
 
 
-def compare(units, outs, labels, keys, best):
-    start, size = units[-1]
-    width = keys[0].shape[1]
-    pairs = 4 * size * (start + size) + 4 * start * size
+def compare(outs, jobs, labels, blocks, best):
+    size = sum(part.shape[0] for part in blocks[0, 0])
+    width = blocks[0, 0][0].shape[1]
+    shape = {key: len(parts) for key, parts in blocks.items()}
+    split = [key for key in shape if key[0] and shape[key] > 1]
+    tiles = sum((high - low) * len(peers) for low, high, _, peers in jobs)
+    queries = 1 + max(k for p, k in shape if p == 0)
     return pl.pallas_call(
-        lambda *refs: compare_kernel(units, outs, *refs),
+        lambda *refs: compare_kernel(size, outs, jobs, shape, *refs),
         out_shape=[jax.ShapeDtypeStruct((1, n), jnp.float32) for _, n in outs],
-        scratch_shapes=[pltpu.VMEM((start + size, width), jnp.bfloat16)],
+        scratch_shapes=[pltpu.VMEM((queries * size, width), jnp.bfloat16)]
+        + [pltpu.VMEM((size, width), jnp.bfloat16)] * len(split),
         compiler_params=pltpu.CompilerParams(vmem_limit_bytes=GRANT),
         cost_estimate=pl.CostEstimate(
-            flops=2 * pairs * width,
-            bytes_accessed=8 * (start + size) * width,
-            transcendentals=0,
+            flops=2 * tiles * size * size * width, bytes_accessed=0, transcendentals=0
         ),
-        name=f"compare{len(units)}",
-    )(*labels, *keys, *best)
+        name=f"compare{len(jobs)}_{tiles}",
+    )(*labels, best, *[part for parts in blocks.values() for part in parts])
 
 
 def unpack_kernel(slot_ref, *refs):
@@ -232,25 +243,39 @@
     def core(array):
         return swap(array, 1)
 
-    last = len(units) - 1
-    own = join([exchange(l, low, 1, 1) for l, (low, _) in zip(label, pieces)], 1)
-    label_x = cross(own)
-    near = jnp.concatenate([own, label_x], axis=0)
+    across, beside, beyond = [None] * BLOCKS, [None] * BLOCKS, [None] * BLOCKS
+    own = [blocks[0], send(1), None, None]
+    across[0], beside[0] = cross(own[0]), core(own[0])
+    *label, beside[0] = tie(*label, beside[0])
+    label = [exchange(l, low, 1, 1) for l, (low, _) in zip(label, pieces)]
+    label = join(label, 1)
+    near = jnp.concatenate([label, cross(label)], axis=0)
     labels = [near, core(near)]
-    queries = []
-    for u in range(last + 1):
-        block = blocks[u]
-        if u == 2:
-            block, labels[1] = tie(block, labels[1])
-        if u >= 3:
-            block, queries[u - 2] = tie(block, queries[u - 2])
-        queries.append(exchange(block, units[u][0], 0, 1))
-    keys, best = [], []
-    for u, (start, size) in enumerate(units):
-        across = cross(queries[u])
-        keys += [queries[u], across, core(queries[u]), core(across)]
-        outs = pieces if u == last else [(0, start + size)]
-        best = list(compare(units[: u + 1], outs, labels, keys, best))
+    blocks[2], beside[0] = tie(blocks[2], beside[0])
+    own[2] = send(2)
+    blocks[3], own[1] = tie(blocks[3], own[1])
+    own[3] = send(3)
+    for u in range(1, BLOCKS):
+        beside[u] = core(own[u])
+        across[u] = cross(own[u])
+    for u in range(BLOCKS - 1):
+        beyond[u] = core(across[u])
+    arrays = [own, across, beside, beyond]
+
+    def given(peers, blocks):
+        return {(peer, k): [arrays[peer][k]] for peer in peers for k in blocks}
+
+    every, row = (0, 1, 2, 3), [(0, slots)]
+    best = jnp.full((1, slots), -1.0, jnp.float32)
+    jobs = [(0, 4, 0, every), (0, 4, 1, every), (0, 4, 2, (0, 2)), (0, 4, 3, (0, 2))]
+    some = given((0, 2), range(4)) | given((1, 3), range(2))
+    (best,) = compare(row, jobs, labels, some, best)
+    across[3], best = tie(across[3], best)
+    beyond[3] = core(across[3])
+    some = given((0,), range(4)) | given((1, 3), (2,))
+    (best,) = compare(row, [(0, 4, 2, (1, 3))], labels, some, best)
+    some = given((0,), range(4)) | given((1, 3), (3,))
+    best = compare(pieces, [(0, 4, 3, (1, 3))], labels, some, best)
     backs = [exchange(b, low, 1, -1) for b, (low, _) in zip(best, pieces)]
     return unpack(slot, backs).reshape(rows)
 

time: 80.5 us -> 72.2 us (0.90)
  waiting for transfers between devices: 42.2 us -> 36.9 us
  Pallas kernels: 15.1 us -> 11.9 us
  starting transfers between devices: 20.1 us -> 21.4 us
  local copies, waits for them, and re-layouts: 2.79 us -> 1.7 us
    pallas_call x5 -> x3, Pallas kernels: 11.4 us -> 7.33 us  [compare(): pl.pallas_call(lambda *refs: compare_kernel(size, outs, jobs, shape, *ref...]
    ppermute x17 -> x14, waiting for transfers between devices: 8.89 us -> 5.37 us  [swap(): return lax.ppermute(array, 'blk', [(i, i ^ mask) for i in range(devices)])]
    ppermute x17 -> x14, starting transfers between devices: 7.31 us -> 9.1 us  [swap(): return lax.ppermute(array, 'blk', [(i, i ^ mask) for i in range(devices)])]
    ppermute x10 -> x9, waiting for transfers between devices: 33.3 us -> 31.6 us  [shift(): lax.ppermute(array, 'blk', [(i, (i + step) % devices) for i in range(devi...]
    unnamed x9 -> x7, local copies, waits for them, and re-layouts: 2.79 us -> 1.69 us
    pallas_call x1, Pallas kernels: 2.63 us -> 3.44 us  [pack(): pl.pallas_call(lambda *refs: pack_kernel(groups, cap, units, pieces, *ref...]
    ppermute x10 -> x9, starting transfers between devices: 12.8 us -> 12.3 us  [shift(): lax.ppermute(array, 'blk', [(i, (i + step) % devices) for i in range(devi...]
  transfers between devices with their start and end apart: 27 -> 23, of which waited for: 13 -> 9; matrix products, arithmetic and copies ran while one was open for 0% -> 1% of each run, Pallas kernels for 10% -> 9%
where the time goes in v2:
time: 72.2 us; the launch traced here: 72 us
  waiting for transfers between devices  36.9 us (51%)
  starting transfers between devices  21.4 us (30%)
  Pallas kernels  11.9 us (16%)
  local copies, waits for them, and re-layouts  1.7 us (2%)
    ppermute x9, waiting for transfers between devices, shift(): lax.ppermute(array, 'blk', [(i, (i + step) % devices) for i in range(devi...  31.6 us
    ppermute x9, starting transfers between devices, shift(): lax.ppermute(array, 'blk', [(i, (i + step) % devices) for i in range(devi...  12.3 us
    ppermute x14, starting transfers between devices, swap(): return lax.ppermute(array, 'blk', [(i, i ^ mask) for i in range(devices)])  9.1 us
    pallas_call x3, Pallas kernels, compare(): pl.pallas_call(lambda *refs: compare_kernel(size, outs, jobs, shape, *ref...  7.33 us
    ppermute x14, waiting for transfers between devices, swap(): return lax.ppermute(array, 'blk', [(i, i ^ mask) for i in range(devices)])  5.37 us
    pallas_call x1, Pallas kernels, pack(): pl.pallas_call(lambda *refs: pack_kernel(groups, cap, units, pieces, *ref...  3.44 us
    unnamed x7, local copies, waits for them, and re-layouts  1.69 us
  transfers between devices with their start and end apart: 23, of which 9 were waited for; matrix products, arithmetic and copies ran while one was open for 1% of the time, Pallas kernels for 9%

profile of v2, /device:TPU:0, one launch (start us, length us, event | category | flops | bytes accessed | tf_op | source)
XLA Modules:
  0.0 72.0 jit_solution(2714415532822021042)
XLA Ops:
  0.0 3.4 %pack.1 = (bf16[256,768]{1,0:T(8,128)(2,1)}, bf16[256,768]{1,0:T(8,128)(2,1)}, bf16[256,768]{1,0:T(8,128)(2,1)}, bf16[256,768]{1,0:T(8,128)(2,1)}, f32[1,256]{1,...) custom-call(f32[512,768]{1,0:T(8,128)} %refs_0_.1, s32[1,512]{1,0:T(1,128)} %bitcast.3, ...), custom_call_target="tpu_custom_call" | custom-call | tf_op jit(solution)/shard_map/pack/pallas_call | solution.py:77
  3.5 0.5 collective-permute-start
  4.0 2.6 %collective-permute-start.13 = (bf16[256,768]{1,0:T(8,128)(2,1)}, bf16[256,768]{1,0:T(8,128)(2,1)S(1)}, u32[]{:S(2)}, u32[]{:S(2)}) collective-permute-start(bf16[256,768]{1,0:T(8,128)(2,1)} %get-tuple-element.34.refs_3_), channel_id=1, source_target_pairs={{0,2},{1,3},{2,0},{3,1},{4,6},{5,7},{6,4},{7,5},{8,10},{9,11},{10,... | collective-permute-start | bytes 1179656 | tf_op jit(solution)/shard_map/ppermute | solution.py:221
  6.5 1.6 %collective-permute-start.6 = (bf16[256,768]{1,0:T(8,128)(2,1)}, bf16[256,768]{1,0:T(8,128)(2,1)S(1)}, u32[]{:S(2)}, u32[]{:S(2)}) collective-permute-start(bf16[256,768]{1,0:T(8,128)(2,1)} %get-tuple-element.40), channel_id=1, source_target_pairs={{0,4},{1,5},{2,6},{3,7},{4,8},{5,9},{6,10},{7,11},{8,12},{9,13},{1... | collective-permute-start | bytes 1179656 | tf_op jit(solution)/shard_map/ppermute | solution.py:218
  8.1 0.0 collective-permute-done.refs_7_
  8.1 1.6 %collective-permute-start.1 = (f32[1,256]{1,0:T(1,128)}, f32[1,256]{1,0:T(1,128)S(1)}, u32[]{:S(2)}, u32[]{:S(2)}) collective-permute-start(f32[1,256]{1,0:T(1,128)} %get-tuple-element.36), channel_id=1, source_target_pairs={{0,4},{1,5},{2,6},{3,7},{4,8},{5,9},{6,10},{7,11},{8,12},{9,13},{1... | collective-permute-start | bytes 3080 | tf_op jit(solution)/shard_map/ppermute | solution.py:218
  9.7 0.7 constant_dynamic-update-slice_fusion.3
  10.4 2.2 %collective-permute-start.2 = (f32[1,256]{1,0:T(1,128)}, f32[1,256]{1,0:T(1,128)S(1)}, u32[]{:S(2)}, u32[]{:S(2)}) collective-permute-start(f32[1,256]{1,0:T(1,128)} %get-tuple-element.37), channel_id=1, source_target_pairs={{0,12},{1,13},{2,14},{3,15},{4,0},{5,1},{6,2},{7,3},{8,4},{9,5},{1... | collective-permute-start | bytes 3080 | tf_op jit(solution)/shard_map/ppermute | solution.py:218
  12.6 0.8 %collective-permute-start.3 = (f32[1,256]{1,0:T(1,128)}, f32[1,256]{1,0:T(1,128)S(1)}, u32[]{:S(2)}, u32[]{:S(2)}) collective-permute-start(f32[1,256]{1,0:T(1,128)} %get-tuple-element.38), channel_id=1, source_target_pairs={{0,8},{1,9},{2,10},{3,11},{4,12},{5,13},{6,14},{7,15},{8,0},{9,1},... | collective-permute-start | bytes 3080 | tf_op jit(solution)/shard_map/ppermute | solution.py:218
  13.4 6.5 %collective-permute-done.1 = f32[1,256]{1,0:T(1,128)S(1)} collective-permute-done((f32[1,256]{1,0:T(1,128)}, f32[1,256]{1,0:T(1,128)S(1)}, u32[]{:S(2)}, u32[]{:S(2)}) %collective-permute-start.1) | collective-permute-done | bytes 1056 | tf_op jit(solution)/shard_map/ppermute | solution.py:218
  19.9 0.0 collective-permute-done.2
  19.9 0.0 collective-permute-done.3
  19.9 0.6 collective-permute-start.4
  20.5 1.7 %collective-permute-start.9 = (bf16[256,768]{1,0:T(8,128)(2,1)}, bf16[256,768]{1,0:T(8,128)(2,1)S(1)}, u32[]{:S(2)}, u32[]{:S(2)}) collective-permute-start(bf16[256,768]{1,0:T(8,128)(2,1)} %get-tuple-element.45), channel_id=1, source_target_pairs={{0,12},{1,13},{2,14},{3,15},{4,0},{5,1},{6,2},{7,3},{8,4},{9,5},{1... | collective-permute-start | bytes 1179656 | tf_op jit(solution)/shard_map/ppermute | solution.py:218
  22.3 0.0 collective-permute-done.6.refs_4_
  22.3 1.5 %collective-permute-start.14 = (bf16[256,768]{1,0:T(8,128)(2,1)S(1)}, bf16[256,768]{1,0:T(8,128)(2,1)S(1)}, u32[]{:S(2)}, u32[]{:S(2)}) collective-permute-start(bf16[256,768]{1,0:T(8,128)(2,1)S(1)} %collective-permute-done.6.refs_4_), channel_id=1, source_target_pairs={{0,2},{1,3},{2,0},{3,1},{4,6},{5,7},{6,4},{7,5},{8,10},{9,11},{10,... | collective-permute-start | bytes 1179656 | tf_op jit(solution)/shard_map/ppermute | solution.py:221
  23.8 0.2 collective-permute-start.7
  23.9 0.0 collective-permute-done.4
  23.9 0.0 collective-permute-start.10
  24.0 0.0 collective-permute-done.13.refs_11_
  24.0 0.6 collective-permute-start.5
  24.5 1.1 %collective-permute-done.5.refs_1_ = f32[2,1024]{1,0:T(2,128)S(1)} collective-permute-done((f32[2,1024]{1,0:T(2,128)S(1)}, f32[2,1024]{1,0:T(2,128)S(1)}, u32[]{:S(2)}, u32[]{:S(2)}) %collective-permute-start.5) | collective-permute-done | bytes 8224 | tf_op jit(solution)/shard_map/ppermute | solution.py:221
  25.7 0.1 collective-permute-start.15
  25.8 6.4 %collective-permute-done.9.refs_5_ = bf16[256,768]{1,0:T(8,128)(2,1)S(1)} collective-permute-done((bf16[256,768]{1,0:T(8,128)(2,1)}, bf16[256,768]{1,0:T(8,128)(2,1)S(1)}, u32[]{:S(2)}, u32[]{:S(2)}) %collective-permute-start.9) | collective-permute-done | bytes 393248 | tf_op jit(solution)/shard_map/ppermute | solution.py:218
  32.2 0.0 collective-permute-start.11
  32.2 0.0 collective-permute-done.14.refs_12_
  32.2 1.5 %collective-permute-start.17 = (bf16[256,768]{1,0:T(8,128)(2,1)S(1)}, bf16[256,768]{1,0:T(8,128)(2,1)S(1)}, u32[]{:S(2)}, u32[]{:S(2)}) collective-permute-start(bf16[256,768]{1,0:T(8,128)(2,1)S(1)} %collective-permute-done.9.refs_5_), channel_id=1, source_target_pairs={{0,2},{1,3},{2,0},{3,1},{4,6},{5,7},{6,4},{7,5},{8,10},{9,11},{10,... | collective-permute-start | bytes 1179656 | tf_op jit(solution)/shard_map/ppermute | solution.py:221
  33.7 13.9 %collective-permute-done.7.refs_6_ = bf16[256,768]{1,0:T(8,128)(2,1)S(1)} collective-permute-done((bf16[256,768]{1,0:T(8,128)(2,1)}, bf16[256,768]{1,0:T(8,128)(2,1)S(1)}, u32[]{:S(2)}, u32[]{:S(2)}) %collective-permute-start.7) | collective-permute-done | bytes 393248 | tf_op jit(solution)/shard_map/ppermute | solution.py:218
  47.6 0.0 collective-permute-start.16
  47.6 0.0 collective-permute-done.10.refs_8_
  47.6 0.5 collective-permute-start.12
  48.1 0.0 collective-permute-done.15.refs_13_
  48.1 1.2 %collective-permute-start.8 = (bf16[256,768]{1,0:T(8,128)(2,1)S(1)}, bf16[256,768]{1,0:T(8,128)(2,1)S(1)}, u32[]{:S(2)}, u32[]{:S(2)}) collective-permute-start(bf16[256,768]{1,0:T(8,128)(2,1)S(1)} %collective-permute-done.7.refs_6_), channel_id=1, source_target_pairs={{0,2},{1,3},{2,0},{3,1},{4,6},{5,7},{6,4},{7,5},{8,10},{9,11},{10,... | collective-permute-start | bytes 1179656 | tf_op jit(solution)/shard_map/ppermute | solution.py:221
  49.4 0.0 collective-permute-done.17.refs_7_
  49.4 0.0 collective-permute-start.18
  49.4 0.0 collective-permute-done.11.refs_9_
  49.4 0.0 collective-permute-done.16.refs_14_
  49.4 0.5 collective-permute-done.12.refs_10_
  49.9 0.0 copy-start.1
  49.9 1.0 %copy-done.1 = bf16[256,768]{1,0:T(8,128)(2,1)S(1)} copy-done((bf16[256,768]{1,0:T(8,128)(2,1)S(1)}, bf16[256,768]{1,0:T(8,128)(2,1)}, u32[]{:S(2)}) %copy-start.1) | copy-done | bytes 393240
  50.9 5.3 %compare4_48.1.refs_2_ = f32[1,1024]{1,0:T(1,128)S(1)} custom-call(f32[2,1024]{1,0:T(2,128)S(1)} %pad_maximum_fusion.refs_0_, f32[2,1024]{1,0:T(2,128)S(1)} %collective-permute-done.5.refs_1_, f32[1,1024]{1,0:T(1,128)S(1)} %broadcast_in_dim.3.refs_2_, bf16[256,768]{1,0:T(8,128)(2,1)S(1)} %copy-done.1, bf16[256,768]{1,0:T(8,128)(2,1)S(1)} %collective-permute-done.6.refs_4_, ...), custom_call_target="tpu_custom_call" | custom-call | flops 4831838208 | tf_op jit(solution)/shard_map/compare4_48/pallas_call | solution.py:164
  56.1 3.1 %collective-permute-done.8.refs_7_ = bf16[256,768]{1,0:T(8,128)(2,1)S(1)} collective-permute-done((bf16[256,768]{1,0:T(8,128)(2,1)S(1)}, bf16[256,768]{1,0:T(8,128)(2,1)S(1)}, u32[]{:S(2)}, u32[]{:S(2)}) %collective-permute-start.8) | collective-permute-done | bytes 393248 | tf_op jit(solution)/shard_map/ppermute | solution.py:221
  59.2 0.0 collective-permute-start.19
  59.2 0.0 collective-permute-done.18.refs_8_
  59.2 1.0 %compare1_8.2.refs_2_ = f32[1,1024]{1,0:T(1,128)S(1)} custom-call(f32[2,1024]{1,0:T(2,128)S(1)} %pad_maximum_fusion.refs_0_, f32[2,1024]{1,0:T(2,128)S(1)} %collective-permute-done.5.refs_1_, f32[1,1024]{1,0:T(1,128)S(1)} %compare4_48.1.refs_2_, bf16[256,768]{1,0:T(8,128)(2,1)S(1)} %copy-done.1, bf16[256,768]{1,0:T(8,128)(2,1)S(1)} %collective-permute-done.6.refs_4_, ...), custom_call_target="tpu_custom_call" | custom-call | flops 805306368 | tf_op jit(solution)/shard_map/compare1_8/pallas_call | solution.py:164
  60.3 0.0 copy-start
  60.3 0.7 collective-permute-done.19.refs_8_
  60.9 1.0 %compare1_8.3 = (f32[1,256]{1,0:T(1,128)S(1)}, f32[1,256]{1,0:T(1,128)S(1)}, f32[1,256]{1,0:T(1,128)S(1)}, f32[1,256]{1,0:T(1,128)S(1)}) custom-call(f32[2,1024]{1,0:T(2,128)S(1)} %pad_maximum_fusion.refs_0_, f32[2,1024]{1,0:T(2,128)S(1)} %collective-permute-done.5.refs_1_, f32[1,1024]{1,0:T(1,128)S(1)} %compare1_8.2.refs_2_, ...), custom_call_target="tpu_custom_call" | custom-call | flops 805306368 | tf_op jit(solution)/shard_map/compare1_8/pallas_call | solution.py:164
  62.0 3.6 %collective-permute-start.20 = (f32[1,256]{1,0:T(1,128)S(1)}, f32[1,256]{1,0:T(1,128)S(1)}, u32[]{:S(2)}, u32[]{:S(2)}) collective-permute-start(f32[1,256]{1,0:T(1,128)S(1)} %get-tuple-element.50), channel_id=1, source_target_pairs={{0,12},{1,13},{2,14},{3,15},{4,0},{5,1},{6,2},{7,3},{8,4},{9,5},{1... | collective-permute-start | bytes 3080 | tf_op jit(solution)/shard_map/ppermute | solution.py:218
  65.6 0.0 collective-permute-start.21
  65.6 0.6 collective-permute-start.22
  66.2 0.7 collective-permute-done.20.refs_1_
  66.9 4.1 %collective-permute-done.21.refs_2_ = f32[1,256]{1,0:T(1,128)S(1)} collective-permute-done((f32[1,256]{1,0:T(1,128)S(1)}, f32[1,256]{1,0:T(1,128)S(1)}, u32[]{:S(2)}, u32[]{:S(2)}) %collective-permute-start.21) | collective-permute-done | bytes 1056 | tf_op jit(solution)/shard_map/ppermute | solution.py:218
  70.9 0.0 collective-permute-done.22.refs_3_
  70.9 0.0 copy-done
  70.9 1.1 %unpack.1 = f32[1,512]{1,0:T(1,128)} custom-call(s32[1,512]{1,0:T(1,128)S(1)} %copy-done, f32[1,256]{1,0:T(1,128)S(1)} %get-tuple-element.49.refs_0_, f32[1,256]{1,0:T(1,128)S(1)} %collective-permute-done.20.refs_1_, f32[1,256]{1,0:T(1,128)S(1)} %collective-permute-done.21.refs_2_, f32[1,256]{1,0:T(1,128)S(1)} %collective-permute-done.22.refs_3_), custom_call_target="tpu_custom_call" | custom-call | tf_op jit(solution)/shard_map/unpack/pallas_call | solution.py:194
  (5 shorter events, 0.0 us)
Async XLA Ops:
  3.5 4.7 %collective-permute-start = (bf16[256,768]{1,0:T(8,128)(2,1)}, bf16[256,768]{1,0:T(8,128)(2,1)S(1)}, u32[]{:S(2)}, u32[]{:S(2)}) collective-permute-start(bf16[256,768]{1,0:T(8,128)(2,1)} %get-tuple-element.34.refs_3_), channel_id=1, source_target_pairs={{0,1},{1,0},{2,3},{3,2},{4,5},{5,4},{6,7},{7,6},{8,9},{9,8},{10,11... | collective-permute-start | bytes 1179656 | tf_op jit(solution)/shard_map/ppermute | solution.py:221
  4.0 20.0 %collective-permute-start.13 = (bf16[256,768]{1,0:T(8,128)(2,1)}, bf16[256,768]{1,0:T(8,128)(2,1)S(1)}, u32[]{:S(2)}, u32[]{:S(2)}) collective-permute-start(bf16[256,768]{1,0:T(8,128)(2,1)} %get-tuple-element.34.refs_3_), channel_id=1, source_target_pairs={{0,2},{1,3},{2,0},{3,1},{4,6},{5,7},{6,4},{7,5},{8,10},{9,11},{10,... | collective-permute-start | bytes 1179656 | tf_op jit(solution)/shard_map/ppermute | solution.py:221
  6.5 15.7 %collective-permute-start.6 = (bf16[256,768]{1,0:T(8,128)(2,1)}, bf16[256,768]{1,0:T(8,128)(2,1)S(1)}, u32[]{:S(2)}, u32[]{:S(2)}) collective-permute-start(bf16[256,768]{1,0:T(8,128)(2,1)} %get-tuple-element.40), channel_id=1, source_target_pairs={{0,4},{1,5},{2,6},{3,7},{4,8},{5,9},{6,10},{7,11},{8,12},{9,13},{1... | collective-permute-start | bytes 1179656 | tf_op jit(solution)/shard_map/ppermute | solution.py:218
  8.1 11.8 %collective-permute-start.1 = (f32[1,256]{1,0:T(1,128)}, f32[1,256]{1,0:T(1,128)S(1)}, u32[]{:S(2)}, u32[]{:S(2)}) collective-permute-start(f32[1,256]{1,0:T(1,128)} %get-tuple-element.36), channel_id=1, source_target_pairs={{0,4},{1,5},{2,6},{3,7},{4,8},{5,9},{6,10},{7,11},{8,12},{9,13},{1... | collective-permute-start | bytes 3080 | tf_op jit(solution)/shard_map/ppermute | solution.py:218
  10.4 9.6 %collective-permute-start.2 = (f32[1,256]{1,0:T(1,128)}, f32[1,256]{1,0:T(1,128)S(1)}, u32[]{:S(2)}, u32[]{:S(2)}) collective-permute-start(f32[1,256]{1,0:T(1,128)} %get-tuple-element.37), channel_id=1, source_target_pairs={{0,12},{1,13},{2,14},{3,15},{4,0},{5,1},{6,2},{7,3},{8,4},{9,5},{1... | collective-permute-start | bytes 3080 | tf_op jit(solution)/shard_map/ppermute | solution.py:218
  12.6 7.3 %collective-permute-start.3 = (f32[1,256]{1,0:T(1,128)}, f32[1,256]{1,0:T(1,128)S(1)}, u32[]{:S(2)}, u32[]{:S(2)}) collective-permute-start(f32[1,256]{1,0:T(1,128)} %get-tuple-element.38), channel_id=1, source_target_pairs={{0,8},{1,9},{2,10},{3,11},{4,12},{5,13},{6,14},{7,15},{8,0},{9,1},... | collective-permute-start | bytes 3080 | tf_op jit(solution)/shard_map/ppermute | solution.py:218
  19.9 4.0 %collective-permute-start.4 = (f32[1,1024]{1,0:T(1,128)S(1)}, f32[1,1024]{1,0:T(1,128)S(1)}, u32[]{:S(2)}, u32[]{:S(2)}) collective-permute-start(f32[1,1024]{1,0:T(1,128)S(1)} %constant_dynamic-update-slice_fusion), channel_id=1, source_target_pairs={{0,2},{1,3},{2,0},{3,1},{4,6},{5,7},{6,4},{7,5},{8,10},{9,11},{10,... | collective-permute-start | bytes 12296 | tf_op jit(solution)/shard_map/ppermute | solution.py:221
  20.5 11.7 %collective-permute-start.9 = (bf16[256,768]{1,0:T(8,128)(2,1)}, bf16[256,768]{1,0:T(8,128)(2,1)S(1)}, u32[]{:S(2)}, u32[]{:S(2)}) collective-permute-start(bf16[256,768]{1,0:T(8,128)(2,1)} %get-tuple-element.45), channel_id=1, source_target_pairs={{0,12},{1,13},{2,14},{3,15},{4,0},{5,1},{6,2},{7,3},{8,4},{9,5},{1... | collective-permute-start | bytes 1179656 | tf_op jit(solution)/shard_map/ppermute | solution.py:218
  22.3 9.9 %collective-permute-start.14 = (bf16[256,768]{1,0:T(8,128)(2,1)S(1)}, bf16[256,768]{1,0:T(8,128)(2,1)S(1)}, u32[]{:S(2)}, u32[]{:S(2)}) collective-permute-start(bf16[256,768]{1,0:T(8,128)(2,1)S(1)} %collective-permute-done.6.refs_4_), channel_id=1, source_target_pairs={{0,2},{1,3},{2,0},{3,1},{4,6},{5,7},{6,4},{7,5},{8,10},{9,11},{10,... | collective-permute-start | bytes 1179656 | tf_op jit(solution)/shard_map/ppermute | solution.py:221
  23.8 23.8 %collective-permute-start.7 = (bf16[256,768]{1,0:T(8,128)(2,1)}, bf16[256,768]{1,0:T(8,128)(2,1)S(1)}, u32[]{:S(2)}, u32[]{:S(2)}) collective-permute-start(bf16[256,768]{1,0:T(8,128)(2,1)} %get-tuple-element.41), channel_id=1, source_target_pairs={{0,8},{1,9},{2,10},{3,11},{4,12},{5,13},{6,14},{7,15},{8,0},{9,1},... | collective-permute-start | bytes 1179656 | tf_op jit(solution)/shard_map/ppermute | solution.py:218
  23.9 23.7 %collective-permute-start.10 = (bf16[256,768]{1,0:T(8,128)(2,1)S(1)}, bf16[256,768]{1,0:T(8,128)(2,1)S(1)}, u32[]{:S(2)}, u32[]{:S(2)}) collective-permute-start(bf16[256,768]{1,0:T(8,128)(2,1)S(1)} %collective-permute-done.6.refs_4_), channel_id=1, source_target_pairs={{0,1},{1,0},{2,3},{3,2},{4,5},{5,4},{6,7},{7,6},{8,9},{9,8},{10,11... | collective-permute-start | bytes 1179656 | tf_op jit(solution)/shard_map/ppermute | solution.py:221
  24.0 1.7 %collective-permute-start.5 = (f32[2,1024]{1,0:T(2,128)S(1)}, f32[2,1024]{1,0:T(2,128)S(1)}, u32[]{:S(2)}, u32[]{:S(2)}) collective-permute-start(f32[2,1024]{1,0:T(2,128)S(1)} %pad_maximum_fusion.refs_0_), channel_id=1, source_target_pairs={{0,1},{1,0},{2,3},{3,2},{4,5},{5,4},{6,7},{7,6},{8,9},{9,8},{10,11... | collective-permute-start | bytes 24584 | tf_op jit(solution)/shard_map/ppermute | solution.py:221
  25.7 22.4 %collective-permute-start.15 = (bf16[256,768]{1,0:T(8,128)(2,1)S(1)}, bf16[256,768]{1,0:T(8,128)(2,1)S(1)}, u32[]{:S(2)}, u32[]{:S(2)}) collective-permute-start(bf16[256,768]{1,0:T(8,128)(2,1)S(1)} %collective-permute-done.13.refs_11_), channel_id=1, source_target_pairs={{0,1},{1,0},{2,3},{3,2},{4,5},{5,4},{6,7},{7,6},{8,9},{9,8},{10,11... | collective-permute-start | bytes 1179656 | tf_op jit(solution)/shard_map/ppermute | solution.py:221
  32.2 17.2 %collective-permute-start.11 = (bf16[256,768]{1,0:T(8,128)(2,1)S(1)}, bf16[256,768]{1,0:T(8,128)(2,1)S(1)}, u32[]{:S(2)}, u32[]{:S(2)}) collective-permute-start(bf16[256,768]{1,0:T(8,128)(2,1)S(1)} %collective-permute-done.9.refs_5_), channel_id=1, source_target_pairs={{0,1},{1,0},{2,3},{3,2},{4,5},{5,4},{6,7},{7,6},{8,9},{9,8},{10,11... | collective-permute-start | bytes 1179656 | tf_op jit(solution)/shard_map/ppermute | solution.py:221
  32.2 17.2 %collective-permute-start.17 = (bf16[256,768]{1,0:T(8,128)(2,1)S(1)}, bf16[256,768]{1,0:T(8,128)(2,1)S(1)}, u32[]{:S(2)}, u32[]{:S(2)}) collective-permute-start(bf16[256,768]{1,0:T(8,128)(2,1)S(1)} %collective-permute-done.9.refs_5_), channel_id=1, source_target_pairs={{0,2},{1,3},{2,0},{3,1},{4,6},{5,7},{6,4},{7,5},{8,10},{9,11},{10,... | collective-permute-start | bytes 1179656 | tf_op jit(solution)/shard_map/ppermute | solution.py:221
  47.6 1.8 %collective-permute-start.16 = (bf16[256,768]{1,0:T(8,128)(2,1)S(1)}, bf16[256,768]{1,0:T(8,128)(2,1)S(1)}, u32[]{:S(2)}, u32[]{:S(2)}) collective-permute-start(bf16[256,768]{1,0:T(8,128)(2,1)S(1)} %collective-permute-done.14.refs_12_), channel_id=1, source_target_pairs={{0,1},{1,0},{2,3},{3,2},{4,5},{5,4},{6,7},{7,6},{8,9},{9,8},{10,11... | collective-permute-start | bytes 1179656 | tf_op jit(solution)/shard_map/ppermute | solution.py:221
  47.6 2.3 %collective-permute-start.12 = (bf16[256,768]{1,0:T(8,128)(2,1)S(1)}, bf16[256,768]{1,0:T(8,128)(2,1)S(1)}, u32[]{:S(2)}, u32[]{:S(2)}) collective-permute-start(bf16[256,768]{1,0:T(8,128)(2,1)S(1)} %collective-permute-done.7.refs_6_), channel_id=1, source_target_pairs={{0,1},{1,0},{2,3},{3,2},{4,5},{5,4},{6,7},{7,6},{8,9},{9,8},{10,11... | collective-permute-start | bytes 1179656 | tf_op jit(solution)/shard_map/ppermute | solution.py:221
  48.1 11.1 %collective-permute-start.8 = (bf16[256,768]{1,0:T(8,128)(2,1)S(1)}, bf16[256,768]{1,0:T(8,128)(2,1)S(1)}, u32[]{:S(2)}, u32[]{:S(2)}) collective-permute-start(bf16[256,768]{1,0:T(8,128)(2,1)S(1)} %collective-permute-done.7.refs_6_), channel_id=1, source_target_pairs={{0,2},{1,3},{2,0},{3,1},{4,6},{5,7},{6,4},{7,5},{8,10},{9,11},{10,... | collective-permute-start | bytes 1179656 | tf_op jit(solution)/shard_map/ppermute | solution.py:221
  49.4 9.8 %collective-permute-start.18 = (bf16[256,768]{1,0:T(8,128)(2,1)S(1)}, bf16[256,768]{1,0:T(8,128)(2,1)S(1)}, u32[]{:S(2)}, u32[]{:S(2)}) collective-permute-start(bf16[256,768]{1,0:T(8,128)(2,1)S(1)} %collective-permute-done.17.refs_7_), channel_id=1, source_target_pairs={{0,1},{1,0},{2,3},{3,2},{4,5},{5,4},{6,7},{7,6},{8,9},{9,8},{10,11... | collective-permute-start | bytes 1179656 | tf_op jit(solution)/shard_map/ppermute | solution.py:221
  49.9 1.0 %copy-start.1 = (bf16[256,768]{1,0:T(8,128)(2,1)S(1)}, bf16[256,768]{1,0:T(8,128)(2,1)}, u32[]{:S(2)}) copy-start(bf16[256,768]{1,0:T(8,128)(2,1)} %get-tuple-element.34.refs_3_) | copy-start | bytes 1179652
  59.2 1.7 %collective-permute-start.19 = (bf16[256,768]{1,0:T(8,128)(2,1)S(1)}, bf16[256,768]{1,0:T(8,128)(2,1)S(1)}, u32[]{:S(2)}, u32[]{:S(2)}) collective-permute-start(bf16[256,768]{1,0:T(8,128)(2,1)S(1)} %collective-permute-done.8.refs_7_), channel_id=1, source_target_pairs={{0,1},{1,0},{2,3},{3,2},{4,5},{5,4},{6,7},{7,6},{8,9},{9,8},{10,11... | collective-permute-start | bytes 1179656 | tf_op jit(solution)/shard_map/ppermute | solution.py:221
  60.3 10.7 %copy-start = (s32[1,512]{1,0:T(1,128)S(1)}, s32[1,512]{1,0:T(1,128)}, u32[]{:S(2)}) copy-start(s32[1,512]{1,0:T(1,128)} %get-tuple-element.29.slot_ref) | copy-start | bytes 6148
  62.0 4.9 %collective-permute-start.20 = (f32[1,256]{1,0:T(1,128)S(1)}, f32[1,256]{1,0:T(1,128)S(1)}, u32[]{:S(2)}, u32[]{:S(2)}) collective-permute-start(f32[1,256]{1,0:T(1,128)S(1)} %get-tuple-element.50), channel_id=1, source_target_pairs={{0,12},{1,13},{2,14},{3,15},{4,0},{5,1},{6,2},{7,3},{8,4},{9,5},{1... | collective-permute-start | bytes 3080 | tf_op jit(solution)/shard_map/ppermute | solution.py:218
  65.6 5.4 %collective-permute-start.21 = (f32[1,256]{1,0:T(1,128)S(1)}, f32[1,256]{1,0:T(1,128)S(1)}, u32[]{:S(2)}, u32[]{:S(2)}) collective-permute-start(f32[1,256]{1,0:T(1,128)S(1)} %get-tuple-element.51), channel_id=1, source_target_pairs={{0,4},{1,5},{2,6},{3,7},{4,8},{5,9},{6,10},{7,11},{8,12},{9,13},{1... | collective-permute-start | bytes 3080 | tf_op jit(solution)/shard_map/ppermute | solution.py:218
  65.6 5.4 %collective-permute-start.22 = (f32[1,256]{1,0:T(1,128)S(1)}, f32[1,256]{1,0:T(1,128)S(1)}, u32[]{:S(2)}, u32[]{:S(2)}) collective-permute-start(f32[1,256]{1,0:T(1,128)S(1)} %get-tuple-element.52), channel_id=1, source_target_pairs={{0,8},{1,9},{2,10},{3,11},{4,12},{5,13},{6,14},{7,15},{8,0},{9,1},... | collective-permute-start | bytes 3080 | tf_op jit(solution)/shard_map/ppermute | solution.py:218

commit v3 on v2

--- a/solution.py
+++ b/solution.py
@@ -92,7 +92,7 @@
 
 
 def compare_kernel(size, outs, jobs, shape, *refs):
-    near, far, best_ref, refs = refs[0], refs[1], refs[2], refs[3:]
+    near, best_ref, refs = refs[0], refs[1], refs[2:]
     count = sum(shape.values())
     pieces, refs = refs[:count], refs[count:]
     outputs, scratch = refs[: len(outs)], refs[len(outs) :]
@@ -118,7 +118,7 @@
             keys[key] = extra.pop()
             for low, ref in parts:
                 keys[key][low : low + ref.shape[0], :] = ref[...]
-    table = jnp.concatenate([near[...], far[...]] * 2, axis=0)
+    table = jnp.concatenate([near[...]] * 2, axis=0)
     columns = {k: table[:, k * size : (k + 1) * size].T for k in sorted({k for _, k in shape})}
     bests = [best_ref[:, k * size : (k + 1) * size] for k in range(BLOCKS)]
     for low, high, k, peers in jobs:
@@ -171,7 +171,7 @@
             flops=2 * tiles * size * size * width, bytes_accessed=0, transcendentals=0
         ),
         name=f"compare{len(jobs)}_{tiles}",
-    )(*labels, best, *[part for parts in blocks.values() for part in parts])
+    )(labels, best, *[part for parts in blocks.values() for part in parts])
 
 
 def unpack_kernel(slot_ref, *refs):
@@ -228,7 +228,7 @@
             out.append(shift(part, sign * shifts[k]) if shifts[k] else part)
         return join(out, axis)
 
-    sent = pack(groups, cap, units, pieces, embedding, row_owner, cluster_id)
+    sent = pack(groups, cap, units, [(0, slots)], embedding, row_owner, cluster_id)
     blocks, label, slot = list(sent[: len(units)]), sent[len(units) : -1], sent[-1]
 
     def tie(*arrays):
@@ -243,39 +243,42 @@
     def core(array):
         return swap(array, 1)
 
-    across, beside, beyond = [None] * BLOCKS, [None] * BLOCKS, [None] * BLOCKS
-    own = [blocks[0], send(1), None, None]
-    across[0], beside[0] = cross(own[0]), core(own[0])
-    *label, beside[0] = tie(*label, beside[0])
-    label = [exchange(l, low, 1, 1) for l, (low, _) in zip(label, pieces)]
-    label = join(label, 1)
+    arrays = [[None] * BLOCKS for _ in range(4)]
+    own, across, beside, beyond = arrays
+
+    def both(function, parts):
+        return [function(part) for part in parts]
+
+    (label,) = label
     near = jnp.concatenate([label, cross(label)], axis=0)
-    labels = [near, core(near)]
-    blocks[2], beside[0] = tie(blocks[2], beside[0])
-    own[2] = send(2)
-    blocks[3], own[1] = tie(blocks[3], own[1])
-    own[3] = send(3)
+    label = jnp.concatenate([near, core(near)], axis=0)
+    blocks[0], label = tie(blocks[0], label)
+    blocks[2], label = tie(blocks[2], label)
+    own[0], own[1], own[2] = [blocks[0]], [send(1)], [send(2)]
+    across[0], beside[0] = both(cross, own[0]), both(core, own[0])
+    label = exchange(label, 0, 1, 1)
+    blocks[3], label = tie(blocks[3], label)
+    blocks[3], *own[1] = tie(blocks[3], *own[1])
+    own[3] = [send(3)]
     for u in range(1, BLOCKS):
-        beside[u] = core(own[u])
-        across[u] = cross(own[u])
+        beside[u], across[u] = both(core, own[u]), both(cross, own[u])
     for u in range(BLOCKS - 1):
-        beyond[u] = core(across[u])
-    arrays = [own, across, beside, beyond]
+        beyond[u] = both(core, across[u])
 
     def given(peers, blocks):
-        return {(peer, k): [arrays[peer][k]] for peer in peers for k in blocks}
+        return {(peer, k): arrays[peer][k] for peer in peers for k in blocks}
 
     every, row = (0, 1, 2, 3), [(0, slots)]
     best = jnp.full((1, slots), -1.0, jnp.float32)
     jobs = [(0, 4, 0, every), (0, 4, 1, every), (0, 4, 2, (0, 2)), (0, 4, 3, (0, 2))]
     some = given((0, 2), range(4)) | given((1, 3), range(2))
-    (best,) = compare(row, jobs, labels, some, best)
-    across[3], best = tie(across[3], best)
-    beyond[3] = core(across[3])
+    (best,) = compare(row, jobs, label, some, best)
+    across[3][0], best = tie(across[3][0], best)
+    beyond[3] = both(core, across[3])
     some = given((0,), range(4)) | given((1, 3), (2,))
-    (best,) = compare(row, [(0, 4, 2, (1, 3))], labels, some, best)
+    (best,) = compare(row, [(0, 4, 2, (1, 3))], label, some, best)
     some = given((0,), range(4)) | given((1, 3), (3,))
-    best = compare(pieces, [(0, 4, 3, (1, 3))], labels, some, best)
+    best = compare(pieces, [(0, 4, 3, (1, 3))], label, some, best)
     backs = [exchange(b, low, 1, -1) for b, (low, _) in zip(best, pieces)]
     return unpack(slot, backs).reshape(rows)
 

time: 72.2 us -> 78.4 us (1.086)
  waiting for transfers between devices: 36.9 us -> 43.5 us
  other arithmetic: 0.01 us -> 1.38 us
  starting transfers between devices: 21.4 us -> 20.2 us
    ppermute x14, waiting for transfers between devices: 5.37 us -> 18.1 us  [swap(): return lax.ppermute(array, 'blk', [(i, i ^ mask) for i in range(devices)])]
    ppermute x9, waiting for transfers between devices: 31.6 us -> 25.4 us  [shift(): lax.ppermute(array, 'blk', [(i, (i + step) % devices) for i in range(devi...]
    ppermute x14, starting transfers between devices: 9.1 us -> 8.2 us  [swap(): return lax.ppermute(array, 'blk', [(i, i ^ mask) for i in range(devices)])]
    unnamed x7 -> x4, local copies, waits for them, and re-layouts: 1.69 us -> 1 us
  transfers between devices with their start and end apart: 23 -> 23, of which waited for: 9 -> 10; matrix products, arithmetic and copies ran while one was open for 1% -> 1% of each run, Pallas kernels for 9% -> 8%
where the time goes in v3:
time: 78.4 us; the launch traced here: 78.2 us
  waiting for transfers between devices  43.5 us (55%)
  starting transfers between devices  20.2 us (26%)
  Pallas kernels  11.9 us (15%)
  other arithmetic  1.38 us (2%)
  local copies, waits for them, and re-layouts  1 us (1%)
    ppermute x9, waiting for transfers between devices, shift(): lax.ppermute(array, 'blk', [(i, (i + step) % devices) for i in range(devi...  25.4 us
    ppermute x14, waiting for transfers between devices, swap(): return lax.ppermute(array, 'blk', [(i, i ^ mask) for i in range(devices)])  18.1 us
    ppermute x9, starting transfers between devices, shift(): lax.ppermute(array, 'blk', [(i, (i + step) % devices) for i in range(devi...  12 us
    ppermute x14, starting transfers between devices, swap(): return lax.ppermute(array, 'blk', [(i, i ^ mask) for i in range(devices)])  8.2 us
    pallas_call x3, Pallas kernels, compare(): pl.pallas_call(lambda *refs: compare_kernel(size, outs, jobs, shape, *ref...  7.38 us
    pallas_call x1, Pallas kernels, pack(): pl.pallas_call(lambda *refs: pack_kernel(groups, cap, units, pieces, *ref...  3.43 us
  transfers between devices with their start and end apart: 23, of which 10 were waited for; matrix products, arithmetic and copies ran while one was open for 1% of the time, Pallas kernels for 8%

profile of v3, /device:TPU:0, one launch (start us, length us, event | category | flops | bytes accessed | tf_op | source)
XLA Modules:
  0.0 78.2 jit_solution(4579486537714817608)
XLA Ops:
  0.0 3.4 %pack.1 = (bf16[256,768]{1,0:T(8,128)(2,1)}, bf16[256,768]{1,0:T(8,128)(2,1)}, bf16[256,768]{1,0:T(8,128)(2,1)}, bf16[256,768]{1,0:T(8,128)(2,1)}, f32[1,1024]{1,0:T(1,128)}, /*index=5*/s32[1,512]{1,0:T(1,128)}) custom-call(f32[512,768]{1,0:T(8,128)} %refs_0_.1, s32[1,512]{1,0:T(1,128)} %bitcast.3, s32[1,512]{1,0:T(1,128)} %bitcast.4), custom_call_target="tpu_custom_call" | custom-call | tf_op jit(solution)/shard_map/pack/pallas_call | solution.py:77
  3.4 3.0 %collective-permute-start = (f32[1,1024]{1,0:T(1,128)}, f32[1,1024]{1,0:T(1,128)S(1)}, u32[]{:S(2)}, u32[]{:S(2)}) collective-permute-start(f32[1,1024]{1,0:T(1,128)} %get-tuple-element.29), channel_id=1, source_target_pairs={{0,2},{1,3},{2,0},{3,1},{4,6},{5,7},{6,4},{7,5},{8,10},{9,11},{10,... | collective-permute-start | bytes 12296 | tf_op jit(solution)/shard_map/ppermute | solution.py:221
  6.4 1.8 %collective-permute-done = f32[1,1024]{1,0:T(1,128)S(1)} collective-permute-done((f32[1,1024]{1,0:T(1,128)}, f32[1,1024]{1,0:T(1,128)S(1)}, u32[]{:S(2)}, u32[]{:S(2)}) %collective-permute-start) | collective-permute-done | bytes 4128 | tf_op jit(solution)/shard_map/ppermute | solution.py:221
  8.2 0.7 pad_maximum_fusion.2
  8.9 0.1 collective-permute-start.1
  9.0 2.2 %collective-permute-start.5 = (bf16[256,768]{1,0:T(8,128)(2,1)}, bf16[256,768]{1,0:T(8,128)(2,1)S(1)}, u32[]{:S(2)}, u32[]{:S(2)}) collective-permute-start(bf16[256,768]{1,0:T(8,128)(2,1)} %get-tuple-element.34), channel_id=1, source_target_pairs={{0,4},{1,5},{2,6},{3,7},{4,8},{5,9},{6,10},{7,11},{8,12},{9,13},{1... | collective-permute-start | bytes 1179656 | tf_op jit(solution)/shard_map/ppermute | solution.py:218
  11.2 0.0 collective-permute-done.1
  11.2 0.7 pad_maximum_fusion
  11.9 3.2 %collective-permute-start.8 = (bf16[256,768]{1,0:T(8,128)(2,1)}, bf16[256,768]{1,0:T(8,128)(2,1)S(1)}, u32[]{:S(2)}, u32[]{:S(2)}) collective-permute-start(bf16[256,768]{1,0:T(8,128)(2,1)} %get-tuple-element.38), channel_id=1, source_target_pairs={{0,12},{1,13},{2,14},{3,15},{4,0},{5,1},{6,2},{7,3},{8,4},{9,5},{1... | collective-permute-start | bytes 1179656 | tf_op jit(solution)/shard_map/ppermute | solution.py:218
  15.0 0.0 collective-permute-start.2
  15.0 3.8 %collective-permute-start.3 = (f32[4,256]{1,0:T(4,128)S(1)}, f32[4,256]{1,0:T(4,128)S(1)}, u32[]{:S(2)}, u32[]{:S(2)}) collective-permute-start(f32[4,256]{1,0:T(4,128)S(1)} %get-tuple-element.47), channel_id=1, source_target_pairs={{0,12},{1,13},{2,14},{3,15},{4,0},{5,1},{6,2},{7,3},{8,4},{9,5},{1... | collective-permute-start | bytes 12296 | tf_op jit(solution)/shard_map/ppermute | solution.py:218
  18.9 0.0 collective-permute-start.4
  18.9 13.0 %collective-permute-done.2 = f32[4,256]{1,0:T(4,128)S(1)} collective-permute-done((f32[4,256]{1,0:T(4,128)S(1)}, f32[4,256]{1,0:T(4,128)S(1)}, u32[]{:S(2)}, u32[]{:S(2)}) %collective-permute-start.2) | collective-permute-done | bytes 4128 | tf_op jit(solution)/shard_map/ppermute | solution.py:218
  31.9 1.5 %collective-permute-start.13 = (bf16[256,768]{1,0:T(8,128)(2,1)}, bf16[256,768]{1,0:T(8,128)(2,1)S(1)}, u32[]{:S(2)}, u32[]{:S(2)}) collective-permute-start(bf16[256,768]{1,0:T(8,128)(2,1)} %get-tuple-element.36.refs_2_), channel_id=1, source_target_pairs={{0,2},{1,3},{2,0},{3,1},{4,6},{5,7},{6,4},{7,5},{8,10},{9,11},{10,... | collective-permute-start | bytes 1179656 | tf_op jit(solution)/shard_map/ppermute | solution.py:221
  33.3 0.0 collective-permute-done.3
  33.3 0.0 collective-permute-start.9
  33.3 0.0 collective-permute-done.4
  33.4 0.0 collective-permute-done.5.refs_3_
  33.4 0.8 %collective-permute-start.6 = (bf16[256,768]{1,0:T(8,128)(2,1)}, bf16[256,768]{1,0:T(8,128)(2,1)S(1)}, u32[]{:S(2)}, u32[]{:S(2)}) collective-permute-start(bf16[256,768]{1,0:T(8,128)(2,1)} %get-tuple-element.35), channel_id=1, source_target_pairs={{0,8},{1,9},{2,10},{3,11},{4,12},{5,13},{6,14},{7,15},{8,0},{9,1},... | collective-permute-start | bytes 1179656 | tf_op jit(solution)/shard_map/ppermute | solution.py:218
  34.2 0.5 collective-permute-start.14
  34.7 0.0 collective-permute-done.8.refs_4_
  34.7 0.0 collective-permute-start.10
  34.7 9.4 %collective-permute-done.13.refs_10_ = bf16[256,768]{1,0:T(8,128)(2,1)S(1)} collective-permute-done((bf16[256,768]{1,0:T(8,128)(2,1)}, bf16[256,768]{1,0:T(8,128)(2,1)S(1)}, u32[]{:S(2)}, u32[]{:S(2)}) %collective-permute-start.13) | collective-permute-done | bytes 393248 | tf_op jit(solution)/shard_map/ppermute | solution.py:221
  44.1 0.0 collective-permute-start.11
  44.1 0.0 collective-permute-done.9.refs_6_
  44.1 1.5 %collective-permute-start.17 = (bf16[256,768]{1,0:T(8,128)(2,1)S(1)}, bf16[256,768]{1,0:T(8,128)(2,1)S(1)}, u32[]{:S(2)}, u32[]{:S(2)}) collective-permute-start(bf16[256,768]{1,0:T(8,128)(2,1)S(1)} %collective-permute-done.8.refs_4_), channel_id=1, source_target_pairs={{0,2},{1,3},{2,0},{3,1},{4,6},{5,7},{6,4},{7,5},{8,10},{9,11},{10,... | collective-permute-start | bytes 1179656 | tf_op jit(solution)/shard_map/ppermute | solution.py:221
  45.6 8.0 %collective-permute-done.6.refs_5_ = bf16[256,768]{1,0:T(8,128)(2,1)S(1)} collective-permute-done((bf16[256,768]{1,0:T(8,128)(2,1)}, bf16[256,768]{1,0:T(8,128)(2,1)S(1)}, u32[]{:S(2)}, u32[]{:S(2)}) %collective-permute-start.6) | collective-permute-done | bytes 393248 | tf_op jit(solution)/shard_map/ppermute | solution.py:218
  53.6 0.1 collective-permute-start.15
  53.6 0.0 collective-permute-done.14.refs_11_
  53.6 0.4 collective-permute-start.12
  54.1 0.0 collective-permute-done.10.refs_7_
  54.1 0.1 collective-permute-start.16
  54.2 0.0 collective-permute-done.11.refs_8_
  54.2 0.9 %collective-permute-start.7 = (bf16[256,768]{1,0:T(8,128)(2,1)S(1)}, bf16[256,768]{1,0:T(8,128)(2,1)S(1)}, u32[]{:S(2)}, u32[]{:S(2)}) collective-permute-start(bf16[256,768]{1,0:T(8,128)(2,1)S(1)} %collective-permute-done.6.refs_5_), channel_id=1, source_target_pairs={{0,2},{1,3},{2,0},{3,1},{4,6},{5,7},{6,4},{7,5},{8,10},{9,11},{10,... | collective-permute-start | bytes 1179656 | tf_op jit(solution)/shard_map/ppermute | solution.py:221
  55.0 5.9 %collective-permute-done.17.refs_6_ = bf16[256,768]{1,0:T(8,128)(2,1)S(1)} collective-permute-done((bf16[256,768]{1,0:T(8,128)(2,1)S(1)}, bf16[256,768]{1,0:T(8,128)(2,1)S(1)}, u32[]{:S(2)}, u32[]{:S(2)}) %collective-permute-start.17) | collective-permute-done | bytes 393248 | tf_op jit(solution)/shard_map/ppermute | solution.py:221
  61.0 0.0 collective-permute-start.18
  61.0 0.0 collective-permute-done.15.refs_12_
  61.0 0.0 collective-permute-done.12.refs_9_
  61.0 0.0 collective-permute-done.16.refs_13_
  61.0 0.0 copy-start.1
  61.0 1.0 %copy-done.1 = bf16[256,768]{1,0:T(8,128)(2,1)S(1)} copy-done((bf16[256,768]{1,0:T(8,128)(2,1)S(1)}, bf16[256,768]{1,0:T(8,128)(2,1)}, u32[]{:S(2)}) %copy-start.1) | copy-done | bytes 393240
  62.0 5.3 %compare4_48.1.refs_1_ = f32[1,1024]{1,0:T(1,128)S(1)} custom-call(f32[4,1024]{1,0:T(4,128)S(1)} %pad_maximum_fusion.1.refs_0_, f32[1,1024]{1,0:T(1,128)S(1)} %broadcast_in_dim.3.refs_1_, bf16[256,768]{1,0:T(8,128)(2,1)S(1)} %copy-done.1, bf16[256,768]{1,0:T(8,128)(2,1)S(1)} %collective-permute-done.5.refs_3_, ...), custom_call_target="tpu_custom_call" | custom-call | flops 4831838208 | tf_op jit(solution)/shard_map/compare4_48/pallas_call | solution.py:164
  67.3 0.4 collective-permute-done.7.refs_6_
  67.8 0.1 collective-permute-start.19
  67.9 0.0 collective-permute-done.18.refs_7_
  67.9 1.0 %compare1_8.2.refs_1_ = f32[1,1024]{1,0:T(1,128)S(1)} custom-call(f32[4,1024]{1,0:T(4,128)S(1)} %pad_maximum_fusion.1.refs_0_, f32[1,1024]{1,0:T(1,128)S(1)} %compare4_48.1.refs_1_, bf16[256,768]{1,0:T(8,128)(2,1)S(1)} %copy-done.1, bf16[256,768]{1,0:T(8,128)(2,1)S(1)} %collective-permute-done.5.refs_3_, ...), custom_call_target="tpu_custom_call" | custom-call | flops 805306368 | tf_op jit(solution)/shard_map/compare1_8/pallas_call | solution.py:164
  68.9 0.0 copy-start
  68.9 0.5 collective-permute-done.19.refs_7_
  69.5 1.0 %compare1_8.3 = (f32[1,256]{1,0:T(1,128)S(1)}, f32[1,256]{1,0:T(1,128)S(1)}, f32[1,256]{1,0:T(1,128)S(1)}, f32[1,256]{1,0:T(1,128)S(1)}) custom-call(f32[4,1024]{1,0:T(4,128)S(1)} %pad_maximum_fusion.1.refs_0_, f32[1,1024]{1,0:T(1,128)S(1)} %compare1_8.2.refs_1_, bf16[256,768]{1,0:T(8,128)(2,1)S(1)} %copy-done.1, ...), custom_call_target="tpu_custom_call" | custom-call | flops 805306368 | tf_op jit(solution)/shard_map/compare1_8/pallas_call | solution.py:164
  70.5 0.5 collective-permute-start.20
  71.0 1.6 %collective-permute-start.21 = (f32[1,256]{1,0:T(1,128)S(1)}, f32[1,256]{1,0:T(1,128)S(1)}, u32[]{:S(2)}, u32[]{:S(2)}) collective-permute-start(f32[1,256]{1,0:T(1,128)S(1)} %get-tuple-element.43), channel_id=1, source_target_pairs={{0,4},{1,5},{2,6},{3,7},{4,8},{5,9},{6,10},{7,11},{8,12},{9,13},{1... | collective-permute-start | bytes 3080 | tf_op jit(solution)/shard_map/ppermute | solution.py:218
  72.6 0.0 collective-permute-start.22
  72.6 1.5 %collective-permute-done.20.refs_1_ = f32[1,256]{1,0:T(1,128)S(1)} collective-permute-done((f32[1,256]{1,0:T(1,128)S(1)}, f32[1,256]{1,0:T(1,128)S(1)}, u32[]{:S(2)}, u32[]{:S(2)}) %collective-permute-start.20) | collective-permute-done | bytes 1056 | tf_op jit(solution)/shard_map/ppermute | solution.py:218
  74.1 2.2 %collective-permute-done.21.refs_2_ = f32[1,256]{1,0:T(1,128)S(1)} collective-permute-done((f32[1,256]{1,0:T(1,128)S(1)}, f32[1,256]{1,0:T(1,128)S(1)}, u32[]{:S(2)}, u32[]{:S(2)}) %collective-permute-start.21) | collective-permute-done | bytes 1056 | tf_op jit(solution)/shard_map/ppermute | solution.py:218
  76.4 0.7 collective-permute-done.22.refs_3_
  77.1 0.0 copy-done
  77.1 1.1 %unpack.1 = f32[1,512]{1,0:T(1,128)} custom-call(s32[1,512]{1,0:T(1,128)S(1)} %copy-done, f32[1,256]{1,0:T(1,128)S(1)} %get-tuple-element.41.refs_0_, f32[1,256]{1,0:T(1,128)S(1)} %collective-permute-done.20.refs_1_, f32[1,256]{1,0:T(1,128)S(1)} %collective-permute-done.21.refs_2_, f32[1,256]{1,0:T(1,128)S(1)} %collective-permute-done.22.refs_3_), custom_call_target="tpu_custom_call" | custom-call | tf_op jit(solution)/shard_map/unpack/pallas_call | solution.py:194
  (3 shorter events, 0.0 us)
Async XLA Ops:
  3.4 4.8 %collective-permute-start = (f32[1,1024]{1,0:T(1,128)}, f32[1,1024]{1,0:T(1,128)S(1)}, u32[]{:S(2)}, u32[]{:S(2)}) collective-permute-start(f32[1,1024]{1,0:T(1,128)} %get-tuple-element.29), channel_id=1, source_target_pairs={{0,2},{1,3},{2,0},{3,1},{4,6},{5,7},{6,4},{7,5},{8,10},{9,11},{10,... | collective-permute-start | bytes 12296 | tf_op jit(solution)/shard_map/ppermute | solution.py:221
  8.9 2.2 %collective-permute-start.1 = (f32[2,1024]{1,0:T(2,128)S(1)}, f32[2,1024]{1,0:T(2,128)S(1)}, u32[]{:S(2)}, u32[]{:S(2)}) collective-permute-start(f32[2,1024]{1,0:T(2,128)S(1)} %pad_maximum_fusion.2), channel_id=1, source_target_pairs={{0,1},{1,0},{2,3},{3,2},{4,5},{5,4},{6,7},{7,6},{8,9},{9,8},{10,11... | collective-permute-start | bytes 24584 | tf_op jit(solution)/shard_map/ppermute | solution.py:221
  9.0 24.4 %collective-permute-start.5 = (bf16[256,768]{1,0:T(8,128)(2,1)}, bf16[256,768]{1,0:T(8,128)(2,1)S(1)}, u32[]{:S(2)}, u32[]{:S(2)}) collective-permute-start(bf16[256,768]{1,0:T(8,128)(2,1)} %get-tuple-element.34), channel_id=1, source_target_pairs={{0,4},{1,5},{2,6},{3,7},{4,8},{5,9},{6,10},{7,11},{8,12},{9,13},{1... | collective-permute-start | bytes 1179656 | tf_op jit(solution)/shard_map/ppermute | solution.py:218
  11.9 22.9 %collective-permute-start.8 = (bf16[256,768]{1,0:T(8,128)(2,1)}, bf16[256,768]{1,0:T(8,128)(2,1)S(1)}, u32[]{:S(2)}, u32[]{:S(2)}) collective-permute-start(bf16[256,768]{1,0:T(8,128)(2,1)} %get-tuple-element.38), channel_id=1, source_target_pairs={{0,12},{1,13},{2,14},{3,15},{4,0},{5,1},{6,2},{7,3},{8,4},{9,5},{1... | collective-permute-start | bytes 1179656 | tf_op jit(solution)/shard_map/ppermute | solution.py:218
  15.0 16.8 %collective-permute-start.2 = (f32[4,256]{1,0:T(4,128)S(1)}, f32[4,256]{1,0:T(4,128)S(1)}, u32[]{:S(2)}, u32[]{:S(2)}) collective-permute-start(f32[4,256]{1,0:T(4,128)S(1)} %get-tuple-element.48), channel_id=1, source_target_pairs={{0,4},{1,5},{2,6},{3,7},{4,8},{5,9},{6,10},{7,11},{8,12},{9,13},{1... | collective-permute-start | bytes 12296 | tf_op jit(solution)/shard_map/ppermute | solution.py:218
  15.0 18.3 %collective-permute-start.3 = (f32[4,256]{1,0:T(4,128)S(1)}, f32[4,256]{1,0:T(4,128)S(1)}, u32[]{:S(2)}, u32[]{:S(2)}) collective-permute-start(f32[4,256]{1,0:T(4,128)S(1)} %get-tuple-element.47), channel_id=1, source_target_pairs={{0,12},{1,13},{2,14},{3,15},{4,0},{5,1},{6,2},{7,3},{8,4},{9,5},{1... | collective-permute-start | bytes 12296 | tf_op jit(solution)/shard_map/ppermute | solution.py:218
  18.9 14.5 %collective-permute-start.4 = (f32[4,256]{1,0:T(4,128)S(1)}, f32[4,256]{1,0:T(4,128)S(1)}, u32[]{:S(2)}, u32[]{:S(2)}) collective-permute-start(f32[4,256]{1,0:T(4,128)S(1)} %get-tuple-element.46), channel_id=1, source_target_pairs={{0,8},{1,9},{2,10},{3,11},{4,12},{5,13},{6,14},{7,15},{8,0},{9,1},... | collective-permute-start | bytes 12296 | tf_op jit(solution)/shard_map/ppermute | solution.py:218
  31.9 12.3 %collective-permute-start.13 = (bf16[256,768]{1,0:T(8,128)(2,1)}, bf16[256,768]{1,0:T(8,128)(2,1)S(1)}, u32[]{:S(2)}, u32[]{:S(2)}) collective-permute-start(bf16[256,768]{1,0:T(8,128)(2,1)} %get-tuple-element.36.refs_2_), channel_id=1, source_target_pairs={{0,2},{1,3},{2,0},{3,1},{4,6},{5,7},{6,4},{7,5},{8,10},{9,11},{10,... | collective-permute-start | bytes 1179656 | tf_op jit(solution)/shard_map/ppermute | solution.py:221
  33.3 10.8 %collective-permute-start.9 = (bf16[256,768]{1,0:T(8,128)(2,1)}, bf16[256,768]{1,0:T(8,128)(2,1)S(1)}, u32[]{:S(2)}, u32[]{:S(2)}) collective-permute-start(bf16[256,768]{1,0:T(8,128)(2,1)} %get-tuple-element.36.refs_2_), channel_id=1, source_target_pairs={{0,1},{1,0},{2,3},{3,2},{4,5},{5,4},{6,7},{7,6},{8,9},{9,8},{10,11... | collective-permute-start | bytes 1179656 | tf_op jit(solution)/shard_map/ppermute | solution.py:221
  33.4 20.2 %collective-permute-start.6 = (bf16[256,768]{1,0:T(8,128)(2,1)}, bf16[256,768]{1,0:T(8,128)(2,1)S(1)}, u32[]{:S(2)}, u32[]{:S(2)}) collective-permute-start(bf16[256,768]{1,0:T(8,128)(2,1)} %get-tuple-element.35), channel_id=1, source_target_pairs={{0,8},{1,9},{2,10},{3,11},{4,12},{5,13},{6,14},{7,15},{8,0},{9,1},... | collective-permute-start | bytes 1179656 | tf_op jit(solution)/shard_map/ppermute | solution.py:218
  34.2 19.5 %collective-permute-start.14 = (bf16[256,768]{1,0:T(8,128)(2,1)S(1)}, bf16[256,768]{1,0:T(8,128)(2,1)S(1)}, u32[]{:S(2)}, u32[]{:S(2)}) collective-permute-start(bf16[256,768]{1,0:T(8,128)(2,1)S(1)} %collective-permute-done.5.refs_3_), channel_id=1, source_target_pairs={{0,2},{1,3},{2,0},{3,1},{4,6},{5,7},{6,4},{7,5},{8,10},{9,11},{10,... | collective-permute-start | bytes 1179656 | tf_op jit(solution)/shard_map/ppermute | solution.py:221
  34.7 19.4 %collective-permute-start.10 = (bf16[256,768]{1,0:T(8,128)(2,1)S(1)}, bf16[256,768]{1,0:T(8,128)(2,1)S(1)}, u32[]{:S(2)}, u32[]{:S(2)}) collective-permute-start(bf16[256,768]{1,0:T(8,128)(2,1)S(1)} %collective-permute-done.5.refs_3_), channel_id=1, source_target_pairs={{0,1},{1,0},{2,3},{3,2},{4,5},{5,4},{6,7},{7,6},{8,9},{9,8},{10,11... | collective-permute-start | bytes 1179656 | tf_op jit(solution)/shard_map/ppermute | solution.py:221
  44.1 10.0 %collective-permute-start.11 = (bf16[256,768]{1,0:T(8,128)(2,1)S(1)}, bf16[256,768]{1,0:T(8,128)(2,1)S(1)}, u32[]{:S(2)}, u32[]{:S(2)}) collective-permute-start(bf16[256,768]{1,0:T(8,128)(2,1)S(1)} %collective-permute-done.8.refs_4_), channel_id=1, source_target_pairs={{0,1},{1,0},{2,3},{3,2},{4,5},{5,4},{6,7},{7,6},{8,9},{9,8},{10,11... | collective-permute-start | bytes 1179656 | tf_op jit(solution)/shard_map/ppermute | solution.py:221
  44.1 16.8 %collective-permute-start.17 = (bf16[256,768]{1,0:T(8,128)(2,1)S(1)}, bf16[256,768]{1,0:T(8,128)(2,1)S(1)}, u32[]{:S(2)}, u32[]{:S(2)}) collective-permute-start(bf16[256,768]{1,0:T(8,128)(2,1)S(1)} %collective-permute-done.8.refs_4_), channel_id=1, source_target_pairs={{0,2},{1,3},{2,0},{3,1},{4,6},{5,7},{6,4},{7,5},{8,10},{9,11},{10,... | collective-permute-start | bytes 1179656 | tf_op jit(solution)/shard_map/ppermute | solution.py:221
  53.6 7.4 %collective-permute-start.15 = (bf16[256,768]{1,0:T(8,128)(2,1)S(1)}, bf16[256,768]{1,0:T(8,128)(2,1)S(1)}, u32[]{:S(2)}, u32[]{:S(2)}) collective-permute-start(bf16[256,768]{1,0:T(8,128)(2,1)S(1)} %collective-permute-done.13.refs_10_), channel_id=1, source_target_pairs={{0,1},{1,0},{2,3},{3,2},{4,5},{5,4},{6,7},{7,6},{8,9},{9,8},{10,11... | collective-permute-start | bytes 1179656 | tf_op jit(solution)/shard_map/ppermute | solution.py:221
  53.6 7.3 %collective-permute-start.12 = (bf16[256,768]{1,0:T(8,128)(2,1)S(1)}, bf16[256,768]{1,0:T(8,128)(2,1)S(1)}, u32[]{:S(2)}, u32[]{:S(2)}) collective-permute-start(bf16[256,768]{1,0:T(8,128)(2,1)S(1)} %collective-permute-done.6.refs_5_), channel_id=1, source_target_pairs={{0,1},{1,0},{2,3},{3,2},{4,5},{5,4},{6,7},{7,6},{8,9},{9,8},{10,11... | collective-permute-start | bytes 1179656 | tf_op jit(solution)/shard_map/ppermute | solution.py:221
  54.1 6.9 %collective-permute-start.16 = (bf16[256,768]{1,0:T(8,128)(2,1)S(1)}, bf16[256,768]{1,0:T(8,128)(2,1)S(1)}, u32[]{:S(2)}, u32[]{:S(2)}) collective-permute-start(bf16[256,768]{1,0:T(8,128)(2,1)S(1)} %collective-permute-done.14.refs_11_), channel_id=1, source_target_pairs={{0,1},{1,0},{2,3},{3,2},{4,5},{5,4},{6,7},{7,6},{8,9},{9,8},{10,11... | collective-permute-start | bytes 1179656 | tf_op jit(solution)/shard_map/ppermute | solution.py:221
  54.2 13.6 %collective-permute-start.7 = (bf16[256,768]{1,0:T(8,128)(2,1)S(1)}, bf16[256,768]{1,0:T(8,128)(2,1)S(1)}, u32[]{:S(2)}, u32[]{:S(2)}) collective-permute-start(bf16[256,768]{1,0:T(8,128)(2,1)S(1)} %collective-permute-done.6.refs_5_), channel_id=1, source_target_pairs={{0,2},{1,3},{2,0},{3,1},{4,6},{5,7},{6,4},{7,5},{8,10},{9,11},{10,... | collective-permute-start | bytes 1179656 | tf_op jit(solution)/shard_map/ppermute | solution.py:221
  61.0 6.9 %collective-permute-start.18 = (bf16[256,768]{1,0:T(8,128)(2,1)S(1)}, bf16[256,768]{1,0:T(8,128)(2,1)S(1)}, u32[]{:S(2)}, u32[]{:S(2)}) collective-permute-start(bf16[256,768]{1,0:T(8,128)(2,1)S(1)} %collective-permute-done.17.refs_6_), channel_id=1, source_target_pairs={{0,1},{1,0},{2,3},{3,2},{4,5},{5,4},{6,7},{7,6},{8,9},{9,8},{10,11... | collective-permute-start | bytes 1179656 | tf_op jit(solution)/shard_map/ppermute | solution.py:221
  61.0 1.0 %copy-start.1 = (bf16[256,768]{1,0:T(8,128)(2,1)S(1)}, bf16[256,768]{1,0:T(8,128)(2,1)}, u32[]{:S(2)}) copy-start(bf16[256,768]{1,0:T(8,128)(2,1)} %get-tuple-element.36.refs_2_) | copy-start | bytes 1179652
  67.8 1.7 %collective-permute-start.19 = (bf16[256,768]{1,0:T(8,128)(2,1)S(1)}, bf16[256,768]{1,0:T(8,128)(2,1)S(1)}, u32[]{:S(2)}, u32[]{:S(2)}) collective-permute-start(bf16[256,768]{1,0:T(8,128)(2,1)S(1)} %collective-permute-done.7.refs_6_), channel_id=1, source_target_pairs={{0,1},{1,0},{2,3},{3,2},{4,5},{5,4},{6,7},{7,6},{8,9},{9,8},{10,11... | collective-permute-start | bytes 1179656 | tf_op jit(solution)/shard_map/ppermute | solution.py:221
  68.9 8.1 %copy-start = (s32[1,512]{1,0:T(1,128)S(1)}, s32[1,512]{1,0:T(1,128)}, u32[]{:S(2)}) copy-start(s32[1,512]{1,0:T(1,128)} %get-tuple-element.25.slot_ref) | copy-start | bytes 6148
  70.5 3.6 %collective-permute-start.20 = (f32[1,256]{1,0:T(1,128)S(1)}, f32[1,256]{1,0:T(1,128)S(1)}, u32[]{:S(2)}, u32[]{:S(2)}) collective-permute-start(f32[1,256]{1,0:T(1,128)S(1)} %get-tuple-element.42), channel_id=1, source_target_pairs={{0,12},{1,13},{2,14},{3,15},{4,0},{5,1},{6,2},{7,3},{8,4},{9,5},{1... | collective-permute-start | bytes 3080 | tf_op jit(solution)/shard_map/ppermute | solution.py:218
  71.0 5.4 %collective-permute-start.21 = (f32[1,256]{1,0:T(1,128)S(1)}, f32[1,256]{1,0:T(1,128)S(1)}, u32[]{:S(2)}, u32[]{:S(2)}) collective-permute-start(f32[1,256]{1,0:T(1,128)S(1)} %get-tuple-element.43), channel_id=1, source_target_pairs={{0,4},{1,5},{2,6},{3,7},{4,8},{5,9},{6,10},{7,11},{8,12},{9,13},{1... | collective-permute-start | bytes 3080 | tf_op jit(solution)/shard_map/ppermute | solution.py:218
  72.6 4.5 %collective-permute-start.22 = (f32[1,256]{1,0:T(1,128)S(1)}, f32[1,256]{1,0:T(1,128)S(1)}, u32[]{:S(2)}, u32[]{:S(2)}) collective-permute-start(f32[1,256]{1,0:T(1,128)S(1)} %get-tuple-element.44), channel_id=1, source_target_pairs={{0,8},{1,9},{2,10},{3,11},{4,12},{5,13},{6,14},{7,15},{8,0},{9,1},... | collective-permute-start | bytes 3080 | tf_op jit(solution)/shard_map/ppermute | solution.py:218

commit v4 on v2

--- a/solution.py
+++ b/solution.py
@@ -6,8 +6,8 @@
 from jax.sharding import PartitionSpec as P
 
 GROUP = 4
-UNITS = (4, 4, 4, 4)
 BLOCKS = 4
+PAD = 16
 STEP = 512
 GRANT = 16 << 20
 NT = (((1,), (1,)), ((), ()))
@@ -25,9 +25,8 @@
     return out
 
 
-def pack_kernel(groups, cap, units, pieces, emb_hbm, owner_hbm, cluster_hbm, *refs):
+def pack_kernel(groups, cap, units, emb_hbm, owner_hbm, cluster_hbm, *refs):
     blocks, refs = refs[: len(units)], refs[len(units) :]
-    labels, refs = refs[: len(pieces)], refs[len(pieces) :]
     slot_ref, emb_ref, unit_ref, owner_ref, cluster_ref, sems = refs
     rows = emb_ref.shape[0]
     part = rows // 4
@@ -52,7 +51,7 @@
     slot_ref[...] = slot
     copies[1].wait()
     label = ((cluster_ref[...] & 15) + 1).astype(jnp.float32).astype(jnp.bfloat16)
-    label = jnp.broadcast_to(label, (16, rows))
+    label = jnp.broadcast_to(label, (PAD, rows))
     for i in range(4):
         copies[2 + i].wait()
         x = emb_ref[i * part : (i + 1) * part, :]
@@ -61,24 +60,26 @@
             jnp.bfloat16
         )
     unit = unit_ref[...]
-    for u, (start, size) in enumerate(units):
+    for ref, (start, size) in zip(blocks, units):
         hot = (iota((size, rows), 0) + start == slot).astype(jnp.bfloat16)
-        blocks[u][...] = jnp.dot(hot, unit, preferred_element_type=jnp.float32).astype(jnp.bfloat16)
-        packed = lax.dot_general(label, hot, NT, preferred_element_type=jnp.float32)
-        packed = packed[0:1, :] - 1.0
-        for i, (low, width) in enumerate(pieces):
-            a, b = max(low, start), min(low + width, start + size)
-            if a < b:
-                labels[i][:, a - low : b - low] = packed[:, a - start : b - start]
-
-
-def pack(groups, cap, units, pieces, embedding, owner, cluster):
+        packed = jnp.dot(hot, unit, preferred_element_type=jnp.float32).astype(jnp.bfloat16)
+        marks = lax.dot_general(label, hot, NT, preferred_element_type=jnp.float32)
+        marks = (marks - 1.0).astype(jnp.bfloat16)
+        for i in range(size // cap):
+            low = i * (cap + PAD)
+            ref[low : low + cap, :] = packed[i * cap : (i + 1) * cap, :]
+            ref[low + cap : low + cap + PAD, :] = jnp.zeros((PAD, unit.shape[1]), jnp.bfloat16)
+            ref[low + cap : low + cap + PAD, 0:cap] = marks[:, i * cap : (i + 1) * cap]
+
+
+def pack(groups, cap, units, embedding, owner, cluster):
     rows, width = embedding.shape
     return pl.pallas_call(
-        lambda *refs: pack_kernel(groups, cap, units, pieces, *refs),
+        lambda *refs: pack_kernel(groups, cap, units, *refs),
         in_specs=[pl.BlockSpec(memory_space=pltpu.HBM)] * 3,
-        out_shape=[jax.ShapeDtypeStruct((n, width), jnp.bfloat16) for _, n in units]
-        + [jax.ShapeDtypeStruct((1, n), jnp.float32) for _, n in pieces]
+        out_shape=[
+            jax.ShapeDtypeStruct((n // cap * (cap + PAD), width), jnp.bfloat16) for _, n in units
+        ]
         + [jax.ShapeDtypeStruct((1, rows), jnp.int32)],
         scratch_shapes=[
             pltpu.VMEM((rows, width), jnp.float32),
@@ -91,35 +92,38 @@
     )(embedding, owner.reshape(1, rows), cluster.reshape(1, rows))
 
 
-def compare_kernel(size, outs, jobs, shape, *refs):
-    near, far, best_ref, refs = refs[0], refs[1], refs[2], refs[3:]
-    count = sum(shape.values())
-    pieces, refs = refs[:count], refs[count:]
-    outputs, scratch = refs[: len(outs)], refs[len(outs) :]
-    place = {}
-    for index, key in enumerate(shape):
-        start = sum(list(shape.values())[:index])
-        low = 0
-        for ref in pieces[start : start + shape[key]]:
-            place.setdefault(key, []).append((low, ref))
-            low += ref.shape[0]
-    query_ref, extra = scratch[0], list(scratch[1:])
-    own = [k for p, k in shape if p == 0]
-    for k in own:
-        for low, ref in place[0, k]:
-            query_ref[k * size + low : k * size + low + ref.shape[0], :] = ref[...]
-    keys = {}
-    for key, parts in place.items():
-        if key[0] == 0:
-            keys[key] = query_ref.at[key[1] * size : (key[1] + 1) * size]
-        elif len(parts) == 1:
-            keys[key] = parts[0][1]
+def compare_kernel(cap, outs, jobs, names, *refs):
+    best_ref, refs = refs[0], refs[1:]
+    given, refs = dict(zip(names, refs)), refs[len(names) :]
+    outputs, scratch = refs[: len(outs)], list(refs[len(outs) :])
+    query_ref = scratch.pop()
+    size = query_ref.shape[0] // BLOCKS
+
+    def unfold(ref, target, low):
+        for i in range(size // cap):
+            start = i * (cap + PAD)
+            target[low + i * cap : low + (i + 1) * cap, :] = ref[start : start + cap, :]
+
+    keys, marks = {}, {}
+    for (peer, k), ref in given.items():
+        parts = []
+        for i in range(size // cap):
+            start = i * (cap + PAD) + cap
+            parts.append(ref[start : start + PAD, 0:cap].astype(jnp.float32))
+        marks[peer, k] = jnp.concatenate(parts, axis=1)[0:1, :]
+        if peer == 0:
+            unfold(ref, query_ref, k * size)
+            keys[peer, k] = query_ref.at[k * size : (k + 1) * size]
+        elif size == cap:
+            keys[peer, k] = ref.at[0:cap]
         else:
-            keys[key] = extra.pop()
-            for low, ref in parts:
-                keys[key][low : low + ref.shape[0], :] = ref[...]
-    table = jnp.concatenate([near[...], far[...]] * 2, axis=0)
-    columns = {k: table[:, k * size : (k + 1) * size].T for k in sorted({k for _, k in shape})}
+            keys[peer, k] = scratch.pop()
+            unfold(ref, keys[peer, k], 0)
+    columns = {}
+    for k in range(BLOCKS):
+        table = [marks.get((peer, k), marks[0, k]) for peer in range(4)]
+        columns[k] = jnp.concatenate(table * 2, axis=0).T
+    near = jnp.concatenate([marks[0, k] for k in range(BLOCKS)], axis=1)
     bests = [best_ref[:, k * size : (k + 1) * size] for k in range(BLOCKS)]
     for low, high, k, peers in jobs:
         for left in range(low, high, STEP // size):
@@ -154,24 +158,22 @@
             ref[:, a - low : b - low] = row[:, a - start : b - start]
 
 
-def compare(outs, jobs, labels, blocks, best):
-    size = sum(part.shape[0] for part in blocks[0, 0])
-    width = blocks[0, 0][0].shape[1]
-    shape = {key: len(parts) for key, parts in blocks.items()}
-    split = [key for key in shape if key[0] and shape[key] > 1]
+def compare(cap, outs, jobs, blocks, best):
+    slots, width = best.shape[1], blocks[0, 0].shape[1]
+    size = slots // BLOCKS
     tiles = sum((high - low) * len(peers) for low, high, _, peers in jobs)
-    queries = 1 + max(k for p, k in shape if p == 0)
+    folded = sum(1 for peer, _ in blocks if peer) if size > cap else 0
     return pl.pallas_call(
-        lambda *refs: compare_kernel(size, outs, jobs, shape, *refs),
+        lambda *refs: compare_kernel(cap, outs, jobs, tuple(blocks), *refs),
         out_shape=[jax.ShapeDtypeStruct((1, n), jnp.float32) for _, n in outs],
-        scratch_shapes=[pltpu.VMEM((queries * size, width), jnp.bfloat16)]
-        + [pltpu.VMEM((size, width), jnp.bfloat16)] * len(split),
+        scratch_shapes=[pltpu.VMEM((size, width), jnp.bfloat16)] * folded
+        + [pltpu.VMEM((slots, width), jnp.bfloat16)],
         compiler_params=pltpu.CompilerParams(vmem_limit_bytes=GRANT),
         cost_estimate=pl.CostEstimate(
             flops=2 * tiles * size * size * width, bytes_accessed=0, transcendentals=0
         ),
         name=f"compare{len(jobs)}_{tiles}",
-    )(*labels, best, *[part for parts in blocks.values() for part in parts])
+    )(best, *blocks.values())
 
 
 def unpack_kernel(slot_ref, *refs):
@@ -209,7 +211,7 @@
     groups = devices // GROUP
     cap = GROUP * max(2, 2 * rows // devices)
     slots = groups * cap
-    units = spans([n * slots // sum(UNITS) for n in UNITS])
+    units = spans([slots // BLOCKS] * BLOCKS)
     pieces = spans([max(cap, 128)] * (slots // max(cap, 128)))
     shifts = [0] + [(k + 1) // 2 if k % 2 else groups - k // 2 for k in range(1, groups)]
 
@@ -228,14 +230,18 @@
             out.append(shift(part, sign * shifts[k]) if shifts[k] else part)
         return join(out, axis)
 
-    sent = pack(groups, cap, units, pieces, embedding, row_owner, cluster_id)
-    blocks, label, slot = list(sent[: len(units)]), sent[len(units) : -1], sent[-1]
+    *blocks, slot = pack(groups, cap, units, embedding, row_owner, cluster_id)
 
     def tie(*arrays):
         return lax.optimization_barrier(arrays)
 
     def send(u):
-        return exchange(blocks[u], units[u][0], 0, 1)
+        array, out = blocks[u], []
+        for i in range(array.shape[0] // (cap + PAD)):
+            part = lax.slice_in_dim(array, i * (cap + PAD), (i + 1) * (cap + PAD))
+            distance = shifts[units[u][0] // cap + i]
+            out.append(shift(part, distance) if distance else part)
+        return join(out, 0)
 
     def cross(array):
         return swap(array, 2)
@@ -243,14 +249,10 @@
     def core(array):
         return swap(array, 1)
 
-    across, beside, beyond = [None] * BLOCKS, [None] * BLOCKS, [None] * BLOCKS
-    own = [blocks[0], send(1), None, None]
+    arrays = [[None] * BLOCKS for _ in range(4)]
+    own, across, beside, beyond = arrays
+    own[0], own[1] = blocks[0], send(1)
     across[0], beside[0] = cross(own[0]), core(own[0])
-    *label, beside[0] = tie(*label, beside[0])
-    label = [exchange(l, low, 1, 1) for l, (low, _) in zip(label, pieces)]
-    label = join(label, 1)
-    near = jnp.concatenate([label, cross(label)], axis=0)
-    labels = [near, core(near)]
     blocks[2], beside[0] = tie(blocks[2], beside[0])
     own[2] = send(2)
     blocks[3], own[1] = tie(blocks[3], own[1])
@@ -260,22 +262,21 @@
         across[u] = cross(own[u])
     for u in range(BLOCKS - 1):
         beyond[u] = core(across[u])
-    arrays = [own, across, beside, beyond]
 
     def given(peers, blocks):
-        return {(peer, k): [arrays[peer][k]] for peer in peers for k in blocks}
+        return {(peer, k): arrays[peer][k] for peer in peers for k in blocks}
 
     every, row = (0, 1, 2, 3), [(0, slots)]
     best = jnp.full((1, slots), -1.0, jnp.float32)
     jobs = [(0, 4, 0, every), (0, 4, 1, every), (0, 4, 2, (0, 2)), (0, 4, 3, (0, 2))]
     some = given((0, 2), range(4)) | given((1, 3), range(2))
-    (best,) = compare(row, jobs, labels, some, best)
+    (best,) = compare(cap, row, jobs, some, best)
     across[3], best = tie(across[3], best)
     beyond[3] = core(across[3])
     some = given((0,), range(4)) | given((1, 3), (2,))
-    (best,) = compare(row, [(0, 4, 2, (1, 3))], labels, some, best)
+    (best,) = compare(cap, row, [(0, 4, 2, (1, 3))], some, best)
     some = given((0,), range(4)) | given((1, 3), (3,))
-    best = compare(pieces, [(0, 4, 3, (1, 3))], labels, some, best)
+    best = compare(cap, pieces, [(0, 4, 3, (1, 3))], some, best)
     backs = [exchange(b, low, 1, -1) for b, (low, _) in zip(best, pieces)]
     return unpack(slot, backs).reshape(rows)
 

time: 72.2 us -> 70.9 us (0.982)
  waiting for transfers between devices: 36.9 us -> 25.1 us
  starting transfers between devices: 21.4 us -> 32.8 us
    ppermute x9 -> x6, starting transfers between devices: 12.3 us -> 26 us  [shift(): lax.ppermute(array, 'blk', [(i, (i + step) % devices) for i in range(devi...]
    ppermute x9 -> x6, waiting for transfers between devices: 31.6 us -> 20.5 us  [shift(): lax.ppermute(array, 'blk', [(i, (i + step) % devices) for i in range(devi...]
    ppermute x14 -> x12, starting transfers between devices: 9.1 us -> 6.75 us  [swap(): return lax.ppermute(array, 'blk', [(i, i ^ mask) for i in range(devices)])]
    ppermute x14 -> x12, waiting for transfers between devices: 5.37 us -> 4.58 us  [swap(): return lax.ppermute(array, 'blk', [(i, i ^ mask) for i in range(devices)])]
    unnamed x7 -> x4, local copies, waits for them, and re-layouts: 1.69 us -> 1.01 us
  transfers between devices with their start and end apart: 23 -> 18, of which waited for: 9 -> 7; matrix products, arithmetic and copies ran while one was open for 1% -> 0% of each run, Pallas kernels for 9% -> 9%
where the time goes in v4:
time: 70.9 us; the launch traced here: 70.7 us
  starting transfers between devices  32.8 us (46%)
  waiting for transfers between devices  25.1 us (35%)
  Pallas kernels  11.8 us (17%)
  local copies, waits for them, and re-layouts  1.01 us (1%)
    ppermute x6, starting transfers between devices, shift(): lax.ppermute(array, 'blk', [(i, (i + step) % devices) for i in range(devi...  26 us
    ppermute x6, waiting for transfers between devices, shift(): lax.ppermute(array, 'blk', [(i, (i + step) % devices) for i in range(devi...  20.5 us
    pallas_call x3, Pallas kernels, compare(): pl.pallas_call(lambda *refs: compare_kernel(cap, outs, jobs, tuple(blocks...  7.31 us
    ppermute x12, starting transfers between devices, swap(): return lax.ppermute(array, 'blk', [(i, i ^ mask) for i in range(devices)])  6.75 us
    ppermute x12, waiting for transfers between devices, swap(): return lax.ppermute(array, 'blk', [(i, i ^ mask) for i in range(devices)])  4.58 us
    pallas_call x1, Pallas kernels, pack(): pl.pallas_call(lambda *refs: pack_kernel(groups, cap, units, *refs), in_s...  3.42 us
  transfers between devices with their start and end apart: 18, of which 7 were waited for; matrix products, arithmetic and copies ran while one was open for 0% of the time, Pallas kernels for 9%

profile of v4, /device:TPU:0, one launch (start us, length us, event | category | flops | bytes accessed | tf_op | source)
XLA Modules:
  0.0 70.7 jit_solution(10522476511566698427)
XLA Ops:
  0.0 3.4 %pack.1 = (bf16[272,768]{1,0:T(8,128)(2,1)}, bf16[272,768]{1,0:T(8,128)(2,1)}, bf16[272,768]{1,0:T(8,128)(2,1)}, bf16[272,768]{1,0:T(8,128)(2,1)}, s32[1,512]{1,0:T(1,128)}) custom-call(f32[512,768]{1,0:T(8,128)} %refs_0_.1, s32[1,512]{1,0:T(1,128)} %bitcast.3, s32[1,512]{1,0:T(1,128)} %bitcast.4), custom_call_target="tpu_custom_call" | custom-call | tf_op jit(solution)/shard_map/pack/pallas_call | solution.py:77
  3.4 0.5 collective-permute-start.3
  4.0 2.6 %collective-permute-start = (bf16[272,768]{1,0:T(8,128)(2,1)}, bf16[272,768]{1,0:T(8,128)(2,1)S(1)}, u32[]{:S(2)}, u32[]{:S(2)}) collective-permute-start(bf16[272,768]{1,0:T(8,128)(2,1)} %get-tuple-element.22), channel_id=1, source_target_pairs={{0,4},{1,5},{2,6},{3,7},{4,8},{5,9},{6,10},{7,11},{8,12},{9,13},{1... | collective-permute-start | bytes 1253384 | tf_op jit(solution)/shard_map/ppermute | solution.py:220
  6.6 1.5 %collective-permute-start.8 = (bf16[272,768]{1,0:T(8,128)(2,1)}, bf16[272,768]{1,0:T(8,128)(2,1)S(1)}, u32[]{:S(2)}, u32[]{:S(2)}) collective-permute-start(bf16[272,768]{1,0:T(8,128)(2,1)} %get-tuple-element.24.refs_1_), channel_id=1, source_target_pairs={{0,2},{1,3},{2,0},{3,1},{4,6},{5,7},{6,4},{7,5},{8,10},{9,11},{10,... | collective-permute-start | bytes 1253384 | tf_op jit(solution)/shard_map/ppermute | solution.py:223
  8.1 0.0 collective-permute-done.3.refs_5_
  8.1 2.4 %collective-permute-start.4 = (bf16[272,768]{1,0:T(8,128)(2,1)}, bf16[272,768]{1,0:T(8,128)(2,1)S(1)}, u32[]{:S(2)}, u32[]{:S(2)}) collective-permute-start(bf16[272,768]{1,0:T(8,128)(2,1)} %get-tuple-element.27), channel_id=1, source_target_pairs={{0,12},{1,13},{2,14},{3,15},{4,0},{5,1},{6,2},{7,3},{8,4},{9,5},{1... | collective-permute-start | bytes 1253384 | tf_op jit(solution)/shard_map/ppermute | solution.py:220
  10.5 8.8 %collective-permute-done.refs_2_ = bf16[272,768]{1,0:T(8,128)(2,1)S(1)} collective-permute-done((bf16[272,768]{1,0:T(8,128)(2,1)}, bf16[272,768]{1,0:T(8,128)(2,1)S(1)}, u32[]{:S(2)}, u32[]{:S(2)}) %collective-permute-start) | collective-permute-done | bytes 417824 | tf_op jit(solution)/shard_map/ppermute | solution.py:220
  19.4 1.6 %collective-permute-start.9 = (bf16[272,768]{1,0:T(8,128)(2,1)S(1)}, bf16[272,768]{1,0:T(8,128)(2,1)S(1)}, u32[]{:S(2)}, u32[]{:S(2)}) collective-permute-start(bf16[272,768]{1,0:T(8,128)(2,1)S(1)} %collective-permute-done.refs_2_), channel_id=1, source_target_pairs={{0,2},{1,3},{2,0},{3,1},{4,6},{5,7},{6,4},{7,5},{8,10},{9,11},{10,... | collective-permute-start | bytes 1253384 | tf_op jit(solution)/shard_map/ppermute | solution.py:223
  21.0 13.7 %collective-permute-start.1 = (bf16[272,768]{1,0:T(8,128)(2,1)}, bf16[272,768]{1,0:T(8,128)(2,1)S(1)}, u32[]{:S(2)}, u32[]{:S(2)}) collective-permute-start(bf16[272,768]{1,0:T(8,128)(2,1)} %get-tuple-element.23), channel_id=1, source_target_pairs={{0,8},{1,9},{2,10},{3,11},{4,12},{5,13},{6,14},{7,15},{8,0},{9,1},... | collective-permute-start | bytes 1253384 | tf_op jit(solution)/shard_map/ppermute | solution.py:220
  34.7 0.0 collective-permute-start.5
  34.7 0.0 collective-permute-done.8.refs_9_
  34.7 0.5 collective-permute-start.10
  35.2 0.0 collective-permute-done.4.refs_3_
  35.2 0.1 collective-permute-start.6
  35.3 0.0 collective-permute-done.9.refs_10_
  35.3 0.5 collective-permute-start.12
  35.9 10.1 %collective-permute-done.1.refs_4_ = bf16[272,768]{1,0:T(8,128)(2,1)S(1)} collective-permute-done((bf16[272,768]{1,0:T(8,128)(2,1)}, bf16[272,768]{1,0:T(8,128)(2,1)S(1)}, u32[]{:S(2)}, u32[]{:S(2)}) %collective-permute-start.1) | collective-permute-done | bytes 417824 | tf_op jit(solution)/shard_map/ppermute | solution.py:220
  45.9 0.0 collective-permute-start.11
  45.9 0.0 collective-permute-done.5.refs_6_
  45.9 0.5 collective-permute-start.7
  46.5 0.0 collective-permute-done.10.refs_11_
  46.5 1.5 %collective-permute-start.2 = (bf16[272,768]{1,0:T(8,128)(2,1)S(1)}, bf16[272,768]{1,0:T(8,128)(2,1)S(1)}, u32[]{:S(2)}, u32[]{:S(2)}) collective-permute-start(bf16[272,768]{1,0:T(8,128)(2,1)S(1)} %collective-permute-done.1.refs_4_), channel_id=1, source_target_pairs={{0,2},{1,3},{2,0},{3,1},{4,6},{5,7},{6,4},{7,5},{8,10},{9,11},{10,... | collective-permute-start | bytes 1253384 | tf_op jit(solution)/shard_map/ppermute | solution.py:223
  47.9 0.0 collective-permute-done.12.refs_5_
  47.9 0.0 collective-permute-start.13
  47.9 0.0 collective-permute-done.6.refs_7_
  48.0 0.0 collective-permute-done.11.refs_12_
  48.0 0.3 collective-permute-done.7.refs_8_
  48.3 0.0 copy-start.1
  48.3 1.0 %copy-done.1 = bf16[272,768]{1,0:T(8,128)(2,1)S(1)} copy-done((bf16[272,768]{1,0:T(8,128)(2,1)S(1)}, bf16[272,768]{1,0:T(8,128)(2,1)}, u32[]{:S(2)}) %copy-start.1) | copy-done | bytes 417816
  49.3 5.2 %compare4_48.1.refs_0_ = f32[1,1024]{1,0:T(1,128)S(1)} custom-call(f32[1,1024]{1,0:T(1,128)S(1)} %broadcast_in_dim.3.refs_0_, bf16[272,768]{1,0:T(8,128)(2,1)S(1)} %copy-done.1, bf16[272,768]{1,0:T(8,128)(2,1)S(1)} %collective-permute-done.refs_2_, bf16[272,768]{1,0:T(8,128)(2,1)S(1)} %collective-permute-done.4.refs_3_, ...), custom_call_target="tpu_custom_call" | custom-call | flops 4831838208 | tf_op jit(solution)/shard_map/compare4_48/pallas_call | solution.py:166
  54.5 3.5 %collective-permute-done.2.refs_5_ = bf16[272,768]{1,0:T(8,128)(2,1)S(1)} collective-permute-done((bf16[272,768]{1,0:T(8,128)(2,1)S(1)}, bf16[272,768]{1,0:T(8,128)(2,1)S(1)}, u32[]{:S(2)}, u32[]{:S(2)}) %collective-permute-start.2) | collective-permute-done | bytes 417824 | tf_op jit(solution)/shard_map/ppermute | solution.py:223
  58.1 0.0 collective-permute-start.14
  58.1 0.0 collective-permute-done.13.refs_6_
  58.1 1.0 %compare1_8.2.refs_0_ = f32[1,1024]{1,0:T(1,128)S(1)} custom-call(f32[1,1024]{1,0:T(1,128)S(1)} %compare4_48.1.refs_0_, bf16[272,768]{1,0:T(8,128)(2,1)S(1)} %copy-done.1, bf16[272,768]{1,0:T(8,128)(2,1)S(1)} %collective-permute-done.refs_2_, bf16[272,768]{1,0:T(8,128)(2,1)S(1)} %collective-permute-done.4.refs_3_, ...), custom_call_target="tpu_custom_call" | custom-call | flops 805306368 | tf_op jit(solution)/shard_map/compare1_8/pallas_call | solution.py:166
  59.1 0.0 copy-start
  59.1 0.7 collective-permute-done.14.refs_6_
  59.8 1.0 %compare1_8.3 = (f32[1,256]{1,0:T(1,128)S(1)}, f32[1,256]{1,0:T(1,128)S(1)}, f32[1,256]{1,0:T(1,128)S(1)}, f32[1,256]{1,0:T(1,128)S(1)}) custom-call(f32[1,1024]{1,0:T(1,128)S(1)} %compare1_8.2.refs_0_, bf16[272,768]{1,0:T(8,128)(2,1)S(1)} %copy-done.1, bf16[272,768]{1,0:T(8,128)(2,1)S(1)} %collective-permute-done.refs_2_, ...), custom_call_target="tpu_custom_call" | custom-call | flops 805306368 | tf_op jit(solution)/shard_map/compare1_8/pallas_call | solution.py:166
  60.9 1.7 %collective-permute-start.15 = (f32[1,256]{1,0:T(1,128)S(1)}, f32[1,256]{1,0:T(1,128)S(1)}, u32[]{:S(2)}, u32[]{:S(2)}) collective-permute-start(f32[1,256]{1,0:T(1,128)S(1)} %get-tuple-element.32), channel_id=1, source_target_pairs={{0,12},{1,13},{2,14},{3,15},{4,0},{5,1},{6,2},{7,3},{8,4},{9,5},{1... | collective-permute-start | bytes 3080 | tf_op jit(solution)/shard_map/ppermute | solution.py:220
  62.6 0.4 collective-permute-start.16
  63.0 5.1 %collective-permute-start.17 = (f32[1,256]{1,0:T(1,128)S(1)}, f32[1,256]{1,0:T(1,128)S(1)}, u32[]{:S(2)}, u32[]{:S(2)}) collective-permute-start(f32[1,256]{1,0:T(1,128)S(1)} %get-tuple-element.34), channel_id=1, source_target_pairs={{0,8},{1,9},{2,10},{3,11},{4,12},{5,13},{6,14},{7,15},{8,0},{9,1},... | collective-permute-start | bytes 3080 | tf_op jit(solution)/shard_map/ppermute | solution.py:220
  68.1 0.0 collective-permute-done.15.refs_1_
  68.1 1.0 %collective-permute-done.16.refs_2_ = f32[1,256]{1,0:T(1,128)S(1)} collective-permute-done((f32[1,256]{1,0:T(1,128)S(1)}, f32[1,256]{1,0:T(1,128)S(1)}, u32[]{:S(2)}, u32[]{:S(2)}) %collective-permute-start.16) | collective-permute-done | bytes 1056 | tf_op jit(solution)/shard_map/ppermute | solution.py:220
  69.1 0.6 collective-permute-done.17.refs_3_
  69.6 0.0 copy-done
  69.6 1.1 %unpack.1 = f32[1,512]{1,0:T(1,128)} custom-call(s32[1,512]{1,0:T(1,128)S(1)} %copy-done, f32[1,256]{1,0:T(1,128)S(1)} %get-tuple-element.31.refs_0_, f32[1,256]{1,0:T(1,128)S(1)} %collective-permute-done.15.refs_1_, f32[1,256]{1,0:T(1,128)S(1)} %collective-permute-done.16.refs_2_, f32[1,256]{1,0:T(1,128)S(1)} %collective-permute-done.17.refs_3_), custom_call_target="tpu_custom_call" | custom-call | tf_op jit(solution)/shard_map/unpack/pallas_call | solution.py:196
  (1 shorter events, 0.0 us)
Async XLA Ops:
  3.4 4.6 %collective-permute-start.3 = (bf16[272,768]{1,0:T(8,128)(2,1)}, bf16[272,768]{1,0:T(8,128)(2,1)S(1)}, u32[]{:S(2)}, u32[]{:S(2)}) collective-permute-start(bf16[272,768]{1,0:T(8,128)(2,1)} %get-tuple-element.24.refs_1_), channel_id=1, source_target_pairs={{0,1},{1,0},{2,3},{3,2},{4,5},{5,4},{6,7},{7,6},{8,9},{9,8},{10,11... | collective-permute-start | bytes 1253384 | tf_op jit(solution)/shard_map/ppermute | solution.py:223
  4.0 15.4 %collective-permute-start = (bf16[272,768]{1,0:T(8,128)(2,1)}, bf16[272,768]{1,0:T(8,128)(2,1)S(1)}, u32[]{:S(2)}, u32[]{:S(2)}) collective-permute-start(bf16[272,768]{1,0:T(8,128)(2,1)} %get-tuple-element.22), channel_id=1, source_target_pairs={{0,4},{1,5},{2,6},{3,7},{4,8},{5,9},{6,10},{7,11},{8,12},{9,13},{1... | collective-permute-start | bytes 1253384 | tf_op jit(solution)/shard_map/ppermute | solution.py:220
  6.6 28.1 %collective-permute-start.8 = (bf16[272,768]{1,0:T(8,128)(2,1)}, bf16[272,768]{1,0:T(8,128)(2,1)S(1)}, u32[]{:S(2)}, u32[]{:S(2)}) collective-permute-start(bf16[272,768]{1,0:T(8,128)(2,1)} %get-tuple-element.24.refs_1_), channel_id=1, source_target_pairs={{0,2},{1,3},{2,0},{3,1},{4,6},{5,7},{6,4},{7,5},{8,10},{9,11},{10,... | collective-permute-start | bytes 1253384 | tf_op jit(solution)/shard_map/ppermute | solution.py:223
  8.1 27.2 %collective-permute-start.4 = (bf16[272,768]{1,0:T(8,128)(2,1)}, bf16[272,768]{1,0:T(8,128)(2,1)S(1)}, u32[]{:S(2)}, u32[]{:S(2)}) collective-permute-start(bf16[272,768]{1,0:T(8,128)(2,1)} %get-tuple-element.27), channel_id=1, source_target_pairs={{0,12},{1,13},{2,14},{3,15},{4,0},{5,1},{6,2},{7,3},{8,4},{9,5},{1... | collective-permute-start | bytes 1253384 | tf_op jit(solution)/shard_map/ppermute | solution.py:220
  19.4 15.9 %collective-permute-start.9 = (bf16[272,768]{1,0:T(8,128)(2,1)S(1)}, bf16[272,768]{1,0:T(8,128)(2,1)S(1)}, u32[]{:S(2)}, u32[]{:S(2)}) collective-permute-start(bf16[272,768]{1,0:T(8,128)(2,1)S(1)} %collective-permute-done.refs_2_), channel_id=1, source_target_pairs={{0,2},{1,3},{2,0},{3,1},{4,6},{5,7},{6,4},{7,5},{8,10},{9,11},{10,... | collective-permute-start | bytes 1253384 | tf_op jit(solution)/shard_map/ppermute | solution.py:223
  21.0 24.9 %collective-permute-start.1 = (bf16[272,768]{1,0:T(8,128)(2,1)}, bf16[272,768]{1,0:T(8,128)(2,1)S(1)}, u32[]{:S(2)}, u32[]{:S(2)}) collective-permute-start(bf16[272,768]{1,0:T(8,128)(2,1)} %get-tuple-element.23), channel_id=1, source_target_pairs={{0,8},{1,9},{2,10},{3,11},{4,12},{5,13},{6,14},{7,15},{8,0},{9,1},... | collective-permute-start | bytes 1253384 | tf_op jit(solution)/shard_map/ppermute | solution.py:220
  34.7 11.2 %collective-permute-start.5 = (bf16[272,768]{1,0:T(8,128)(2,1)S(1)}, bf16[272,768]{1,0:T(8,128)(2,1)S(1)}, u32[]{:S(2)}, u32[]{:S(2)}) collective-permute-start(bf16[272,768]{1,0:T(8,128)(2,1)S(1)} %collective-permute-done.refs_2_), channel_id=1, source_target_pairs={{0,1},{1,0},{2,3},{3,2},{4,5},{5,4},{6,7},{7,6},{8,9},{9,8},{10,11... | collective-permute-start | bytes 1253384 | tf_op jit(solution)/shard_map/ppermute | solution.py:223
  34.7 11.7 %collective-permute-start.10 = (bf16[272,768]{1,0:T(8,128)(2,1)S(1)}, bf16[272,768]{1,0:T(8,128)(2,1)S(1)}, u32[]{:S(2)}, u32[]{:S(2)}) collective-permute-start(bf16[272,768]{1,0:T(8,128)(2,1)S(1)} %collective-permute-done.8.refs_9_), channel_id=1, source_target_pairs={{0,1},{1,0},{2,3},{3,2},{4,5},{5,4},{6,7},{7,6},{8,9},{9,8},{10,11... | collective-permute-start | bytes 1253384 | tf_op jit(solution)/shard_map/ppermute | solution.py:223
  35.2 12.7 %collective-permute-start.6 = (bf16[272,768]{1,0:T(8,128)(2,1)S(1)}, bf16[272,768]{1,0:T(8,128)(2,1)S(1)}, u32[]{:S(2)}, u32[]{:S(2)}) collective-permute-start(bf16[272,768]{1,0:T(8,128)(2,1)S(1)} %collective-permute-done.4.refs_3_), channel_id=1, source_target_pairs={{0,1},{1,0},{2,3},{3,2},{4,5},{5,4},{6,7},{7,6},{8,9},{9,8},{10,11... | collective-permute-start | bytes 1253384 | tf_op jit(solution)/shard_map/ppermute | solution.py:223
  35.3 12.6 %collective-permute-start.12 = (bf16[272,768]{1,0:T(8,128)(2,1)S(1)}, bf16[272,768]{1,0:T(8,128)(2,1)S(1)}, u32[]{:S(2)}, u32[]{:S(2)}) collective-permute-start(bf16[272,768]{1,0:T(8,128)(2,1)S(1)} %collective-permute-done.4.refs_3_), channel_id=1, source_target_pairs={{0,2},{1,3},{2,0},{3,1},{4,6},{5,7},{6,4},{7,5},{8,10},{9,11},{10,... | collective-permute-start | bytes 1253384 | tf_op jit(solution)/shard_map/ppermute | solution.py:223
  45.9 2.0 %collective-permute-start.11 = (bf16[272,768]{1,0:T(8,128)(2,1)S(1)}, bf16[272,768]{1,0:T(8,128)(2,1)S(1)}, u32[]{:S(2)}, u32[]{:S(2)}) collective-permute-start(bf16[272,768]{1,0:T(8,128)(2,1)S(1)} %collective-permute-done.9.refs_10_), channel_id=1, source_target_pairs={{0,1},{1,0},{2,3},{3,2},{4,5},{5,4},{6,7},{7,6},{8,9},{9,8},{10,11... | collective-permute-start | bytes 1253384 | tf_op jit(solution)/shard_map/ppermute | solution.py:223
  45.9 2.3 %collective-permute-start.7 = (bf16[272,768]{1,0:T(8,128)(2,1)S(1)}, bf16[272,768]{1,0:T(8,128)(2,1)S(1)}, u32[]{:S(2)}, u32[]{:S(2)}) collective-permute-start(bf16[272,768]{1,0:T(8,128)(2,1)S(1)} %collective-permute-done.1.refs_4_), channel_id=1, source_target_pairs={{0,1},{1,0},{2,3},{3,2},{4,5},{5,4},{6,7},{7,6},{8,9},{9,8},{10,11... | collective-permute-start | bytes 1253384 | tf_op jit(solution)/shard_map/ppermute | solution.py:223
  46.5 11.6 %collective-permute-start.2 = (bf16[272,768]{1,0:T(8,128)(2,1)S(1)}, bf16[272,768]{1,0:T(8,128)(2,1)S(1)}, u32[]{:S(2)}, u32[]{:S(2)}) collective-permute-start(bf16[272,768]{1,0:T(8,128)(2,1)S(1)} %collective-permute-done.1.refs_4_), channel_id=1, source_target_pairs={{0,2},{1,3},{2,0},{3,1},{4,6},{5,7},{6,4},{7,5},{8,10},{9,11},{10,... | collective-permute-start | bytes 1253384 | tf_op jit(solution)/shard_map/ppermute | solution.py:223
  47.9 10.1 %collective-permute-start.13 = (bf16[272,768]{1,0:T(8,128)(2,1)S(1)}, bf16[272,768]{1,0:T(8,128)(2,1)S(1)}, u32[]{:S(2)}, u32[]{:S(2)}) collective-permute-start(bf16[272,768]{1,0:T(8,128)(2,1)S(1)} %collective-permute-done.12.refs_5_), channel_id=1, source_target_pairs={{0,1},{1,0},{2,3},{3,2},{4,5},{5,4},{6,7},{7,6},{8,9},{9,8},{10,11... | collective-permute-start | bytes 1253384 | tf_op jit(solution)/shard_map/ppermute | solution.py:223
  48.3 1.0 %copy-start.1 = (bf16[272,768]{1,0:T(8,128)(2,1)S(1)}, bf16[272,768]{1,0:T(8,128)(2,1)}, u32[]{:S(2)}) copy-start(bf16[272,768]{1,0:T(8,128)(2,1)} %get-tuple-element.24.refs_1_) | copy-start | bytes 1253380
  58.1 1.8 %collective-permute-start.14 = (bf16[272,768]{1,0:T(8,128)(2,1)S(1)}, bf16[272,768]{1,0:T(8,128)(2,1)S(1)}, u32[]{:S(2)}, u32[]{:S(2)}) collective-permute-start(bf16[272,768]{1,0:T(8,128)(2,1)S(1)} %collective-permute-done.2.refs_5_), channel_id=1, source_target_pairs={{0,1},{1,0},{2,3},{3,2},{4,5},{5,4},{6,7},{7,6},{8,9},{9,8},{10,11... | collective-permute-start | bytes 1253384 | tf_op jit(solution)/shard_map/ppermute | solution.py:223
  59.1 10.5 %copy-start = (s32[1,512]{1,0:T(1,128)S(1)}, s32[1,512]{1,0:T(1,128)}, u32[]{:S(2)}) copy-start(s32[1,512]{1,0:T(1,128)} %get-tuple-element.20.slot_ref) | copy-start | bytes 6148
  60.9 7.2 %collective-permute-start.15 = (f32[1,256]{1,0:T(1,128)S(1)}, f32[1,256]{1,0:T(1,128)S(1)}, u32[]{:S(2)}, u32[]{:S(2)}) collective-permute-start(f32[1,256]{1,0:T(1,128)S(1)} %get-tuple-element.32), channel_id=1, source_target_pairs={{0,12},{1,13},{2,14},{3,15},{4,0},{5,1},{6,2},{7,3},{8,4},{9,5},{1... | collective-permute-start | bytes 3080 | tf_op jit(solution)/shard_map/ppermute | solution.py:220
  62.6 6.5 %collective-permute-start.16 = (f32[1,256]{1,0:T(1,128)S(1)}, f32[1,256]{1,0:T(1,128)S(1)}, u32[]{:S(2)}, u32[]{:S(2)}) collective-permute-start(f32[1,256]{1,0:T(1,128)S(1)} %get-tuple-element.33), channel_id=1, source_target_pairs={{0,4},{1,5},{2,6},{3,7},{4,8},{5,9},{6,10},{7,11},{8,12},{9,13},{1... | collective-permute-start | bytes 3080 | tf_op jit(solution)/shard_map/ppermute | solution.py:220
  63.0 6.7 %collective-permute-start.17 = (f32[1,256]{1,0:T(1,128)S(1)}, f32[1,256]{1,0:T(1,128)S(1)}, u32[]{:S(2)}, u32[]{:S(2)}) collective-permute-start(f32[1,256]{1,0:T(1,128)S(1)} %get-tuple-element.34), channel_id=1, source_target_pairs={{0,8},{1,9},{2,10},{3,11},{4,12},{5,13},{6,14},{7,15},{8,0},{9,1},... | collective-permute-start | bytes 3080 | tf_op jit(solution)/shard_map/ppermute | solution.py:220

commit v5 on v4

--- a/solution.py
+++ b/solution.py
@@ -7,6 +7,7 @@
 
 GROUP = 4
 BLOCKS = 4
+UNITS = (4, 4, 4, 4)
 PAD = 16
 STEP = 512
 GRANT = 16 << 20
@@ -65,11 +66,12 @@
         packed = jnp.dot(hot, unit, preferred_element_type=jnp.float32).astype(jnp.bfloat16)
         marks = lax.dot_general(label, hot, NT, preferred_element_type=jnp.float32)
         marks = (marks - 1.0).astype(jnp.bfloat16)
-        for i in range(size // cap):
-            low = i * (cap + PAD)
-            ref[low : low + cap, :] = packed[i * cap : (i + 1) * cap, :]
-            ref[low + cap : low + cap + PAD, :] = jnp.zeros((PAD, unit.shape[1]), jnp.bfloat16)
-            ref[low + cap : low + cap + PAD, 0:cap] = marks[:, i * cap : (i + 1) * cap]
+        sub = min(cap, size)
+        for i in range(size // sub):
+            low = i * (sub + PAD)
+            ref[low : low + sub, :] = packed[i * sub : (i + 1) * sub, :]
+            ref[low + sub : low + sub + PAD, :] = jnp.zeros((PAD, unit.shape[1]), jnp.bfloat16)
+            ref[low + sub : low + sub + PAD, 0:sub] = marks[:, i * sub : (i + 1) * sub]
 
 
 def pack(groups, cap, units, embedding, owner, cluster):
@@ -78,7 +80,8 @@
         lambda *refs: pack_kernel(groups, cap, units, *refs),
         in_specs=[pl.BlockSpec(memory_space=pltpu.HBM)] * 3,
         out_shape=[
-            jax.ShapeDtypeStruct((n // cap * (cap + PAD), width), jnp.bfloat16) for _, n in units
+            jax.ShapeDtypeStruct((n + n // min(cap, n) * PAD, width), jnp.bfloat16)
+            for _, n in units
         ]
         + [jax.ShapeDtypeStruct((1, rows), jnp.int32)],
         scratch_shapes=[
@@ -94,31 +97,38 @@
 
 def compare_kernel(cap, outs, jobs, names, *refs):
     best_ref, refs = refs[0], refs[1:]
-    given, refs = dict(zip(names, refs)), refs[len(names) :]
+    given = {}
+    for name, ref in zip(names, refs):
+        given.setdefault(name, []).append(ref)
+    refs = refs[len(names) :]
     outputs, scratch = refs[: len(outs)], list(refs[len(outs) :])
     query_ref = scratch.pop()
     size = query_ref.shape[0] // BLOCKS
 
-    def unfold(ref, target, low):
-        for i in range(size // cap):
-            start = i * (cap + PAD)
-            target[low + i * cap : low + (i + 1) * cap, :] = ref[start : start + cap, :]
+    def unfold(parts, target, low):
+        for ref in parts:
+            sub = min(cap, size // len(parts))
+            for start in range(0, ref.shape[0], sub + PAD):
+                target[low : low + sub, :] = ref[start : start + sub, :]
+                low += sub
 
     keys, marks = {}, {}
-    for (peer, k), ref in given.items():
-        parts = []
-        for i in range(size // cap):
-            start = i * (cap + PAD) + cap
-            parts.append(ref[start : start + PAD, 0:cap].astype(jnp.float32))
-        marks[peer, k] = jnp.concatenate(parts, axis=1)[0:1, :]
+    for (peer, k), parts in given.items():
+        sub = min(cap, size // len(parts))
+        row = [
+            ref[start + sub : start + sub + PAD, 0:sub].astype(jnp.float32)
+            for ref in parts
+            for start in range(0, ref.shape[0], sub + PAD)
+        ]
+        marks[peer, k] = jnp.concatenate(row, axis=1)[0:1, :]
         if peer == 0:
-            unfold(ref, query_ref, k * size)
+            unfold(parts, query_ref, k * size)
             keys[peer, k] = query_ref.at[k * size : (k + 1) * size]
-        elif size == cap:
-            keys[peer, k] = ref.at[0:cap]
+        elif size == sub:
+            keys[peer, k] = parts[0].at[0:size]
         else:
             keys[peer, k] = scratch.pop()
-            unfold(ref, keys[peer, k], 0)
+            unfold(parts, keys[peer, k], 0)
     columns = {}
     for k in range(BLOCKS):
         table = [marks.get((peer, k), marks[0, k]) for peer in range(4)]
@@ -159,21 +169,22 @@
 
 
 def compare(cap, outs, jobs, blocks, best):
-    slots, width = best.shape[1], blocks[0, 0].shape[1]
+    slots, width = best.shape[1], blocks[0, 0][0].shape[1]
     size = slots // BLOCKS
     tiles = sum((high - low) * len(peers) for low, high, _, peers in jobs)
-    folded = sum(1 for peer, _ in blocks if peer) if size > cap else 0
+    folded = [key for key, parts in blocks.items() if key[0] and size > min(cap, size // len(parts))]
+    names = tuple(key for key, parts in blocks.items() for _ in parts)
     return pl.pallas_call(
-        lambda *refs: compare_kernel(cap, outs, jobs, tuple(blocks), *refs),
+        lambda *refs: compare_kernel(cap, outs, jobs, names, *refs),
         out_shape=[jax.ShapeDtypeStruct((1, n), jnp.float32) for _, n in outs],
-        scratch_shapes=[pltpu.VMEM((size, width), jnp.bfloat16)] * folded
+        scratch_shapes=[pltpu.VMEM((size, width), jnp.bfloat16)] * len(folded)
         + [pltpu.VMEM((slots, width), jnp.bfloat16)],
         compiler_params=pltpu.CompilerParams(vmem_limit_bytes=GRANT),
         cost_estimate=pl.CostEstimate(
             flops=2 * tiles * size * size * width, bytes_accessed=0, transcendentals=0
         ),
         name=f"compare{len(jobs)}_{tiles}",
-    )(best, *blocks.values())
+    )(best, *[part for parts in blocks.values() for part in parts])
 
 
 def unpack_kernel(slot_ref, *refs):
@@ -211,7 +222,7 @@
     groups = devices // GROUP
     cap = GROUP * max(2, 2 * rows // devices)
     slots = groups * cap
-    units = spans([slots // BLOCKS] * BLOCKS)
+    units = spans([slots // 16 * n for n in UNITS])
     pieces = spans([max(cap, 128)] * (slots // max(cap, 128)))
     shifts = [0] + [(k + 1) // 2 if k % 2 else groups - k // 2 for k in range(1, groups)]
 
@@ -236,30 +247,26 @@
         return lax.optimization_barrier(arrays)
 
     def send(u):
-        array, out = blocks[u], []
-        for i in range(array.shape[0] // (cap + PAD)):
-            part = lax.slice_in_dim(array, i * (cap + PAD), (i + 1) * (cap + PAD))
-            distance = shifts[units[u][0] // cap + i]
+        (start, size), out = units[u], []
+        sub = min(cap, size)
+        for i in range(size // sub):
+            part = lax.slice_in_dim(blocks[u], i * (sub + PAD), (i + 1) * (sub + PAD))
+            distance = shifts[(start + i * sub) // cap]
             out.append(shift(part, distance) if distance else part)
         return join(out, 0)
 
-    def cross(array):
-        return swap(array, 2)
-
-    def core(array):
-        return swap(array, 1)
+    def cross(parts):
+        return [swap(part, 2) for part in parts]
+
+    def core(parts):
+        return [swap(part, 1) for part in parts]
 
     arrays = [[None] * BLOCKS for _ in range(4)]
     own, across, beside, beyond = arrays
-    own[0], own[1] = blocks[0], send(1)
-    across[0], beside[0] = cross(own[0]), core(own[0])
-    blocks[2], beside[0] = tie(blocks[2], beside[0])
-    own[2] = send(2)
-    blocks[3], own[1] = tie(blocks[3], own[1])
-    own[3] = send(3)
-    for u in range(1, BLOCKS):
-        beside[u] = core(own[u])
-        across[u] = cross(own[u])
+    sent = [blocks[0]] + [send(u) for u in range(1, len(units))]
+    own[:] = [sent[0]], [sent[1]], [sent[2]], sent[3:]
+    for u in range(BLOCKS):
+        beside[u], across[u] = core(own[u]), cross(own[u])
     for u in range(BLOCKS - 1):
         beyond[u] = core(across[u])
 
@@ -268,13 +275,11 @@
 
     every, row = (0, 1, 2, 3), [(0, slots)]
     best = jnp.full((1, slots), -1.0, jnp.float32)
-    jobs = [(0, 4, 0, every), (0, 4, 1, every), (0, 4, 2, (0, 2)), (0, 4, 3, (0, 2))]
-    some = given((0, 2), range(4)) | given((1, 3), range(2))
+    jobs = [(0, 4, 0, every), (0, 4, 1, every), (0, 4, 2, every), (0, 4, 3, (0, 2))]
+    some = given((0, 2), range(4)) | given((1, 3), range(3))
     (best,) = compare(cap, row, jobs, some, best)
-    across[3], best = tie(across[3], best)
+    across[3][-1], best = tie(across[3][-1], best)
     beyond[3] = core(across[3])
-    some = given((0,), range(4)) | given((1, 3), (2,))
-    (best,) = compare(cap, row, [(0, 4, 2, (1, 3))], some, best)
     some = given((0,), range(4)) | given((1, 3), (3,))
     best = compare(cap, pieces, [(0, 4, 3, (1, 3))], some, best)
     backs = [exchange(b, low, 1, -1) for b, (low, _) in zip(best, pieces)]

time: 70.9 us -> 70.5 us (level)
  starting transfers between devices: 32.8 us -> 19.6 us
  waiting for transfers between devices: 25.1 us -> 38 us
    ppermute x6, starting transfers between devices: 26 us -> 12.2 us  [shift(): lax.ppermute(array, 'blk', [(i, (i + step) % devices) for i in range(devi...]
    ppermute x6, waiting for transfers between devices: 20.5 us -> 32.5 us  [shift(): lax.ppermute(array, 'blk', [(i, (i + step) % devices) for i in range(devi...]
    ppermute x12, waiting for transfers between devices: 4.58 us -> 5.49 us  [swap(): return lax.ppermute(array, 'blk', [(i, i ^ mask) for i in range(devices)])]
    pallas_call x3 -> x2, Pallas kernels: 7.31 us -> 7.13 us  [compare(): pl.pallas_call(lambda *refs: compare_kernel(cap, outs, jobs, names, *refs...]
  transfers between devices with their start and end apart: 18 -> 18, of which waited for: 7 -> 10; matrix products, arithmetic and copies ran while one was open for 0% -> 0% of each run, Pallas kernels for 9% -> 9%
where the time goes in v5:
time: 70.5 us; the launch traced here: 70.4 us
  waiting for transfers between devices  38 us (54%)
  starting transfers between devices  19.6 us (28%)
  Pallas kernels  11.6 us (16%)
  local copies, waits for them, and re-layouts  1.01 us (1%)
    ppermute x6, waiting for transfers between devices, shift(): lax.ppermute(array, 'blk', [(i, (i + step) % devices) for i in range(devi...  32.5 us
    ppermute x6, starting transfers between devices, shift(): lax.ppermute(array, 'blk', [(i, (i + step) % devices) for i in range(devi...  12.2 us
    ppermute x12, starting transfers between devices, swap(): return lax.ppermute(array, 'blk', [(i, i ^ mask) for i in range(devices)])  7.44 us
    pallas_call x2, Pallas kernels, compare(): pl.pallas_call(lambda *refs: compare_kernel(cap, outs, jobs, names, *refs...  7.13 us
    ppermute x12, waiting for transfers between devices, swap(): return lax.ppermute(array, 'blk', [(i, i ^ mask) for i in range(devices)])  5.49 us
    pallas_call x1, Pallas kernels, pack(): pl.pallas_call(lambda *refs: pack_kernel(groups, cap, units, *refs), in_s...  3.42 us
  transfers between devices with their start and end apart: 18, of which 10 were waited for; matrix products, arithmetic and copies ran while one was open for 0% of the time, Pallas kernels for 9%

profile of v5, /device:TPU:0, one launch (start us, length us, event | category | flops | bytes accessed | tf_op | source)
XLA Modules:
  0.0 70.4 jit_solution(2200747189608146728)
XLA Ops:
  0.0 3.4 %pack.1 = (bf16[272,768]{1,0:T(8,128)(2,1)}, bf16[272,768]{1,0:T(8,128)(2,1)}, bf16[272,768]{1,0:T(8,128)(2,1)}, bf16[272,768]{1,0:T(8,128)(2,1)}, s32[1,512]{1,0:T(1,128)}) custom-call(f32[512,768]{1,0:T(8,128)} %refs_0_.1, s32[1,512]{1,0:T(1,128)} %bitcast.3, s32[1,512]{1,0:T(1,128)} %bitcast.4), custom_call_target="tpu_custom_call" | custom-call | tf_op jit(solution)/shard_map/pack/pallas_call | solution.py:79
  3.4 3.1 %collective-permute-start.2 = (bf16[272,768]{1,0:T(8,128)(2,1)}, bf16[272,768]{1,0:T(8,128)(2,1)S(1)}, u32[]{:S(2)}, u32[]{:S(2)}) collective-permute-start(bf16[272,768]{1,0:T(8,128)(2,1)} %get-tuple-element.19), channel_id=1, source_target_pairs={{0,4},{1,5},{2,6},{3,7},{4,8},{5,9},{6,10},{7,11},{8,12},{9,13},{1... | collective-permute-start | bytes 1253384 | tf_op jit(solution)/shard_map/ppermute | solution.py:231
  6.5 2.1 %collective-permute-start.3 = (bf16[272,768]{1,0:T(8,128)(2,1)}, bf16[272,768]{1,0:T(8,128)(2,1)S(1)}, u32[]{:S(2)}, u32[]{:S(2)}) collective-permute-start(bf16[272,768]{1,0:T(8,128)(2,1)} %get-tuple-element.20), channel_id=1, source_target_pairs={{0,12},{1,13},{2,14},{3,15},{4,0},{5,1},{6,2},{7,3},{8,4},{9,5},{1... | collective-permute-start | bytes 1253384 | tf_op jit(solution)/shard_map/ppermute | solution.py:231
  8.6 1.6 %collective-permute-start.8 = (bf16[272,768]{1,0:T(8,128)(2,1)}, bf16[272,768]{1,0:T(8,128)(2,1)S(1)}, u32[]{:S(2)}, u32[]{:S(2)}) collective-permute-start(bf16[272,768]{1,0:T(8,128)(2,1)} %get-tuple-element.18.refs_1_), channel_id=1, source_target_pairs={{0,2},{1,3},{2,0},{3,1},{4,6},{5,7},{6,4},{7,5},{8,10},{9,11},{10,... | collective-permute-start | bytes 1253384 | tf_op jit(solution)/shard_map/ppermute | solution.py:234
  10.2 0.8 %collective-permute-start = (bf16[272,768]{1,0:T(8,128)(2,1)}, bf16[272,768]{1,0:T(8,128)(2,1)S(1)}, u32[]{:S(2)}, u32[]{:S(2)}) collective-permute-start(bf16[272,768]{1,0:T(8,128)(2,1)} %get-tuple-element.17), channel_id=1, source_target_pairs={{0,8},{1,9},{2,10},{3,11},{4,12},{5,13},{6,14},{7,15},{8,0},{9,1},... | collective-permute-start | bytes 1253384 | tf_op jit(solution)/shard_map/ppermute | solution.py:231
  11.0 0.0 collective-permute-start.4
  11.0 8.2 %collective-permute-done.2.refs_2_ = bf16[272,768]{1,0:T(8,128)(2,1)S(1)} collective-permute-done((bf16[272,768]{1,0:T(8,128)(2,1)}, bf16[272,768]{1,0:T(8,128)(2,1)S(1)}, u32[]{:S(2)}, u32[]{:S(2)}) %collective-permute-start.2) | collective-permute-done | bytes 417824 | tf_op jit(solution)/shard_map/ppermute | solution.py:231
  19.3 1.7 %collective-permute-start.9 = (bf16[272,768]{1,0:T(8,128)(2,1)S(1)}, bf16[272,768]{1,0:T(8,128)(2,1)S(1)}, u32[]{:S(2)}, u32[]{:S(2)}) collective-permute-start(bf16[272,768]{1,0:T(8,128)(2,1)S(1)} %collective-permute-done.2.refs_2_), channel_id=1, source_target_pairs={{0,2},{1,3},{2,0},{3,1},{4,6},{5,7},{6,4},{7,5},{8,10},{9,11},{10,... | collective-permute-start | bytes 1253384 | tf_op jit(solution)/shard_map/ppermute | solution.py:234
  21.0 5.8 %collective-permute-done.3.refs_3_ = bf16[272,768]{1,0:T(8,128)(2,1)S(1)} collective-permute-done((bf16[272,768]{1,0:T(8,128)(2,1)}, bf16[272,768]{1,0:T(8,128)(2,1)S(1)}, u32[]{:S(2)}, u32[]{:S(2)}) %collective-permute-start.3) | collective-permute-done | bytes 417824 | tf_op jit(solution)/shard_map/ppermute | solution.py:231
  26.8 1.5 %collective-permute-start.10 = (bf16[272,768]{1,0:T(8,128)(2,1)S(1)}, bf16[272,768]{1,0:T(8,128)(2,1)S(1)}, u32[]{:S(2)}, u32[]{:S(2)}) collective-permute-start(bf16[272,768]{1,0:T(8,128)(2,1)S(1)} %collective-permute-done.3.refs_3_), channel_id=1, source_target_pairs={{0,2},{1,3},{2,0},{3,1},{4,6},{5,7},{6,4},{7,5},{8,10},{9,11},{10,... | collective-permute-start | bytes 1253384 | tf_op jit(solution)/shard_map/ppermute | solution.py:234
  28.3 0.0 collective-permute-done.8.refs_9_
  28.3 0.0 collective-permute-start.11
  28.3 17.0 %collective-permute-done.refs_4_ = bf16[272,768]{1,0:T(8,128)(2,1)S(1)} collective-permute-done((bf16[272,768]{1,0:T(8,128)(2,1)}, bf16[272,768]{1,0:T(8,128)(2,1)S(1)}, u32[]{:S(2)}, u32[]{:S(2)}) %collective-permute-start) | collective-permute-done | bytes 417824 | tf_op jit(solution)/shard_map/ppermute | solution.py:231
  45.3 0.0 collective-permute-start.5
  45.3 0.0 collective-permute-done.4.refs_5_
  45.3 0.5 collective-permute-start.6
  45.8 0.0 collective-permute-done.9.refs_10_
  45.8 0.1 collective-permute-start.7
  45.8 0.0 collective-permute-done.10.refs_11_
  45.8 0.4 collective-permute-start.12
  46.3 0.0 collective-permute-done.11.refs_12_
  46.3 0.1 collective-permute-start.13
  46.4 0.7 collective-permute-done.5.refs_6_
  47.0 1.5 %collective-permute-start.1 = (bf16[272,768]{1,0:T(8,128)(2,1)S(1)}, bf16[272,768]{1,0:T(8,128)(2,1)S(1)}, u32[]{:S(2)}, u32[]{:S(2)}) collective-permute-start(bf16[272,768]{1,0:T(8,128)(2,1)S(1)} %collective-permute-done.refs_4_), channel_id=1, source_target_pairs={{0,2},{1,3},{2,0},{3,1},{4,6},{5,7},{6,4},{7,5},{8,10},{9,11},{10,... | collective-permute-start | bytes 1253384 | tf_op jit(solution)/shard_map/ppermute | solution.py:234
  48.5 0.0 collective-permute-done.6.refs_7_
  48.5 0.0 collective-permute-done.7.refs_8_
  48.5 0.3 collective-permute-done.12.refs_13_
  48.8 0.6 collective-permute-done.13.refs_14_
  49.4 0.0 copy-start.1
  49.4 1.0 %copy-done.1 = bf16[272,768]{1,0:T(8,128)(2,1)S(1)} copy-done((bf16[272,768]{1,0:T(8,128)(2,1)S(1)}, bf16[272,768]{1,0:T(8,128)(2,1)}, u32[]{:S(2)}) %copy-start.1) | copy-done | bytes 417816
  50.4 6.1 %compare4_56.1.refs_0_ = f32[1,1024]{1,0:T(1,128)S(1)} custom-call(f32[1,1024]{1,0:T(1,128)S(1)} %broadcast_in_dim.3.refs_0_, bf16[272,768]{1,0:T(8,128)(2,1)S(1)} %copy-done.1, bf16[272,768]{1,0:T(8,128)(2,1)S(1)} %collective-permute-done.2.refs_2_, bf16[272,768]{1,0:T(8,128)(2,1)S(1)} %collective-permute-done.3.refs_3_, ...), custom_call_target="tpu_custom_call" | custom-call | flops 5637144576 | tf_op jit(solution)/shard_map/compare4_56/pallas_call | solution.py:177
  56.5 0.0 copy-start
  56.5 2.2 %collective-permute-done.1.refs_5_ = bf16[272,768]{1,0:T(8,128)(2,1)S(1)} collective-permute-done((bf16[272,768]{1,0:T(8,128)(2,1)S(1)}, bf16[272,768]{1,0:T(8,128)(2,1)S(1)}, u32[]{:S(2)}, u32[]{:S(2)}) %collective-permute-start.1) | collective-permute-done | bytes 417824 | tf_op jit(solution)/shard_map/ppermute | solution.py:234
  58.7 0.0 collective-permute-start.14
  58.7 1.8 %collective-permute-done.14.refs_6_ = bf16[272,768]{1,0:T(8,128)(2,1)S(1)} collective-permute-done((bf16[272,768]{1,0:T(8,128)(2,1)S(1)}, bf16[272,768]{1,0:T(8,128)(2,1)S(1)}, u32[]{:S(2)}, u32[]{:S(2)}) %collective-permute-start.14) | collective-permute-done | bytes 417824 | tf_op jit(solution)/shard_map/ppermute | solution.py:234
  60.5 1.0 %compare1_8.1 = (f32[1,256]{1,0:T(1,128)S(1)}, f32[1,256]{1,0:T(1,128)S(1)}, f32[1,256]{1,0:T(1,128)S(1)}, f32[1,256]{1,0:T(1,128)S(1)}) custom-call(f32[1,1024]{1,0:T(1,128)S(1)} %compare4_56.1.refs_0_, bf16[272,768]{1,0:T(8,128)(2,1)S(1)} %copy-done.1, bf16[272,768]{1,0:T(8,128)(2,1)S(1)} %collective-permute-done.2.refs_2_, ...), custom_call_target="tpu_custom_call" | custom-call | flops 805306368 | tf_op jit(solution)/shard_map/compare1_8/pallas_call | solution.py:177
  61.5 1.7 %collective-permute-start.15 = (f32[1,256]{1,0:T(1,128)S(1)}, f32[1,256]{1,0:T(1,128)S(1)}, u32[]{:S(2)}, u32[]{:S(2)}) collective-permute-start(f32[1,256]{1,0:T(1,128)S(1)} %get-tuple-element.24), channel_id=1, source_target_pairs={{0,12},{1,13},{2,14},{3,15},{4,0},{5,1},{6,2},{7,3},{8,4},{9,5},{1... | collective-permute-start | bytes 3080 | tf_op jit(solution)/shard_map/ppermute | solution.py:231
  63.2 0.8 %collective-permute-start.16 = (f32[1,256]{1,0:T(1,128)S(1)}, f32[1,256]{1,0:T(1,128)S(1)}, u32[]{:S(2)}, u32[]{:S(2)}) collective-permute-start(f32[1,256]{1,0:T(1,128)S(1)} %get-tuple-element.25), channel_id=1, source_target_pairs={{0,4},{1,5},{2,6},{3,7},{4,8},{5,9},{6,10},{7,11},{8,12},{9,13},{1... | collective-permute-start | bytes 3080 | tf_op jit(solution)/shard_map/ppermute | solution.py:231
  63.9 3.8 %collective-permute-start.17 = (f32[1,256]{1,0:T(1,128)S(1)}, f32[1,256]{1,0:T(1,128)S(1)}, u32[]{:S(2)}, u32[]{:S(2)}) collective-permute-start(f32[1,256]{1,0:T(1,128)S(1)} %get-tuple-element.26), channel_id=1, source_target_pairs={{0,8},{1,9},{2,10},{3,11},{4,12},{5,13},{6,14},{7,15},{8,0},{9,1},... | collective-permute-start | bytes 3080 | tf_op jit(solution)/shard_map/ppermute | solution.py:231
  67.7 0.0 collective-permute-done.15.refs_1_
  67.7 1.0 %collective-permute-done.16.refs_2_ = f32[1,256]{1,0:T(1,128)S(1)} collective-permute-done((f32[1,256]{1,0:T(1,128)S(1)}, f32[1,256]{1,0:T(1,128)S(1)}, u32[]{:S(2)}, u32[]{:S(2)}) %collective-permute-start.16) | collective-permute-done | bytes 1056 | tf_op jit(solution)/shard_map/ppermute | solution.py:231
  68.7 0.6 collective-permute-done.17.refs_3_
  69.3 0.0 copy-done
  69.3 1.1 %unpack.1 = f32[1,512]{1,0:T(1,128)} custom-call(s32[1,512]{1,0:T(1,128)S(1)} %copy-done, f32[1,256]{1,0:T(1,128)S(1)} %get-tuple-element.23.refs_0_, f32[1,256]{1,0:T(1,128)S(1)} %collective-permute-done.15.refs_1_, f32[1,256]{1,0:T(1,128)S(1)} %collective-permute-done.16.refs_2_, f32[1,256]{1,0:T(1,128)S(1)} %collective-permute-done.17.refs_3_), custom_call_target="tpu_custom_call" | custom-call | tf_op jit(solution)/shard_map/unpack/pallas_call | solution.py:207
  (1 shorter events, 0.0 us)
Async XLA Ops:
  3.4 15.8 %collective-permute-start.2 = (bf16[272,768]{1,0:T(8,128)(2,1)}, bf16[272,768]{1,0:T(8,128)(2,1)S(1)}, u32[]{:S(2)}, u32[]{:S(2)}) collective-permute-start(bf16[272,768]{1,0:T(8,128)(2,1)} %get-tuple-element.19), channel_id=1, source_target_pairs={{0,4},{1,5},{2,6},{3,7},{4,8},{5,9},{6,10},{7,11},{8,12},{9,13},{1... | collective-permute-start | bytes 1253384 | tf_op jit(solution)/shard_map/ppermute | solution.py:231
  6.5 20.3 %collective-permute-start.3 = (bf16[272,768]{1,0:T(8,128)(2,1)}, bf16[272,768]{1,0:T(8,128)(2,1)S(1)}, u32[]{:S(2)}, u32[]{:S(2)}) collective-permute-start(bf16[272,768]{1,0:T(8,128)(2,1)} %get-tuple-element.20), channel_id=1, source_target_pairs={{0,12},{1,13},{2,14},{3,15},{4,0},{5,1},{6,2},{7,3},{8,4},{9,5},{1... | collective-permute-start | bytes 1253384 | tf_op jit(solution)/shard_map/ppermute | solution.py:231
  8.6 19.7 %collective-permute-start.8 = (bf16[272,768]{1,0:T(8,128)(2,1)}, bf16[272,768]{1,0:T(8,128)(2,1)S(1)}, u32[]{:S(2)}, u32[]{:S(2)}) collective-permute-start(bf16[272,768]{1,0:T(8,128)(2,1)} %get-tuple-element.18.refs_1_), channel_id=1, source_target_pairs={{0,2},{1,3},{2,0},{3,1},{4,6},{5,7},{6,4},{7,5},{8,10},{9,11},{10,... | collective-permute-start | bytes 1253384 | tf_op jit(solution)/shard_map/ppermute | solution.py:234
  10.2 35.0 %collective-permute-start = (bf16[272,768]{1,0:T(8,128)(2,1)}, bf16[272,768]{1,0:T(8,128)(2,1)S(1)}, u32[]{:S(2)}, u32[]{:S(2)}) collective-permute-start(bf16[272,768]{1,0:T(8,128)(2,1)} %get-tuple-element.17), channel_id=1, source_target_pairs={{0,8},{1,9},{2,10},{3,11},{4,12},{5,13},{6,14},{7,15},{8,0},{9,1},... | collective-permute-start | bytes 1253384 | tf_op jit(solution)/shard_map/ppermute | solution.py:231
  11.0 34.2 %collective-permute-start.4 = (bf16[272,768]{1,0:T(8,128)(2,1)}, bf16[272,768]{1,0:T(8,128)(2,1)S(1)}, u32[]{:S(2)}, u32[]{:S(2)}) collective-permute-start(bf16[272,768]{1,0:T(8,128)(2,1)} %get-tuple-element.18.refs_1_), channel_id=1, source_target_pairs={{0,1},{1,0},{2,3},{3,2},{4,5},{5,4},{6,7},{7,6},{8,9},{9,8},{10,11... | collective-permute-start | bytes 1253384 | tf_op jit(solution)/shard_map/ppermute | solution.py:234
  19.3 26.5 %collective-permute-start.9 = (bf16[272,768]{1,0:T(8,128)(2,1)S(1)}, bf16[272,768]{1,0:T(8,128)(2,1)S(1)}, u32[]{:S(2)}, u32[]{:S(2)}) collective-permute-start(bf16[272,768]{1,0:T(8,128)(2,1)S(1)} %collective-permute-done.2.refs_2_), channel_id=1, source_target_pairs={{0,2},{1,3},{2,0},{3,1},{4,6},{5,7},{6,4},{7,5},{8,10},{9,11},{10,... | collective-permute-start | bytes 1253384 | tf_op jit(solution)/shard_map/ppermute | solution.py:234
  26.8 19.1 %collective-permute-start.10 = (bf16[272,768]{1,0:T(8,128)(2,1)S(1)}, bf16[272,768]{1,0:T(8,128)(2,1)S(1)}, u32[]{:S(2)}, u32[]{:S(2)}) collective-permute-start(bf16[272,768]{1,0:T(8,128)(2,1)S(1)} %collective-permute-done.3.refs_3_), channel_id=1, source_target_pairs={{0,2},{1,3},{2,0},{3,1},{4,6},{5,7},{6,4},{7,5},{8,10},{9,11},{10,... | collective-permute-start | bytes 1253384 | tf_op jit(solution)/shard_map/ppermute | solution.py:234
  28.3 18.0 %collective-permute-start.11 = (bf16[272,768]{1,0:T(8,128)(2,1)S(1)}, bf16[272,768]{1,0:T(8,128)(2,1)S(1)}, u32[]{:S(2)}, u32[]{:S(2)}) collective-permute-start(bf16[272,768]{1,0:T(8,128)(2,1)S(1)} %collective-permute-done.8.refs_9_), channel_id=1, source_target_pairs={{0,1},{1,0},{2,3},{3,2},{4,5},{5,4},{6,7},{7,6},{8,9},{9,8},{10,11... | collective-permute-start | bytes 1253384 | tf_op jit(solution)/shard_map/ppermute | solution.py:234
  45.3 1.8 %collective-permute-start.5 = (bf16[272,768]{1,0:T(8,128)(2,1)S(1)}, bf16[272,768]{1,0:T(8,128)(2,1)S(1)}, u32[]{:S(2)}, u32[]{:S(2)}) collective-permute-start(bf16[272,768]{1,0:T(8,128)(2,1)S(1)} %collective-permute-done.2.refs_2_), channel_id=1, source_target_pairs={{0,1},{1,0},{2,3},{3,2},{4,5},{5,4},{6,7},{7,6},{8,9},{9,8},{10,11... | collective-permute-start | bytes 1253384 | tf_op jit(solution)/shard_map/ppermute | solution.py:234
  45.3 3.2 %collective-permute-start.6 = (bf16[272,768]{1,0:T(8,128)(2,1)S(1)}, bf16[272,768]{1,0:T(8,128)(2,1)S(1)}, u32[]{:S(2)}, u32[]{:S(2)}) collective-permute-start(bf16[272,768]{1,0:T(8,128)(2,1)S(1)} %collective-permute-done.3.refs_3_), channel_id=1, source_target_pairs={{0,1},{1,0},{2,3},{3,2},{4,5},{5,4},{6,7},{7,6},{8,9},{9,8},{10,11... | collective-permute-start | bytes 1253384 | tf_op jit(solution)/shard_map/ppermute | solution.py:234
  45.8 2.7 %collective-permute-start.7 = (bf16[272,768]{1,0:T(8,128)(2,1)S(1)}, bf16[272,768]{1,0:T(8,128)(2,1)S(1)}, u32[]{:S(2)}, u32[]{:S(2)}) collective-permute-start(bf16[272,768]{1,0:T(8,128)(2,1)S(1)} %collective-permute-done.refs_4_), channel_id=1, source_target_pairs={{0,1},{1,0},{2,3},{3,2},{4,5},{5,4},{6,7},{7,6},{8,9},{9,8},{10,11... | collective-permute-start | bytes 1253384 | tf_op jit(solution)/shard_map/ppermute | solution.py:234
  45.8 3.0 %collective-permute-start.12 = (bf16[272,768]{1,0:T(8,128)(2,1)S(1)}, bf16[272,768]{1,0:T(8,128)(2,1)S(1)}, u32[]{:S(2)}, u32[]{:S(2)}) collective-permute-start(bf16[272,768]{1,0:T(8,128)(2,1)S(1)} %collective-permute-done.9.refs_10_), channel_id=1, source_target_pairs={{0,1},{1,0},{2,3},{3,2},{4,5},{5,4},{6,7},{7,6},{8,9},{9,8},{10,11... | collective-permute-start | bytes 1253384 | tf_op jit(solution)/shard_map/ppermute | solution.py:234
  46.3 3.1 %collective-permute-start.13 = (bf16[272,768]{1,0:T(8,128)(2,1)S(1)}, bf16[272,768]{1,0:T(8,128)(2,1)S(1)}, u32[]{:S(2)}, u32[]{:S(2)}) collective-permute-start(bf16[272,768]{1,0:T(8,128)(2,1)S(1)} %collective-permute-done.10.refs_11_), channel_id=1, source_target_pairs={{0,1},{1,0},{2,3},{3,2},{4,5},{5,4},{6,7},{7,6},{8,9},{9,8},{10,11... | collective-permute-start | bytes 1253384 | tf_op jit(solution)/shard_map/ppermute | solution.py:234
  47.0 11.7 %collective-permute-start.1 = (bf16[272,768]{1,0:T(8,128)(2,1)S(1)}, bf16[272,768]{1,0:T(8,128)(2,1)S(1)}, u32[]{:S(2)}, u32[]{:S(2)}) collective-permute-start(bf16[272,768]{1,0:T(8,128)(2,1)S(1)} %collective-permute-done.refs_4_), channel_id=1, source_target_pairs={{0,2},{1,3},{2,0},{3,1},{4,6},{5,7},{6,4},{7,5},{8,10},{9,11},{10,... | collective-permute-start | bytes 1253384 | tf_op jit(solution)/shard_map/ppermute | solution.py:234
  49.4 1.0 %copy-start.1 = (bf16[272,768]{1,0:T(8,128)(2,1)S(1)}, bf16[272,768]{1,0:T(8,128)(2,1)}, u32[]{:S(2)}) copy-start(bf16[272,768]{1,0:T(8,128)(2,1)} %get-tuple-element.18.refs_1_) | copy-start | bytes 1253380
  56.5 12.7 %copy-start = (s32[1,512]{1,0:T(1,128)S(1)}, s32[1,512]{1,0:T(1,128)}, u32[]{:S(2)}) copy-start(s32[1,512]{1,0:T(1,128)} %get-tuple-element.16.slot_ref) | copy-start | bytes 6148
  58.7 1.8 %collective-permute-start.14 = (bf16[272,768]{1,0:T(8,128)(2,1)S(1)}, bf16[272,768]{1,0:T(8,128)(2,1)S(1)}, u32[]{:S(2)}, u32[]{:S(2)}) collective-permute-start(bf16[272,768]{1,0:T(8,128)(2,1)S(1)} %collective-permute-done.1.refs_5_), channel_id=1, source_target_pairs={{0,1},{1,0},{2,3},{3,2},{4,5},{5,4},{6,7},{7,6},{8,9},{9,8},{10,11... | collective-permute-start | bytes 1253384 | tf_op jit(solution)/shard_map/ppermute | solution.py:234
  61.5 6.2 %collective-permute-start.15 = (f32[1,256]{1,0:T(1,128)S(1)}, f32[1,256]{1,0:T(1,128)S(1)}, u32[]{:S(2)}, u32[]{:S(2)}) collective-permute-start(f32[1,256]{1,0:T(1,128)S(1)} %get-tuple-element.24), channel_id=1, source_target_pairs={{0,12},{1,13},{2,14},{3,15},{4,0},{5,1},{6,2},{7,3},{8,4},{9,5},{1... | collective-permute-start | bytes 3080 | tf_op jit(solution)/shard_map/ppermute | solution.py:231
  63.2 5.5 %collective-permute-start.16 = (f32[1,256]{1,0:T(1,128)S(1)}, f32[1,256]{1,0:T(1,128)S(1)}, u32[]{:S(2)}, u32[]{:S(2)}) collective-permute-start(f32[1,256]{1,0:T(1,128)S(1)} %get-tuple-element.25), channel_id=1, source_target_pairs={{0,4},{1,5},{2,6},{3,7},{4,8},{5,9},{6,10},{7,11},{8,12},{9,13},{1... | collective-permute-start | bytes 3080 | tf_op jit(solution)/shard_map/ppermute | solution.py:231
  63.9 5.3 %collective-permute-start.17 = (f32[1,256]{1,0:T(1,128)S(1)}, f32[1,256]{1,0:T(1,128)S(1)}, u32[]{:S(2)}, u32[]{:S(2)}) collective-permute-start(f32[1,256]{1,0:T(1,128)S(1)} %get-tuple-element.26), channel_id=1, source_target_pairs={{0,8},{1,9},{2,10},{3,11},{4,12},{5,13},{6,14},{7,15},{8,0},{9,1},... | collective-permute-start | bytes 3080 | tf_op jit(solution)/shard_map/ppermute | solution.py:231

commit v6 on v5

--- a/solution.py
+++ b/solution.py
@@ -49,7 +49,7 @@
     count = jnp.dot(member.astype(jnp.bfloat16), earlier, preferred_element_type=jnp.float32)
     rank = jnp.sum(jnp.where(member, count, 0.0), axis=0, keepdims=True)
     slot = place * cap + rank.astype(jnp.int32)
-    slot_ref[...] = slot
+    slot_ref[...] = (owner_ref[...] >> 2) * cap + rank.astype(jnp.int32)
     copies[1].wait()
     label = ((cluster_ref[...] & 15) + 1).astype(jnp.float32).astype(jnp.bfloat16)
     label = jnp.broadcast_to(label, (PAD, rows))
@@ -101,7 +101,7 @@
     for name, ref in zip(names, refs):
         given.setdefault(name, []).append(ref)
     refs = refs[len(names) :]
-    outputs, scratch = refs[: len(outs)], list(refs[len(outs) :])
+    outputs, scratch = refs[: max(len(outs), 1)], list(refs[max(len(outs), 1) :])
     query_ref = scratch.pop()
     size = query_ref.shape[0] // BLOCKS
 
@@ -157,7 +157,15 @@
             for q in range(left, right):
                 part = best[:, (q - left) * size : (q - left + 1) * size]
                 bests[q] = jnp.maximum(bests[q], part)
-    for q in range(BLOCKS):
+    if not outs:
+        whole = jnp.concatenate(bests, axis=1)
+        groups = whole.shape[1] // cap
+        mine = lax.axis_index("blk") // GROUP
+        for k in range(groups):
+            step = (k + 1) // 2 if k % 2 else groups - k // 2
+            source = (mine - step + groups) & (groups - 1)
+            outputs[0][pl.ds(source, 1), :] = whole[:, k * cap : (k + 1) * cap]
+    for q in range(BLOCKS if outs else 0):
         spread(outputs, outs, q * size, bests[q])
 
 
@@ -176,7 +184,10 @@
     names = tuple(key for key, parts in blocks.items() for _ in parts)
     return pl.pallas_call(
         lambda *refs: compare_kernel(cap, outs, jobs, names, *refs),
-        out_shape=[jax.ShapeDtypeStruct((1, n), jnp.float32) for _, n in outs],
+        out_shape=[
+            jax.ShapeDtypeStruct(shape, jnp.float32)
+            for shape in [(1, n) for _, n in outs] or [(slots // cap, cap)]
+        ],
         scratch_shapes=[pltpu.VMEM((size, width), jnp.bfloat16)] * len(folded)
         + [pltpu.VMEM((slots, width), jnp.bfloat16)],
         compiler_params=pltpu.CompilerParams(vmem_limit_bytes=GRANT),
@@ -187,29 +198,26 @@
     )(best, *[part for parts in blocks.values() for part in parts])
 
 
-def unpack_kernel(slot_ref, *refs):
-    out_ref = refs[-1]
+def unpack_kernel(slot_ref, back_ref, out_ref):
     slot = slot_ref[...]
     rows = slot.shape[1]
+    count, size = back_ref.shape
+    table = jnp.concatenate([back_ref[...]] * max(8 // count, 1), axis=0).T
     total = jnp.zeros((8, rows), jnp.float32)
-    start = 0
-    for ref in refs[:-1]:
-        size = ref.shape[1]
-        column = jnp.broadcast_to(ref[...], (8, size)).T[:, 0:1]
-        hit = iota((size, rows), 0) + start == slot
-        part = jnp.where(hit, column, 0.0)
+    for i in range(count):
+        hit = iota((size, rows), 0) + i * size == slot
+        part = jnp.where(hit, table[:, i : i + 1], 0.0)
         total = total + jnp.sum(part.reshape(size // 8, 8, rows), axis=0)
-        start += size
     out_ref[...] = jnp.sum(total, axis=0, keepdims=True)
 
 
-def unpack(slot, backs):
+def unpack(slot, back):
     return pl.pallas_call(
         unpack_kernel,
         out_shape=jax.ShapeDtypeStruct(slot.shape, jnp.float32),
         compiler_params=pltpu.CompilerParams(vmem_limit_bytes=GRANT),
         name="unpack",
-    )(slot, *backs)
+    )(slot, back)
 
 
 def join(parts, axis):
@@ -223,7 +231,6 @@
     cap = GROUP * max(2, 2 * rows // devices)
     slots = groups * cap
     units = spans([slots // 16 * n for n in UNITS])
-    pieces = spans([max(cap, 128)] * (slots // max(cap, 128)))
     shifts = [0] + [(k + 1) // 2 if k % 2 else groups - k // 2 for k in range(1, groups)]
 
     def shift(array, distance):
@@ -232,14 +239,6 @@
 
     def swap(array, mask):
         return lax.ppermute(array, "blk", [(i, i ^ mask) for i in range(devices)])
-
-    def exchange(array, start, axis, sign):
-        size, out = array.shape[axis], []
-        for k in range(start // cap, (start + size - 1) // cap + 1):
-            a, b = max(k * cap - start, 0), min((k + 1) * cap - start, size)
-            part = lax.slice_in_dim(array, a, b, axis=axis)
-            out.append(shift(part, sign * shifts[k]) if shifts[k] else part)
-        return join(out, axis)
 
     *blocks, slot = pack(groups, cap, units, embedding, row_owner, cluster_id)
 
@@ -263,7 +262,9 @@
 
     arrays = [[None] * BLOCKS for _ in range(4)]
     own, across, beside, beyond = arrays
-    sent = [blocks[0]] + [send(u) for u in range(1, len(units))]
+    sent = [blocks[0], send(1)]
+    blocks[2], blocks[3], sent[1] = tie(blocks[2], blocks[3], sent[1])
+    sent += [send(2), send(3)]
     own[:] = [sent[0]], [sent[1]], [sent[2]], sent[3:]
     for u in range(BLOCKS):
         beside[u], across[u] = core(own[u]), cross(own[u])
@@ -275,15 +276,21 @@
 
     every, row = (0, 1, 2, 3), [(0, slots)]
     best = jnp.full((1, slots), -1.0, jnp.float32)
-    jobs = [(0, 4, 0, every), (0, 4, 1, every), (0, 4, 2, every), (0, 4, 3, (0, 2))]
-    some = given((0, 2), range(4)) | given((1, 3), range(3))
+    jobs = [(0, 4, 0, every), (0, 4, 1, every), (0, 4, 2, (0, 2)), (0, 4, 3, (0, 2))]
+    some = given((0, 2), range(4)) | given((1, 3), range(2))
     (best,) = compare(cap, row, jobs, some, best)
     across[3][-1], best = tie(across[3][-1], best)
     beyond[3] = core(across[3])
+    some = given((0,), range(4)) | given((1, 3), (2,))
+    (best,) = compare(cap, row, [(0, 4, 2, (1, 3))], some, best)
     some = given((0,), range(4)) | given((1, 3), (3,))
-    best = compare(cap, pieces, [(0, 4, 3, (1, 3))], some, best)
-    backs = [exchange(b, low, 1, -1) for b, (low, _) in zip(best, pieces)]
-    return unpack(slot, backs).reshape(rows)
+    (best,) = compare(cap, [], [(0, 4, 3, (1, 3))], some, best)
+    rings = [[g * GROUP + p for g in range(groups)] for p in range(GROUP)]
+    back = lax.all_to_all(
+        best, "blk", split_axis=0, concat_axis=0, tiled=True, axis_index_groups=rings
+    )
+    wide = max(cap, 128)
+    return unpack(slot, back.reshape(slots // wide, wide)).reshape(rows)
 
 
 def solution(mesh):

time: 70.5 us -> 73.4 us (1.041)
  blocking collectives: 0 us -> 11 us
  starting transfers between devices: 19.6 us -> 11.5 us
    all_to_all x0 -> x1, blocking collectives: none -> 11 us  [on_device(): lax.all_to_all(best, 'blk', split_axis=0, concat_axis=0, tiled=True, axis...]
    ppermute x6 -> x3, starting transfers between devices: 12.2 us -> 4.82 us  [shift(): lax.ppermute(array, 'blk', [(i, (i + step) % devices) for i in range(devi...]
    ppermute x12, waiting for transfers between devices: 5.49 us -> 4.59 us  [swap(): return lax.ppermute(array, 'blk', [(i, i ^ mask) for i in range(devices)])]
    ppermute x12, starting transfers between devices: 7.44 us -> 6.67 us  [swap(): return lax.ppermute(array, 'blk', [(i, i ^ mask) for i in range(devices)])]
    ppermute x6 -> x3, waiting for transfers between devices: 32.5 us -> 33.2 us  [shift(): lax.ppermute(array, 'blk', [(i, (i + step) % devices) for i in range(devi...]
    pallas_call x2 -> x3, Pallas kernels: 7.13 us -> 7.32 us  [compare(): pl.pallas_call(lambda *refs: compare_kernel(cap, outs, jobs, names, *refs...]
  transfers between devices with their start and end apart: 18 -> 15, of which waited for: 10 -> 6; matrix products, arithmetic and copies ran while one was open for 0% -> 0% of each run, Pallas kernels for 9% -> 9%
where the time goes in v6:
time: 73.4 us; the launch traced here: 73.2 us
  waiting for transfers between devices  37.8 us (51%)
  Pallas kernels  11.8 us (16%)
  starting transfers between devices  11.5 us (16%)
  blocking collectives  11 us (15%)
  local copies, waits for them, and re-layouts  1.02 us (1%)
    ppermute x3, waiting for transfers between devices, shift(): lax.ppermute(array, 'blk', [(i, (i + step) % devices) for i in range(devi...  33.2 us
    all_to_all x1, blocking collectives, on_device(): lax.all_to_all(best, 'blk', split_axis=0, concat_axis=0, tiled=True, axis...  11 us
    pallas_call x3, Pallas kernels, compare(): pl.pallas_call(lambda *refs: compare_kernel(cap, outs, jobs, names, *refs...  7.32 us
    ppermute x12, starting transfers between devices, swap(): return lax.ppermute(array, 'blk', [(i, i ^ mask) for i in range(devices)])  6.67 us
    ppermute x3, starting transfers between devices, shift(): lax.ppermute(array, 'blk', [(i, (i + step) % devices) for i in range(devi...  4.82 us
    ppermute x12, waiting for transfers between devices, swap(): return lax.ppermute(array, 'blk', [(i, i ^ mask) for i in range(devices)])  4.59 us
    pallas_call x1, Pallas kernels, pack(): pl.pallas_call(lambda *refs: pack_kernel(groups, cap, units, *refs), in_s...  3.42 us
  transfers between devices with their start and end apart: 15, of which 6 were waited for; matrix products, arithmetic and copies ran while one was open for 0% of the time, Pallas kernels for 9%

profile of v6, /device:TPU:0, one launch (start us, length us, event | category | flops | bytes accessed | tf_op | source)
XLA Modules:
  0.0 73.2 jit_solution(6072151931258889046)
XLA Ops:
  0.0 3.4 %pack.1 = (bf16[272,768]{1,0:T(8,128)(2,1)}, bf16[272,768]{1,0:T(8,128)(2,1)}, bf16[272,768]{1,0:T(8,128)(2,1)}, bf16[272,768]{1,0:T(8,128)(2,1)}, s32[1,512]{1,0:T(1,128)}) custom-call(f32[512,768]{1,0:T(8,128)} %refs_0_.1, s32[1,512]{1,0:T(1,128)} %bitcast.9, s32[1,512]{1,0:T(1,128)} %bitcast.10), custom_call_target="tpu_custom_call" | custom-call | tf_op jit(solution)/shard_map/pack/pallas_call | solution.py:79
  3.4 3.1 %collective-permute-start = (bf16[272,768]{1,0:T(8,128)(2,1)}, bf16[272,768]{1,0:T(8,128)(2,1)S(1)}, u32[]{:S(2)}, u32[]{:S(2)}) collective-permute-start(bf16[272,768]{1,0:T(8,128)(2,1)} %get-tuple-element.18), channel_id=1, source_target_pairs={{0,4},{1,5},{2,6},{3,7},{4,8},{5,9},{6,10},{7,11},{8,12},{9,13},{1... | collective-permute-start | bytes 1253384 | tf_op jit(solution)/shard_map/ppermute | solution.py:238
  6.5 1.5 %collective-permute-start.8 = (bf16[272,768]{1,0:T(8,128)(2,1)}, bf16[272,768]{1,0:T(8,128)(2,1)S(1)}, u32[]{:S(2)}, u32[]{:S(2)}) collective-permute-start(bf16[272,768]{1,0:T(8,128)(2,1)} %get-tuple-element.20.refs_1_), channel_id=1, source_target_pairs={{0,2},{1,3},{2,0},{3,1},{4,6},{5,7},{6,4},{7,5},{8,10},{9,11},{10,... | collective-permute-start | bytes 1253384 | tf_op jit(solution)/shard_map/ppermute | solution.py:241
  8.0 0.0 collective-permute-start.4
  8.0 10.4 %collective-permute-done.refs_2_ = bf16[272,768]{1,0:T(8,128)(2,1)S(1)} collective-permute-done((bf16[272,768]{1,0:T(8,128)(2,1)}, bf16[272,768]{1,0:T(8,128)(2,1)S(1)}, u32[]{:S(2)}, u32[]{:S(2)}) %collective-permute-start) | collective-permute-done | bytes 417824 | tf_op jit(solution)/shard_map/ppermute | solution.py:238
  18.4 1.7 %collective-permute-start.3 = (bf16[272,768]{1,0:T(8,128)(2,1)}, bf16[272,768]{1,0:T(8,128)(2,1)S(1)}, u32[]{:S(2)}, u32[]{:S(2)}) collective-permute-start(bf16[272,768]{1,0:T(8,128)(2,1)} %get-tuple-element.22), channel_id=1, source_target_pairs={{0,12},{1,13},{2,14},{3,15},{4,0},{5,1},{6,2},{7,3},{8,4},{9,5},{1... | collective-permute-start | bytes 1253384 | tf_op jit(solution)/shard_map/ppermute | solution.py:238
  20.1 1.5 %collective-permute-start.9 = (bf16[272,768]{1,0:T(8,128)(2,1)S(1)}, bf16[272,768]{1,0:T(8,128)(2,1)S(1)}, u32[]{:S(2)}, u32[]{:S(2)}) collective-permute-start(bf16[272,768]{1,0:T(8,128)(2,1)S(1)} %collective-permute-done.refs_2_), channel_id=1, source_target_pairs={{0,2},{1,3},{2,0},{3,1},{4,6},{5,7},{6,4},{7,5},{8,10},{9,11},{10,... | collective-permute-start | bytes 1253384 | tf_op jit(solution)/shard_map/ppermute | solution.py:241
  21.6 0.0 collective-permute-start.1
  21.6 0.0 collective-permute-done.8.refs_9_
  21.6 0.0 collective-permute-start.5
  21.6 0.0 collective-permute-done.4.refs_5_
  21.6 0.5 collective-permute-start.10
  22.1 8.7 %collective-permute-done.3.refs_3_ = bf16[272,768]{1,0:T(8,128)(2,1)S(1)} collective-permute-done((bf16[272,768]{1,0:T(8,128)(2,1)}, bf16[272,768]{1,0:T(8,128)(2,1)S(1)}, u32[]{:S(2)}, u32[]{:S(2)}) %collective-permute-start.3) | collective-permute-done | bytes 417824 | tf_op jit(solution)/shard_map/ppermute | solution.py:238
  30.8 0.0 collective-permute-start.6
  30.8 0.0 collective-permute-done.9.refs_10_
  30.8 1.2 %collective-permute-start.12 = (bf16[272,768]{1,0:T(8,128)(2,1)S(1)}, bf16[272,768]{1,0:T(8,128)(2,1)S(1)}, u32[]{:S(2)}, u32[]{:S(2)}) collective-permute-start(bf16[272,768]{1,0:T(8,128)(2,1)S(1)} %collective-permute-done.3.refs_3_), channel_id=1, source_target_pairs={{0,2},{1,3},{2,0},{3,1},{4,6},{5,7},{6,4},{7,5},{8,10},{9,11},{10,... | collective-permute-start | bytes 1253384 | tf_op jit(solution)/shard_map/ppermute | solution.py:241
  32.0 14.1 %collective-permute-done.1.refs_4_ = bf16[272,768]{1,0:T(8,128)(2,1)S(1)} collective-permute-done((bf16[272,768]{1,0:T(8,128)(2,1)}, bf16[272,768]{1,0:T(8,128)(2,1)S(1)}, u32[]{:S(2)}, u32[]{:S(2)}) %collective-permute-start.1) | collective-permute-done | bytes 417824 | tf_op jit(solution)/shard_map/ppermute | solution.py:238
  46.2 0.0 collective-permute-start.11
  46.2 0.0 collective-permute-done.5.refs_6_
  46.2 0.5 collective-permute-start.7
  46.7 0.0 collective-permute-done.10.refs_11_
  46.7 1.5 %collective-permute-start.2 = (bf16[272,768]{1,0:T(8,128)(2,1)S(1)}, bf16[272,768]{1,0:T(8,128)(2,1)S(1)}, u32[]{:S(2)}, u32[]{:S(2)}) collective-permute-start(bf16[272,768]{1,0:T(8,128)(2,1)S(1)} %collective-permute-done.1.refs_4_), channel_id=1, source_target_pairs={{0,2},{1,3},{2,0},{3,1},{4,6},{5,7},{6,4},{7,5},{8,10},{9,11},{10,... | collective-permute-start | bytes 1253384 | tf_op jit(solution)/shard_map/ppermute | solution.py:241
  48.2 0.0 collective-permute-done.12.refs_5_
  48.2 0.0 collective-permute-start.13
  48.2 0.0 collective-permute-done.11.refs_12_
  48.2 0.0 collective-permute-done.6.refs_7_
  48.2 0.3 collective-permute-done.7.refs_8_
  48.5 0.0 copy-start.1
  48.5 1.0 %copy-done.1 = bf16[272,768]{1,0:T(8,128)(2,1)S(1)} copy-done((bf16[272,768]{1,0:T(8,128)(2,1)S(1)}, bf16[272,768]{1,0:T(8,128)(2,1)}, u32[]{:S(2)}) %copy-start.1) | copy-done | bytes 417816
  49.5 5.2 %compare4_48.1.refs_0_ = f32[1,1024]{1,0:T(1,128)S(1)} custom-call(f32[1,1024]{1,0:T(1,128)S(1)} %broadcast_in_dim.3.refs_0_, bf16[272,768]{1,0:T(8,128)(2,1)S(1)} %copy-done.1, bf16[272,768]{1,0:T(8,128)(2,1)S(1)} %collective-permute-done.refs_2_, bf16[272,768]{1,0:T(8,128)(2,1)S(1)} %collective-permute-done.3.refs_3_, ...), custom_call_target="tpu_custom_call" | custom-call | flops 4831838208 | tf_op jit(solution)/shard_map/compare4_48/pallas_call | solution.py:185
  54.8 3.5 %collective-permute-done.2.refs_5_ = bf16[272,768]{1,0:T(8,128)(2,1)S(1)} collective-permute-done((bf16[272,768]{1,0:T(8,128)(2,1)S(1)}, bf16[272,768]{1,0:T(8,128)(2,1)S(1)}, u32[]{:S(2)}, u32[]{:S(2)}) %collective-permute-start.2) | collective-permute-done | bytes 417824 | tf_op jit(solution)/shard_map/ppermute | solution.py:241
  58.3 0.0 collective-permute-start.14
  58.3 0.0 collective-permute-done.13.refs_6_
  58.3 1.0 %compare1_8.2.refs_0_ = f32[1,1024]{1,0:T(1,128)S(1)} custom-call(f32[1,1024]{1,0:T(1,128)S(1)} %compare4_48.1.refs_0_, bf16[272,768]{1,0:T(8,128)(2,1)S(1)} %copy-done.1, bf16[272,768]{1,0:T(8,128)(2,1)S(1)} %collective-permute-done.refs_2_, bf16[272,768]{1,0:T(8,128)(2,1)S(1)} %collective-permute-done.3.refs_3_, ...), custom_call_target="tpu_custom_call" | custom-call | flops 805306368 | tf_op jit(solution)/shard_map/compare1_8/pallas_call | solution.py:185
  59.4 0.0 copy-start
  59.4 0.7 collective-permute-done.14.refs_6_
  60.1 1.0 %compare1_8.3 = f32[4,256]{1,0:T(4,128)S(1)} custom-call(f32[1,1024]{1,0:T(1,128)S(1)} %compare1_8.2.refs_0_, bf16[272,768]{1,0:T(8,128)(2,1)S(1)} %copy-done.1, bf16[272,768]{1,0:T(8,128)(2,1)S(1)} %collective-permute-done.refs_2_, bf16[272,768]{1,0:T(8,128)(2,1)S(1)} %collective-permute-done.3.refs_3_, ...), custom_call_target="tpu_custom_call" | custom-call | flops 805306368 | tf_op jit(solution)/shard_map/compare1_8/pallas_call | solution.py:185
  61.1 11.0 %all_to_all.11 = f32[4,1,256]{2,1,0:T(1,128)S(1)} all-to-all(f32[4,1,256]{2,1,0:T(1,128)S(1)} %copy.4), channel_id=1, replica_groups={{0,4,8,12},{1,5,9,13},{2,6,10,14},{3,7,11,15},{16,20,24,28},{17,21,25,2..., dimensions={0} | all-to-all | bytes 8192 | tf_op jit(solution)/shard_map/all_to_all | solution.py:289
  72.2 0.0 copy-done
  72.2 1.1 %unpack.1 = f32[1,512]{1,0:T(1,128)} custom-call(s32[1,512]{1,0:T(1,128)S(1)} %copy-done, f32[4,256]{1,0:T(4,128)S(1)} %bitcast.7), custom_call_target="tpu_custom_call" | custom-call | tf_op jit(solution)/shard_map/unpack/pallas_call | solution.py:215
  (3 shorter events, 0.0 us)
Async XLA Ops:
  3.4 15.0 %collective-permute-start = (bf16[272,768]{1,0:T(8,128)(2,1)}, bf16[272,768]{1,0:T(8,128)(2,1)S(1)}, u32[]{:S(2)}, u32[]{:S(2)}) collective-permute-start(bf16[272,768]{1,0:T(8,128)(2,1)} %get-tuple-element.18), channel_id=1, source_target_pairs={{0,4},{1,5},{2,6},{3,7},{4,8},{5,9},{6,10},{7,11},{8,12},{9,13},{1... | collective-permute-start | bytes 1253384 | tf_op jit(solution)/shard_map/ppermute | solution.py:238
  6.5 15.1 %collective-permute-start.8 = (bf16[272,768]{1,0:T(8,128)(2,1)}, bf16[272,768]{1,0:T(8,128)(2,1)S(1)}, u32[]{:S(2)}, u32[]{:S(2)}) collective-permute-start(bf16[272,768]{1,0:T(8,128)(2,1)} %get-tuple-element.20.refs_1_), channel_id=1, source_target_pairs={{0,2},{1,3},{2,0},{3,1},{4,6},{5,7},{6,4},{7,5},{8,10},{9,11},{10,... | collective-permute-start | bytes 1253384 | tf_op jit(solution)/shard_map/ppermute | solution.py:241
  8.0 13.6 %collective-permute-start.4 = (bf16[272,768]{1,0:T(8,128)(2,1)}, bf16[272,768]{1,0:T(8,128)(2,1)S(1)}, u32[]{:S(2)}, u32[]{:S(2)}) collective-permute-start(bf16[272,768]{1,0:T(8,128)(2,1)} %get-tuple-element.20.refs_1_), channel_id=1, source_target_pairs={{0,1},{1,0},{2,3},{3,2},{4,5},{5,4},{6,7},{7,6},{8,9},{9,8},{10,11... | collective-permute-start | bytes 1253384 | tf_op jit(solution)/shard_map/ppermute | solution.py:241
  18.4 12.4 %collective-permute-start.3 = (bf16[272,768]{1,0:T(8,128)(2,1)}, bf16[272,768]{1,0:T(8,128)(2,1)S(1)}, u32[]{:S(2)}, u32[]{:S(2)}) collective-permute-start(bf16[272,768]{1,0:T(8,128)(2,1)} %get-tuple-element.22), channel_id=1, source_target_pairs={{0,12},{1,13},{2,14},{3,15},{4,0},{5,1},{6,2},{7,3},{8,4},{9,5},{1... | collective-permute-start | bytes 1253384 | tf_op jit(solution)/shard_map/ppermute | solution.py:238
  20.1 10.7 %collective-permute-start.9 = (bf16[272,768]{1,0:T(8,128)(2,1)S(1)}, bf16[272,768]{1,0:T(8,128)(2,1)S(1)}, u32[]{:S(2)}, u32[]{:S(2)}) collective-permute-start(bf16[272,768]{1,0:T(8,128)(2,1)S(1)} %collective-permute-done.refs_2_), channel_id=1, source_target_pairs={{0,2},{1,3},{2,0},{3,1},{4,6},{5,7},{6,4},{7,5},{8,10},{9,11},{10,... | collective-permute-start | bytes 1253384 | tf_op jit(solution)/shard_map/ppermute | solution.py:241
  21.6 24.6 %collective-permute-start.1 = (bf16[272,768]{1,0:T(8,128)(2,1)}, bf16[272,768]{1,0:T(8,128)(2,1)S(1)}, u32[]{:S(2)}, u32[]{:S(2)}) collective-permute-start(bf16[272,768]{1,0:T(8,128)(2,1)} %get-tuple-element.19), channel_id=1, source_target_pairs={{0,8},{1,9},{2,10},{3,11},{4,12},{5,13},{6,14},{7,15},{8,0},{9,1},... | collective-permute-start | bytes 1253384 | tf_op jit(solution)/shard_map/ppermute | solution.py:238
  21.6 24.6 %collective-permute-start.5 = (bf16[272,768]{1,0:T(8,128)(2,1)S(1)}, bf16[272,768]{1,0:T(8,128)(2,1)S(1)}, u32[]{:S(2)}, u32[]{:S(2)}) collective-permute-start(bf16[272,768]{1,0:T(8,128)(2,1)S(1)} %collective-permute-done.refs_2_), channel_id=1, source_target_pairs={{0,1},{1,0},{2,3},{3,2},{4,5},{5,4},{6,7},{7,6},{8,9},{9,8},{10,11... | collective-permute-start | bytes 1253384 | tf_op jit(solution)/shard_map/ppermute | solution.py:241
  21.6 25.0 %collective-permute-start.10 = (bf16[272,768]{1,0:T(8,128)(2,1)S(1)}, bf16[272,768]{1,0:T(8,128)(2,1)S(1)}, u32[]{:S(2)}, u32[]{:S(2)}) collective-permute-start(bf16[272,768]{1,0:T(8,128)(2,1)S(1)} %collective-permute-done.8.refs_9_), channel_id=1, source_target_pairs={{0,1},{1,0},{2,3},{3,2},{4,5},{5,4},{6,7},{7,6},{8,9},{9,8},{10,11... | collective-permute-start | bytes 1253384 | tf_op jit(solution)/shard_map/ppermute | solution.py:241
  30.8 17.3 %collective-permute-start.6 = (bf16[272,768]{1,0:T(8,128)(2,1)S(1)}, bf16[272,768]{1,0:T(8,128)(2,1)S(1)}, u32[]{:S(2)}, u32[]{:S(2)}) collective-permute-start(bf16[272,768]{1,0:T(8,128)(2,1)S(1)} %collective-permute-done.3.refs_3_), channel_id=1, source_target_pairs={{0,1},{1,0},{2,3},{3,2},{4,5},{5,4},{6,7},{7,6},{8,9},{9,8},{10,11... | collective-permute-start | bytes 1253384 | tf_op jit(solution)/shard_map/ppermute | solution.py:241
  30.8 17.3 %collective-permute-start.12 = (bf16[272,768]{1,0:T(8,128)(2,1)S(1)}, bf16[272,768]{1,0:T(8,128)(2,1)S(1)}, u32[]{:S(2)}, u32[]{:S(2)}) collective-permute-start(bf16[272,768]{1,0:T(8,128)(2,1)S(1)} %collective-permute-done.3.refs_3_), channel_id=1, source_target_pairs={{0,2},{1,3},{2,0},{3,1},{4,6},{5,7},{6,4},{7,5},{8,10},{9,11},{10,... | collective-permute-start | bytes 1253384 | tf_op jit(solution)/shard_map/ppermute | solution.py:241
  46.2 2.0 %collective-permute-start.11 = (bf16[272,768]{1,0:T(8,128)(2,1)S(1)}, bf16[272,768]{1,0:T(8,128)(2,1)S(1)}, u32[]{:S(2)}, u32[]{:S(2)}) collective-permute-start(bf16[272,768]{1,0:T(8,128)(2,1)S(1)} %collective-permute-done.9.refs_10_), channel_id=1, source_target_pairs={{0,1},{1,0},{2,3},{3,2},{4,5},{5,4},{6,7},{7,6},{8,9},{9,8},{10,11... | collective-permute-start | bytes 1253384 | tf_op jit(solution)/shard_map/ppermute | solution.py:241
  46.2 2.3 %collective-permute-start.7 = (bf16[272,768]{1,0:T(8,128)(2,1)S(1)}, bf16[272,768]{1,0:T(8,128)(2,1)S(1)}, u32[]{:S(2)}, u32[]{:S(2)}) collective-permute-start(bf16[272,768]{1,0:T(8,128)(2,1)S(1)} %collective-permute-done.1.refs_4_), channel_id=1, source_target_pairs={{0,1},{1,0},{2,3},{3,2},{4,5},{5,4},{6,7},{7,6},{8,9},{9,8},{10,11... | collective-permute-start | bytes 1253384 | tf_op jit(solution)/shard_map/ppermute | solution.py:241
  46.7 11.6 %collective-permute-start.2 = (bf16[272,768]{1,0:T(8,128)(2,1)S(1)}, bf16[272,768]{1,0:T(8,128)(2,1)S(1)}, u32[]{:S(2)}, u32[]{:S(2)}) collective-permute-start(bf16[272,768]{1,0:T(8,128)(2,1)S(1)} %collective-permute-done.1.refs_4_), channel_id=1, source_target_pairs={{0,2},{1,3},{2,0},{3,1},{4,6},{5,7},{6,4},{7,5},{8,10},{9,11},{10,... | collective-permute-start | bytes 1253384 | tf_op jit(solution)/shard_map/ppermute | solution.py:241
  48.2 10.1 %collective-permute-start.13 = (bf16[272,768]{1,0:T(8,128)(2,1)S(1)}, bf16[272,768]{1,0:T(8,128)(2,1)S(1)}, u32[]{:S(2)}, u32[]{:S(2)}) collective-permute-start(bf16[272,768]{1,0:T(8,128)(2,1)S(1)} %collective-permute-done.12.refs_5_), channel_id=1, source_target_pairs={{0,1},{1,0},{2,3},{3,2},{4,5},{5,4},{6,7},{7,6},{8,9},{9,8},{10,11... | collective-permute-start | bytes 1253384 | tf_op jit(solution)/shard_map/ppermute | solution.py:241
  48.5 1.0 %copy-start.1 = (bf16[272,768]{1,0:T(8,128)(2,1)S(1)}, bf16[272,768]{1,0:T(8,128)(2,1)}, u32[]{:S(2)}) copy-start(bf16[272,768]{1,0:T(8,128)(2,1)} %get-tuple-element.20.refs_1_) | copy-start | bytes 1253380
  58.3 1.8 %collective-permute-start.14 = (bf16[272,768]{1,0:T(8,128)(2,1)S(1)}, bf16[272,768]{1,0:T(8,128)(2,1)S(1)}, u32[]{:S(2)}, u32[]{:S(2)}) collective-permute-start(bf16[272,768]{1,0:T(8,128)(2,1)S(1)} %collective-permute-done.2.refs_5_), channel_id=1, source_target_pairs={{0,1},{1,0},{2,3},{3,2},{4,5},{5,4},{6,7},{7,6},{8,9},{9,8},{10,11... | collective-permute-start | bytes 1253384 | tf_op jit(solution)/shard_map/ppermute | solution.py:241
  59.4 12.8 %copy-start = (s32[1,512]{1,0:T(1,128)S(1)}, s32[1,512]{1,0:T(1,128)}, u32[]{:S(2)}) copy-start(s32[1,512]{1,0:T(1,128)} %get-tuple-element.15.slot_ref) | copy-start | bytes 6148

commit v7 on v5

--- a/solution.py
+++ b/solution.py
@@ -7,7 +7,7 @@
 
 GROUP = 4
 BLOCKS = 4
-UNITS = (4, 4, 4, 4)
+UNITS = (4, 4, 4, 2, 2)
 PAD = 16
 STEP = 512
 GRANT = 16 << 20
@@ -263,9 +263,16 @@
 
     arrays = [[None] * BLOCKS for _ in range(4)]
     own, across, beside, beyond = arrays
-    sent = [blocks[0]] + [send(u) for u in range(1, len(units))]
+    sent = [blocks[0], send(1)]
+    blocks[2], blocks[3], sent[1] = tie(blocks[2], blocks[3], sent[1])
+    sent += [send(2), send(3)]
+    blocks[4], sent[2] = tie(blocks[4], sent[2])
+    sent += [send(4)]
     own[:] = [sent[0]], [sent[1]], [sent[2]], sent[3:]
-    for u in range(BLOCKS):
+    across[0] = cross(own[0])
+    own[0][0], own[2][0] = tie(own[0][0], own[2][0])
+    beside[0] = core(own[0])
+    for u in range(1, BLOCKS):
         beside[u], across[u] = core(own[u]), cross(own[u])
     for u in range(BLOCKS - 1):
         beyond[u] = core(across[u])
@@ -275,6 +282,7 @@
 
     every, row = (0, 1, 2, 3), [(0, slots)]
     best = jnp.full((1, slots), -1.0, jnp.float32)
+    best, across[3][0] = tie(best, across[3][0])
     jobs = [(0, 4, 0, every), (0, 4, 1, every), (0, 4, 2, every), (0, 4, 3, (0, 2))]
     some = given((0, 2), range(4)) | given((1, 3), range(3))
     (best,) = compare(cap, row, jobs, some, best)

time: 70.5 us -> 71.9 us (1.020)
  waiting for transfers between devices: 38 us -> 43.6 us
  starting transfers between devices: 19.6 us -> 15.5 us
    ppermute x6 -> x7, starting transfers between devices: 12.2 us -> 6.97 us  [shift(): lax.ppermute(array, 'blk', [(i, (i + step) % devices) for i in range(devi...]
    ppermute x6 -> x7, waiting for transfers between devices: 32.5 us -> 36.7 us  [shift(): lax.ppermute(array, 'blk', [(i, (i + step) % devices) for i in range(devi...]
    ppermute x12 -> x15, waiting for transfers between devices: 5.49 us -> 6.84 us  [swap(): return lax.ppermute(array, 'blk', [(i, i ^ mask) for i in range(devices)])]
    ppermute x12 -> x15, starting transfers between devices: 7.44 us -> 8.53 us  [swap(): return lax.ppermute(array, 'blk', [(i, i ^ mask) for i in range(devices)])]
  transfers between devices with their start and end apart: 18 -> 22, of which waited for: 10 -> 9; matrix products, arithmetic and copies ran while one was open for 0% -> 0% of each run, Pallas kernels for 9% -> 8%
where the time goes in v7:
time: 71.9 us; the launch traced here: 71.8 us
  waiting for transfers between devices  43.6 us (61%)
  starting transfers between devices  15.5 us (22%)
  Pallas kernels  11.6 us (16%)
  local copies, waits for them, and re-layouts  1.01 us (1%)
    ppermute x7, waiting for transfers between devices, shift(): lax.ppermute(array, 'blk', [(i, (i + step) % devices) for i in range(devi...  36.7 us
    ppermute x15, starting transfers between devices, swap(): return lax.ppermute(array, 'blk', [(i, i ^ mask) for i in range(devices)])  8.53 us
    pallas_call x2, Pallas kernels, compare(): pl.pallas_call(lambda *refs: compare_kernel(cap, outs, jobs, names, *refs...  7.13 us
    ppermute x7, starting transfers between devices, shift(): lax.ppermute(array, 'blk', [(i, (i + step) % devices) for i in range(devi...  6.97 us
    ppermute x15, waiting for transfers between devices, swap(): return lax.ppermute(array, 'blk', [(i, i ^ mask) for i in range(devices)])  6.84 us
    pallas_call x1, Pallas kernels, pack(): pl.pallas_call(lambda *refs: pack_kernel(groups, cap, units, *refs), in_s...  3.36 us
  transfers between devices with their start and end apart: 22, of which 9 were waited for; matrix products, arithmetic and copies ran while one was open for 0% of the time, Pallas kernels for 8%

profile of v7, /device:TPU:0, one launch (start us, length us, event | category | flops | bytes accessed | tf_op | source)
XLA Modules:
  0.0 71.8 jit_solution(6681390737246343487)
XLA Ops:
  0.0 3.4 %pack.1 = (bf16[272,768]{1,0:T(8,128)(2,1)}, bf16[272,768]{1,0:T(8,128)(2,1)}, bf16[272,768]{1,0:T(8,128)(2,1)}, bf16[144,768]{1,0:T(8,128)(2,1)}, bf16[144,768]{1,0:T(8,128)(2,1)}, /*index=5*/s32[1,512]{1,0:T(1,128)}) custom-call(f32[512,768]{1,0:T(8,128)} %refs_0_.1, s32[1,512]{1,0:T(1,128)} %bitcast.3, s32[1,512]{1,0:T(1,128)} %bitcast.4), custom_call_target="tpu_custom_call" | custom-call | tf_op jit(solution)/shard_map/pack/pallas_call | solution.py:79
  3.4 3.1 %collective-permute-start = (bf16[272,768]{1,0:T(8,128)(2,1)}, bf16[272,768]{1,0:T(8,128)(2,1)S(1)}, u32[]{:S(2)}, u32[]{:S(2)}) collective-permute-start(bf16[272,768]{1,0:T(8,128)(2,1)} %get-tuple-element.30), channel_id=1, source_target_pairs={{0,4},{1,5},{2,6},{3,7},{4,8},{5,9},{6,10},{7,11},{8,12},{9,13},{1... | collective-permute-start | bytes 1253384 | tf_op jit(solution)/shard_map/ppermute | solution.py:231
  6.4 1.5 %collective-permute-start.11 = (bf16[272,768]{1,0:T(8,128)(2,1)}, bf16[272,768]{1,0:T(8,128)(2,1)S(1)}, u32[]{:S(2)}, u32[]{:S(2)}) collective-permute-start(bf16[272,768]{1,0:T(8,128)(2,1)} %get-tuple-element.37.refs_1_), channel_id=1, source_target_pairs={{0,2},{1,3},{2,0},{3,1},{4,6},{5,7},{6,4},{7,5},{8,10},{9,11},{10,... | collective-permute-start | bytes 1253384 | tf_op jit(solution)/shard_map/ppermute | solution.py:234
  7.9 10.4 %collective-permute-done.refs_2_ = bf16[272,768]{1,0:T(8,128)(2,1)S(1)} collective-permute-done((bf16[272,768]{1,0:T(8,128)(2,1)}, bf16[272,768]{1,0:T(8,128)(2,1)S(1)}, u32[]{:S(2)}, u32[]{:S(2)}) %collective-permute-start) | collective-permute-done | bytes 417824 | tf_op jit(solution)/shard_map/ppermute | solution.py:231
  18.3 1.7 %collective-permute-start.1 = (bf16[272,768]{1,0:T(8,128)(2,1)}, bf16[272,768]{1,0:T(8,128)(2,1)S(1)}, u32[]{:S(2)}, u32[]{:S(2)}) collective-permute-start(bf16[272,768]{1,0:T(8,128)(2,1)} %get-tuple-element.31), channel_id=1, source_target_pairs={{0,12},{1,13},{2,14},{3,15},{4,0},{5,1},{6,2},{7,3},{8,4},{9,5},{1... | collective-permute-start | bytes 1253384 | tf_op jit(solution)/shard_map/ppermute | solution.py:231
  20.1 1.5 %collective-permute-start.12 = (bf16[272,768]{1,0:T(8,128)(2,1)S(1)}, bf16[272,768]{1,0:T(8,128)(2,1)S(1)}, u32[]{:S(2)}, u32[]{:S(2)}) collective-permute-start(bf16[272,768]{1,0:T(8,128)(2,1)S(1)} %collective-permute-done.refs_2_), channel_id=1, source_target_pairs={{0,2},{1,3},{2,0},{3,1},{4,6},{5,7},{6,4},{7,5},{8,10},{9,11},{10,... | collective-permute-start | bytes 1253384 | tf_op jit(solution)/shard_map/ppermute | solution.py:234
  21.6 0.0 collective-permute-start.4
  21.6 0.0 collective-permute-start.7
  21.6 0.0 collective-permute-done.11.refs_11_
  21.6 0.5 collective-permute-start.14
  22.1 8.7 %collective-permute-done.1.refs_3_ = bf16[272,768]{1,0:T(8,128)(2,1)S(1)} collective-permute-done((bf16[272,768]{1,0:T(8,128)(2,1)}, bf16[272,768]{1,0:T(8,128)(2,1)S(1)}, u32[]{:S(2)}, u32[]{:S(2)}) %collective-permute-start.1) | collective-permute-done | bytes 417824 | tf_op jit(solution)/shard_map/ppermute | solution.py:231
  30.8 1.2 %collective-permute-start.13 = (bf16[272,768]{1,0:T(8,128)(2,1)S(1)}, bf16[272,768]{1,0:T(8,128)(2,1)S(1)}, u32[]{:S(2)}, u32[]{:S(2)}) collective-permute-start(bf16[272,768]{1,0:T(8,128)(2,1)S(1)} %collective-permute-done.1.refs_3_), channel_id=1, source_target_pairs={{0,2},{1,3},{2,0},{3,1},{4,6},{5,7},{6,4},{7,5},{8,10},{9,11},{10,... | collective-permute-start | bytes 1253384 | tf_op jit(solution)/shard_map/ppermute | solution.py:234
  32.0 5.7 %collective-permute-done.4.refs_4_ = bf16[144,768]{1,0:T(8,128)(2,1)S(1)} collective-permute-done((bf16[144,768]{1,0:T(8,128)(2,1)}, bf16[144,768]{1,0:T(8,128)(2,1)S(1)}, u32[]{:S(2)}, u32[]{:S(2)}) %collective-permute-start.4) | collective-permute-done | bytes 221216 | tf_op jit(solution)/shard_map/ppermute | solution.py:231
  37.7 1.5 %collective-permute-start.5 = (bf16[144,768]{1,0:T(8,128)(2,1)S(1)}, bf16[144,768]{1,0:T(8,128)(2,1)S(1)}, u32[]{:S(2)}, u32[]{:S(2)}) collective-permute-start(bf16[144,768]{1,0:T(8,128)(2,1)S(1)} %collective-permute-done.4.refs_4_), channel_id=1, source_target_pairs={{0,2},{1,3},{2,0},{3,1},{4,6},{5,7},{6,4},{7,5},{8,10},{9,11},{10,... | collective-permute-start | bytes 663560 | tf_op jit(solution)/shard_map/ppermute | solution.py:234
  39.2 0.0 collective-permute-done.12.refs_12_
  39.2 0.0 collective-permute-start.9
  39.2 0.0 collective-permute-done.7.refs_7_
  39.2 0.1 collective-permute-start.2
  39.3 0.0 collective-permute-done.14.refs_14_
  39.3 0.5 collective-permute-start.8
  39.8 5.1 %collective-permute-done.5.refs_6_ = bf16[144,768]{1,0:T(8,128)(2,1)S(1)} collective-permute-done((bf16[144,768]{1,0:T(8,128)(2,1)S(1)}, bf16[144,768]{1,0:T(8,128)(2,1)S(1)}, u32[]{:S(2)}, u32[]{:S(2)}) %collective-permute-start.5) | collective-permute-done | bytes 221216 | tf_op jit(solution)/shard_map/ppermute | solution.py:234
  44.8 0.0 collective-permute-start.6
  44.8 0.0 collective-permute-done.9.refs_9_
  44.8 0.5 collective-permute-start.15
  45.3 0.0 collective-permute-done.13.refs_13_
  45.3 0.1 collective-permute-start.16
  45.4 7.5 %collective-permute-done.2.refs_5_ = bf16[144,768]{1,0:T(8,128)(2,1)S(1)} collective-permute-done((bf16[144,768]{1,0:T(8,128)(2,1)}, bf16[144,768]{1,0:T(8,128)(2,1)S(1)}, u32[]{:S(2)}, u32[]{:S(2)}) %collective-permute-start.2) | collective-permute-done | bytes 221216 | tf_op jit(solution)/shard_map/ppermute | solution.py:231
  52.9 0.0 collective-permute-start.10
  52.9 0.0 collective-permute-done.8.refs_8_
  52.9 0.5 collective-permute-start.17
  53.4 0.0 collective-permute-done.6.refs_6_
  53.4 0.5 collective-permute-start.3
  53.9 0.0 collective-permute-done.15.refs_15_
  53.9 0.4 collective-permute-done.10.refs_10_
  54.3 0.0 collective-permute-done.16.refs_16_
  54.3 0.0 copy-start.1
  54.4 1.0 %copy-done.1 = bf16[272,768]{1,0:T(8,128)(2,1)S(1)} copy-done((bf16[272,768]{1,0:T(8,128)(2,1)S(1)}, bf16[272,768]{1,0:T(8,128)(2,1)}, u32[]{:S(2)}) %copy-start.1) | copy-done | bytes 417816
  55.4 6.1 %compare4_56.1.refs_0_ = f32[1,1024]{1,0:T(1,128)S(1)} custom-call(f32[1,1024]{1,0:T(1,128)S(1)} %broadcast_in_dim.3.refs_0_, bf16[272,768]{1,0:T(8,128)(2,1)S(1)} %copy-done.1, bf16[272,768]{1,0:T(8,128)(2,1)S(1)} %collective-permute-done.refs_2_, bf16[272,768]{1,0:T(8,128)(2,1)S(1)} %collective-permute-done.1.refs_3_, ...), custom_call_target="tpu_custom_call" | custom-call | flops 5637144576 | tf_op jit(solution)/shard_map/compare4_56/pallas_call | solution.py:177
  61.5 0.0 copy-start
  61.5 0.0 collective-permute-done.3.refs_7_
  61.5 0.2 collective-permute-start.18
  61.7 0.0 collective-permute-done.17.refs_8_
  61.7 1.3 %collective-permute-done.18.refs_9_ = bf16[144,768]{1,0:T(8,128)(2,1)S(1)} collective-permute-done((bf16[144,768]{1,0:T(8,128)(2,1)S(1)}, bf16[144,768]{1,0:T(8,128)(2,1)S(1)}, u32[]{:S(2)}, u32[]{:S(2)}) %collective-permute-start.18) | collective-permute-done | bytes 221216 | tf_op jit(solution)/shard_map/ppermute | solution.py:234
  63.0 1.0 %compare1_8.1 = (f32[1,256]{1,0:T(1,128)S(1)}, f32[1,256]{1,0:T(1,128)S(1)}, f32[1,256]{1,0:T(1,128)S(1)}, f32[1,256]{1,0:T(1,128)S(1)}) custom-call(f32[1,1024]{1,0:T(1,128)S(1)} %compare4_56.1.refs_0_, bf16[272,768]{1,0:T(8,128)(2,1)S(1)} %copy-done.1, bf16[272,768]{1,0:T(8,128)(2,1)S(1)} %collective-permute-done.refs_2_, ...), custom_call_target="tpu_custom_call" | custom-call | flops 805306368 | tf_op jit(solution)/shard_map/compare1_8/pallas_call | solution.py:177
  64.1 1.2 %collective-permute-start.19 = (f32[1,256]{1,0:T(1,128)S(1)}, f32[1,256]{1,0:T(1,128)S(1)}, u32[]{:S(2)}, u32[]{:S(2)}) collective-permute-start(f32[1,256]{1,0:T(1,128)S(1)} %get-tuple-element.44), channel_id=1, source_target_pairs={{0,12},{1,13},{2,14},{3,15},{4,0},{5,1},{6,2},{7,3},{8,4},{9,5},{1... | collective-permute-start | bytes 3080 | tf_op jit(solution)/shard_map/ppermute | solution.py:231
  65.3 0.8 %collective-permute-start.20 = (f32[1,256]{1,0:T(1,128)S(1)}, f32[1,256]{1,0:T(1,128)S(1)}, u32[]{:S(2)}, u32[]{:S(2)}) collective-permute-start(f32[1,256]{1,0:T(1,128)S(1)} %get-tuple-element.45), channel_id=1, source_target_pairs={{0,4},{1,5},{2,6},{3,7},{4,8},{5,9},{6,10},{7,11},{8,12},{9,13},{1... | collective-permute-start | bytes 3080 | tf_op jit(solution)/shard_map/ppermute | solution.py:231
  66.1 0.0 collective-permute-start.21
  66.1 1.5 %collective-permute-done.19.refs_1_ = f32[1,256]{1,0:T(1,128)S(1)} collective-permute-done((f32[1,256]{1,0:T(1,128)S(1)}, f32[1,256]{1,0:T(1,128)S(1)}, u32[]{:S(2)}, u32[]{:S(2)}) %collective-permute-start.19) | collective-permute-done | bytes 1056 | tf_op jit(solution)/shard_map/ppermute | solution.py:231
  67.7 3.0 %collective-permute-done.20.refs_2_ = f32[1,256]{1,0:T(1,128)S(1)} collective-permute-done((f32[1,256]{1,0:T(1,128)S(1)}, f32[1,256]{1,0:T(1,128)S(1)}, u32[]{:S(2)}, u32[]{:S(2)}) %collective-permute-start.20) | collective-permute-done | bytes 1056 | tf_op jit(solution)/shard_map/ppermute | solution.py:231
  70.7 0.0 collective-permute-done.21.refs_3_
  70.7 0.0 copy-done
  70.7 1.1 %unpack.1 = f32[1,512]{1,0:T(1,128)} custom-call(s32[1,512]{1,0:T(1,128)S(1)} %copy-done, f32[1,256]{1,0:T(1,128)S(1)} %get-tuple-element.43.refs_0_, f32[1,256]{1,0:T(1,128)S(1)} %collective-permute-done.19.refs_1_, f32[1,256]{1,0:T(1,128)S(1)} %collective-permute-done.20.refs_2_, f32[1,256]{1,0:T(1,128)S(1)} %collective-permute-done.21.refs_3_), custom_call_target="tpu_custom_call" | custom-call | tf_op jit(solution)/shard_map/unpack/pallas_call | solution.py:207
  (1 shorter events, 0.0 us)
Async XLA Ops:
  3.4 15.0 %collective-permute-start = (bf16[272,768]{1,0:T(8,128)(2,1)}, bf16[272,768]{1,0:T(8,128)(2,1)S(1)}, u32[]{:S(2)}, u32[]{:S(2)}) collective-permute-start(bf16[272,768]{1,0:T(8,128)(2,1)} %get-tuple-element.30), channel_id=1, source_target_pairs={{0,4},{1,5},{2,6},{3,7},{4,8},{5,9},{6,10},{7,11},{8,12},{9,13},{1... | collective-permute-start | bytes 1253384 | tf_op jit(solution)/shard_map/ppermute | solution.py:231
  6.4 15.1 %collective-permute-start.11 = (bf16[272,768]{1,0:T(8,128)(2,1)}, bf16[272,768]{1,0:T(8,128)(2,1)S(1)}, u32[]{:S(2)}, u32[]{:S(2)}) collective-permute-start(bf16[272,768]{1,0:T(8,128)(2,1)} %get-tuple-element.37.refs_1_), channel_id=1, source_target_pairs={{0,2},{1,3},{2,0},{3,1},{4,6},{5,7},{6,4},{7,5},{8,10},{9,11},{10,... | collective-permute-start | bytes 1253384 | tf_op jit(solution)/shard_map/ppermute | solution.py:234
  18.3 12.4 %collective-permute-start.1 = (bf16[272,768]{1,0:T(8,128)(2,1)}, bf16[272,768]{1,0:T(8,128)(2,1)S(1)}, u32[]{:S(2)}, u32[]{:S(2)}) collective-permute-start(bf16[272,768]{1,0:T(8,128)(2,1)} %get-tuple-element.31), channel_id=1, source_target_pairs={{0,12},{1,13},{2,14},{3,15},{4,0},{5,1},{6,2},{7,3},{8,4},{9,5},{1... | collective-permute-start | bytes 1253384 | tf_op jit(solution)/shard_map/ppermute | solution.py:231
  20.1 19.1 %collective-permute-start.12 = (bf16[272,768]{1,0:T(8,128)(2,1)S(1)}, bf16[272,768]{1,0:T(8,128)(2,1)S(1)}, u32[]{:S(2)}, u32[]{:S(2)}) collective-permute-start(bf16[272,768]{1,0:T(8,128)(2,1)S(1)} %collective-permute-done.refs_2_), channel_id=1, source_target_pairs={{0,2},{1,3},{2,0},{3,1},{4,6},{5,7},{6,4},{7,5},{8,10},{9,11},{10,... | collective-permute-start | bytes 1253384 | tf_op jit(solution)/shard_map/ppermute | solution.py:234
  21.6 16.1 %collective-permute-start.4 = (bf16[144,768]{1,0:T(8,128)(2,1)}, bf16[144,768]{1,0:T(8,128)(2,1)S(1)}, u32[]{:S(2)}, u32[]{:S(2)}) collective-permute-start(bf16[144,768]{1,0:T(8,128)(2,1)} %get-tuple-element.33), channel_id=1, source_target_pairs={{0,8},{1,9},{2,10},{3,11},{4,12},{5,13},{6,14},{7,15},{8,0},{9,1},... | collective-permute-start | bytes 663560 | tf_op jit(solution)/shard_map/ppermute | solution.py:231
  21.6 17.6 %collective-permute-start.7 = (bf16[272,768]{1,0:T(8,128)(2,1)S(1)}, bf16[272,768]{1,0:T(8,128)(2,1)S(1)}, u32[]{:S(2)}, u32[]{:S(2)}) collective-permute-start(bf16[272,768]{1,0:T(8,128)(2,1)S(1)} %collective-permute-done.refs_2_), channel_id=1, source_target_pairs={{0,1},{1,0},{2,3},{3,2},{4,5},{5,4},{6,7},{7,6},{8,9},{9,8},{10,11... | collective-permute-start | bytes 1253384 | tf_op jit(solution)/shard_map/ppermute | solution.py:234
  21.6 17.7 %collective-permute-start.14 = (bf16[272,768]{1,0:T(8,128)(2,1)S(1)}, bf16[272,768]{1,0:T(8,128)(2,1)S(1)}, u32[]{:S(2)}, u32[]{:S(2)}) collective-permute-start(bf16[272,768]{1,0:T(8,128)(2,1)S(1)} %collective-permute-done.11.refs_11_), channel_id=1, source_target_pairs={{0,1},{1,0},{2,3},{3,2},{4,5},{5,4},{6,7},{7,6},{8,9},{9,8},{10,11... | collective-permute-start | bytes 1253384 | tf_op jit(solution)/shard_map/ppermute | solution.py:234
  30.8 14.6 %collective-permute-start.13 = (bf16[272,768]{1,0:T(8,128)(2,1)S(1)}, bf16[272,768]{1,0:T(8,128)(2,1)S(1)}, u32[]{:S(2)}, u32[]{:S(2)}) collective-permute-start(bf16[272,768]{1,0:T(8,128)(2,1)S(1)} %collective-permute-done.1.refs_3_), channel_id=1, source_target_pairs={{0,2},{1,3},{2,0},{3,1},{4,6},{5,7},{6,4},{7,5},{8,10},{9,11},{10,... | collective-permute-start | bytes 1253384 | tf_op jit(solution)/shard_map/ppermute | solution.py:234
  37.7 7.1 %collective-permute-start.5 = (bf16[144,768]{1,0:T(8,128)(2,1)S(1)}, bf16[144,768]{1,0:T(8,128)(2,1)S(1)}, u32[]{:S(2)}, u32[]{:S(2)}) collective-permute-start(bf16[144,768]{1,0:T(8,128)(2,1)S(1)} %collective-permute-done.4.refs_4_), channel_id=1, source_target_pairs={{0,2},{1,3},{2,0},{3,1},{4,6},{5,7},{6,4},{7,5},{8,10},{9,11},{10,... | collective-permute-start | bytes 663560 | tf_op jit(solution)/shard_map/ppermute | solution.py:234
  39.2 5.7 %collective-permute-start.9 = (bf16[144,768]{1,0:T(8,128)(2,1)S(1)}, bf16[144,768]{1,0:T(8,128)(2,1)S(1)}, u32[]{:S(2)}, u32[]{:S(2)}) collective-permute-start(bf16[144,768]{1,0:T(8,128)(2,1)S(1)} %collective-permute-done.4.refs_4_), channel_id=1, source_target_pairs={{0,1},{1,0},{2,3},{3,2},{4,5},{5,4},{6,7},{7,6},{8,9},{9,8},{10,11... | collective-permute-start | bytes 663560 | tf_op jit(solution)/shard_map/ppermute | solution.py:234
  39.2 13.7 %collective-permute-start.2 = (bf16[144,768]{1,0:T(8,128)(2,1)}, bf16[144,768]{1,0:T(8,128)(2,1)S(1)}, u32[]{:S(2)}, u32[]{:S(2)}) collective-permute-start(bf16[144,768]{1,0:T(8,128)(2,1)} %get-tuple-element.32), channel_id=1, source_target_pairs={{0,8},{1,9},{2,10},{3,11},{4,12},{5,13},{6,14},{7,15},{8,0},{9,1},... | collective-permute-start | bytes 663560 | tf_op jit(solution)/shard_map/ppermute | solution.py:231
  39.3 13.6 %collective-permute-start.8 = (bf16[272,768]{1,0:T(8,128)(2,1)S(1)}, bf16[272,768]{1,0:T(8,128)(2,1)S(1)}, u32[]{:S(2)}, u32[]{:S(2)}) collective-permute-start(bf16[272,768]{1,0:T(8,128)(2,1)S(1)} %collective-permute-done.1.refs_3_), channel_id=1, source_target_pairs={{0,1},{1,0},{2,3},{3,2},{4,5},{5,4},{6,7},{7,6},{8,9},{9,8},{10,11... | collective-permute-start | bytes 1253384 | tf_op jit(solution)/shard_map/ppermute | solution.py:234
  44.8 8.6 %collective-permute-start.6 = (bf16[272,768]{1,0:T(8,128)(2,1)}, bf16[272,768]{1,0:T(8,128)(2,1)S(1)}, u32[]{:S(2)}, u32[]{:S(2)}) collective-permute-start(bf16[272,768]{1,0:T(8,128)(2,1)} %get-tuple-element.37.refs_1_), channel_id=1, source_target_pairs={{0,1},{1,0},{2,3},{3,2},{4,5},{5,4},{6,7},{7,6},{8,9},{9,8},{10,11... | collective-permute-start | bytes 1253384 | tf_op jit(solution)/shard_map/ppermute | solution.py:234
  44.8 9.1 %collective-permute-start.15 = (bf16[272,768]{1,0:T(8,128)(2,1)S(1)}, bf16[272,768]{1,0:T(8,128)(2,1)S(1)}, u32[]{:S(2)}, u32[]{:S(2)}) collective-permute-start(bf16[272,768]{1,0:T(8,128)(2,1)S(1)} %collective-permute-done.12.refs_12_), channel_id=1, source_target_pairs={{0,1},{1,0},{2,3},{3,2},{4,5},{5,4},{6,7},{7,6},{8,9},{9,8},{10,11... | collective-permute-start | bytes 1253384 | tf_op jit(solution)/shard_map/ppermute | solution.py:234
  45.3 9.0 %collective-permute-start.16 = (bf16[272,768]{1,0:T(8,128)(2,1)S(1)}, bf16[272,768]{1,0:T(8,128)(2,1)S(1)}, u32[]{:S(2)}, u32[]{:S(2)}) collective-permute-start(bf16[272,768]{1,0:T(8,128)(2,1)S(1)} %collective-permute-done.13.refs_13_), channel_id=1, source_target_pairs={{0,1},{1,0},{2,3},{3,2},{4,5},{5,4},{6,7},{7,6},{8,9},{9,8},{10,11... | collective-permute-start | bytes 1253384 | tf_op jit(solution)/shard_map/ppermute | solution.py:234
  52.9 1.5 %collective-permute-start.10 = (bf16[144,768]{1,0:T(8,128)(2,1)S(1)}, bf16[144,768]{1,0:T(8,128)(2,1)S(1)}, u32[]{:S(2)}, u32[]{:S(2)}) collective-permute-start(bf16[144,768]{1,0:T(8,128)(2,1)S(1)} %collective-permute-done.2.refs_5_), channel_id=1, source_target_pairs={{0,1},{1,0},{2,3},{3,2},{4,5},{5,4},{6,7},{7,6},{8,9},{9,8},{10,11... | collective-permute-start | bytes 663560 | tf_op jit(solution)/shard_map/ppermute | solution.py:234
  52.9 8.8 %collective-permute-start.17 = (bf16[144,768]{1,0:T(8,128)(2,1)S(1)}, bf16[144,768]{1,0:T(8,128)(2,1)S(1)}, u32[]{:S(2)}, u32[]{:S(2)}) collective-permute-start(bf16[144,768]{1,0:T(8,128)(2,1)S(1)} %collective-permute-done.5.refs_6_), channel_id=1, source_target_pairs={{0,1},{1,0},{2,3},{3,2},{4,5},{5,4},{6,7},{7,6},{8,9},{9,8},{10,11... | collective-permute-start | bytes 663560 | tf_op jit(solution)/shard_map/ppermute | solution.py:234
  53.4 8.1 %collective-permute-start.3 = (bf16[144,768]{1,0:T(8,128)(2,1)S(1)}, bf16[144,768]{1,0:T(8,128)(2,1)S(1)}, u32[]{:S(2)}, u32[]{:S(2)}) collective-permute-start(bf16[144,768]{1,0:T(8,128)(2,1)S(1)} %collective-permute-done.2.refs_5_), channel_id=1, source_target_pairs={{0,2},{1,3},{2,0},{3,1},{4,6},{5,7},{6,4},{7,5},{8,10},{9,11},{10,... | collective-permute-start | bytes 663560 | tf_op jit(solution)/shard_map/ppermute | solution.py:234
  54.3 1.0 %copy-start.1 = (bf16[272,768]{1,0:T(8,128)(2,1)S(1)}, bf16[272,768]{1,0:T(8,128)(2,1)}, u32[]{:S(2)}) copy-start(bf16[272,768]{1,0:T(8,128)(2,1)} %get-tuple-element.37.refs_1_) | copy-start | bytes 1253380
  61.5 9.2 %copy-start = (s32[1,512]{1,0:T(1,128)S(1)}, s32[1,512]{1,0:T(1,128)}, u32[]{:S(2)}) copy-start(s32[1,512]{1,0:T(1,128)} %get-tuple-element.26.slot_ref) | copy-start | bytes 6148
  61.5 1.5 %collective-permute-start.18 = (bf16[144,768]{1,0:T(8,128)(2,1)S(1)}, bf16[144,768]{1,0:T(8,128)(2,1)S(1)}, u32[]{:S(2)}, u32[]{:S(2)}) collective-permute-start(bf16[144,768]{1,0:T(8,128)(2,1)S(1)} %collective-permute-done.3.refs_7_), channel_id=1, source_target_pairs={{0,1},{1,0},{2,3},{3,2},{4,5},{5,4},{6,7},{7,6},{8,9},{9,8},{10,11... | collective-permute-start | bytes 663560 | tf_op jit(solution)/shard_map/ppermute | solution.py:234
  64.1 3.6 %collective-permute-start.19 = (f32[1,256]{1,0:T(1,128)S(1)}, f32[1,256]{1,0:T(1,128)S(1)}, u32[]{:S(2)}, u32[]{:S(2)}) collective-permute-start(f32[1,256]{1,0:T(1,128)S(1)} %get-tuple-element.44), channel_id=1, source_target_pairs={{0,12},{1,13},{2,14},{3,15},{4,0},{5,1},{6,2},{7,3},{8,4},{9,5},{1... | collective-permute-start | bytes 3080 | tf_op jit(solution)/shard_map/ppermute | solution.py:231
  65.3 5.4 %collective-permute-start.20 = (f32[1,256]{1,0:T(1,128)S(1)}, f32[1,256]{1,0:T(1,128)S(1)}, u32[]{:S(2)}, u32[]{:S(2)}) collective-permute-start(f32[1,256]{1,0:T(1,128)S(1)} %get-tuple-element.45), channel_id=1, source_target_pairs={{0,4},{1,5},{2,6},{3,7},{4,8},{5,9},{6,10},{7,11},{8,12},{9,13},{1... | collective-permute-start | bytes 3080 | tf_op jit(solution)/shard_map/ppermute | solution.py:231
  66.1 4.5 %collective-permute-start.21 = (f32[1,256]{1,0:T(1,128)S(1)}, f32[1,256]{1,0:T(1,128)S(1)}, u32[]{:S(2)}, u32[]{:S(2)}) collective-permute-start(f32[1,256]{1,0:T(1,128)S(1)} %get-tuple-element.46), channel_id=1, source_target_pairs={{0,8},{1,9},{2,10},{3,11},{4,12},{5,13},{6,14},{7,15},{8,0},{9,1},... | collective-permute-start | bytes 3080 | tf_op jit(solution)/shard_map/ppermute | solution.py:231

commit v8 on v5

--- a/solution.py
+++ b/solution.py
@@ -265,16 +265,47 @@
     own, across, beside, beyond = arrays
     sent = [blocks[0]] + [send(u) for u in range(1, len(units))]
     own[:] = [sent[0]], [sent[1]], [sent[2]], sent[3:]
+    every, row = (0, 1, 2, 3), [(0, slots)]
+    floor = jnp.full((1, slots), -1.0, jnp.float32)
+
+    def given(peers, blocks):
+        return {(peer, k): arrays[peer][k] for peer in peers for k in blocks}
+
+    if cap == slots // BLOCKS:
+        last = [blocks[3]]
+        opposite = cross(last)
+        diagonal = core(opposite)
+        across[0] = cross(own[0])
+        own[0], own[1] = tie(own[0], own[1])
+        beside[0] = core(own[0])
+        for u in (1, 2):
+            beside[u], across[u] = core(own[u]), cross(own[u])
+        for u in range(3):
+            beyond[u] = core(across[u])
+        beside[3] = core(own[3])
+        some = {(0, k): last for k in range(BLOCKS)} | {(1, 3): opposite, (3, 3): diagonal}
+        (source,) = compare(cap, row, [(0, 1, 3, (1, 3))], some, floor)
+        some = {(0, k): across[k] for k in range(3)}
+        some |= {(0, 3): own[3], (1, 3): own[3], (2, 3): beside[3]}
+        (theirs,) = compare(cap, row, [(0, 3, 3, (1, 2))], some, floor)
+        mine = swap(theirs, 2)
+        some = given(every, range(3)) | {(0, 3): own[0]}
+        (best,) = compare(cap, row, [(0, 3, k, every) for k in range(3)], some, floor)
+        jobs = [(3, 4, k, every) for k in range(3)] + [(0, 4, 3, (0, 2))]
+        some = given(every, range(3)) | given((0, 2), (3,))
+        best = list(compare(cap, pieces, jobs, some, best))
+        for k in range(3):
+            best[k] = jnp.maximum(best[k], mine[:, k * cap : (k + 1) * cap])
+        backs = [exchange(b, low, 1, -1) for b, (low, _) in zip(best, pieces)]
+        backs[3] = jnp.maximum(backs[3], source[:, :cap])
+        return unpack(slot, backs).reshape(rows)
+
     for u in range(BLOCKS):
         beside[u], across[u] = core(own[u]), cross(own[u])
     for u in range(BLOCKS - 1):
         beyond[u] = core(across[u])
 
-    def given(peers, blocks):
-        return {(peer, k): arrays[peer][k] for peer in peers for k in blocks}
-
-    every, row = (0, 1, 2, 3), [(0, slots)]
-    best = jnp.full((1, slots), -1.0, jnp.float32)
+    best = floor
     jobs = [(0, 4, 0, every), (0, 4, 1, every), (0, 4, 2, every), (0, 4, 3, (0, 2))]
     some = given((0, 2), range(4)) | given((1, 3), range(3))
     (best,) = compare(cap, row, jobs, some, best)

time: 70.5 us -> 76.8 us (1.089)
  starting transfers between devices: 19.6 us -> 29.2 us
  waiting for transfers between devices: 38 us -> 34.1 us
    ppermute x6, starting transfers between devices: 12.2 us -> 22.5 us  [shift(): lax.ppermute(array, 'blk', [(i, (i + step) % devices) for i in range(devi...]
    ppermute x12 -> x13, waiting for transfers between devices: 5.49 us -> 1.08 us  [swap(): return lax.ppermute(array, 'blk', [(i, i ^ mask) for i in range(devices)])]
    ppermute x12 -> x13, starting transfers between devices: 7.44 us -> 6.76 us  [swap(): return lax.ppermute(array, 'blk', [(i, i ^ mask) for i in range(devices)])]
    pallas_call x2 -> x4, Pallas kernels: 7.13 us -> 7.63 us  [compare(): pl.pallas_call(lambda *refs: compare_kernel(cap, outs, jobs, names, *refs...]
  transfers between devices with their start and end apart: 18 -> 19, of which waited for: 10 -> 6; matrix products, arithmetic and copies ran while one was open for 0% -> 0% of each run, Pallas kernels for 9% -> 10%
where the time goes in v8:
time: 76.8 us; the launch traced here: 76.7 us
  waiting for transfers between devices  34.1 us (44%)
  starting transfers between devices  29.2 us (38%)
  Pallas kernels  12.2 us (16%)
  local copies, waits for them, and re-layouts  1.02 us (1%)
    ppermute x6, waiting for transfers between devices, shift(): lax.ppermute(array, 'blk', [(i, (i + step) % devices) for i in range(devi...  33.1 us
    ppermute x6, starting transfers between devices, shift(): lax.ppermute(array, 'blk', [(i, (i + step) % devices) for i in range(devi...  22.5 us
    pallas_call x4, Pallas kernels, compare(): pl.pallas_call(lambda *refs: compare_kernel(cap, outs, jobs, names, *refs...  7.63 us
    ppermute x13, starting transfers between devices, swap(): return lax.ppermute(array, 'blk', [(i, i ^ mask) for i in range(devices)])  6.76 us
    pallas_call x1, Pallas kernels, pack(): pl.pallas_call(lambda *refs: pack_kernel(groups, cap, units, *refs), in_s...  3.44 us
  transfers between devices with their start and end apart: 19, of which 6 were waited for; matrix products, arithmetic and copies ran while one was open for 0% of the time, Pallas kernels for 10%

profile of v8, /device:TPU:0, one launch (start us, length us, event | category | flops | bytes accessed | tf_op | source)
XLA Modules:
  0.0 76.7 jit_solution(5515932145644389385)
XLA Ops:
  0.0 3.4 %pack.1 = (bf16[272,768]{1,0:T(8,128)(2,1)}, bf16[272,768]{1,0:T(8,128)(2,1)}, bf16[272,768]{1,0:T(8,128)(2,1)}, bf16[272,768]{1,0:T(8,128)(2,1)}, s32[1,512]{1,0:T(1,128)}) custom-call(f32[512,768]{1,0:T(8,128)} %refs_0_.1, s32[1,512]{1,0:T(1,128)} %bitcast.3, s32[1,512]{1,0:T(1,128)} %bitcast.4), custom_call_target="tpu_custom_call" | custom-call | tf_op jit(solution)/shard_map/pack/pallas_call | solution.py:79
  3.4 3.1 %collective-permute-start = (bf16[272,768]{1,0:T(8,128)(2,1)}, bf16[272,768]{1,0:T(8,128)(2,1)S(1)}, u32[]{:S(2)}, u32[]{:S(2)}) collective-permute-start(bf16[272,768]{1,0:T(8,128)(2,1)} %get-tuple-element.18), channel_id=1, source_target_pairs={{0,4},{1,5},{2,6},{3,7},{4,8},{5,9},{6,10},{7,11},{8,12},{9,13},{1... | collective-permute-start | bytes 1253384 | tf_op jit(solution)/shard_map/ppermute | solution.py:231
  6.5 2.1 %collective-permute-start.1 = (bf16[272,768]{1,0:T(8,128)(2,1)}, bf16[272,768]{1,0:T(8,128)(2,1)S(1)}, u32[]{:S(2)}, u32[]{:S(2)}) collective-permute-start(bf16[272,768]{1,0:T(8,128)(2,1)} %get-tuple-element.21), channel_id=1, source_target_pairs={{0,12},{1,13},{2,14},{3,15},{4,0},{5,1},{6,2},{7,3},{8,4},{9,5},{1... | collective-permute-start | bytes 1253384 | tf_op jit(solution)/shard_map/ppermute | solution.py:231
  8.6 1.6 %collective-permute-start.2 = (bf16[272,768]{1,0:T(8,128)(2,1)}, bf16[272,768]{1,0:T(8,128)(2,1)S(1)}, u32[]{:S(2)}, u32[]{:S(2)}) collective-permute-start(bf16[272,768]{1,0:T(8,128)(2,1)} %get-tuple-element.19.refs_1_.refs_13_), channel_id=1, source_target_pairs={{0,2},{1,3},{2,0},{3,1},{4,6},{5,7},{6,4},{7,5},{8,10},{9,11},{10,... | collective-permute-start | bytes 1253384 | tf_op jit(solution)/shard_map/ppermute | solution.py:234
  10.3 0.4 collective-permute-start.17
  10.6 0.9 %collective-permute-start.11 = (bf16[272,768]{1,0:T(8,128)(2,1)}, bf16[272,768]{1,0:T(8,128)(2,1)S(1)}, u32[]{:S(2)}, u32[]{:S(2)}) collective-permute-start(bf16[272,768]{1,0:T(8,128)(2,1)} %get-tuple-element.22.refs_1_.refs_2_.refs_3_.refs_4_), channel_id=1, source_target_pairs={{0,8},{1,9},{2,10},{3,11},{4,12},{5,13},{6,14},{7,15},{8,0},{9,1},... | collective-permute-start | bytes 1253384 | tf_op jit(solution)/shard_map/ppermute | solution.py:231
  11.6 7.7 %collective-permute-done.refs_2_ = bf16[272,768]{1,0:T(8,128)(2,1)S(1)} collective-permute-done((bf16[272,768]{1,0:T(8,128)(2,1)}, bf16[272,768]{1,0:T(8,128)(2,1)S(1)}, u32[]{:S(2)}, u32[]{:S(2)}) %collective-permute-start) | collective-permute-done | bytes 417824 | tf_op jit(solution)/shard_map/ppermute | solution.py:231
  19.3 0.0 collective-permute-start.5
  19.3 7.5 %collective-permute-done.1.refs_3_ = bf16[272,768]{1,0:T(8,128)(2,1)S(1)} collective-permute-done((bf16[272,768]{1,0:T(8,128)(2,1)}, bf16[272,768]{1,0:T(8,128)(2,1)S(1)}, u32[]{:S(2)}, u32[]{:S(2)}) %collective-permute-start.1) | collective-permute-done | bytes 417824 | tf_op jit(solution)/shard_map/ppermute | solution.py:231
  26.8 1.5 %collective-permute-start.3 = (bf16[272,768]{1,0:T(8,128)(2,1)S(1)}, bf16[272,768]{1,0:T(8,128)(2,1)S(1)}, u32[]{:S(2)}, u32[]{:S(2)}) collective-permute-start(bf16[272,768]{1,0:T(8,128)(2,1)S(1)} %collective-permute-done.refs_2_), channel_id=1, source_target_pairs={{0,2},{1,3},{2,0},{3,1},{4,6},{5,7},{6,4},{7,5},{8,10},{9,11},{10,... | collective-permute-start | bytes 1253384 | tf_op jit(solution)/shard_map/ppermute | solution.py:234
  28.3 0.0 collective-permute-done.2.refs_4_.refs_1_
  28.3 0.5 collective-permute-start.4
  28.8 0.1 collective-permute-done.17.refs_5_
  28.9 0.0 collective-permute-start.18
  28.9 16.3 %collective-permute-done.11.refs_13_.refs_4_.refs_5_ = bf16[272,768]{1,0:T(8,128)(2,1)S(1)} collective-permute-done((bf16[272,768]{1,0:T(8,128)(2,1)}, bf16[272,768]{1,0:T(8,128)(2,1)S(1)}, u32[]{:S(2)}, u32[]{:S(2)}) %collective-permute-start.11) | collective-permute-done | bytes 417824 | tf_op jit(solution)/shard_map/ppermute | solution.py:231
  45.3 0.0 collective-permute-start.12
  45.3 0.0 collective-permute-done.5.refs_7_
  45.3 0.5 collective-permute-start.6
  45.8 0.0 collective-permute-done.3.refs_5_.refs_2_
  45.8 0.1 collective-permute-start.7
  45.9 0.9 %collective-permute-done.4.refs_6_.refs_3_ = bf16[272,768]{1,0:T(8,128)(2,1)S(1)} collective-permute-done((bf16[272,768]{1,0:T(8,128)(2,1)S(1)}, bf16[272,768]{1,0:T(8,128)(2,1)S(1)}, u32[]{:S(2)}, u32[]{:S(2)}) %collective-permute-start.4) | collective-permute-done | bytes 417824 | tf_op jit(solution)/shard_map/ppermute | solution.py:234
  46.8 0.0 collective-permute-start.8
  46.8 0.0 collective-permute-done.18.refs_6_
  46.8 0.5 collective-permute-start.9
  47.3 0.0 collective-permute-done.12.refs_14_.refs_6_
  47.3 0.1 collective-permute-start.10
  47.4 0.0 copy-start
  47.4 1.0 %copy-done = bf16[272,768]{1,0:T(8,128)(2,1)S(1)} copy-done((bf16[272,768]{1,0:T(8,128)(2,1)S(1)}, bf16[272,768]{1,0:T(8,128)(2,1)}, u32[]{:S(2)}) %copy-start) | copy-done | bytes 417816
  48.4 0.4 compare1_2.1
  48.8 0.0 copy-start.2
  48.8 0.8 %compare1_6.1 = f32[1,1024]{1,0:T(1,128)S(1)} custom-call(f32[1,1024]{1,0:T(1,128)S(1)} %broadcast_in_dim.3.refs_0_, bf16[272,768]{1,0:T(8,128)(2,1)S(1)} %collective-permute-done.2.refs_4_.refs_1_, bf16[272,768]{1,0:T(8,128)(2,1)S(1)} %collective-permute-done.3.refs_5_.refs_2_, bf16[272,768]{1,0:T(8,128)(2,1)S(1)} %collective-permute-done.4.refs_6_.refs_3_, ...), custom_call_target="tpu_custom_call" | custom-call | flops 603979776 | tf_op jit(solution)/shard_map/compare1_6/pallas_call | solution.py:177
  49.7 0.0 collective-permute-done.6.refs_8_
  49.7 1.5 %collective-permute-start.13 = (f32[1,1024]{1,0:T(1,128)S(1)}, f32[1,1024]{1,0:T(1,128)S(1)}, u32[]{:S(2)}, u32[]{:S(2)}) collective-permute-start(f32[1,1024]{1,0:T(1,128)S(1)} %compare1_6.1), channel_id=1, source_target_pairs={{0,2},{1,3},{2,0},{3,1},{4,6},{5,7},{6,4},{7,5},{8,10},{9,11},{10,... | collective-permute-start | bytes 12296 | tf_op jit(solution)/shard_map/ppermute | solution.py:234
  51.2 0.0 collective-permute-done.7.refs_9_
  51.2 0.0 collective-permute-done.8.refs_10_
  51.2 0.0 collective-permute-done.9.refs_11_
  51.2 0.0 collective-permute-done.10.refs_12_
  51.2 0.0 copy-done.2
  51.3 4.0 %compare3_36.1.refs_0_ = f32[1,1024]{1,0:T(1,128)S(1)} custom-call(f32[1,1024]{1,0:T(1,128)S(1)} %broadcast_in_dim.3.refs_0_, bf16[272,768]{1,0:T(8,128)(2,1)S(1)} %copy-done.2, bf16[272,768]{1,0:T(8,128)(2,1)S(1)} %collective-permute-done.refs_2_, bf16[272,768]{1,0:T(8,128)(2,1)S(1)} %collective-permute-done.1.refs_3_, ...), custom_call_target="tpu_custom_call" | custom-call | flops 3623878656 | tf_op jit(solution)/shard_map/compare3_36/pallas_call | solution.py:177
  55.3 0.0 copy-start.1
  55.3 2.3 %compare4_20.1 = (f32[1,256]{1,0:T(1,128)S(1)}, f32[1,256]{1,0:T(1,128)S(1)}, f32[1,256]{1,0:T(1,128)S(1)}, f32[1,256]{1,0:T(1,128)S(1)}) custom-call(f32[1,1024]{1,0:T(1,128)S(1)} %compare3_36.1.refs_0_, bf16[272,768]{1,0:T(8,128)(2,1)S(1)} %copy-done.2, bf16[272,768]{1,0:T(8,128)(2,1)S(1)} %collective-permute-done.refs_2_, ...), custom_call_target="tpu_custom_call" | custom-call | flops 2013265920 | tf_op jit(solution)/shard_map/compare4_20/pallas_call | solution.py:177
  57.7 12.5 %collective-permute-start.16 = (f32[1,256]{1,0:T(1,128)S(1)}, f32[1,256]{1,0:T(1,128)S(1)}, u32[]{:S(2)}, u32[]{:S(2)}) collective-permute-start(f32[1,256]{1,0:T(1,128)S(1)} %get-tuple-element.26), channel_id=1, source_target_pairs={{0,8},{1,9},{2,10},{3,11},{4,12},{5,13},{6,14},{7,15},{8,0},{9,1},... | collective-permute-start | bytes 3080 | tf_op jit(solution)/shard_map/ppermute | solution.py:231
  70.1 0.0 collective-permute-done.13
  70.2 0.1 collective-permute-start.15
  70.2 3.8 %collective-permute-start.14 = (f32[1,256]{1,0:T(1,128)S(1)}, f32[1,256]{1,0:T(1,128)S(1)}, u32[]{:S(2)}, u32[]{:S(2)}) collective-permute-start(f32[1,256]{1,0:T(1,128)S(1)} %get-tuple-element.28), channel_id=1, source_target_pairs={{0,12},{1,13},{2,14},{3,15},{4,0},{5,1},{6,2},{7,3},{8,4},{9,5},{1... | collective-permute-start | bytes 3080 | tf_op jit(solution)/shard_map/ppermute | solution.py:231
  74.0 0.0 collective-permute-done.16
  74.0 1.5 %collective-permute-done.15.refs_2_ = f32[1,256]{1,0:T(1,128)S(1)} collective-permute-done((f32[1,256]{1,0:T(1,128)S(1)}, f32[1,256]{1,0:T(1,128)S(1)}, u32[]{:S(2)}, u32[]{:S(2)}) %collective-permute-start.15) | collective-permute-done | bytes 1056 | tf_op jit(solution)/shard_map/ppermute | solution.py:231
  75.6 0.0 collective-permute-done.14.refs_1_
  75.6 0.0 copy-done.1
  75.6 1.1 %unpack.1 = f32[1,512]{1,0:T(1,128)} custom-call(s32[1,512]{1,0:T(1,128)S(1)} %copy-done.1, f32[1,256]{1,0:T(1,128)S(1)} %get-tuple-element.29.refs_0_, f32[1,256]{1,0:T(1,128)S(1)} %collective-permute-done.14.refs_1_, f32[1,256]{1,0:T(1,128)S(1)} %collective-permute-done.15.refs_2_, f32[1,256]{1,0:T(1,128)S(1)} %slice_maximum_fusion.refs_3_), custom_call_target="tpu_custom_call" | custom-call | tf_op jit(solution)/shard_map/unpack/pallas_call | solution.py:207
  (3 shorter events, 0.0 us)
Async XLA Ops:
  3.4 15.8 %collective-permute-start = (bf16[272,768]{1,0:T(8,128)(2,1)}, bf16[272,768]{1,0:T(8,128)(2,1)S(1)}, u32[]{:S(2)}, u32[]{:S(2)}) collective-permute-start(bf16[272,768]{1,0:T(8,128)(2,1)} %get-tuple-element.18), channel_id=1, source_target_pairs={{0,4},{1,5},{2,6},{3,7},{4,8},{5,9},{6,10},{7,11},{8,12},{9,13},{1... | collective-permute-start | bytes 1253384 | tf_op jit(solution)/shard_map/ppermute | solution.py:231
  6.5 20.3 %collective-permute-start.1 = (bf16[272,768]{1,0:T(8,128)(2,1)}, bf16[272,768]{1,0:T(8,128)(2,1)S(1)}, u32[]{:S(2)}, u32[]{:S(2)}) collective-permute-start(bf16[272,768]{1,0:T(8,128)(2,1)} %get-tuple-element.21), channel_id=1, source_target_pairs={{0,12},{1,13},{2,14},{3,15},{4,0},{5,1},{6,2},{7,3},{8,4},{9,5},{1... | collective-permute-start | bytes 1253384 | tf_op jit(solution)/shard_map/ppermute | solution.py:231
  8.6 19.7 %collective-permute-start.2 = (bf16[272,768]{1,0:T(8,128)(2,1)}, bf16[272,768]{1,0:T(8,128)(2,1)S(1)}, u32[]{:S(2)}, u32[]{:S(2)}) collective-permute-start(bf16[272,768]{1,0:T(8,128)(2,1)} %get-tuple-element.19.refs_1_.refs_13_), channel_id=1, source_target_pairs={{0,2},{1,3},{2,0},{3,1},{4,6},{5,7},{6,4},{7,5},{8,10},{9,11},{10,... | collective-permute-start | bytes 1253384 | tf_op jit(solution)/shard_map/ppermute | solution.py:234
  10.3 18.7 %collective-permute-start.17 = (bf16[272,768]{1,0:T(8,128)(2,1)}, bf16[272,768]{1,0:T(8,128)(2,1)S(1)}, u32[]{:S(2)}, u32[]{:S(2)}) collective-permute-start(bf16[272,768]{1,0:T(8,128)(2,1)} %get-tuple-element.22.refs_1_.refs_2_.refs_3_.refs_4_), channel_id=1, source_target_pairs={{0,2},{1,3},{2,0},{3,1},{4,6},{5,7},{6,4},{7,5},{8,10},{9,11},{10,... | collective-permute-start | bytes 1253384 | tf_op jit(solution)/shard_map/ppermute | solution.py:234
  10.6 34.6 %collective-permute-start.11 = (bf16[272,768]{1,0:T(8,128)(2,1)}, bf16[272,768]{1,0:T(8,128)(2,1)S(1)}, u32[]{:S(2)}, u32[]{:S(2)}) collective-permute-start(bf16[272,768]{1,0:T(8,128)(2,1)} %get-tuple-element.22.refs_1_.refs_2_.refs_3_.refs_4_), channel_id=1, source_target_pairs={{0,8},{1,9},{2,10},{3,11},{4,12},{5,13},{6,14},{7,15},{8,0},{9,1},... | collective-permute-start | bytes 1253384 | tf_op jit(solution)/shard_map/ppermute | solution.py:231
  19.3 26.0 %collective-permute-start.5 = (bf16[272,768]{1,0:T(8,128)(2,1)}, bf16[272,768]{1,0:T(8,128)(2,1)S(1)}, u32[]{:S(2)}, u32[]{:S(2)}) collective-permute-start(bf16[272,768]{1,0:T(8,128)(2,1)} %get-tuple-element.19.refs_1_.refs_13_), channel_id=1, source_target_pairs={{0,1},{1,0},{2,3},{3,2},{4,5},{5,4},{6,7},{7,6},{8,9},{9,8},{10,11... | collective-permute-start | bytes 1253384 | tf_op jit(solution)/shard_map/ppermute | solution.py:234
  26.8 19.0 %collective-permute-start.3 = (bf16[272,768]{1,0:T(8,128)(2,1)S(1)}, bf16[272,768]{1,0:T(8,128)(2,1)S(1)}, u32[]{:S(2)}, u32[]{:S(2)}) collective-permute-start(bf16[272,768]{1,0:T(8,128)(2,1)S(1)} %collective-permute-done.refs_2_), channel_id=1, source_target_pairs={{0,2},{1,3},{2,0},{3,1},{4,6},{5,7},{6,4},{7,5},{8,10},{9,11},{10,... | collective-permute-start | bytes 1253384 | tf_op jit(solution)/shard_map/ppermute | solution.py:234
  28.3 18.5 %collective-permute-start.4 = (bf16[272,768]{1,0:T(8,128)(2,1)S(1)}, bf16[272,768]{1,0:T(8,128)(2,1)S(1)}, u32[]{:S(2)}, u32[]{:S(2)}) collective-permute-start(bf16[272,768]{1,0:T(8,128)(2,1)S(1)} %collective-permute-done.1.refs_3_), channel_id=1, source_target_pairs={{0,2},{1,3},{2,0},{3,1},{4,6},{5,7},{6,4},{7,5},{8,10},{9,11},{10,... | collective-permute-start | bytes 1253384 | tf_op jit(solution)/shard_map/ppermute | solution.py:234
  28.9 17.9 %collective-permute-start.18 = (bf16[272,768]{1,0:T(8,128)(2,1)S(1)}, bf16[272,768]{1,0:T(8,128)(2,1)S(1)}, u32[]{:S(2)}, u32[]{:S(2)}) collective-permute-start(bf16[272,768]{1,0:T(8,128)(2,1)S(1)} %collective-permute-done.17.refs_5_), channel_id=1, source_target_pairs={{0,1},{1,0},{2,3},{3,2},{4,5},{5,4},{6,7},{7,6},{8,9},{9,8},{10,11... | collective-permute-start | bytes 1253384 | tf_op jit(solution)/shard_map/ppermute | solution.py:234
  45.3 2.0 %collective-permute-start.12 = (bf16[272,768]{1,0:T(8,128)(2,1)S(1)}, bf16[272,768]{1,0:T(8,128)(2,1)S(1)}, u32[]{:S(2)}, u32[]{:S(2)}) collective-permute-start(bf16[272,768]{1,0:T(8,128)(2,1)S(1)} %collective-permute-done.11.refs_13_.refs_4_.refs_5_), channel_id=1, source_target_pairs={{0,1},{1,0},{2,3},{3,2},{4,5},{5,4},{6,7},{7,6},{8,9},{9,8},{10,11... | collective-permute-start | bytes 1253384 | tf_op jit(solution)/shard_map/ppermute | solution.py:234
  45.3 4.4 %collective-permute-start.6 = (bf16[272,768]{1,0:T(8,128)(2,1)S(1)}, bf16[272,768]{1,0:T(8,128)(2,1)S(1)}, u32[]{:S(2)}, u32[]{:S(2)}) collective-permute-start(bf16[272,768]{1,0:T(8,128)(2,1)S(1)} %collective-permute-done.refs_2_), channel_id=1, source_target_pairs={{0,1},{1,0},{2,3},{3,2},{4,5},{5,4},{6,7},{7,6},{8,9},{9,8},{10,11... | collective-permute-start | bytes 1253384 | tf_op jit(solution)/shard_map/ppermute | solution.py:234
  45.8 5.4 %collective-permute-start.7 = (bf16[272,768]{1,0:T(8,128)(2,1)S(1)}, bf16[272,768]{1,0:T(8,128)(2,1)S(1)}, u32[]{:S(2)}, u32[]{:S(2)}) collective-permute-start(bf16[272,768]{1,0:T(8,128)(2,1)S(1)} %collective-permute-done.1.refs_3_), channel_id=1, source_target_pairs={{0,1},{1,0},{2,3},{3,2},{4,5},{5,4},{6,7},{7,6},{8,9},{9,8},{10,11... | collective-permute-start | bytes 1253384 | tf_op jit(solution)/shard_map/ppermute | solution.py:234
  46.8 4.4 %collective-permute-start.8 = (bf16[272,768]{1,0:T(8,128)(2,1)S(1)}, bf16[272,768]{1,0:T(8,128)(2,1)S(1)}, u32[]{:S(2)}, u32[]{:S(2)}) collective-permute-start(bf16[272,768]{1,0:T(8,128)(2,1)S(1)} %collective-permute-done.2.refs_4_.refs_1_), channel_id=1, source_target_pairs={{0,1},{1,0},{2,3},{3,2},{4,5},{5,4},{6,7},{7,6},{8,9},{9,8},{10,11... | collective-permute-start | bytes 1253384 | tf_op jit(solution)/shard_map/ppermute | solution.py:234
  46.8 4.4 %collective-permute-start.9 = (bf16[272,768]{1,0:T(8,128)(2,1)S(1)}, bf16[272,768]{1,0:T(8,128)(2,1)S(1)}, u32[]{:S(2)}, u32[]{:S(2)}) collective-permute-start(bf16[272,768]{1,0:T(8,128)(2,1)S(1)} %collective-permute-done.3.refs_5_.refs_2_), channel_id=1, source_target_pairs={{0,1},{1,0},{2,3},{3,2},{4,5},{5,4},{6,7},{7,6},{8,9},{9,8},{10,11... | collective-permute-start | bytes 1253384 | tf_op jit(solution)/shard_map/ppermute | solution.py:234
  47.3 3.9 %collective-permute-start.10 = (bf16[272,768]{1,0:T(8,128)(2,1)S(1)}, bf16[272,768]{1,0:T(8,128)(2,1)S(1)}, u32[]{:S(2)}, u32[]{:S(2)}) collective-permute-start(bf16[272,768]{1,0:T(8,128)(2,1)S(1)} %collective-permute-done.4.refs_6_.refs_3_), channel_id=1, source_target_pairs={{0,1},{1,0},{2,3},{3,2},{4,5},{5,4},{6,7},{7,6},{8,9},{9,8},{10,11... | collective-permute-start | bytes 1253384 | tf_op jit(solution)/shard_map/ppermute | solution.py:234
  47.4 1.0 %copy-start = (bf16[272,768]{1,0:T(8,128)(2,1)S(1)}, bf16[272,768]{1,0:T(8,128)(2,1)}, u32[]{:S(2)}) copy-start(bf16[272,768]{1,0:T(8,128)(2,1)} %get-tuple-element.22.refs_1_.refs_2_.refs_3_.refs_4_) | copy-start | bytes 1253380
  48.8 2.4 %copy-start.2 = (bf16[272,768]{1,0:T(8,128)(2,1)S(1)}, bf16[272,768]{1,0:T(8,128)(2,1)}, u32[]{:S(2)}) copy-start(bf16[272,768]{1,0:T(8,128)(2,1)} %get-tuple-element.19.refs_1_.refs_13_) | copy-start | bytes 1253380
  49.7 20.5 %collective-permute-start.13 = (f32[1,1024]{1,0:T(1,128)S(1)}, f32[1,1024]{1,0:T(1,128)S(1)}, u32[]{:S(2)}, u32[]{:S(2)}) collective-permute-start(f32[1,1024]{1,0:T(1,128)S(1)} %compare1_6.1), channel_id=1, source_target_pairs={{0,2},{1,3},{2,0},{3,1},{4,6},{5,7},{6,4},{7,5},{8,10},{9,11},{10,... | collective-permute-start | bytes 12296 | tf_op jit(solution)/shard_map/ppermute | solution.py:234
  55.3 20.3 %copy-start.1 = (s32[1,512]{1,0:T(1,128)S(1)}, s32[1,512]{1,0:T(1,128)}, u32[]{:S(2)}) copy-start(s32[1,512]{1,0:T(1,128)} %get-tuple-element.16.slot_ref) | copy-start | bytes 6148
  57.7 16.4 %collective-permute-start.16 = (f32[1,256]{1,0:T(1,128)S(1)}, f32[1,256]{1,0:T(1,128)S(1)}, u32[]{:S(2)}, u32[]{:S(2)}) collective-permute-start(f32[1,256]{1,0:T(1,128)S(1)} %get-tuple-element.26), channel_id=1, source_target_pairs={{0,8},{1,9},{2,10},{3,11},{4,12},{5,13},{6,14},{7,15},{8,0},{9,1},... | collective-permute-start | bytes 3080 | tf_op jit(solution)/shard_map/ppermute | solution.py:231
  70.2 5.4 %collective-permute-start.15 = (f32[1,256]{1,0:T(1,128)S(1)}, f32[1,256]{1,0:T(1,128)S(1)}, u32[]{:S(2)}, u32[]{:S(2)}) collective-permute-start(f32[1,256]{1,0:T(1,128)S(1)} %get-tuple-element.27), channel_id=1, source_target_pairs={{0,4},{1,5},{2,6},{3,7},{4,8},{5,9},{6,10},{7,11},{8,12},{9,13},{1... | collective-permute-start | bytes 3080 | tf_op jit(solution)/shard_map/ppermute | solution.py:231
  70.2 5.4 %collective-permute-start.14 = (f32[1,256]{1,0:T(1,128)S(1)}, f32[1,256]{1,0:T(1,128)S(1)}, u32[]{:S(2)}, u32[]{:S(2)}) collective-permute-start(f32[1,256]{1,0:T(1,128)S(1)} %get-tuple-element.28), channel_id=1, source_target_pairs={{0,12},{1,13},{2,14},{3,15},{4,0},{5,1},{6,2},{7,3},{8,4},{9,5},{1... | collective-permute-start | bytes 3080 | tf_op jit(solution)/shard_map/ppermute | solution.py:231

commit v9 on v8

--- a/solution.py
+++ b/solution.py
@@ -263,7 +263,12 @@
 
     arrays = [[None] * BLOCKS for _ in range(4)]
     own, across, beside, beyond = arrays
-    sent = [blocks[0]] + [send(u) for u in range(1, len(units))]
+    sent = [blocks[0], send(1)]
+    heads = blocks[2], blocks[3]
+    *heads, sent[1] = tie(*heads, sent[1])
+    last = [blocks[3]]
+    blocks[2:] = heads
+    sent += [send(2), send(3)]
     own[:] = [sent[0]], [sent[1]], [sent[2]], sent[3:]
     every, row = (0, 1, 2, 3), [(0, slots)]
     floor = jnp.full((1, slots), -1.0, jnp.float32)
@@ -272,7 +277,6 @@
         return {(peer, k): arrays[peer][k] for peer in peers for k in blocks}
 
     if cap == slots // BLOCKS:
-        last = [blocks[3]]
         opposite = cross(last)
         diagonal = core(opposite)
         across[0] = cross(own[0])

time: 76.8 us -> 67.6 us (0.88)
  starting transfers between devices: 29.2 us -> 16.7 us
  waiting for transfers between devices: 34.1 us -> 37.4 us
    ppermute x6, starting transfers between devices: 22.5 us -> 9.14 us  [shift(): lax.ppermute(array, 'blk', [(i, (i + step) % devices) for i in range(devi...]
    ppermute x13, waiting for transfers between devices: 1.08 us -> 7.22 us  [swap(): return lax.ppermute(array, 'blk', [(i, i ^ mask) for i in range(devices)])]
    ppermute x6, waiting for transfers between devices: 33.1 us -> 30.2 us  [shift(): lax.ppermute(array, 'blk', [(i, (i + step) % devices) for i in range(devi...]
    ppermute x13, starting transfers between devices: 6.76 us -> 7.54 us  [swap(): return lax.ppermute(array, 'blk', [(i, i ^ mask) for i in range(devices)])]
  transfers between devices with their start and end apart: 19 -> 19, of which waited for: 6 -> 8; matrix products, arithmetic and copies ran while one was open for 0% -> 0% of each run, Pallas kernels for 10% -> 11%
where the time goes in v9:
time: 67.6 us; the launch traced here: 67.4 us
  waiting for transfers between devices  37.4 us (55%)
  starting transfers between devices  16.7 us (25%)
  Pallas kernels  12.2 us (18%)
  local copies, waits for them, and re-layouts  1.02 us (2%)
    ppermute x6, waiting for transfers between devices, shift(): lax.ppermute(array, 'blk', [(i, (i + step) % devices) for i in range(devi...  30.2 us
    ppermute x6, starting transfers between devices, shift(): lax.ppermute(array, 'blk', [(i, (i + step) % devices) for i in range(devi...  9.14 us
    pallas_call x4, Pallas kernels, compare(): pl.pallas_call(lambda *refs: compare_kernel(cap, outs, jobs, names, *refs...  7.65 us
    ppermute x13, starting transfers between devices, swap(): return lax.ppermute(array, 'blk', [(i, i ^ mask) for i in range(devices)])  7.54 us
    ppermute x13, waiting for transfers between devices, swap(): return lax.ppermute(array, 'blk', [(i, i ^ mask) for i in range(devices)])  7.22 us
    pallas_call x1, Pallas kernels, pack(): pl.pallas_call(lambda *refs: pack_kernel(groups, cap, units, *refs), in_s...  3.44 us
  transfers between devices with their start and end apart: 19, of which 8 were waited for; matrix products, arithmetic and copies ran while one was open for 0% of the time, Pallas kernels for 11%

profile of v9, /device:TPU:0, one launch (start us, length us, event | category | flops | bytes accessed | tf_op | source)
XLA Modules:
  0.0 67.4 jit_solution(16802851043159897982)
XLA Ops:
  0.0 3.4 %pack.1 = (bf16[272,768]{1,0:T(8,128)(2,1)}, bf16[272,768]{1,0:T(8,128)(2,1)}, bf16[272,768]{1,0:T(8,128)(2,1)}, bf16[272,768]{1,0:T(8,128)(2,1)}, s32[1,512]{1,0:T(1,128)}) custom-call(f32[512,768]{1,0:T(8,128)} %refs_0_.1, s32[1,512]{1,0:T(1,128)} %bitcast.3, s32[1,512]{1,0:T(1,128)} %bitcast.4), custom_call_target="tpu_custom_call" | custom-call | tf_op jit(solution)/shard_map/pack/pallas_call | solution.py:79
  3.4 3.1 %collective-permute-start = (bf16[272,768]{1,0:T(8,128)(2,1)}, bf16[272,768]{1,0:T(8,128)(2,1)S(1)}, u32[]{:S(2)}, u32[]{:S(2)}) collective-permute-start(bf16[272,768]{1,0:T(8,128)(2,1)} %get-tuple-element.23), channel_id=1, source_target_pairs={{0,4},{1,5},{2,6},{3,7},{4,8},{5,9},{6,10},{7,11},{8,12},{9,13},{1... | collective-permute-start | bytes 1253384 | tf_op jit(solution)/shard_map/ppermute | solution.py:231
  6.5 1.5 %collective-permute-start.2 = (bf16[272,768]{1,0:T(8,128)(2,1)}, bf16[272,768]{1,0:T(8,128)(2,1)S(1)}, u32[]{:S(2)}, u32[]{:S(2)}) collective-permute-start(bf16[272,768]{1,0:T(8,128)(2,1)} %get-tuple-element.25.refs_1_.refs_13_), channel_id=1, source_target_pairs={{0,2},{1,3},{2,0},{3,1},{4,6},{5,7},{6,4},{7,5},{8,10},{9,11},{10,... | collective-permute-start | bytes 1253384 | tf_op jit(solution)/shard_map/ppermute | solution.py:234
  8.0 0.5 collective-permute-start.17
  8.6 9.9 %collective-permute-done.refs_2_ = bf16[272,768]{1,0:T(8,128)(2,1)S(1)} collective-permute-done((bf16[272,768]{1,0:T(8,128)(2,1)}, bf16[272,768]{1,0:T(8,128)(2,1)S(1)}, u32[]{:S(2)}, u32[]{:S(2)}) %collective-permute-start) | collective-permute-done | bytes 417824 | tf_op jit(solution)/shard_map/ppermute | solution.py:231
  18.4 1.7 %collective-permute-start.1 = (bf16[272,768]{1,0:T(8,128)(2,1)}, bf16[272,768]{1,0:T(8,128)(2,1)S(1)}, u32[]{:S(2)}, u32[]{:S(2)}) collective-permute-start(bf16[272,768]{1,0:T(8,128)(2,1)} %get-tuple-element.27), channel_id=1, source_target_pairs={{0,12},{1,13},{2,14},{3,15},{4,0},{5,1},{6,2},{7,3},{8,4},{9,5},{1... | collective-permute-start | bytes 1253384 | tf_op jit(solution)/shard_map/ppermute | solution.py:231
  20.2 0.0 collective-permute-start.11
  20.2 0.0 collective-permute-start.5
  20.2 0.0 collective-permute-done.2.refs_4_.refs_1_
  20.2 1.6 %collective-permute-start.3 = (bf16[272,768]{1,0:T(8,128)(2,1)S(1)}, bf16[272,768]{1,0:T(8,128)(2,1)S(1)}, u32[]{:S(2)}, u32[]{:S(2)}) collective-permute-start(bf16[272,768]{1,0:T(8,128)(2,1)S(1)} %collective-permute-done.refs_2_), channel_id=1, source_target_pairs={{0,2},{1,3},{2,0},{3,1},{4,6},{5,7},{6,4},{7,5},{8,10},{9,11},{10,... | collective-permute-start | bytes 1253384 | tf_op jit(solution)/shard_map/ppermute | solution.py:234
  21.7 6.5 %collective-permute-done.17.refs_5_ = bf16[272,768]{1,0:T(8,128)(2,1)S(1)} collective-permute-done((bf16[272,768]{1,0:T(8,128)(2,1)}, bf16[272,768]{1,0:T(8,128)(2,1)S(1)}, u32[]{:S(2)}, u32[]{:S(2)}) %collective-permute-start.17) | collective-permute-done | bytes 417824 | tf_op jit(solution)/shard_map/ppermute | solution.py:234
  28.3 0.0 collective-permute-start.18
  28.3 2.6 %collective-permute-done.1.refs_3_ = bf16[272,768]{1,0:T(8,128)(2,1)S(1)} collective-permute-done((bf16[272,768]{1,0:T(8,128)(2,1)}, bf16[272,768]{1,0:T(8,128)(2,1)S(1)}, u32[]{:S(2)}, u32[]{:S(2)}) %collective-permute-start.1) | collective-permute-done | bytes 417824 | tf_op jit(solution)/shard_map/ppermute | solution.py:231
  30.9 1.2 %collective-permute-start.4 = (bf16[272,768]{1,0:T(8,128)(2,1)S(1)}, bf16[272,768]{1,0:T(8,128)(2,1)S(1)}, u32[]{:S(2)}, u32[]{:S(2)}) collective-permute-start(bf16[272,768]{1,0:T(8,128)(2,1)S(1)} %collective-permute-done.1.refs_3_), channel_id=1, source_target_pairs={{0,2},{1,3},{2,0},{3,1},{4,6},{5,7},{6,4},{7,5},{8,10},{9,11},{10,... | collective-permute-start | bytes 1253384 | tf_op jit(solution)/shard_map/ppermute | solution.py:234
  32.0 14.1 %collective-permute-done.11.refs_13_.refs_4_.refs_5_ = bf16[272,768]{1,0:T(8,128)(2,1)S(1)} collective-permute-done((bf16[272,768]{1,0:T(8,128)(2,1)}, bf16[272,768]{1,0:T(8,128)(2,1)S(1)}, u32[]{:S(2)}, u32[]{:S(2)}) %collective-permute-start.11) | collective-permute-done | bytes 417824 | tf_op jit(solution)/shard_map/ppermute | solution.py:231
  46.2 0.0 collective-permute-start.12
  46.2 0.0 collective-permute-done.5.refs_7_
  46.2 0.5 collective-permute-start.6
  46.7 0.0 collective-permute-done.3.refs_5_.refs_2_
  46.7 0.1 collective-permute-start.8
  46.8 0.0 collective-permute-done.18.refs_6_
  46.8 0.4 collective-permute-start.7
  47.2 0.0 collective-permute-done.4.refs_6_.refs_3_
  47.2 0.1 collective-permute-start.9
  47.3 0.7 collective-permute-done.12.refs_14_.refs_6_
  47.9 0.1 collective-permute-start.10
  48.1 0.0 copy-start
  48.1 1.0 %copy-done = bf16[272,768]{1,0:T(8,128)(2,1)S(1)} copy-done((bf16[272,768]{1,0:T(8,128)(2,1)S(1)}, bf16[272,768]{1,0:T(8,128)(2,1)}, u32[]{:S(2)}) %copy-start) | copy-done | bytes 417816
  49.1 0.4 compare1_2.1
  49.5 0.0 copy-start.2
  49.6 0.8 %compare1_6.1 = f32[1,1024]{1,0:T(1,128)S(1)} custom-call(f32[1,1024]{1,0:T(1,128)S(1)} %broadcast_in_dim.3.refs_0_, bf16[272,768]{1,0:T(8,128)(2,1)S(1)} %collective-permute-done.2.refs_4_.refs_1_, bf16[272,768]{1,0:T(8,128)(2,1)S(1)} %collective-permute-done.3.refs_5_.refs_2_, bf16[272,768]{1,0:T(8,128)(2,1)S(1)} %collective-permute-done.4.refs_6_.refs_3_, ...), custom_call_target="tpu_custom_call" | custom-call | flops 603979776 | tf_op jit(solution)/shard_map/compare1_6/pallas_call | solution.py:177
  50.4 0.0 collective-permute-done.6.refs_8_
  50.4 1.5 %collective-permute-start.13 = (f32[1,1024]{1,0:T(1,128)S(1)}, f32[1,1024]{1,0:T(1,128)S(1)}, u32[]{:S(2)}, u32[]{:S(2)}) collective-permute-start(f32[1,1024]{1,0:T(1,128)S(1)} %compare1_6.1), channel_id=1, source_target_pairs={{0,2},{1,3},{2,0},{3,1},{4,6},{5,7},{6,4},{7,5},{8,10},{9,11},{10,... | collective-permute-start | bytes 12296 | tf_op jit(solution)/shard_map/ppermute | solution.py:234
  51.9 0.0 collective-permute-done.8.refs_10_
  51.9 0.0 collective-permute-done.9.refs_11_
  51.9 0.0 collective-permute-done.7.refs_9_
  51.9 0.0 collective-permute-done.10.refs_12_
  52.0 0.0 copy-done.2
  52.0 4.0 %compare3_36.1.refs_0_ = f32[1,1024]{1,0:T(1,128)S(1)} custom-call(f32[1,1024]{1,0:T(1,128)S(1)} %broadcast_in_dim.3.refs_0_, bf16[272,768]{1,0:T(8,128)(2,1)S(1)} %copy-done.2, bf16[272,768]{1,0:T(8,128)(2,1)S(1)} %collective-permute-done.refs_2_, bf16[272,768]{1,0:T(8,128)(2,1)S(1)} %collective-permute-done.1.refs_3_, ...), custom_call_target="tpu_custom_call" | custom-call | flops 3623878656 | tf_op jit(solution)/shard_map/compare3_36/pallas_call | solution.py:177
  56.0 0.0 copy-start.1
  56.0 2.3 %compare4_20.1 = (f32[1,256]{1,0:T(1,128)S(1)}, f32[1,256]{1,0:T(1,128)S(1)}, f32[1,256]{1,0:T(1,128)S(1)}, f32[1,256]{1,0:T(1,128)S(1)}) custom-call(f32[1,1024]{1,0:T(1,128)S(1)} %compare3_36.1.refs_0_, bf16[272,768]{1,0:T(8,128)(2,1)S(1)} %copy-done.2, bf16[272,768]{1,0:T(8,128)(2,1)S(1)} %collective-permute-done.refs_2_, ...), custom_call_target="tpu_custom_call" | custom-call | flops 2013265920 | tf_op jit(solution)/shard_map/compare4_20/pallas_call | solution.py:177
  58.4 0.1 collective-permute-start.16
  58.4 0.0 collective-permute-done.13
  58.5 4.2 %collective-permute-start.15 = (f32[1,256]{1,0:T(1,128)S(1)}, f32[1,256]{1,0:T(1,128)S(1)}, u32[]{:S(2)}, u32[]{:S(2)}) collective-permute-start(f32[1,256]{1,0:T(1,128)S(1)} %get-tuple-element.33), channel_id=1, source_target_pairs={{0,4},{1,5},{2,6},{3,7},{4,8},{5,9},{6,10},{7,11},{8,12},{9,13},{1... | collective-permute-start | bytes 3080 | tf_op jit(solution)/shard_map/ppermute | solution.py:231
  62.7 0.0 collective-permute-start.14
  62.7 0.2 collective-permute-done.16
  62.9 1.1 %collective-permute-done.15.refs_2_ = f32[1,256]{1,0:T(1,128)S(1)} collective-permute-done((f32[1,256]{1,0:T(1,128)S(1)}, f32[1,256]{1,0:T(1,128)S(1)}, u32[]{:S(2)}, u32[]{:S(2)}) %collective-permute-start.15) | collective-permute-done | bytes 1056 | tf_op jit(solution)/shard_map/ppermute | solution.py:231
  64.0 2.3 %collective-permute-done.14.refs_1_ = f32[1,256]{1,0:T(1,128)S(1)} collective-permute-done((f32[1,256]{1,0:T(1,128)S(1)}, f32[1,256]{1,0:T(1,128)S(1)}, u32[]{:S(2)}, u32[]{:S(2)}) %collective-permute-start.14) | collective-permute-done | bytes 1056 | tf_op jit(solution)/shard_map/ppermute | solution.py:231
  66.3 0.0 copy-done.1
  66.3 1.1 %unpack.1 = f32[1,512]{1,0:T(1,128)} custom-call(s32[1,512]{1,0:T(1,128)S(1)} %copy-done.1, f32[1,256]{1,0:T(1,128)S(1)} %get-tuple-element.35.refs_0_, f32[1,256]{1,0:T(1,128)S(1)} %collective-permute-done.14.refs_1_, f32[1,256]{1,0:T(1,128)S(1)} %collective-permute-done.15.refs_2_, f32[1,256]{1,0:T(1,128)S(1)} %slice_maximum_fusion.refs_3_), custom_call_target="tpu_custom_call" | custom-call | tf_op jit(solution)/shard_map/unpack/pallas_call | solution.py:207
  (3 shorter events, 0.0 us)
Async XLA Ops:
  3.4 15.0 %collective-permute-start = (bf16[272,768]{1,0:T(8,128)(2,1)}, bf16[272,768]{1,0:T(8,128)(2,1)S(1)}, u32[]{:S(2)}, u32[]{:S(2)}) collective-permute-start(bf16[272,768]{1,0:T(8,128)(2,1)} %get-tuple-element.23), channel_id=1, source_target_pairs={{0,4},{1,5},{2,6},{3,7},{4,8},{5,9},{6,10},{7,11},{8,12},{9,13},{1... | collective-permute-start | bytes 1253384 | tf_op jit(solution)/shard_map/ppermute | solution.py:231
  6.5 13.6 %collective-permute-start.2 = (bf16[272,768]{1,0:T(8,128)(2,1)}, bf16[272,768]{1,0:T(8,128)(2,1)S(1)}, u32[]{:S(2)}, u32[]{:S(2)}) collective-permute-start(bf16[272,768]{1,0:T(8,128)(2,1)} %get-tuple-element.25.refs_1_.refs_13_), channel_id=1, source_target_pairs={{0,2},{1,3},{2,0},{3,1},{4,6},{5,7},{6,4},{7,5},{8,10},{9,11},{10,... | collective-permute-start | bytes 1253384 | tf_op jit(solution)/shard_map/ppermute | solution.py:234
  8.0 20.2 %collective-permute-start.17 = (bf16[272,768]{1,0:T(8,128)(2,1)}, bf16[272,768]{1,0:T(8,128)(2,1)S(1)}, u32[]{:S(2)}, u32[]{:S(2)}) collective-permute-start(bf16[272,768]{1,0:T(8,128)(2,1)} %get-tuple-element.28.refs_1_.refs_2_.refs_3_.refs_4_), channel_id=1, source_target_pairs={{0,2},{1,3},{2,0},{3,1},{4,6},{5,7},{6,4},{7,5},{8,10},{9,11},{10,... | collective-permute-start | bytes 1253384 | tf_op jit(solution)/shard_map/ppermute | solution.py:234
  18.4 12.4 %collective-permute-start.1 = (bf16[272,768]{1,0:T(8,128)(2,1)}, bf16[272,768]{1,0:T(8,128)(2,1)S(1)}, u32[]{:S(2)}, u32[]{:S(2)}) collective-permute-start(bf16[272,768]{1,0:T(8,128)(2,1)} %get-tuple-element.27), channel_id=1, source_target_pairs={{0,12},{1,13},{2,14},{3,15},{4,0},{5,1},{6,2},{7,3},{8,4},{9,5},{1... | collective-permute-start | bytes 1253384 | tf_op jit(solution)/shard_map/ppermute | solution.py:231
  20.2 26.0 %collective-permute-start.11 = (bf16[272,768]{1,0:T(8,128)(2,1)}, bf16[272,768]{1,0:T(8,128)(2,1)S(1)}, u32[]{:S(2)}, u32[]{:S(2)}) collective-permute-start(bf16[272,768]{1,0:T(8,128)(2,1)} %get-tuple-element.28.refs_1_.refs_2_.refs_3_.refs_4_), channel_id=1, source_target_pairs={{0,8},{1,9},{2,10},{3,11},{4,12},{5,13},{6,14},{7,15},{8,0},{9,1},... | collective-permute-start | bytes 1253384 | tf_op jit(solution)/shard_map/ppermute | solution.py:231
  20.2 26.0 %collective-permute-start.5 = (bf16[272,768]{1,0:T(8,128)(2,1)}, bf16[272,768]{1,0:T(8,128)(2,1)S(1)}, u32[]{:S(2)}, u32[]{:S(2)}) collective-permute-start(bf16[272,768]{1,0:T(8,128)(2,1)} %get-tuple-element.25.refs_1_.refs_13_), channel_id=1, source_target_pairs={{0,1},{1,0},{2,3},{3,2},{4,5},{5,4},{6,7},{7,6},{8,9},{9,8},{10,11... | collective-permute-start | bytes 1253384 | tf_op jit(solution)/shard_map/ppermute | solution.py:234
  20.2 26.5 %collective-permute-start.3 = (bf16[272,768]{1,0:T(8,128)(2,1)S(1)}, bf16[272,768]{1,0:T(8,128)(2,1)S(1)}, u32[]{:S(2)}, u32[]{:S(2)}) collective-permute-start(bf16[272,768]{1,0:T(8,128)(2,1)S(1)} %collective-permute-done.refs_2_), channel_id=1, source_target_pairs={{0,2},{1,3},{2,0},{3,1},{4,6},{5,7},{6,4},{7,5},{8,10},{9,11},{10,... | collective-permute-start | bytes 1253384 | tf_op jit(solution)/shard_map/ppermute | solution.py:234
  28.3 18.5 %collective-permute-start.18 = (bf16[272,768]{1,0:T(8,128)(2,1)S(1)}, bf16[272,768]{1,0:T(8,128)(2,1)S(1)}, u32[]{:S(2)}, u32[]{:S(2)}) collective-permute-start(bf16[272,768]{1,0:T(8,128)(2,1)S(1)} %collective-permute-done.17.refs_5_), channel_id=1, source_target_pairs={{0,1},{1,0},{2,3},{3,2},{4,5},{5,4},{6,7},{7,6},{8,9},{9,8},{10,11... | collective-permute-start | bytes 1253384 | tf_op jit(solution)/shard_map/ppermute | solution.py:234
  30.9 16.4 %collective-permute-start.4 = (bf16[272,768]{1,0:T(8,128)(2,1)S(1)}, bf16[272,768]{1,0:T(8,128)(2,1)S(1)}, u32[]{:S(2)}, u32[]{:S(2)}) collective-permute-start(bf16[272,768]{1,0:T(8,128)(2,1)S(1)} %collective-permute-done.1.refs_3_), channel_id=1, source_target_pairs={{0,2},{1,3},{2,0},{3,1},{4,6},{5,7},{6,4},{7,5},{8,10},{9,11},{10,... | collective-permute-start | bytes 1253384 | tf_op jit(solution)/shard_map/ppermute | solution.py:234
  46.2 1.8 %collective-permute-start.12 = (bf16[272,768]{1,0:T(8,128)(2,1)S(1)}, bf16[272,768]{1,0:T(8,128)(2,1)S(1)}, u32[]{:S(2)}, u32[]{:S(2)}) collective-permute-start(bf16[272,768]{1,0:T(8,128)(2,1)S(1)} %collective-permute-done.11.refs_13_.refs_4_.refs_5_), channel_id=1, source_target_pairs={{0,1},{1,0},{2,3},{3,2},{4,5},{5,4},{6,7},{7,6},{8,9},{9,8},{10,11... | collective-permute-start | bytes 1253384 | tf_op jit(solution)/shard_map/ppermute | solution.py:234
  46.2 4.2 %collective-permute-start.6 = (bf16[272,768]{1,0:T(8,128)(2,1)S(1)}, bf16[272,768]{1,0:T(8,128)(2,1)S(1)}, u32[]{:S(2)}, u32[]{:S(2)}) collective-permute-start(bf16[272,768]{1,0:T(8,128)(2,1)S(1)} %collective-permute-done.refs_2_), channel_id=1, source_target_pairs={{0,1},{1,0},{2,3},{3,2},{4,5},{5,4},{6,7},{7,6},{8,9},{9,8},{10,11... | collective-permute-start | bytes 1253384 | tf_op jit(solution)/shard_map/ppermute | solution.py:234
  46.7 5.2 %collective-permute-start.8 = (bf16[272,768]{1,0:T(8,128)(2,1)S(1)}, bf16[272,768]{1,0:T(8,128)(2,1)S(1)}, u32[]{:S(2)}, u32[]{:S(2)}) collective-permute-start(bf16[272,768]{1,0:T(8,128)(2,1)S(1)} %collective-permute-done.2.refs_4_.refs_1_), channel_id=1, source_target_pairs={{0,1},{1,0},{2,3},{3,2},{4,5},{5,4},{6,7},{7,6},{8,9},{9,8},{10,11... | collective-permute-start | bytes 1253384 | tf_op jit(solution)/shard_map/ppermute | solution.py:234
  46.8 5.2 %collective-permute-start.7 = (bf16[272,768]{1,0:T(8,128)(2,1)S(1)}, bf16[272,768]{1,0:T(8,128)(2,1)S(1)}, u32[]{:S(2)}, u32[]{:S(2)}) collective-permute-start(bf16[272,768]{1,0:T(8,128)(2,1)S(1)} %collective-permute-done.1.refs_3_), channel_id=1, source_target_pairs={{0,1},{1,0},{2,3},{3,2},{4,5},{5,4},{6,7},{7,6},{8,9},{9,8},{10,11... | collective-permute-start | bytes 1253384 | tf_op jit(solution)/shard_map/ppermute | solution.py:234
  47.2 4.7 %collective-permute-start.9 = (bf16[272,768]{1,0:T(8,128)(2,1)S(1)}, bf16[272,768]{1,0:T(8,128)(2,1)S(1)}, u32[]{:S(2)}, u32[]{:S(2)}) collective-permute-start(bf16[272,768]{1,0:T(8,128)(2,1)S(1)} %collective-permute-done.3.refs_5_.refs_2_), channel_id=1, source_target_pairs={{0,1},{1,0},{2,3},{3,2},{4,5},{5,4},{6,7},{7,6},{8,9},{9,8},{10,11... | collective-permute-start | bytes 1253384 | tf_op jit(solution)/shard_map/ppermute | solution.py:234
  47.9 4.0 %collective-permute-start.10 = (bf16[272,768]{1,0:T(8,128)(2,1)S(1)}, bf16[272,768]{1,0:T(8,128)(2,1)S(1)}, u32[]{:S(2)}, u32[]{:S(2)}) collective-permute-start(bf16[272,768]{1,0:T(8,128)(2,1)S(1)} %collective-permute-done.4.refs_6_.refs_3_), channel_id=1, source_target_pairs={{0,1},{1,0},{2,3},{3,2},{4,5},{5,4},{6,7},{7,6},{8,9},{9,8},{10,11... | collective-permute-start | bytes 1253384 | tf_op jit(solution)/shard_map/ppermute | solution.py:234
  48.1 1.0 %copy-start = (bf16[272,768]{1,0:T(8,128)(2,1)S(1)}, bf16[272,768]{1,0:T(8,128)(2,1)}, u32[]{:S(2)}) copy-start(bf16[272,768]{1,0:T(8,128)(2,1)} %get-tuple-element.28.refs_1_.refs_2_.refs_3_.refs_4_) | copy-start | bytes 1253380
  49.5 2.4 %copy-start.2 = (bf16[272,768]{1,0:T(8,128)(2,1)S(1)}, bf16[272,768]{1,0:T(8,128)(2,1)}, u32[]{:S(2)}) copy-start(bf16[272,768]{1,0:T(8,128)(2,1)} %get-tuple-element.25.refs_1_.refs_13_) | copy-start | bytes 1253380
  50.4 8.1 %collective-permute-start.13 = (f32[1,1024]{1,0:T(1,128)S(1)}, f32[1,1024]{1,0:T(1,128)S(1)}, u32[]{:S(2)}, u32[]{:S(2)}) collective-permute-start(f32[1,1024]{1,0:T(1,128)S(1)} %compare1_6.1), channel_id=1, source_target_pairs={{0,2},{1,3},{2,0},{3,1},{4,6},{5,7},{6,4},{7,5},{8,10},{9,11},{10,... | collective-permute-start | bytes 12296 | tf_op jit(solution)/shard_map/ppermute | solution.py:234
  56.0 10.3 %copy-start.1 = (s32[1,512]{1,0:T(1,128)S(1)}, s32[1,512]{1,0:T(1,128)}, u32[]{:S(2)}) copy-start(s32[1,512]{1,0:T(1,128)} %get-tuple-element.19.slot_ref) | copy-start | bytes 6148
  58.4 4.5 %collective-permute-start.16 = (f32[1,256]{1,0:T(1,128)S(1)}, f32[1,256]{1,0:T(1,128)S(1)}, u32[]{:S(2)}, u32[]{:S(2)}) collective-permute-start(f32[1,256]{1,0:T(1,128)S(1)} %get-tuple-element.32), channel_id=1, source_target_pairs={{0,8},{1,9},{2,10},{3,11},{4,12},{5,13},{6,14},{7,15},{8,0},{9,1},... | collective-permute-start | bytes 3080 | tf_op jit(solution)/shard_map/ppermute | solution.py:231
  58.5 5.5 %collective-permute-start.15 = (f32[1,256]{1,0:T(1,128)S(1)}, f32[1,256]{1,0:T(1,128)S(1)}, u32[]{:S(2)}, u32[]{:S(2)}) collective-permute-start(f32[1,256]{1,0:T(1,128)S(1)} %get-tuple-element.33), channel_id=1, source_target_pairs={{0,4},{1,5},{2,6},{3,7},{4,8},{5,9},{6,10},{7,11},{8,12},{9,13},{1... | collective-permute-start | bytes 3080 | tf_op jit(solution)/shard_map/ppermute | solution.py:231
  62.7 3.6 %collective-permute-start.14 = (f32[1,256]{1,0:T(1,128)S(1)}, f32[1,256]{1,0:T(1,128)S(1)}, u32[]{:S(2)}, u32[]{:S(2)}) collective-permute-start(f32[1,256]{1,0:T(1,128)S(1)} %get-tuple-element.34), channel_id=1, source_target_pairs={{0,12},{1,13},{2,14},{3,15},{4,0},{5,1},{6,2},{7,3},{8,4},{9,5},{1... | collective-permute-start | bytes 3080 | tf_op jit(solution)/shard_map/ppermute | solution.py:231

commit v10 on v9

--- a/solution.py
+++ b/solution.py
@@ -282,13 +282,16 @@
         across[0] = cross(own[0])
         own[0], own[1] = tie(own[0], own[1])
         beside[0] = core(own[0])
+        some = {(0, k): last for k in range(BLOCKS)} | {(1, 3): opposite, (3, 3): diagonal}
+        (source,) = compare(cap, row, [(0, 1, 3, (1, 3))], some, floor)
         for u in (1, 2):
-            beside[u], across[u] = core(own[u]), cross(own[u])
+            beside[u] = core(own[u])
+            if u == 2:
+                own[2][0], source = tie(own[2][0], source)
+            across[u] = cross(own[u])
         for u in range(3):
             beyond[u] = core(across[u])
         beside[3] = core(own[3])
-        some = {(0, k): last for k in range(BLOCKS)} | {(1, 3): opposite, (3, 3): diagonal}
-        (source,) = compare(cap, row, [(0, 1, 3, (1, 3))], some, floor)
         some = {(0, k): across[k] for k in range(3)}
         some |= {(0, 3): own[3], (1, 3): own[3], (2, 3): beside[3]}
         (theirs,) = compare(cap, row, [(0, 3, 3, (1, 2))], some, floor)

time: 67.6 us -> 69.4 us (1.027)
  waiting for transfers between devices: 37.4 us -> 39.2 us
    ppermute x13, waiting for transfers between devices: 7.22 us -> 9.59 us  [swap(): return lax.ppermute(array, 'blk', [(i, i ^ mask) for i in range(devices)])]
    ppermute x13, starting transfers between devices: 7.54 us -> 8.6 us  [swap(): return lax.ppermute(array, 'blk', [(i, i ^ mask) for i in range(devices)])]
    ppermute x6, starting transfers between devices: 9.14 us -> 8.1 us  [shift(): lax.ppermute(array, 'blk', [(i, (i + step) % devices) for i in range(devi...]
  transfers between devices with their start and end apart: 19 -> 19, of which waited for: 8 -> 7; matrix products, arithmetic and copies ran while one was open for 0% -> 0% of each run, Pallas kernels for 11% -> 11%
where the time goes in v10:
time: 69.4 us; the launch traced here: 69.2 us
  waiting for transfers between devices  39.2 us (56%)
  starting transfers between devices  16.7 us (24%)
  Pallas kernels  12.2 us (18%)
  local copies, waits for them, and re-layouts  1.01 us (1%)
    ppermute x6, waiting for transfers between devices, shift(): lax.ppermute(array, 'blk', [(i, (i + step) % devices) for i in range(devi...  29.6 us
    ppermute x13, waiting for transfers between devices, swap(): return lax.ppermute(array, 'blk', [(i, i ^ mask) for i in range(devices)])  9.59 us
    ppermute x13, starting transfers between devices, swap(): return lax.ppermute(array, 'blk', [(i, i ^ mask) for i in range(devices)])  8.6 us
    ppermute x6, starting transfers between devices, shift(): lax.ppermute(array, 'blk', [(i, (i + step) % devices) for i in range(devi...  8.1 us
    pallas_call x4, Pallas kernels, compare(): pl.pallas_call(lambda *refs: compare_kernel(cap, outs, jobs, names, *refs...  7.63 us
    pallas_call x1, Pallas kernels, pack(): pl.pallas_call(lambda *refs: pack_kernel(groups, cap, units, *refs), in_s...  3.44 us
  transfers between devices with their start and end apart: 19, of which 7 were waited for; matrix products, arithmetic and copies ran while one was open for 0% of the time, Pallas kernels for 11%

profile of v10, /device:TPU:0, one launch (start us, length us, event | category | flops | bytes accessed | tf_op | source)
XLA Modules:
  0.0 69.2 jit_solution(1099948328204396577)
XLA Ops:
  0.0 3.4 %pack.1 = (bf16[272,768]{1,0:T(8,128)(2,1)}, bf16[272,768]{1,0:T(8,128)(2,1)}, bf16[272,768]{1,0:T(8,128)(2,1)}, bf16[272,768]{1,0:T(8,128)(2,1)}, s32[1,512]{1,0:T(1,128)}) custom-call(f32[512,768]{1,0:T(8,128)} %refs_0_.1, s32[1,512]{1,0:T(1,128)} %bitcast.3, s32[1,512]{1,0:T(1,128)} %bitcast.4), custom_call_target="tpu_custom_call" | custom-call | tf_op jit(solution)/shard_map/pack/pallas_call | solution.py:79
  3.4 3.0 %collective-permute-start.2 = (bf16[272,768]{1,0:T(8,128)(2,1)}, bf16[272,768]{1,0:T(8,128)(2,1)S(1)}, u32[]{:S(2)}, u32[]{:S(2)}) collective-permute-start(bf16[272,768]{1,0:T(8,128)(2,1)} %get-tuple-element.31.refs_1_.refs_2_.refs_3_.refs_4_), channel_id=1, source_target_pairs={{0,2},{1,3},{2,0},{3,1},{4,6},{5,7},{6,4},{7,5},{8,10},{9,11},{10,... | collective-permute-start | bytes 1253384 | tf_op jit(solution)/shard_map/ppermute | solution.py:234
  6.5 1.6 %collective-permute-start = (bf16[272,768]{1,0:T(8,128)(2,1)}, bf16[272,768]{1,0:T(8,128)(2,1)S(1)}, u32[]{:S(2)}, u32[]{:S(2)}) collective-permute-start(bf16[272,768]{1,0:T(8,128)(2,1)} %get-tuple-element.25), channel_id=1, source_target_pairs={{0,4},{1,5},{2,6},{3,7},{4,8},{5,9},{6,10},{7,11},{8,12},{9,13},{1... | collective-permute-start | bytes 1253384 | tf_op jit(solution)/shard_map/ppermute | solution.py:231
  8.0 8.3 %collective-permute-done.2.refs_5_ = bf16[272,768]{1,0:T(8,128)(2,1)S(1)} collective-permute-done((bf16[272,768]{1,0:T(8,128)(2,1)}, bf16[272,768]{1,0:T(8,128)(2,1)S(1)}, u32[]{:S(2)}, u32[]{:S(2)}) %collective-permute-start.2) | collective-permute-done | bytes 417824 | tf_op jit(solution)/shard_map/ppermute | solution.py:234
  16.3 0.0 collective-permute-start.3
  16.3 3.3 %collective-permute-done.refs_2_ = bf16[272,768]{1,0:T(8,128)(2,1)S(1)} collective-permute-done((bf16[272,768]{1,0:T(8,128)(2,1)}, bf16[272,768]{1,0:T(8,128)(2,1)S(1)}, u32[]{:S(2)}, u32[]{:S(2)}) %collective-permute-start) | collective-permute-done | bytes 417824 | tf_op jit(solution)/shard_map/ppermute | solution.py:231
  19.6 1.7 %collective-permute-start.1 = (bf16[272,768]{1,0:T(8,128)(2,1)}, bf16[272,768]{1,0:T(8,128)(2,1)S(1)}, u32[]{:S(2)}, u32[]{:S(2)}) collective-permute-start(bf16[272,768]{1,0:T(8,128)(2,1)} %get-tuple-element.29), channel_id=1, source_target_pairs={{0,12},{1,13},{2,14},{3,15},{4,0},{5,1},{6,2},{7,3},{8,4},{9,5},{1... | collective-permute-start | bytes 1253384 | tf_op jit(solution)/shard_map/ppermute | solution.py:231
  21.4 0.0 collective-permute-start.13
  21.4 0.5 collective-permute-start.4
  21.9 1.5 %collective-permute-start.5 = (bf16[272,768]{1,0:T(8,128)(2,1)S(1)}, bf16[272,768]{1,0:T(8,128)(2,1)S(1)}, u32[]{:S(2)}, u32[]{:S(2)}) collective-permute-start(bf16[272,768]{1,0:T(8,128)(2,1)S(1)} %collective-permute-done.refs_2_), channel_id=1, source_target_pairs={{0,2},{1,3},{2,0},{3,1},{4,6},{5,7},{6,4},{7,5},{8,10},{9,11},{10,... | collective-permute-start | bytes 1253384 | tf_op jit(solution)/shard_map/ppermute | solution.py:234
  23.4 0.0 collective-permute-done.3.refs_6_
  23.4 0.0 collective-permute-start.7
  23.4 0.0 copy-start
  23.4 1.0 %copy-done = bf16[272,768]{1,0:T(8,128)(2,1)S(1)} copy-done((bf16[272,768]{1,0:T(8,128)(2,1)S(1)}, bf16[272,768]{1,0:T(8,128)(2,1)}, u32[]{:S(2)}) %copy-start) | copy-done | bytes 417816
  24.4 0.4 compare1_2.1
  24.8 0.0 copy-start.2
  24.8 6.9 %collective-permute-done.1.refs_3_ = bf16[272,768]{1,0:T(8,128)(2,1)S(1)} collective-permute-done((bf16[272,768]{1,0:T(8,128)(2,1)}, bf16[272,768]{1,0:T(8,128)(2,1)S(1)}, u32[]{:S(2)}, u32[]{:S(2)}) %collective-permute-start.1) | collective-permute-done | bytes 417824 | tf_op jit(solution)/shard_map/ppermute | solution.py:231
  31.8 0.5 collective-permute-start.6
  32.3 15.5 %collective-permute-done.13.refs_13_.refs_4_.refs_5_ = bf16[272,768]{1,0:T(8,128)(2,1)S(1)} collective-permute-done((bf16[272,768]{1,0:T(8,128)(2,1)}, bf16[272,768]{1,0:T(8,128)(2,1)S(1)}, u32[]{:S(2)}, u32[]{:S(2)}) %collective-permute-start.13) | collective-permute-done | bytes 417824 | tf_op jit(solution)/shard_map/ppermute | solution.py:231
  47.7 0.0 collective-permute-start.14
  47.8 0.0 collective-permute-done.4.refs_4_.refs_1_
  47.8 0.5 collective-permute-start.8
  48.3 0.0 collective-permute-done.5.refs_5_.refs_2_
  48.3 0.1 collective-permute-start.10
  48.3 0.0 collective-permute-done.7.refs_7_
  48.3 0.4 collective-permute-start.9
  48.8 1.3 %collective-permute-done.6.refs_6_.refs_3_ = bf16[272,768]{1,0:T(8,128)(2,1)S(1)} collective-permute-done((bf16[272,768]{1,0:T(8,128)(2,1)S(1)}, bf16[272,768]{1,0:T(8,128)(2,1)S(1)}, u32[]{:S(2)}, u32[]{:S(2)}) %collective-permute-start.6) | collective-permute-done | bytes 417824 | tf_op jit(solution)/shard_map/ppermute | solution.py:234
  50.1 0.0 collective-permute-start.11
  50.1 0.0 collective-permute-done.14.refs_14_.refs_6_
  50.1 0.5 collective-permute-start.12
  50.6 0.8 %compare1_6.1 = f32[1,1024]{1,0:T(1,128)S(1)} custom-call(f32[1,1024]{1,0:T(1,128)S(1)} %broadcast_in_dim.3.refs_0_, bf16[272,768]{1,0:T(8,128)(2,1)S(1)} %collective-permute-done.4.refs_4_.refs_1_, bf16[272,768]{1,0:T(8,128)(2,1)S(1)} %collective-permute-done.5.refs_5_.refs_2_, bf16[272,768]{1,0:T(8,128)(2,1)S(1)} %collective-permute-done.6.refs_6_.refs_3_, ...), custom_call_target="tpu_custom_call" | custom-call | flops 603979776 | tf_op jit(solution)/shard_map/compare1_6/pallas_call | solution.py:177
  51.4 0.0 collective-permute-done.8.refs_8_
  51.4 1.6 %collective-permute-start.15 = (f32[1,1024]{1,0:T(1,128)S(1)}, f32[1,1024]{1,0:T(1,128)S(1)}, u32[]{:S(2)}, u32[]{:S(2)}) collective-permute-start(f32[1,1024]{1,0:T(1,128)S(1)} %compare1_6.1), channel_id=1, source_target_pairs={{0,2},{1,3},{2,0},{3,1},{4,6},{5,7},{6,4},{7,5},{8,10},{9,11},{10,... | collective-permute-start | bytes 12296 | tf_op jit(solution)/shard_map/ppermute | solution.py:234
  53.0 0.0 collective-permute-done.10.refs_10_
  53.0 0.0 collective-permute-done.9.refs_9_
  53.0 0.0 collective-permute-done.11.refs_11_
  53.0 0.0 collective-permute-done.12.refs_12_
  53.0 0.0 copy-done.2
  53.0 4.0 %compare3_36.1.refs_0_ = f32[1,1024]{1,0:T(1,128)S(1)} custom-call(f32[1,1024]{1,0:T(1,128)S(1)} %broadcast_in_dim.3.refs_0_, bf16[272,768]{1,0:T(8,128)(2,1)S(1)} %copy-done.2, bf16[272,768]{1,0:T(8,128)(2,1)S(1)} %collective-permute-done.refs_2_, bf16[272,768]{1,0:T(8,128)(2,1)S(1)} %collective-permute-done.1.refs_3_, ...), custom_call_target="tpu_custom_call" | custom-call | flops 3623878656 | tf_op jit(solution)/shard_map/compare3_36/pallas_call | solution.py:177
  57.1 0.0 copy-start.1
  57.1 2.3 %compare4_20.1 = (f32[1,256]{1,0:T(1,128)S(1)}, f32[1,256]{1,0:T(1,128)S(1)}, f32[1,256]{1,0:T(1,128)S(1)}, f32[1,256]{1,0:T(1,128)S(1)}) custom-call(f32[1,1024]{1,0:T(1,128)S(1)} %compare3_36.1.refs_0_, bf16[272,768]{1,0:T(8,128)(2,1)S(1)} %copy-done.2, bf16[272,768]{1,0:T(8,128)(2,1)S(1)} %collective-permute-done.refs_2_, ...), custom_call_target="tpu_custom_call" | custom-call | flops 2013265920 | tf_op jit(solution)/shard_map/compare4_20/pallas_call | solution.py:177
  59.4 2.7 %collective-permute-start.18 = (f32[1,256]{1,0:T(1,128)S(1)}, f32[1,256]{1,0:T(1,128)S(1)}, u32[]{:S(2)}, u32[]{:S(2)}) collective-permute-start(f32[1,256]{1,0:T(1,128)S(1)} %get-tuple-element.35), channel_id=1, source_target_pairs={{0,8},{1,9},{2,10},{3,11},{4,12},{5,13},{6,14},{7,15},{8,0},{9,1},... | collective-permute-start | bytes 3080 | tf_op jit(solution)/shard_map/ppermute | solution.py:231
  62.1 0.0 collective-permute-done.15
  62.1 0.6 collective-permute-start.16
  62.7 1.5 %collective-permute-start.17 = (f32[1,256]{1,0:T(1,128)S(1)}, f32[1,256]{1,0:T(1,128)S(1)}, u32[]{:S(2)}, u32[]{:S(2)}) collective-permute-start(f32[1,256]{1,0:T(1,128)S(1)} %get-tuple-element.37), channel_id=1, source_target_pairs={{0,4},{1,5},{2,6},{3,7},{4,8},{5,9},{6,10},{7,11},{8,12},{9,13},{1... | collective-permute-start | bytes 3080 | tf_op jit(solution)/shard_map/ppermute | solution.py:231
  64.2 0.0 collective-permute-done.18
  64.2 1.5 %collective-permute-done.16.refs_1_ = f32[1,256]{1,0:T(1,128)S(1)} collective-permute-done((f32[1,256]{1,0:T(1,128)S(1)}, f32[1,256]{1,0:T(1,128)S(1)}, u32[]{:S(2)}, u32[]{:S(2)}) %collective-permute-start.16) | collective-permute-done | bytes 1056 | tf_op jit(solution)/shard_map/ppermute | solution.py:231
  65.8 2.3 %collective-permute-done.17.refs_2_ = f32[1,256]{1,0:T(1,128)S(1)} collective-permute-done((f32[1,256]{1,0:T(1,128)S(1)}, f32[1,256]{1,0:T(1,128)S(1)}, u32[]{:S(2)}, u32[]{:S(2)}) %collective-permute-start.17) | collective-permute-done | bytes 1056 | tf_op jit(solution)/shard_map/ppermute | solution.py:231
  68.1 0.0 copy-done.1
  68.1 1.1 %unpack.1 = f32[1,512]{1,0:T(1,128)} custom-call(s32[1,512]{1,0:T(1,128)S(1)} %copy-done.1, f32[1,256]{1,0:T(1,128)S(1)} %get-tuple-element.39.refs_0_, f32[1,256]{1,0:T(1,128)S(1)} %collective-permute-done.16.refs_1_, f32[1,256]{1,0:T(1,128)S(1)} %collective-permute-done.17.refs_2_, f32[1,256]{1,0:T(1,128)S(1)} %slice_maximum_fusion.3.refs_3_), custom_call_target="tpu_custom_call" | custom-call | tf_op jit(solution)/shard_map/unpack/pallas_call | solution.py:207
  (3 shorter events, 0.0 us)
Async XLA Ops:
  3.4 12.9 %collective-permute-start.2 = (bf16[272,768]{1,0:T(8,128)(2,1)}, bf16[272,768]{1,0:T(8,128)(2,1)S(1)}, u32[]{:S(2)}, u32[]{:S(2)}) collective-permute-start(bf16[272,768]{1,0:T(8,128)(2,1)} %get-tuple-element.31.refs_1_.refs_2_.refs_3_.refs_4_), channel_id=1, source_target_pairs={{0,2},{1,3},{2,0},{3,1},{4,6},{5,7},{6,4},{7,5},{8,10},{9,11},{10,... | collective-permute-start | bytes 1253384 | tf_op jit(solution)/shard_map/ppermute | solution.py:234
  6.5 13.2 %collective-permute-start = (bf16[272,768]{1,0:T(8,128)(2,1)}, bf16[272,768]{1,0:T(8,128)(2,1)S(1)}, u32[]{:S(2)}, u32[]{:S(2)}) collective-permute-start(bf16[272,768]{1,0:T(8,128)(2,1)} %get-tuple-element.25), channel_id=1, source_target_pairs={{0,4},{1,5},{2,6},{3,7},{4,8},{5,9},{6,10},{7,11},{8,12},{9,13},{1... | collective-permute-start | bytes 1253384 | tf_op jit(solution)/shard_map/ppermute | solution.py:231
  16.3 7.1 %collective-permute-start.3 = (bf16[272,768]{1,0:T(8,128)(2,1)S(1)}, bf16[272,768]{1,0:T(8,128)(2,1)S(1)}, u32[]{:S(2)}, u32[]{:S(2)}) collective-permute-start(bf16[272,768]{1,0:T(8,128)(2,1)S(1)} %collective-permute-done.2.refs_5_), channel_id=1, source_target_pairs={{0,1},{1,0},{2,3},{3,2},{4,5},{5,4},{6,7},{7,6},{8,9},{9,8},{10,11... | collective-permute-start | bytes 1253384 | tf_op jit(solution)/shard_map/ppermute | solution.py:234
  19.6 12.2 %collective-permute-start.1 = (bf16[272,768]{1,0:T(8,128)(2,1)}, bf16[272,768]{1,0:T(8,128)(2,1)S(1)}, u32[]{:S(2)}, u32[]{:S(2)}) collective-permute-start(bf16[272,768]{1,0:T(8,128)(2,1)} %get-tuple-element.29), channel_id=1, source_target_pairs={{0,12},{1,13},{2,14},{3,15},{4,0},{5,1},{6,2},{7,3},{8,4},{9,5},{1... | collective-permute-start | bytes 1253384 | tf_op jit(solution)/shard_map/ppermute | solution.py:231
  21.4 26.4 %collective-permute-start.13 = (bf16[272,768]{1,0:T(8,128)(2,1)}, bf16[272,768]{1,0:T(8,128)(2,1)S(1)}, u32[]{:S(2)}, u32[]{:S(2)}) collective-permute-start(bf16[272,768]{1,0:T(8,128)(2,1)} %get-tuple-element.31.refs_1_.refs_2_.refs_3_.refs_4_), channel_id=1, source_target_pairs={{0,8},{1,9},{2,10},{3,11},{4,12},{5,13},{6,14},{7,15},{8,0},{9,1},... | collective-permute-start | bytes 1253384 | tf_op jit(solution)/shard_map/ppermute | solution.py:231
  21.4 26.4 %collective-permute-start.4 = (bf16[272,768]{1,0:T(8,128)(2,1)}, bf16[272,768]{1,0:T(8,128)(2,1)S(1)}, u32[]{:S(2)}, u32[]{:S(2)}) collective-permute-start(bf16[272,768]{1,0:T(8,128)(2,1)} %get-tuple-element.27.refs_1_.refs_13_), channel_id=1, source_target_pairs={{0,2},{1,3},{2,0},{3,1},{4,6},{5,7},{6,4},{7,5},{8,10},{9,11},{10,... | collective-permute-start | bytes 1253384 | tf_op jit(solution)/shard_map/ppermute | solution.py:234
  21.9 26.4 %collective-permute-start.5 = (bf16[272,768]{1,0:T(8,128)(2,1)S(1)}, bf16[272,768]{1,0:T(8,128)(2,1)S(1)}, u32[]{:S(2)}, u32[]{:S(2)}) collective-permute-start(bf16[272,768]{1,0:T(8,128)(2,1)S(1)} %collective-permute-done.refs_2_), channel_id=1, source_target_pairs={{0,2},{1,3},{2,0},{3,1},{4,6},{5,7},{6,4},{7,5},{8,10},{9,11},{10,... | collective-permute-start | bytes 1253384 | tf_op jit(solution)/shard_map/ppermute | solution.py:234
  23.4 24.9 %collective-permute-start.7 = (bf16[272,768]{1,0:T(8,128)(2,1)}, bf16[272,768]{1,0:T(8,128)(2,1)S(1)}, u32[]{:S(2)}, u32[]{:S(2)}) collective-permute-start(bf16[272,768]{1,0:T(8,128)(2,1)} %get-tuple-element.27.refs_1_.refs_13_), channel_id=1, source_target_pairs={{0,1},{1,0},{2,3},{3,2},{4,5},{5,4},{6,7},{7,6},{8,9},{9,8},{10,11... | collective-permute-start | bytes 1253384 | tf_op jit(solution)/shard_map/ppermute | solution.py:234
  23.4 1.0 %copy-start = (bf16[272,768]{1,0:T(8,128)(2,1)S(1)}, bf16[272,768]{1,0:T(8,128)(2,1)}, u32[]{:S(2)}) copy-start(bf16[272,768]{1,0:T(8,128)(2,1)} %get-tuple-element.31.refs_1_.refs_2_.refs_3_.refs_4_) | copy-start | bytes 1253380
  24.8 28.2 %copy-start.2 = (bf16[272,768]{1,0:T(8,128)(2,1)S(1)}, bf16[272,768]{1,0:T(8,128)(2,1)}, u32[]{:S(2)}) copy-start(bf16[272,768]{1,0:T(8,128)(2,1)} %get-tuple-element.27.refs_1_.refs_13_) | copy-start | bytes 1253380
  31.8 18.3 %collective-permute-start.6 = (bf16[272,768]{1,0:T(8,128)(2,1)S(1)}, bf16[272,768]{1,0:T(8,128)(2,1)S(1)}, u32[]{:S(2)}, u32[]{:S(2)}) collective-permute-start(bf16[272,768]{1,0:T(8,128)(2,1)S(1)} %collective-permute-done.1.refs_3_), channel_id=1, source_target_pairs={{0,2},{1,3},{2,0},{3,1},{4,6},{5,7},{6,4},{7,5},{8,10},{9,11},{10,... | collective-permute-start | bytes 1253384 | tf_op jit(solution)/shard_map/ppermute | solution.py:234
  47.7 2.3 %collective-permute-start.14 = (bf16[272,768]{1,0:T(8,128)(2,1)S(1)}, bf16[272,768]{1,0:T(8,128)(2,1)S(1)}, u32[]{:S(2)}, u32[]{:S(2)}) collective-permute-start(bf16[272,768]{1,0:T(8,128)(2,1)S(1)} %collective-permute-done.13.refs_13_.refs_4_.refs_5_), channel_id=1, source_target_pairs={{0,1},{1,0},{2,3},{3,2},{4,5},{5,4},{6,7},{7,6},{8,9},{9,8},{10,11... | collective-permute-start | bytes 1253384 | tf_op jit(solution)/shard_map/ppermute | solution.py:234
  47.8 3.7 %collective-permute-start.8 = (bf16[272,768]{1,0:T(8,128)(2,1)S(1)}, bf16[272,768]{1,0:T(8,128)(2,1)S(1)}, u32[]{:S(2)}, u32[]{:S(2)}) collective-permute-start(bf16[272,768]{1,0:T(8,128)(2,1)S(1)} %collective-permute-done.refs_2_), channel_id=1, source_target_pairs={{0,1},{1,0},{2,3},{3,2},{4,5},{5,4},{6,7},{7,6},{8,9},{9,8},{10,11... | collective-permute-start | bytes 1253384 | tf_op jit(solution)/shard_map/ppermute | solution.py:234
  48.3 4.7 %collective-permute-start.10 = (bf16[272,768]{1,0:T(8,128)(2,1)S(1)}, bf16[272,768]{1,0:T(8,128)(2,1)S(1)}, u32[]{:S(2)}, u32[]{:S(2)}) collective-permute-start(bf16[272,768]{1,0:T(8,128)(2,1)S(1)} %collective-permute-done.4.refs_4_.refs_1_), channel_id=1, source_target_pairs={{0,1},{1,0},{2,3},{3,2},{4,5},{5,4},{6,7},{7,6},{8,9},{9,8},{10,11... | collective-permute-start | bytes 1253384 | tf_op jit(solution)/shard_map/ppermute | solution.py:234
  48.3 4.7 %collective-permute-start.9 = (bf16[272,768]{1,0:T(8,128)(2,1)S(1)}, bf16[272,768]{1,0:T(8,128)(2,1)S(1)}, u32[]{:S(2)}, u32[]{:S(2)}) collective-permute-start(bf16[272,768]{1,0:T(8,128)(2,1)S(1)} %collective-permute-done.1.refs_3_), channel_id=1, source_target_pairs={{0,1},{1,0},{2,3},{3,2},{4,5},{5,4},{6,7},{7,6},{8,9},{9,8},{10,11... | collective-permute-start | bytes 1253384 | tf_op jit(solution)/shard_map/ppermute | solution.py:234
  50.1 2.9 %collective-permute-start.11 = (bf16[272,768]{1,0:T(8,128)(2,1)S(1)}, bf16[272,768]{1,0:T(8,128)(2,1)S(1)}, u32[]{:S(2)}, u32[]{:S(2)}) collective-permute-start(bf16[272,768]{1,0:T(8,128)(2,1)S(1)} %collective-permute-done.5.refs_5_.refs_2_), channel_id=1, source_target_pairs={{0,1},{1,0},{2,3},{3,2},{4,5},{5,4},{6,7},{7,6},{8,9},{9,8},{10,11... | collective-permute-start | bytes 1253384 | tf_op jit(solution)/shard_map/ppermute | solution.py:234
  50.1 2.9 %collective-permute-start.12 = (bf16[272,768]{1,0:T(8,128)(2,1)S(1)}, bf16[272,768]{1,0:T(8,128)(2,1)S(1)}, u32[]{:S(2)}, u32[]{:S(2)}) collective-permute-start(bf16[272,768]{1,0:T(8,128)(2,1)S(1)} %collective-permute-done.6.refs_6_.refs_3_), channel_id=1, source_target_pairs={{0,1},{1,0},{2,3},{3,2},{4,5},{5,4},{6,7},{7,6},{8,9},{9,8},{10,11... | collective-permute-start | bytes 1253384 | tf_op jit(solution)/shard_map/ppermute | solution.py:234
  51.4 10.7 %collective-permute-start.15 = (f32[1,1024]{1,0:T(1,128)S(1)}, f32[1,1024]{1,0:T(1,128)S(1)}, u32[]{:S(2)}, u32[]{:S(2)}) collective-permute-start(f32[1,1024]{1,0:T(1,128)S(1)} %compare1_6.1), channel_id=1, source_target_pairs={{0,2},{1,3},{2,0},{3,1},{4,6},{5,7},{6,4},{7,5},{8,10},{9,11},{10,... | collective-permute-start | bytes 12296 | tf_op jit(solution)/shard_map/ppermute | solution.py:234
  57.1 11.0 %copy-start.1 = (s32[1,512]{1,0:T(1,128)S(1)}, s32[1,512]{1,0:T(1,128)}, u32[]{:S(2)}) copy-start(s32[1,512]{1,0:T(1,128)} %get-tuple-element.21.slot_ref) | copy-start | bytes 6148
  59.4 4.8 %collective-permute-start.18 = (f32[1,256]{1,0:T(1,128)S(1)}, f32[1,256]{1,0:T(1,128)S(1)}, u32[]{:S(2)}, u32[]{:S(2)}) collective-permute-start(f32[1,256]{1,0:T(1,128)S(1)} %get-tuple-element.35), channel_id=1, source_target_pairs={{0,8},{1,9},{2,10},{3,11},{4,12},{5,13},{6,14},{7,15},{8,0},{9,1},... | collective-permute-start | bytes 3080 | tf_op jit(solution)/shard_map/ppermute | solution.py:231
  62.1 3.6 %collective-permute-start.16 = (f32[1,256]{1,0:T(1,128)S(1)}, f32[1,256]{1,0:T(1,128)S(1)}, u32[]{:S(2)}, u32[]{:S(2)}) collective-permute-start(f32[1,256]{1,0:T(1,128)S(1)} %get-tuple-element.38), channel_id=1, source_target_pairs={{0,12},{1,13},{2,14},{3,15},{4,0},{5,1},{6,2},{7,3},{8,4},{9,5},{1... | collective-permute-start | bytes 3080 | tf_op jit(solution)/shard_map/ppermute | solution.py:231
  62.7 5.4 %collective-permute-start.17 = (f32[1,256]{1,0:T(1,128)S(1)}, f32[1,256]{1,0:T(1,128)S(1)}, u32[]{:S(2)}, u32[]{:S(2)}) collective-permute-start(f32[1,256]{1,0:T(1,128)S(1)} %get-tuple-element.37), channel_id=1, source_target_pairs={{0,4},{1,5},{2,6},{3,7},{4,8},{5,9},{6,10},{7,11},{8,12},{9,13},{1... | collective-permute-start | bytes 3080 | tf_op jit(solution)/shard_map/ppermute | solution.py:231

commit v11 on v9

--- a/solution.py
+++ b/solution.py
@@ -287,8 +287,6 @@
         for u in range(3):
             beyond[u] = core(across[u])
         beside[3] = core(own[3])
-        some = {(0, k): last for k in range(BLOCKS)} | {(1, 3): opposite, (3, 3): diagonal}
-        (source,) = compare(cap, row, [(0, 1, 3, (1, 3))], some, floor)
         some = {(0, k): across[k] for k in range(3)}
         some |= {(0, 3): own[3], (1, 3): own[3], (2, 3): beside[3]}
         (theirs,) = compare(cap, row, [(0, 3, 3, (1, 2))], some, floor)
@@ -301,6 +299,10 @@
         for k in range(3):
             best[k] = jnp.maximum(best[k], mine[:, k * cap : (k + 1) * cap])
         backs = [exchange(b, low, 1, -1) for b, (low, _) in zip(best, pieces)]
+        floor, best[0] = tie(floor, best[0])
+        backs[0] = best[0]
+        some = {(0, k): last for k in range(BLOCKS)} | {(1, 3): opposite, (3, 3): diagonal}
+        (source,) = compare(cap, row, [(0, 1, 3, (1, 3))], some, floor)
         backs[3] = jnp.maximum(backs[3], source[:, :cap])
         return unpack(slot, backs).reshape(rows)
 

time: 67.6 us -> 67.6 us (level)
  local copies, waits for them, and re-layouts: 1.02 us -> 0.02 us
  starting transfers between devices: 16.7 us -> 17.4 us
    ppermute x6, waiting for transfers between devices: 30.2 us -> 36.4 us  [shift(): lax.ppermute(array, 'blk', [(i, (i + step) % devices) for i in range(devi...]
    ppermute x13, waiting for transfers between devices: 7.22 us -> 1.31 us  [swap(): return lax.ppermute(array, 'blk', [(i, i ^ mask) for i in range(devices)])]
    unnamed x6, local copies, waits for them, and re-layouts: 1.01 us -> 0.01 us
  transfers between devices with their start and end apart: 19 -> 19, of which waited for: 8 -> 5; matrix products, arithmetic and copies ran while one was open for 0% -> 0% of each run, Pallas kernels for 11% -> 11%
where the time goes in v11:
time: 67.6 us; the launch traced here: 67.4 us
  waiting for transfers between devices  37.7 us (56%)
  starting transfers between devices  17.4 us (26%)
  Pallas kernels  12.1 us (18%)
    ppermute x6, waiting for transfers between devices, shift(): lax.ppermute(array, 'blk', [(i, (i + step) % devices) for i in range(devi...  36.4 us
    ppermute x6, starting transfers between devices, shift(): lax.ppermute(array, 'blk', [(i, (i + step) % devices) for i in range(devi...  9.53 us
    ppermute x13, starting transfers between devices, swap(): return lax.ppermute(array, 'blk', [(i, i ^ mask) for i in range(devices)])  7.87 us
    pallas_call x4, Pallas kernels, compare(): pl.pallas_call(lambda *refs: compare_kernel(cap, outs, jobs, names, *refs...  7.62 us
    pallas_call x1, Pallas kernels, pack(): pl.pallas_call(lambda *refs: pack_kernel(groups, cap, units, *refs), in_s...  3.44 us
  transfers between devices with their start and end apart: 19, of which 5 were waited for; matrix products, arithmetic and copies ran while one was open for 0% of the time, Pallas kernels for 11%

profile of v11, /device:TPU:0, one launch (start us, length us, event | category | flops | bytes accessed | tf_op | source)
XLA Modules:
  0.0 67.4 jit_solution(12372273513217980335)
XLA Ops:
  0.0 3.4 %pack.1 = (bf16[272,768]{1,0:T(8,128)(2,1)}, bf16[272,768]{1,0:T(8,128)(2,1)}, bf16[272,768]{1,0:T(8,128)(2,1)}, bf16[272,768]{1,0:T(8,128)(2,1)}, s32[1,512]{1,0:T(1,128)}) custom-call(f32[512,768]{1,0:T(8,128)} %refs_0_.1, s32[1,512]{1,0:T(1,128)} %bitcast.3, s32[1,512]{1,0:T(1,128)} %bitcast.4), custom_call_target="tpu_custom_call" | custom-call | tf_op jit(solution)/shard_map/pack/pallas_call | solution.py:79
  3.4 0.0 copy-start.2
  3.5 3.1 %collective-permute-start = (bf16[272,768]{1,0:T(8,128)(2,1)}, bf16[272,768]{1,0:T(8,128)(2,1)S(1)}, u32[]{:S(2)}, u32[]{:S(2)}) collective-permute-start(bf16[272,768]{1,0:T(8,128)(2,1)} %get-tuple-element.25), channel_id=1, source_target_pairs={{0,4},{1,5},{2,6},{3,7},{4,8},{5,9},{6,10},{7,11},{8,12},{9,13},{1... | collective-permute-start | bytes 1253384 | tf_op jit(solution)/shard_map/ppermute | solution.py:231
  6.5 1.5 %collective-permute-start.2 = (bf16[272,768]{1,0:T(8,128)(2,1)}, bf16[272,768]{1,0:T(8,128)(2,1)S(1)}, u32[]{:S(2)}, u32[]{:S(2)}) collective-permute-start(bf16[272,768]{1,0:T(8,128)(2,1)} %get-tuple-element.27.refs_1_.refs_13_), channel_id=1, source_target_pairs={{0,2},{1,3},{2,0},{3,1},{4,6},{5,7},{6,4},{7,5},{8,10},{9,11},{10,... | collective-permute-start | bytes 1253384 | tf_op jit(solution)/shard_map/ppermute | solution.py:234
  8.0 10.4 %collective-permute-done.refs_2_ = bf16[272,768]{1,0:T(8,128)(2,1)S(1)} collective-permute-done((bf16[272,768]{1,0:T(8,128)(2,1)}, bf16[272,768]{1,0:T(8,128)(2,1)S(1)}, u32[]{:S(2)}, u32[]{:S(2)}) %collective-permute-start) | collective-permute-done | bytes 417824 | tf_op jit(solution)/shard_map/ppermute | solution.py:231
  18.4 1.7 %collective-permute-start.1 = (bf16[272,768]{1,0:T(8,128)(2,1)}, bf16[272,768]{1,0:T(8,128)(2,1)S(1)}, u32[]{:S(2)}, u32[]{:S(2)}) collective-permute-start(bf16[272,768]{1,0:T(8,128)(2,1)} %get-tuple-element.29), channel_id=1, source_target_pairs={{0,12},{1,13},{2,14},{3,15},{4,0},{5,1},{6,2},{7,3},{8,4},{9,5},{1... | collective-permute-start | bytes 1253384 | tf_op jit(solution)/shard_map/ppermute | solution.py:231
  20.2 0.0 collective-permute-start.11
  20.2 1.5 %collective-permute-start.17 = (bf16[272,768]{1,0:T(8,128)(2,1)}, bf16[272,768]{1,0:T(8,128)(2,1)S(1)}, u32[]{:S(2)}, u32[]{:S(2)}) collective-permute-start(bf16[272,768]{1,0:T(8,128)(2,1)} %get-tuple-element.30.refs_1_.refs_2_.refs_3_.refs_4_), channel_id=1, source_target_pairs={{0,2},{1,3},{2,0},{3,1},{4,6},{5,7},{6,4},{7,5},{8,10},{9,11},{10,... | collective-permute-start | bytes 1253384 | tf_op jit(solution)/shard_map/ppermute | solution.py:234
  21.7 0.0 collective-permute-start.5
  21.7 0.0 collective-permute-done.2.refs_4_.refs_1_
  21.7 0.5 collective-permute-start.3
  22.2 8.7 %collective-permute-done.1.refs_3_ = bf16[272,768]{1,0:T(8,128)(2,1)S(1)} collective-permute-done((bf16[272,768]{1,0:T(8,128)(2,1)}, bf16[272,768]{1,0:T(8,128)(2,1)S(1)}, u32[]{:S(2)}, u32[]{:S(2)}) %collective-permute-start.1) | collective-permute-done | bytes 417824 | tf_op jit(solution)/shard_map/ppermute | solution.py:231
  30.9 1.2 %collective-permute-start.4 = (bf16[272,768]{1,0:T(8,128)(2,1)S(1)}, bf16[272,768]{1,0:T(8,128)(2,1)S(1)}, u32[]{:S(2)}, u32[]{:S(2)}) collective-permute-start(bf16[272,768]{1,0:T(8,128)(2,1)S(1)} %collective-permute-done.1.refs_3_), channel_id=1, source_target_pairs={{0,2},{1,3},{2,0},{3,1},{4,6},{5,7},{6,4},{7,5},{8,10},{9,11},{10,... | collective-permute-start | bytes 1253384 | tf_op jit(solution)/shard_map/ppermute | solution.py:234
  32.1 14.1 %collective-permute-done.11.refs_13_.refs_4_.refs_5_ = bf16[272,768]{1,0:T(8,128)(2,1)S(1)} collective-permute-done((bf16[272,768]{1,0:T(8,128)(2,1)}, bf16[272,768]{1,0:T(8,128)(2,1)S(1)}, u32[]{:S(2)}, u32[]{:S(2)}) %collective-permute-start.11) | collective-permute-done | bytes 417824 | tf_op jit(solution)/shard_map/ppermute | solution.py:231
  46.2 0.0 collective-permute-start.12
  46.2 0.0 collective-permute-done.17.refs_5_
  46.2 0.5 collective-permute-start.6
  46.7 0.0 collective-permute-done.5.refs_7_
  46.7 0.1 collective-permute-start.8
  46.8 0.0 collective-permute-done.3.refs_5_.refs_2_
  46.8 0.4 collective-permute-start.7
  47.2 1.3 %collective-permute-done.4.refs_6_.refs_3_ = bf16[272,768]{1,0:T(8,128)(2,1)S(1)} collective-permute-done((bf16[272,768]{1,0:T(8,128)(2,1)S(1)}, bf16[272,768]{1,0:T(8,128)(2,1)S(1)}, u32[]{:S(2)}, u32[]{:S(2)}) %collective-permute-start.4) | collective-permute-done | bytes 417824 | tf_op jit(solution)/shard_map/ppermute | solution.py:234
  48.5 0.0 collective-permute-start.9
  48.5 0.0 collective-permute-done.12.refs_14_.refs_6_
  48.5 0.5 collective-permute-start.10
  49.0 0.8 %compare1_6.1 = f32[1,1024]{1,0:T(1,128)S(1)} custom-call(f32[1,1024]{1,0:T(1,128)S(1)} %broadcast_in_dim.3.refs_0_, bf16[272,768]{1,0:T(8,128)(2,1)S(1)} %collective-permute-done.2.refs_4_.refs_1_, bf16[272,768]{1,0:T(8,128)(2,1)S(1)} %collective-permute-done.3.refs_5_.refs_2_, bf16[272,768]{1,0:T(8,128)(2,1)S(1)} %collective-permute-done.4.refs_6_.refs_3_, ...), custom_call_target="tpu_custom_call" | custom-call | flops 603979776 | tf_op jit(solution)/shard_map/compare1_6/pallas_call | solution.py:177
  49.9 0.0 collective-permute-done.6.refs_8_
  49.9 0.1 collective-permute-start.18
  50.0 0.0 collective-permute-done.8.refs_10_
  50.0 1.6 %collective-permute-start.13 = (f32[1,1024]{1,0:T(1,128)S(1)}, f32[1,1024]{1,0:T(1,128)S(1)}, u32[]{:S(2)}, u32[]{:S(2)}) collective-permute-start(f32[1,1024]{1,0:T(1,128)S(1)} %compare1_6.1), channel_id=1, source_target_pairs={{0,2},{1,3},{2,0},{3,1},{4,6},{5,7},{6,4},{7,5},{8,10},{9,11},{10,... | collective-permute-start | bytes 12296 | tf_op jit(solution)/shard_map/ppermute | solution.py:234
  51.5 0.0 collective-permute-done.9.refs_11_
  51.5 0.0 collective-permute-done.7.refs_9_
  51.5 0.0 collective-permute-done.10.refs_12_
  51.5 0.0 copy-done.2
  51.5 4.0 %compare3_36.1.refs_0_ = f32[1,1024]{1,0:T(1,128)S(1)} custom-call(f32[1,1024]{1,0:T(1,128)S(1)} %broadcast_in_dim.3.refs_0_, bf16[272,768]{1,0:T(8,128)(2,1)S(1)} %copy-done.2, bf16[272,768]{1,0:T(8,128)(2,1)S(1)} %collective-permute-done.refs_2_, bf16[272,768]{1,0:T(8,128)(2,1)S(1)} %collective-permute-done.1.refs_3_, ...), custom_call_target="tpu_custom_call" | custom-call | flops 3623878656 | tf_op jit(solution)/shard_map/compare3_36/pallas_call | solution.py:177
  55.6 0.0 copy-start
  55.6 2.3 %compare4_20.1 = (f32[1,256]{1,0:T(1,128)S(1)}, f32[1,256]{1,0:T(1,128)S(1)}, f32[1,256]{1,0:T(1,128)S(1)}, f32[1,256]{1,0:T(1,128)S(1)}) custom-call(f32[1,1024]{1,0:T(1,128)S(1)} %compare3_36.1.refs_0_, bf16[272,768]{1,0:T(8,128)(2,1)S(1)} %copy-done.2, bf16[272,768]{1,0:T(8,128)(2,1)S(1)} %collective-permute-done.refs_2_, ...), custom_call_target="tpu_custom_call" | custom-call | flops 2013265920 | tf_op jit(solution)/shard_map/compare4_20/pallas_call | solution.py:177
  58.0 0.0 copy-start.1
  58.0 0.0 collective-permute-done.13
  58.0 0.8 %collective-permute-start.15 = (f32[1,256]{1,0:T(1,128)S(1)}, f32[1,256]{1,0:T(1,128)S(1)}, u32[]{:S(2)}, u32[]{:S(2)}) collective-permute-start(f32[1,256]{1,0:T(1,128)S(1)} %get-tuple-element.37), channel_id=1, source_target_pairs={{0,4},{1,5},{2,6},{3,7},{4,8},{5,9},{6,10},{7,11},{8,12},{9,13},{1... | collective-permute-start | bytes 3080 | tf_op jit(solution)/shard_map/ppermute | solution.py:231
  58.8 3.1 %collective-permute-start.14 = (f32[1,256]{1,0:T(1,128)S(1)}, f32[1,256]{1,0:T(1,128)S(1)}, u32[]{:S(2)}, u32[]{:S(2)}) collective-permute-start(f32[1,256]{1,0:T(1,128)S(1)} %get-tuple-element.38), channel_id=1, source_target_pairs={{0,12},{1,13},{2,14},{3,15},{4,0},{5,1},{6,2},{7,3},{8,4},{9,5},{1... | collective-permute-start | bytes 3080 | tf_op jit(solution)/shard_map/ppermute | solution.py:231
  61.9 0.8 %collective-permute-start.16 = (f32[1,256]{1,0:T(1,128)S(1)}, f32[1,256]{1,0:T(1,128)S(1)}, u32[]{:S(2)}, u32[]{:S(2)}) collective-permute-start(f32[1,256]{1,0:T(1,128)S(1)} %get-tuple-element.35), channel_id=1, source_target_pairs={{0,8},{1,9},{2,10},{3,11},{4,12},{5,13},{6,14},{7,15},{8,0},{9,1},... | collective-permute-start | bytes 3080 | tf_op jit(solution)/shard_map/ppermute | solution.py:231
  62.7 0.0 collective-permute-done.18.refs_6_
  62.7 0.0 copy-done
  62.7 0.4 compare1_2.1
  63.1 3.2 %collective-permute-done.16 = f32[1,256]{1,0:T(1,128)S(1)} collective-permute-done((f32[1,256]{1,0:T(1,128)S(1)}, f32[1,256]{1,0:T(1,128)S(1)}, u32[]{:S(2)}, u32[]{:S(2)}) %collective-permute-start.16) | collective-permute-done | bytes 1056 | tf_op jit(solution)/shard_map/ppermute | solution.py:231
  66.3 0.0 collective-permute-done.15.refs_2_
  66.3 0.0 collective-permute-done.14.refs_1_
  66.3 0.0 copy-done.1
  66.4 1.1 %unpack.1 = f32[1,512]{1,0:T(1,128)} custom-call(s32[1,512]{1,0:T(1,128)S(1)} %copy-done.1, f32[1,256]{1,0:T(1,128)S(1)} %get-tuple-element.32.refs_0_, f32[1,256]{1,0:T(1,128)S(1)} %collective-permute-done.14.refs_1_, f32[1,256]{1,0:T(1,128)S(1)} %collective-permute-done.15.refs_2_, f32[1,256]{1,0:T(1,128)S(1)} %slice_maximum_fusion.refs_3_), custom_call_target="tpu_custom_call" | custom-call | tf_op jit(solution)/shard_map/unpack/pallas_call | solution.py:207
  (3 shorter events, 0.0 us)
Async XLA Ops:
  3.4 48.1 %copy-start.2 = (bf16[272,768]{1,0:T(8,128)(2,1)S(1)}, bf16[272,768]{1,0:T(8,128)(2,1)}, u32[]{:S(2)}) copy-start(bf16[272,768]{1,0:T(8,128)(2,1)} %get-tuple-element.27.refs_1_.refs_13_) | copy-start | bytes 1253380
  3.5 15.0 %collective-permute-start = (bf16[272,768]{1,0:T(8,128)(2,1)}, bf16[272,768]{1,0:T(8,128)(2,1)S(1)}, u32[]{:S(2)}, u32[]{:S(2)}) collective-permute-start(bf16[272,768]{1,0:T(8,128)(2,1)} %get-tuple-element.25), channel_id=1, source_target_pairs={{0,4},{1,5},{2,6},{3,7},{4,8},{5,9},{6,10},{7,11},{8,12},{9,13},{1... | collective-permute-start | bytes 1253384 | tf_op jit(solution)/shard_map/ppermute | solution.py:231
  6.5 15.1 %collective-permute-start.2 = (bf16[272,768]{1,0:T(8,128)(2,1)}, bf16[272,768]{1,0:T(8,128)(2,1)S(1)}, u32[]{:S(2)}, u32[]{:S(2)}) collective-permute-start(bf16[272,768]{1,0:T(8,128)(2,1)} %get-tuple-element.27.refs_1_.refs_13_), channel_id=1, source_target_pairs={{0,2},{1,3},{2,0},{3,1},{4,6},{5,7},{6,4},{7,5},{8,10},{9,11},{10,... | collective-permute-start | bytes 1253384 | tf_op jit(solution)/shard_map/ppermute | solution.py:234
  18.4 12.4 %collective-permute-start.1 = (bf16[272,768]{1,0:T(8,128)(2,1)}, bf16[272,768]{1,0:T(8,128)(2,1)S(1)}, u32[]{:S(2)}, u32[]{:S(2)}) collective-permute-start(bf16[272,768]{1,0:T(8,128)(2,1)} %get-tuple-element.29), channel_id=1, source_target_pairs={{0,12},{1,13},{2,14},{3,15},{4,0},{5,1},{6,2},{7,3},{8,4},{9,5},{1... | collective-permute-start | bytes 1253384 | tf_op jit(solution)/shard_map/ppermute | solution.py:231
  20.2 26.0 %collective-permute-start.11 = (bf16[272,768]{1,0:T(8,128)(2,1)}, bf16[272,768]{1,0:T(8,128)(2,1)S(1)}, u32[]{:S(2)}, u32[]{:S(2)}) collective-permute-start(bf16[272,768]{1,0:T(8,128)(2,1)} %get-tuple-element.30.refs_1_.refs_2_.refs_3_.refs_4_), channel_id=1, source_target_pairs={{0,8},{1,9},{2,10},{3,11},{4,12},{5,13},{6,14},{7,15},{8,0},{9,1},... | collective-permute-start | bytes 1253384 | tf_op jit(solution)/shard_map/ppermute | solution.py:231
  20.2 26.0 %collective-permute-start.17 = (bf16[272,768]{1,0:T(8,128)(2,1)}, bf16[272,768]{1,0:T(8,128)(2,1)S(1)}, u32[]{:S(2)}, u32[]{:S(2)}) collective-permute-start(bf16[272,768]{1,0:T(8,128)(2,1)} %get-tuple-element.30.refs_1_.refs_2_.refs_3_.refs_4_), channel_id=1, source_target_pairs={{0,2},{1,3},{2,0},{3,1},{4,6},{5,7},{6,4},{7,5},{8,10},{9,11},{10,... | collective-permute-start | bytes 1253384 | tf_op jit(solution)/shard_map/ppermute | solution.py:234
  21.7 25.1 %collective-permute-start.5 = (bf16[272,768]{1,0:T(8,128)(2,1)}, bf16[272,768]{1,0:T(8,128)(2,1)S(1)}, u32[]{:S(2)}, u32[]{:S(2)}) collective-permute-start(bf16[272,768]{1,0:T(8,128)(2,1)} %get-tuple-element.27.refs_1_.refs_13_), channel_id=1, source_target_pairs={{0,1},{1,0},{2,3},{3,2},{4,5},{5,4},{6,7},{7,6},{8,9},{9,8},{10,11... | collective-permute-start | bytes 1253384 | tf_op jit(solution)/shard_map/ppermute | solution.py:234
  21.7 25.1 %collective-permute-start.3 = (bf16[272,768]{1,0:T(8,128)(2,1)S(1)}, bf16[272,768]{1,0:T(8,128)(2,1)S(1)}, u32[]{:S(2)}, u32[]{:S(2)}) collective-permute-start(bf16[272,768]{1,0:T(8,128)(2,1)S(1)} %collective-permute-done.refs_2_), channel_id=1, source_target_pairs={{0,2},{1,3},{2,0},{3,1},{4,6},{5,7},{6,4},{7,5},{8,10},{9,11},{10,... | collective-permute-start | bytes 1253384 | tf_op jit(solution)/shard_map/ppermute | solution.py:234
  30.9 17.6 %collective-permute-start.4 = (bf16[272,768]{1,0:T(8,128)(2,1)S(1)}, bf16[272,768]{1,0:T(8,128)(2,1)S(1)}, u32[]{:S(2)}, u32[]{:S(2)}) collective-permute-start(bf16[272,768]{1,0:T(8,128)(2,1)S(1)} %collective-permute-done.1.refs_3_), channel_id=1, source_target_pairs={{0,2},{1,3},{2,0},{3,1},{4,6},{5,7},{6,4},{7,5},{8,10},{9,11},{10,... | collective-permute-start | bytes 1253384 | tf_op jit(solution)/shard_map/ppermute | solution.py:234
  46.2 2.3 %collective-permute-start.12 = (bf16[272,768]{1,0:T(8,128)(2,1)S(1)}, bf16[272,768]{1,0:T(8,128)(2,1)S(1)}, u32[]{:S(2)}, u32[]{:S(2)}) collective-permute-start(bf16[272,768]{1,0:T(8,128)(2,1)S(1)} %collective-permute-done.11.refs_13_.refs_4_.refs_5_), channel_id=1, source_target_pairs={{0,1},{1,0},{2,3},{3,2},{4,5},{5,4},{6,7},{7,6},{8,9},{9,8},{10,11... | collective-permute-start | bytes 1253384 | tf_op jit(solution)/shard_map/ppermute | solution.py:234
  46.2 3.7 %collective-permute-start.6 = (bf16[272,768]{1,0:T(8,128)(2,1)S(1)}, bf16[272,768]{1,0:T(8,128)(2,1)S(1)}, u32[]{:S(2)}, u32[]{:S(2)}) collective-permute-start(bf16[272,768]{1,0:T(8,128)(2,1)S(1)} %collective-permute-done.refs_2_), channel_id=1, source_target_pairs={{0,1},{1,0},{2,3},{3,2},{4,5},{5,4},{6,7},{7,6},{8,9},{9,8},{10,11... | collective-permute-start | bytes 1253384 | tf_op jit(solution)/shard_map/ppermute | solution.py:234
  46.7 3.2 %collective-permute-start.8 = (bf16[272,768]{1,0:T(8,128)(2,1)S(1)}, bf16[272,768]{1,0:T(8,128)(2,1)S(1)}, u32[]{:S(2)}, u32[]{:S(2)}) collective-permute-start(bf16[272,768]{1,0:T(8,128)(2,1)S(1)} %collective-permute-done.2.refs_4_.refs_1_), channel_id=1, source_target_pairs={{0,1},{1,0},{2,3},{3,2},{4,5},{5,4},{6,7},{7,6},{8,9},{9,8},{10,11... | collective-permute-start | bytes 1253384 | tf_op jit(solution)/shard_map/ppermute | solution.py:234
  46.8 4.7 %collective-permute-start.7 = (bf16[272,768]{1,0:T(8,128)(2,1)S(1)}, bf16[272,768]{1,0:T(8,128)(2,1)S(1)}, u32[]{:S(2)}, u32[]{:S(2)}) collective-permute-start(bf16[272,768]{1,0:T(8,128)(2,1)S(1)} %collective-permute-done.1.refs_3_), channel_id=1, source_target_pairs={{0,1},{1,0},{2,3},{3,2},{4,5},{5,4},{6,7},{7,6},{8,9},{9,8},{10,11... | collective-permute-start | bytes 1253384 | tf_op jit(solution)/shard_map/ppermute | solution.py:234
  48.5 3.0 %collective-permute-start.9 = (bf16[272,768]{1,0:T(8,128)(2,1)S(1)}, bf16[272,768]{1,0:T(8,128)(2,1)S(1)}, u32[]{:S(2)}, u32[]{:S(2)}) collective-permute-start(bf16[272,768]{1,0:T(8,128)(2,1)S(1)} %collective-permute-done.3.refs_5_.refs_2_), channel_id=1, source_target_pairs={{0,1},{1,0},{2,3},{3,2},{4,5},{5,4},{6,7},{7,6},{8,9},{9,8},{10,11... | collective-permute-start | bytes 1253384 | tf_op jit(solution)/shard_map/ppermute | solution.py:234
  48.5 3.0 %collective-permute-start.10 = (bf16[272,768]{1,0:T(8,128)(2,1)S(1)}, bf16[272,768]{1,0:T(8,128)(2,1)S(1)}, u32[]{:S(2)}, u32[]{:S(2)}) collective-permute-start(bf16[272,768]{1,0:T(8,128)(2,1)S(1)} %collective-permute-done.4.refs_6_.refs_3_), channel_id=1, source_target_pairs={{0,1},{1,0},{2,3},{3,2},{4,5},{5,4},{6,7},{7,6},{8,9},{9,8},{10,11... | collective-permute-start | bytes 1253384 | tf_op jit(solution)/shard_map/ppermute | solution.py:234
  49.9 12.8 %collective-permute-start.18 = (bf16[272,768]{1,0:T(8,128)(2,1)S(1)}, bf16[272,768]{1,0:T(8,128)(2,1)S(1)}, u32[]{:S(2)}, u32[]{:S(2)}) collective-permute-start(bf16[272,768]{1,0:T(8,128)(2,1)S(1)} %collective-permute-done.17.refs_5_), channel_id=1, source_target_pairs={{0,1},{1,0},{2,3},{3,2},{4,5},{5,4},{6,7},{7,6},{8,9},{9,8},{10,11... | collective-permute-start | bytes 1253384 | tf_op jit(solution)/shard_map/ppermute | solution.py:234
  50.0 8.0 %collective-permute-start.13 = (f32[1,1024]{1,0:T(1,128)S(1)}, f32[1,1024]{1,0:T(1,128)S(1)}, u32[]{:S(2)}, u32[]{:S(2)}) collective-permute-start(f32[1,1024]{1,0:T(1,128)S(1)} %compare1_6.1), channel_id=1, source_target_pairs={{0,2},{1,3},{2,0},{3,1},{4,6},{5,7},{6,4},{7,5},{8,10},{9,11},{10,... | collective-permute-start | bytes 12296 | tf_op jit(solution)/shard_map/ppermute | solution.py:234
  55.6 7.1 %copy-start = (bf16[272,768]{1,0:T(8,128)(2,1)S(1)}, bf16[272,768]{1,0:T(8,128)(2,1)}, u32[]{:S(2)}) copy-start(bf16[272,768]{1,0:T(8,128)(2,1)} %get-tuple-element.30.refs_1_.refs_2_.refs_3_.refs_4_) | copy-start | bytes 1253380
  58.0 8.4 %copy-start.1 = (s32[1,512]{1,0:T(1,128)S(1)}, s32[1,512]{1,0:T(1,128)}, u32[]{:S(2)}) copy-start(s32[1,512]{1,0:T(1,128)} %get-tuple-element.21.slot_ref) | copy-start | bytes 6148
  58.0 8.4 %collective-permute-start.15 = (f32[1,256]{1,0:T(1,128)S(1)}, f32[1,256]{1,0:T(1,128)S(1)}, u32[]{:S(2)}, u32[]{:S(2)}) collective-permute-start(f32[1,256]{1,0:T(1,128)S(1)} %get-tuple-element.37), channel_id=1, source_target_pairs={{0,4},{1,5},{2,6},{3,7},{4,8},{5,9},{6,10},{7,11},{8,12},{9,13},{1... | collective-permute-start | bytes 3080 | tf_op jit(solution)/shard_map/ppermute | solution.py:231
  58.8 7.6 %collective-permute-start.14 = (f32[1,256]{1,0:T(1,128)S(1)}, f32[1,256]{1,0:T(1,128)S(1)}, u32[]{:S(2)}, u32[]{:S(2)}) collective-permute-start(f32[1,256]{1,0:T(1,128)S(1)} %get-tuple-element.38), channel_id=1, source_target_pairs={{0,12},{1,13},{2,14},{3,15},{4,0},{5,1},{6,2},{7,3},{8,4},{9,5},{1... | collective-permute-start | bytes 3080 | tf_op jit(solution)/shard_map/ppermute | solution.py:231
  61.9 4.5 %collective-permute-start.16 = (f32[1,256]{1,0:T(1,128)S(1)}, f32[1,256]{1,0:T(1,128)S(1)}, u32[]{:S(2)}, u32[]{:S(2)}) collective-permute-start(f32[1,256]{1,0:T(1,128)S(1)} %get-tuple-element.35), channel_id=1, source_target_pairs={{0,8},{1,9},{2,10},{3,11},{4,12},{5,13},{6,14},{7,15},{8,0},{9,1},... | collective-permute-start | bytes 3080 | tf_op jit(solution)/shard_map/ppermute | solution.py:231

commit v12 on v11

--- a/solution.py
+++ b/solution.py
@@ -291,11 +291,9 @@
         some |= {(0, 3): own[3], (1, 3): own[3], (2, 3): beside[3]}
         (theirs,) = compare(cap, row, [(0, 3, 3, (1, 2))], some, floor)
         mine = swap(theirs, 2)
-        some = given(every, range(3)) | {(0, 3): own[0]}
-        (best,) = compare(cap, row, [(0, 3, k, every) for k in range(3)], some, floor)
-        jobs = [(3, 4, k, every) for k in range(3)] + [(0, 4, 3, (0, 2))]
+        jobs = [(0, 4, k, every) for k in range(3)] + [(0, 4, 3, (0, 2))]
         some = given(every, range(3)) | given((0, 2), (3,))
-        best = list(compare(cap, pieces, jobs, some, best))
+        best = list(compare(cap, pieces, jobs, some, floor))
         for k in range(3):
             best[k] = jnp.maximum(best[k], mine[:, k * cap : (k + 1) * cap])
         backs = [exchange(b, low, 1, -1) for b, (low, _) in zip(best, pieces)]

time: 67.6 us -> 67.4 us (level)
    pallas_call x4 -> x3, Pallas kernels: 7.62 us -> 7.36 us  [compare(): pl.pallas_call(lambda *refs: compare_kernel(cap, outs, jobs, names, *refs...]
  transfers between devices with their start and end apart: 19 -> 19, of which waited for: 5 -> 6; matrix products, arithmetic and copies ran while one was open for 0% -> 0% of each run, Pallas kernels for 11% -> 11%
where the time goes in v12:
time: 67.4 us; the launch traced here: 67.2 us
  waiting for transfers between devices  37.8 us (56%)
  starting transfers between devices  17.4 us (26%)
  Pallas kernels  11.9 us (18%)
    ppermute x6, waiting for transfers between devices, shift(): lax.ppermute(array, 'blk', [(i, (i + step) % devices) for i in range(devi...  36.5 us
    ppermute x6, starting transfers between devices, shift(): lax.ppermute(array, 'blk', [(i, (i + step) % devices) for i in range(devi...  9.54 us
    ppermute x13, starting transfers between devices, swap(): return lax.ppermute(array, 'blk', [(i, i ^ mask) for i in range(devices)])  7.87 us
    pallas_call x3, Pallas kernels, compare(): pl.pallas_call(lambda *refs: compare_kernel(cap, outs, jobs, names, *refs...  7.36 us
    pallas_call x1, Pallas kernels, pack(): pl.pallas_call(lambda *refs: pack_kernel(groups, cap, units, *refs), in_s...  3.44 us
  transfers between devices with their start and end apart: 19, of which 6 were waited for; matrix products, arithmetic and copies ran while one was open for 0% of the time, Pallas kernels for 11%

profile of v12, /device:TPU:0, one launch (start us, length us, event | category | flops | bytes accessed | tf_op | source)
XLA Modules:
  0.0 67.2 jit_solution(1663867086575427909)
XLA Ops:
  0.0 3.4 %pack.1 = (bf16[272,768]{1,0:T(8,128)(2,1)}, bf16[272,768]{1,0:T(8,128)(2,1)}, bf16[272,768]{1,0:T(8,128)(2,1)}, bf16[272,768]{1,0:T(8,128)(2,1)}, s32[1,512]{1,0:T(1,128)}) custom-call(f32[512,768]{1,0:T(8,128)} %refs_0_.1, s32[1,512]{1,0:T(1,128)} %bitcast.3, s32[1,512]{1,0:T(1,128)} %bitcast.4), custom_call_target="tpu_custom_call" | custom-call | tf_op jit(solution)/shard_map/pack/pallas_call | solution.py:79
  3.4 0.0 copy-start.2
  3.5 3.1 %collective-permute-start = (bf16[272,768]{1,0:T(8,128)(2,1)}, bf16[272,768]{1,0:T(8,128)(2,1)S(1)}, u32[]{:S(2)}, u32[]{:S(2)}) collective-permute-start(bf16[272,768]{1,0:T(8,128)(2,1)} %get-tuple-element.25), channel_id=1, source_target_pairs={{0,4},{1,5},{2,6},{3,7},{4,8},{5,9},{6,10},{7,11},{8,12},{9,13},{1... | collective-permute-start | bytes 1253384 | tf_op jit(solution)/shard_map/ppermute | solution.py:231
  6.5 1.5 %collective-permute-start.2 = (bf16[272,768]{1,0:T(8,128)(2,1)}, bf16[272,768]{1,0:T(8,128)(2,1)S(1)}, u32[]{:S(2)}, u32[]{:S(2)}) collective-permute-start(bf16[272,768]{1,0:T(8,128)(2,1)} %get-tuple-element.27.refs_1_), channel_id=1, source_target_pairs={{0,2},{1,3},{2,0},{3,1},{4,6},{5,7},{6,4},{7,5},{8,10},{9,11},{10,... | collective-permute-start | bytes 1253384 | tf_op jit(solution)/shard_map/ppermute | solution.py:234
  8.0 10.4 %collective-permute-done.refs_2_ = bf16[272,768]{1,0:T(8,128)(2,1)S(1)} collective-permute-done((bf16[272,768]{1,0:T(8,128)(2,1)}, bf16[272,768]{1,0:T(8,128)(2,1)S(1)}, u32[]{:S(2)}, u32[]{:S(2)}) %collective-permute-start) | collective-permute-done | bytes 417824 | tf_op jit(solution)/shard_map/ppermute | solution.py:231
  18.4 1.7 %collective-permute-start.1 = (bf16[272,768]{1,0:T(8,128)(2,1)}, bf16[272,768]{1,0:T(8,128)(2,1)S(1)}, u32[]{:S(2)}, u32[]{:S(2)}) collective-permute-start(bf16[272,768]{1,0:T(8,128)(2,1)} %get-tuple-element.29), channel_id=1, source_target_pairs={{0,12},{1,13},{2,14},{3,15},{4,0},{5,1},{6,2},{7,3},{8,4},{9,5},{1... | collective-permute-start | bytes 1253384 | tf_op jit(solution)/shard_map/ppermute | solution.py:231
  20.2 0.0 collective-permute-start.11
  20.2 1.5 %collective-permute-start.17 = (bf16[272,768]{1,0:T(8,128)(2,1)}, bf16[272,768]{1,0:T(8,128)(2,1)S(1)}, u32[]{:S(2)}, u32[]{:S(2)}) collective-permute-start(bf16[272,768]{1,0:T(8,128)(2,1)} %get-tuple-element.30.refs_1_.refs_2_.refs_3_.refs_4_), channel_id=1, source_target_pairs={{0,2},{1,3},{2,0},{3,1},{4,6},{5,7},{6,4},{7,5},{8,10},{9,11},{10,... | collective-permute-start | bytes 1253384 | tf_op jit(solution)/shard_map/ppermute | solution.py:234
  21.7 0.5 collective-permute-start.3
  22.2 0.0 collective-permute-done.2.refs_4_.refs_1_
  22.2 0.0 collective-permute-start.5
  22.2 8.7 %collective-permute-done.1.refs_3_ = bf16[272,768]{1,0:T(8,128)(2,1)S(1)} collective-permute-done((bf16[272,768]{1,0:T(8,128)(2,1)}, bf16[272,768]{1,0:T(8,128)(2,1)S(1)}, u32[]{:S(2)}, u32[]{:S(2)}) %collective-permute-start.1) | collective-permute-done | bytes 417824 | tf_op jit(solution)/shard_map/ppermute | solution.py:231
  30.9 1.2 %collective-permute-start.4 = (bf16[272,768]{1,0:T(8,128)(2,1)S(1)}, bf16[272,768]{1,0:T(8,128)(2,1)S(1)}, u32[]{:S(2)}, u32[]{:S(2)}) collective-permute-start(bf16[272,768]{1,0:T(8,128)(2,1)S(1)} %collective-permute-done.1.refs_3_), channel_id=1, source_target_pairs={{0,2},{1,3},{2,0},{3,1},{4,6},{5,7},{6,4},{7,5},{8,10},{9,11},{10,... | collective-permute-start | bytes 1253384 | tf_op jit(solution)/shard_map/ppermute | solution.py:234
  32.1 14.1 %collective-permute-done.11.refs_13_.refs_4_.refs_5_ = bf16[272,768]{1,0:T(8,128)(2,1)S(1)} collective-permute-done((bf16[272,768]{1,0:T(8,128)(2,1)}, bf16[272,768]{1,0:T(8,128)(2,1)S(1)}, u32[]{:S(2)}, u32[]{:S(2)}) %collective-permute-start.11) | collective-permute-done | bytes 417824 | tf_op jit(solution)/shard_map/ppermute | solution.py:231
  46.2 0.0 collective-permute-start.12
  46.2 0.0 collective-permute-done.17.refs_5_
  46.2 0.5 collective-permute-start.6
  46.7 0.0 collective-permute-done.3.refs_5_.refs_2_
  46.7 0.1 collective-permute-start.8
  46.8 0.0 collective-permute-done.5.refs_7_
  46.8 0.4 collective-permute-start.7
  47.2 1.3 %collective-permute-done.4.refs_6_.refs_3_ = bf16[272,768]{1,0:T(8,128)(2,1)S(1)} collective-permute-done((bf16[272,768]{1,0:T(8,128)(2,1)S(1)}, bf16[272,768]{1,0:T(8,128)(2,1)S(1)}, u32[]{:S(2)}, u32[]{:S(2)}) %collective-permute-start.4) | collective-permute-done | bytes 417824 | tf_op jit(solution)/shard_map/ppermute | solution.py:234
  48.5 0.0 collective-permute-start.9
  48.5 0.0 collective-permute-done.12.refs_14_.refs_6_
  48.5 0.5 collective-permute-start.10
  49.0 0.8 %compare1_6.1 = f32[1,1024]{1,0:T(1,128)S(1)} custom-call(f32[1,1024]{1,0:T(1,128)S(1)} %broadcast_in_dim.3.refs_0_, bf16[272,768]{1,0:T(8,128)(2,1)S(1)} %collective-permute-done.2.refs_4_.refs_1_, bf16[272,768]{1,0:T(8,128)(2,1)S(1)} %collective-permute-done.3.refs_5_.refs_2_, bf16[272,768]{1,0:T(8,128)(2,1)S(1)} %collective-permute-done.4.refs_6_.refs_3_, ...), custom_call_target="tpu_custom_call" | custom-call | flops 603979776 | tf_op jit(solution)/shard_map/compare1_6/pallas_call | solution.py:177
  49.9 0.0 copy-start
  49.9 0.0 collective-permute-done.6.refs_8_
  49.9 0.1 collective-permute-start.18
  50.0 0.0 collective-permute-done.8.refs_10_
  50.0 1.6 %collective-permute-start.13 = (f32[1,1024]{1,0:T(1,128)S(1)}, f32[1,1024]{1,0:T(1,128)S(1)}, u32[]{:S(2)}, u32[]{:S(2)}) collective-permute-start(f32[1,1024]{1,0:T(1,128)S(1)} %compare1_6.1), channel_id=1, source_target_pairs={{0,2},{1,3},{2,0},{3,1},{4,6},{5,7},{6,4},{7,5},{8,10},{9,11},{10,... | collective-permute-start | bytes 12296 | tf_op jit(solution)/shard_map/ppermute | solution.py:234
  51.5 0.0 collective-permute-done.7.refs_9_
  51.5 0.0 collective-permute-done.9.refs_11_
  51.5 0.0 collective-permute-done.10.refs_12_
  51.5 0.0 copy-done.2
  51.6 6.1 %compare4_56.1 = (f32[1,256]{1,0:T(1,128)S(1)}, f32[1,256]{1,0:T(1,128)S(1)}, f32[1,256]{1,0:T(1,128)S(1)}, f32[1,256]{1,0:T(1,128)S(1)}) custom-call(f32[1,1024]{1,0:T(1,128)S(1)} %broadcast_in_dim.3.refs_0_, bf16[272,768]{1,0:T(8,128)(2,1)S(1)} %copy-done.2, bf16[272,768]{1,0:T(8,128)(2,1)S(1)} %collective-permute-done.refs_2_, ...), custom_call_target="tpu_custom_call" | custom-call | flops 5637144576 | tf_op jit(solution)/shard_map/compare4_56/pallas_call | solution.py:177
  57.6 0.0 copy-start.1
  57.7 0.0 collective-permute-done.13
  57.7 3.1 %collective-permute-start.14 = (f32[1,256]{1,0:T(1,128)S(1)}, f32[1,256]{1,0:T(1,128)S(1)}, u32[]{:S(2)}, u32[]{:S(2)}) collective-permute-start(f32[1,256]{1,0:T(1,128)S(1)} %get-tuple-element.38), channel_id=1, source_target_pairs={{0,12},{1,13},{2,14},{3,15},{4,0},{5,1},{6,2},{7,3},{8,4},{9,5},{1... | collective-permute-start | bytes 3080 | tf_op jit(solution)/shard_map/ppermute | solution.py:231
  60.8 0.0 collective-permute-start.15
  60.8 1.6 %collective-permute-start.16 = (f32[1,256]{1,0:T(1,128)S(1)}, f32[1,256]{1,0:T(1,128)S(1)}, u32[]{:S(2)}, u32[]{:S(2)}) collective-permute-start(f32[1,256]{1,0:T(1,128)S(1)} %get-tuple-element.35), channel_id=1, source_target_pairs={{0,8},{1,9},{2,10},{3,11},{4,12},{5,13},{6,14},{7,15},{8,0},{9,1},... | collective-permute-start | bytes 3080 | tf_op jit(solution)/shard_map/ppermute | solution.py:231
  62.4 0.0 collective-permute-done.18.refs_6_
  62.4 0.0 copy-done
  62.4 0.4 compare1_2.1
  62.9 2.4 %collective-permute-done.16 = f32[1,256]{1,0:T(1,128)S(1)} collective-permute-done((f32[1,256]{1,0:T(1,128)S(1)}, f32[1,256]{1,0:T(1,128)S(1)}, u32[]{:S(2)}, u32[]{:S(2)}) %collective-permute-start.16) | collective-permute-done | bytes 1056 | tf_op jit(solution)/shard_map/ppermute | solution.py:231
  65.3 0.0 collective-permute-done.14.refs_1_
  65.3 0.9 %collective-permute-done.15.refs_2_ = f32[1,256]{1,0:T(1,128)S(1)} collective-permute-done((f32[1,256]{1,0:T(1,128)S(1)}, f32[1,256]{1,0:T(1,128)S(1)}, u32[]{:S(2)}, u32[]{:S(2)}) %collective-permute-start.15) | collective-permute-done | bytes 1056 | tf_op jit(solution)/shard_map/ppermute | solution.py:231
  66.1 0.0 copy-done.1
  66.2 1.1 %unpack.1 = f32[1,512]{1,0:T(1,128)} custom-call(s32[1,512]{1,0:T(1,128)S(1)} %copy-done.1, f32[1,256]{1,0:T(1,128)S(1)} %get-tuple-element.32.refs_0_, f32[1,256]{1,0:T(1,128)S(1)} %collective-permute-done.14.refs_1_, f32[1,256]{1,0:T(1,128)S(1)} %collective-permute-done.15.refs_2_, f32[1,256]{1,0:T(1,128)S(1)} %slice_maximum_fusion.refs_3_), custom_call_target="tpu_custom_call" | custom-call | tf_op jit(solution)/shard_map/unpack/pallas_call | solution.py:207
  (3 shorter events, 0.0 us)
Async XLA Ops:
  3.4 48.1 %copy-start.2 = (bf16[272,768]{1,0:T(8,128)(2,1)S(1)}, bf16[272,768]{1,0:T(8,128)(2,1)}, u32[]{:S(2)}) copy-start(bf16[272,768]{1,0:T(8,128)(2,1)} %get-tuple-element.27.refs_1_) | copy-start | bytes 1253380
  3.5 15.0 %collective-permute-start = (bf16[272,768]{1,0:T(8,128)(2,1)}, bf16[272,768]{1,0:T(8,128)(2,1)S(1)}, u32[]{:S(2)}, u32[]{:S(2)}) collective-permute-start(bf16[272,768]{1,0:T(8,128)(2,1)} %get-tuple-element.25), channel_id=1, source_target_pairs={{0,4},{1,5},{2,6},{3,7},{4,8},{5,9},{6,10},{7,11},{8,12},{9,13},{1... | collective-permute-start | bytes 1253384 | tf_op jit(solution)/shard_map/ppermute | solution.py:231
  6.5 15.7 %collective-permute-start.2 = (bf16[272,768]{1,0:T(8,128)(2,1)}, bf16[272,768]{1,0:T(8,128)(2,1)S(1)}, u32[]{:S(2)}, u32[]{:S(2)}) collective-permute-start(bf16[272,768]{1,0:T(8,128)(2,1)} %get-tuple-element.27.refs_1_), channel_id=1, source_target_pairs={{0,2},{1,3},{2,0},{3,1},{4,6},{5,7},{6,4},{7,5},{8,10},{9,11},{10,... | collective-permute-start | bytes 1253384 | tf_op jit(solution)/shard_map/ppermute | solution.py:234
  18.4 12.4 %collective-permute-start.1 = (bf16[272,768]{1,0:T(8,128)(2,1)}, bf16[272,768]{1,0:T(8,128)(2,1)S(1)}, u32[]{:S(2)}, u32[]{:S(2)}) collective-permute-start(bf16[272,768]{1,0:T(8,128)(2,1)} %get-tuple-element.29), channel_id=1, source_target_pairs={{0,12},{1,13},{2,14},{3,15},{4,0},{5,1},{6,2},{7,3},{8,4},{9,5},{1... | collective-permute-start | bytes 1253384 | tf_op jit(solution)/shard_map/ppermute | solution.py:231
  20.2 26.0 %collective-permute-start.11 = (bf16[272,768]{1,0:T(8,128)(2,1)}, bf16[272,768]{1,0:T(8,128)(2,1)S(1)}, u32[]{:S(2)}, u32[]{:S(2)}) collective-permute-start(bf16[272,768]{1,0:T(8,128)(2,1)} %get-tuple-element.30.refs_1_.refs_2_.refs_3_.refs_4_), channel_id=1, source_target_pairs={{0,8},{1,9},{2,10},{3,11},{4,12},{5,13},{6,14},{7,15},{8,0},{9,1},... | collective-permute-start | bytes 1253384 | tf_op jit(solution)/shard_map/ppermute | solution.py:231
  20.2 26.0 %collective-permute-start.17 = (bf16[272,768]{1,0:T(8,128)(2,1)}, bf16[272,768]{1,0:T(8,128)(2,1)S(1)}, u32[]{:S(2)}, u32[]{:S(2)}) collective-permute-start(bf16[272,768]{1,0:T(8,128)(2,1)} %get-tuple-element.30.refs_1_.refs_2_.refs_3_.refs_4_), channel_id=1, source_target_pairs={{0,2},{1,3},{2,0},{3,1},{4,6},{5,7},{6,4},{7,5},{8,10},{9,11},{10,... | collective-permute-start | bytes 1253384 | tf_op jit(solution)/shard_map/ppermute | solution.py:234
  21.7 25.1 %collective-permute-start.3 = (bf16[272,768]{1,0:T(8,128)(2,1)S(1)}, bf16[272,768]{1,0:T(8,128)(2,1)S(1)}, u32[]{:S(2)}, u32[]{:S(2)}) collective-permute-start(bf16[272,768]{1,0:T(8,128)(2,1)S(1)} %collective-permute-done.refs_2_), channel_id=1, source_target_pairs={{0,2},{1,3},{2,0},{3,1},{4,6},{5,7},{6,4},{7,5},{8,10},{9,11},{10,... | collective-permute-start | bytes 1253384 | tf_op jit(solution)/shard_map/ppermute | solution.py:234
  22.2 24.6 %collective-permute-start.5 = (bf16[272,768]{1,0:T(8,128)(2,1)}, bf16[272,768]{1,0:T(8,128)(2,1)S(1)}, u32[]{:S(2)}, u32[]{:S(2)}) collective-permute-start(bf16[272,768]{1,0:T(8,128)(2,1)} %get-tuple-element.27.refs_1_), channel_id=1, source_target_pairs={{0,1},{1,0},{2,3},{3,2},{4,5},{5,4},{6,7},{7,6},{8,9},{9,8},{10,11... | collective-permute-start | bytes 1253384 | tf_op jit(solution)/shard_map/ppermute | solution.py:234
  30.9 17.6 %collective-permute-start.4 = (bf16[272,768]{1,0:T(8,128)(2,1)S(1)}, bf16[272,768]{1,0:T(8,128)(2,1)S(1)}, u32[]{:S(2)}, u32[]{:S(2)}) collective-permute-start(bf16[272,768]{1,0:T(8,128)(2,1)S(1)} %collective-permute-done.1.refs_3_), channel_id=1, source_target_pairs={{0,2},{1,3},{2,0},{3,1},{4,6},{5,7},{6,4},{7,5},{8,10},{9,11},{10,... | collective-permute-start | bytes 1253384 | tf_op jit(solution)/shard_map/ppermute | solution.py:234
  46.2 2.3 %collective-permute-start.12 = (bf16[272,768]{1,0:T(8,128)(2,1)S(1)}, bf16[272,768]{1,0:T(8,128)(2,1)S(1)}, u32[]{:S(2)}, u32[]{:S(2)}) collective-permute-start(bf16[272,768]{1,0:T(8,128)(2,1)S(1)} %collective-permute-done.11.refs_13_.refs_4_.refs_5_), channel_id=1, source_target_pairs={{0,1},{1,0},{2,3},{3,2},{4,5},{5,4},{6,7},{7,6},{8,9},{9,8},{10,11... | collective-permute-start | bytes 1253384 | tf_op jit(solution)/shard_map/ppermute | solution.py:234
  46.2 3.7 %collective-permute-start.6 = (bf16[272,768]{1,0:T(8,128)(2,1)S(1)}, bf16[272,768]{1,0:T(8,128)(2,1)S(1)}, u32[]{:S(2)}, u32[]{:S(2)}) collective-permute-start(bf16[272,768]{1,0:T(8,128)(2,1)S(1)} %collective-permute-done.refs_2_), channel_id=1, source_target_pairs={{0,1},{1,0},{2,3},{3,2},{4,5},{5,4},{6,7},{7,6},{8,9},{9,8},{10,11... | collective-permute-start | bytes 1253384 | tf_op jit(solution)/shard_map/ppermute | solution.py:234
  46.7 3.3 %collective-permute-start.8 = (bf16[272,768]{1,0:T(8,128)(2,1)S(1)}, bf16[272,768]{1,0:T(8,128)(2,1)S(1)}, u32[]{:S(2)}, u32[]{:S(2)}) collective-permute-start(bf16[272,768]{1,0:T(8,128)(2,1)S(1)} %collective-permute-done.2.refs_4_.refs_1_), channel_id=1, source_target_pairs={{0,1},{1,0},{2,3},{3,2},{4,5},{5,4},{6,7},{7,6},{8,9},{9,8},{10,11... | collective-permute-start | bytes 1253384 | tf_op jit(solution)/shard_map/ppermute | solution.py:234
  46.8 4.7 %collective-permute-start.7 = (bf16[272,768]{1,0:T(8,128)(2,1)S(1)}, bf16[272,768]{1,0:T(8,128)(2,1)S(1)}, u32[]{:S(2)}, u32[]{:S(2)}) collective-permute-start(bf16[272,768]{1,0:T(8,128)(2,1)S(1)} %collective-permute-done.1.refs_3_), channel_id=1, source_target_pairs={{0,1},{1,0},{2,3},{3,2},{4,5},{5,4},{6,7},{7,6},{8,9},{9,8},{10,11... | collective-permute-start | bytes 1253384 | tf_op jit(solution)/shard_map/ppermute | solution.py:234
  48.5 3.0 %collective-permute-start.9 = (bf16[272,768]{1,0:T(8,128)(2,1)S(1)}, bf16[272,768]{1,0:T(8,128)(2,1)S(1)}, u32[]{:S(2)}, u32[]{:S(2)}) collective-permute-start(bf16[272,768]{1,0:T(8,128)(2,1)S(1)} %collective-permute-done.3.refs_5_.refs_2_), channel_id=1, source_target_pairs={{0,1},{1,0},{2,3},{3,2},{4,5},{5,4},{6,7},{7,6},{8,9},{9,8},{10,11... | collective-permute-start | bytes 1253384 | tf_op jit(solution)/shard_map/ppermute | solution.py:234
  48.5 3.0 %collective-permute-start.10 = (bf16[272,768]{1,0:T(8,128)(2,1)S(1)}, bf16[272,768]{1,0:T(8,128)(2,1)S(1)}, u32[]{:S(2)}, u32[]{:S(2)}) collective-permute-start(bf16[272,768]{1,0:T(8,128)(2,1)S(1)} %collective-permute-done.4.refs_6_.refs_3_), channel_id=1, source_target_pairs={{0,1},{1,0},{2,3},{3,2},{4,5},{5,4},{6,7},{7,6},{8,9},{9,8},{10,11... | collective-permute-start | bytes 1253384 | tf_op jit(solution)/shard_map/ppermute | solution.py:234
  49.9 12.5 %copy-start = (bf16[272,768]{1,0:T(8,128)(2,1)S(1)}, bf16[272,768]{1,0:T(8,128)(2,1)}, u32[]{:S(2)}) copy-start(bf16[272,768]{1,0:T(8,128)(2,1)} %get-tuple-element.30.refs_1_.refs_2_.refs_3_.refs_4_) | copy-start | bytes 1253380
  49.9 12.5 %collective-permute-start.18 = (bf16[272,768]{1,0:T(8,128)(2,1)S(1)}, bf16[272,768]{1,0:T(8,128)(2,1)S(1)}, u32[]{:S(2)}, u32[]{:S(2)}) collective-permute-start(bf16[272,768]{1,0:T(8,128)(2,1)S(1)} %collective-permute-done.17.refs_5_), channel_id=1, source_target_pairs={{0,1},{1,0},{2,3},{3,2},{4,5},{5,4},{6,7},{7,6},{8,9},{9,8},{10,11... | collective-permute-start | bytes 1253384 | tf_op jit(solution)/shard_map/ppermute | solution.py:234
  50.0 7.7 %collective-permute-start.13 = (f32[1,1024]{1,0:T(1,128)S(1)}, f32[1,1024]{1,0:T(1,128)S(1)}, u32[]{:S(2)}, u32[]{:S(2)}) collective-permute-start(f32[1,1024]{1,0:T(1,128)S(1)} %compare1_6.1), channel_id=1, source_target_pairs={{0,2},{1,3},{2,0},{3,1},{4,6},{5,7},{6,4},{7,5},{8,10},{9,11},{10,... | collective-permute-start | bytes 12296 | tf_op jit(solution)/shard_map/ppermute | solution.py:234
  57.6 8.5 %copy-start.1 = (s32[1,512]{1,0:T(1,128)S(1)}, s32[1,512]{1,0:T(1,128)}, u32[]{:S(2)}) copy-start(s32[1,512]{1,0:T(1,128)} %get-tuple-element.21.slot_ref) | copy-start | bytes 6148
  57.7 7.6 %collective-permute-start.14 = (f32[1,256]{1,0:T(1,128)S(1)}, f32[1,256]{1,0:T(1,128)S(1)}, u32[]{:S(2)}, u32[]{:S(2)}) collective-permute-start(f32[1,256]{1,0:T(1,128)S(1)} %get-tuple-element.38), channel_id=1, source_target_pairs={{0,12},{1,13},{2,14},{3,15},{4,0},{5,1},{6,2},{7,3},{8,4},{9,5},{1... | collective-permute-start | bytes 3080 | tf_op jit(solution)/shard_map/ppermute | solution.py:231
  60.8 5.4 %collective-permute-start.15 = (f32[1,256]{1,0:T(1,128)S(1)}, f32[1,256]{1,0:T(1,128)S(1)}, u32[]{:S(2)}, u32[]{:S(2)}) collective-permute-start(f32[1,256]{1,0:T(1,128)S(1)} %get-tuple-element.37), channel_id=1, source_target_pairs={{0,4},{1,5},{2,6},{3,7},{4,8},{5,9},{6,10},{7,11},{8,12},{9,13},{1... | collective-permute-start | bytes 3080 | tf_op jit(solution)/shard_map/ppermute | solution.py:231
  60.8 4.5 %collective-permute-start.16 = (f32[1,256]{1,0:T(1,128)S(1)}, f32[1,256]{1,0:T(1,128)S(1)}, u32[]{:S(2)}, u32[]{:S(2)}) collective-permute-start(f32[1,256]{1,0:T(1,128)S(1)} %get-tuple-element.35), channel_id=1, source_target_pairs={{0,8},{1,9},{2,10},{3,11},{4,12},{5,13},{6,14},{7,15},{8,0},{9,1},... | collective-permute-start | bytes 3080 | tf_op jit(solution)/shard_map/ppermute | solution.py:231
